TPU v7x, 32 devices: a whole 2x2x4 slice. The times are simulated.
32 devices in a mesh: gz: 8 (over y, x, core), gy: 4 (over z).
Axes of the slice: x: 2, y: 2, z: 4, core: 2. Of those that a mesh axis runs over, the one named last changes fastest.
Arguments:
- velocity: float32 [3, 128, 128, 512], P(None, 'gz', 'gy'), may hold values from -5 to 8
- diffusion: float32 [128, 512], P('gy'), may hold values from 0.5 to 1000
- wall_types: int32 [128, 512], P('gy'), may hold values from 0 to 3
- stretch_index: int32 [128], replicated, may hold values from 0 to 6
- bulk_target: float32 [1], replicated, may hold values from 0.5 to 1.5
Outputs:
- velocity_out: float32 [3, 128, 128, 512], P(None, 'gz', 'gy')
All inputs are finite; a program needn't handle non-finite values.
Results may differ from a plain program's by a relative error of at most 0.0028.
Values sent between devices are 32-bit elements; how exact they have to be, the bound alone decides.
No kernel may reach another device: no remote copies, remote signals or barrier semaphores. Data moves between devices by JAX's collectives and lax.ppermute only.
A program may use at most 192 MiB of HBM per device.

v0:
```python
import jax
import jax.numpy as jnp
from jax import lax
from jax.sharding import PartitionSpec as P


def from_behind(block, axis, distance):
    devices = range(lax.axis_size(axis))
    route = [(i - distance, i) for i in devices if i - distance in devices]
    return lax.ppermute(block, axis, route)


def spacing(stretch_index):
    return 0.5 + 0.25 * stretch_index.astype(jnp.float32)


def face_tables(heights):
    faces = 2.0 / (heights[:-1] + heights[1:])
    padding = jnp.zeros((1,), jnp.float32)
    return (jnp.concatenate([padding, faces]), jnp.concatenate([faces, padding]))


def cell_rows(heights, face_left, face_right, is_first, is_last, diffusion, lower_wall, upper_wall):
    left_sum = face_left + is_first * lower_wall
    right_sum = face_right + is_last * upper_wall
    diagonal = heights + diffusion * (left_sum + right_sum)
    return (-diffusion * face_left, diagonal, -diffusion * face_right)


def scan_thomas(lower_band, diagonal, upper_band, rhs_rows):

    def forward(carry, row_data):
        ratio_prev, value_prev = carry
        low_row, diag_row, upper_row, right_row = row_data
        divisor = diag_row - low_row * ratio_prev
        factor = upper_row / divisor
        solved_row = (right_row - low_row[None] * value_prev) / divisor[None]
        return ((factor, solved_row), (factor, solved_row))

    zero_state = (
        jnp.zeros(diagonal.shape[1:], jnp.float32),
        jnp.zeros(rhs_rows.shape[1:], jnp.float32),
    )
    _, (factors, values) = lax.scan(
        forward, zero_state, (lower_band, diagonal, upper_band, rhs_rows)
    )

    def backward(following, row_data):
        factor, solved_row = row_data
        current = solved_row - factor[None] * following
        return (current, current)

    _, solved = lax.scan(
        backward, jnp.zeros(rhs_rows.shape[1:], jnp.float32), (factors, values), reverse=True
    )
    return solved


def corrected(streamwise, potential, heights, bulk_target, volume):
    partial_flow = jnp.sum(heights[:, None, None] * streamwise)
    partial_weight = jnp.sum(heights[:, None, None] * potential)
    flow_total, weight_total = lax.psum((partial_flow, partial_weight), ("gz", "gy"))
    return streamwise + (bulk_target[0] * volume - flow_total) / weight_total * potential


def shards(velocity, diffusion, wall_types, stretch_index, bulk_target):
    position = lax.axis_index("gz")
    devices_z = lax.axis_size("gz")
    local_cells = velocity.shape[1]
    lines_y = velocity.shape[2]
    lines_x = velocity.shape[3]
    cells_total = local_cells * devices_z
    heights_all = spacing(stretch_index)
    left_all, right_all = face_tables(heights_all)
    volume = jnp.sum(heights_all) * (lines_y * lax.axis_size("gy")) * lines_x
    bottom_flag = (wall_types % 2).astype(jnp.float32)
    top_flag = (wall_types // 2).astype(jnp.float32)
    lower_wall = bottom_flag * (2.0 / heights_all[0])
    upper_wall = top_flag * (2.0 / heights_all[cells_total - 1])
    offset = position * local_cells
    heights = lax.dynamic_slice_in_dim(heights_all, offset, local_cells)
    face_left = lax.dynamic_slice_in_dim(left_all, offset, local_cells)
    face_right = lax.dynamic_slice_in_dim(right_all, offset, local_cells)
    cell_ids = offset + jnp.arange(local_cells, dtype=jnp.int32)
    is_first = (cell_ids == 0).astype(jnp.float32)
    is_last = (cell_ids == cells_total - 1).astype(jnp.float32)
    lower_band, diagonal, upper_band = cell_rows(
        heights[:, None, None],
        face_left[:, None, None],
        face_right[:, None, None],
        is_first[:, None, None],
        is_last[:, None, None],
        diffusion[None],
        lower_wall[None],
        upper_wall[None],
    )
    unit_part = jnp.broadcast_to(heights[:, None, None, None], (local_cells, 1, lines_y, lines_x))
    rhs_rows = jnp.concatenate(
        [heights[:, None, None, None] * jnp.moveaxis(velocity, 0, 1), unit_part], axis=1
    )
    inner_count = local_cells - 1
    couple_left = jnp.concatenate(
        [
            (-lower_band[0])[None, None],
            jnp.zeros((inner_count - 1, 1, lines_y, lines_x), jnp.float32),
        ],
        axis=0,
    )
    couple_right = jnp.concatenate(
        [
            jnp.zeros((inner_count - 1, 1, lines_y, lines_x), jnp.float32),
            (-upper_band[inner_count - 1])[None, None],
        ],
        axis=0,
    )
    inner_rhs = jnp.concatenate([rhs_rows[:inner_count], couple_left, couple_right], axis=1)
    keep_upper = (jnp.arange(inner_count, dtype=jnp.int32) < inner_count - 1).astype(jnp.float32)
    inner_upper = upper_band[:inner_count] * keep_upper[:, None, None]
    interior = scan_thomas(lower_band[:inner_count], diagonal[:inner_count], inner_upper, inner_rhs)
    neighbour = from_behind(interior[0], "gz", -1)
    last_row = interior[inner_count - 1]
    edge_lower = lower_band[local_cells - 1]
    edge_diagonal = diagonal[local_cells - 1]
    edge_upper = upper_band[local_cells - 1]
    reduced_lower = edge_lower * last_row[4]
    reduced_diagonal = edge_lower * last_row[5] + edge_diagonal + edge_upper * neighbour[4]
    reduced_upper = edge_upper * neighbour[5]
    reduced_rhs = (
        rhs_rows[local_cells - 1]
        - edge_lower[None] * last_row[:4]
        - edge_upper[None] * neighbour[:4]
    )
    reduced = jnp.concatenate(
        [reduced_lower[None], reduced_diagonal[None], reduced_upper[None], reduced_rhs], axis=0
    )
    gathered = lax.all_gather(reduced[None], "gz", axis=0, tiled=True)
    solved_all = scan_thomas(gathered[:, 0], gathered[:, 1], gathered[:, 2], gathered[:, 3:])
    own_value = lax.dynamic_index_in_dim(solved_all, position, 0, keepdims=False)
    prev_value = lax.dynamic_index_in_dim(
        solved_all, jnp.maximum(position - 1, 0), 0, keepdims=False
    ) * (position > 0).astype(jnp.float32)
    inner_values = (
        interior[:, :4] + interior[:, 4:5] * prev_value[None] + interior[:, 5:6] * own_value[None]
    )
    complete = jnp.concatenate([inner_values, own_value[None]], axis=0)
    streamwise = corrected(complete[:, 0], complete[:, 3], heights, bulk_target, volume)
    return jnp.stack([streamwise, complete[:, 1], complete[:, 2]], axis=0)


def solution(mesh):
    return jax.shard_map(
        shards,
        mesh=mesh,
        in_specs=(P(None, "gz", "gy", None), P("gy", None), P("gy", None), P(), P()),
        out_specs=P(None, "gz", "gy", None),
        check_vma=False,
    )
```

profile of v0, /device:TPU:0, one launch (start us, length us, event | category | flops | bytes accessed | tf_op | source)
XLA Modules:
  0.0 293.4 jit_solution(17454031398100693911)
XLA Ops:
  11.9 2.4 broadcast_multiply_fusion
  16.4 2.5 fusion.5
  22.4 2.8 select_maximum_fusion
  25.2 3.3 %broadcast.84.clone = f32[15,6,32,512]{3,2,1,0:T(8,128)} broadcast(f32[]{:T(128)} %constant.163.clone.1), dimensions={} | broadcast | bytes 5898244 | tf_op jit(solution)/shard_map/broadcast.13
  28.5 56.0 %while.68 = (s32[]{:T(128)}, f32[32,512]{1,0:T(8,128)}, f32[6,32,512]{2,1,0:T(8,128)}, f32[15,32,512]{2,1,0:T(8,128)}, f32[15,6,32,512]{3,2,1,0:T(8,128)}, /*ind...) while((s32[]{:T(128)}, f32[32,512]{1,0:T(8,128)}, ...), condition=%wide.region_1.2_spmd.clone, body=%wide.region_0.0_spmd.clone.sunk | while | flops 458755 | bytes 2229368 | solution.py:44
  30.1 2.0 bitcast_dynamic-update-slice_fusion.13
  33.7 2.1 bitcast_dynamic-update-slice_fusion.13
  37.5 2.1 bitcast_dynamic-update-slice_fusion.13
  41.2 2.1 bitcast_dynamic-update-slice_fusion.13
  45.0 2.1 bitcast_dynamic-update-slice_fusion.13
  48.7 2.2 bitcast_dynamic-update-slice_fusion.13
  52.5 2.2 bitcast_dynamic-update-slice_fusion.13
  56.2 2.2 bitcast_dynamic-update-slice_fusion.13
  60.0 2.1 bitcast_dynamic-update-slice_fusion.13
  63.7 2.1 bitcast_dynamic-update-slice_fusion.13
  67.5 2.1 bitcast_dynamic-update-slice_fusion.13
  71.2 2.1 bitcast_dynamic-update-slice_fusion.13
  74.9 2.1 bitcast_dynamic-update-slice_fusion.13
  78.7 2.2 bitcast_dynamic-update-slice_fusion.13
  82.4 2.1 bitcast_dynamic-update-slice_fusion.13
  84.6 3.3 %broadcast.84 = f32[15,6,32,512]{3,2,1,0:T(8,128)} broadcast(f32[]{:T(128)} %constant.163.clone.1), dimensions={} | broadcast | bytes 5898244 | tf_op jit(solution)/shard_map/broadcast.13
  87.9 52.1 %while.69 = (s32[]{:T(128)}, f32[6,32,512]{2,1,0:T(8,128)S(1)}, f32[15,6,32,512]{3,2,1,0:T(8,128)}, f32[15,6,32,512]{3,2,1,0:T(8,128)}, f32[15,32,512]{2,1,0:T(8,128)}, /*index=5*/s32[]{:T(128)}, s32[]{:T(128)}, s32[]{:T(128)}) while((s32[]{:T(128)}, f32[6,32,512]{2,1,0:T(8,128)S(1)}, f32[15,6,32,512]{3,2,1,0:T(8,128)}, ...), condition=%wide.region_3.4_spmd.clone, body=%wide.region_2.3_spmd.clone.sunk | while | flops 294916 | bytes 1769587 | solution.py:53
  89.3 2.0 bitcast_dynamic-update-slice_fusion.14
  92.8 2.0 bitcast_dynamic-update-slice_fusion.14
  96.3 2.0 bitcast_dynamic-update-slice_fusion.14
  99.7 2.0 bitcast_dynamic-update-slice_fusion.14
  103.2 2.0 bitcast_dynamic-update-slice_fusion.14
  106.7 2.0 bitcast_dynamic-update-slice_fusion.14
  110.2 2.0 bitcast_dynamic-update-slice_fusion.14
  113.6 2.0 bitcast_dynamic-update-slice_fusion.14
  117.1 2.0 bitcast_dynamic-update-slice_fusion.14
  120.6 2.0 bitcast_dynamic-update-slice_fusion.14
  124.0 2.0 bitcast_dynamic-update-slice_fusion.14
  127.5 2.0 bitcast_dynamic-update-slice_fusion.14
  131.0 2.0 bitcast_dynamic-update-slice_fusion.14
  134.5 2.0 bitcast_dynamic-update-slice_fusion.14
  137.9 2.0 bitcast_dynamic-update-slice_fusion.14
  142.3 2.3 collective-permute-done
  148.8 3.0 %slice_bitcast_fusion.1 = (f32[15,32,512]{2,1,0:T(8,128)}, f32[15,32,512]{2,1,0:T(8,128)}) fusion(f32[15,6,32,512]{3,2,1,0:T(8,128)} %get-tuple-element.309), kind=kLoop, calls=%fused_computation.60 | loop fusion | bytes 3932160 | tf_op jit(solution)/shard_map/mul | solution.py:143
  151.8 37.9 %all-gather.3.cloned.1.call-done = f32[56,32,512]{2,1,0:T(8,128)} async-done(((f32[7,32,512]{2,1,0:T(8,128)}), f32[56,32,512]{2,1,0:T(8,128)}) %all-gather.3.cloned.1.call-update) | async-done | bytes 3670032 | tf_op jit(solution)/shard_map/all_gather | solution.py:136
  189.8 3.2 %slice.155 = f32[8,4,32,512]{3,2,1,0:T(8,128)} slice(f32[8,7,32,512]{3,2,1,0:T(8,128)} %bitcast.131), slice={[0:8], [3:7], [0:32], [0:512]} | slice | bytes 4194304 | tf_op jit(solution)/shard_map/slice | solution.py:137
  193.0 2.5 slice_bitcast_fusion.2
  195.8 20.8 %while.70 = (s32[]{:T(128)}, f32[32,512]{1,0:T(8,128)S(1)}, f32[4,32,512]{2,1,0:T(8,128)S(1)}, f32[8,32,512]{2,1,0:T(8,128)}, f32[8,4,32,512]{3,2,1,0:T(8,128)S(...) while((s32[]{:T(128)}, f32[32,512]{1,0:T(8,128)S(1)}, ...), condition=%wide.region_5.6_spmd.clone, body=%wide.region_4.5_spmd.clone.sunk | while | flops 327683 | bytes 1704572 | solution.py:44
  218.1 13.6 %while.71 = (s32[]{:T(128)}, f32[4,32,512]{2,1,0:T(8,128)S(1)}, f32[8,4,32,512]{3,2,1,0:T(8,128)}, f32[8,4,32,512]{3,2,1,0:T(8,128)S(1)}, f32[8,32,512]{2,1,0:T(8,128)}, /*index=5*/s32[]{:T(128)}, s32[]{:T(128)}, s32[]{:T(128)}) while((s32[]{:T(128)}, f32[4,32,512]{2,1,0:T(8,128)S(1)}, f32[8,4,32,512]{3,2,1,0:T(8,128)}, ...), condition=%wide.region_7.8_spmd.clone, body=%wide.region_6.7_spmd.clone.sunk | while | flops 196612 | bytes 1245299 | solution.py:53
  234.6 3.5 %fusion.4 = f32[15,4,32,512]{3,2,0,1:T(8,128)S(1)} fusion(f32[4,32,512]{2,1,0:T(8,128)S(1)} %fusion.29, f32[15,32,512]{2,1,0:T(8,128)} %get-tuple-element.488, f32[4,32,512]{2,1,0:T(8,128)S(1)} %multiply_bitcast_fusion, f32[15,32,512]{2,1,0:T(8,128)} %get-tuple-element.487, f32[15,6,32,512]{3,2,1,0:T(8,128)} %get-tuple-element.309), kind=kLoop, calls=%fused_computation.42 | loop fusion | flops 3932160 | bytes 10354688 | tf_op jit(solution)/shard_map/add | solution.py:143
  241.1 39.6 %all-reduce.2 = (f32[]{:T(128)}, f32[]{:T(128)}) all-reduce(f32[]{:T(128)} %get-tuple-element.410, f32[]{:T(128)} %get-tuple-element.409), channel_id=1, replica_groups=mesh['gz'=8,'gy'=4] {'gz','gy'}, use_global_device_ids=true, to_apply=%region_10.11 | all-reduce | flops 2 | bytes 16 | tf_op jit(solution)/shard_map/psum | solution.py:62
  282.0 2.6 add_bitcast_fusion
  284.5 2.0 pad_maximum_fusion
  (115 shorter events, 102.5 us)
Async XLA Ops:
  6.5 183.2 %all-gather.3.cloned.1.call-start = ((), (), s32[]{:S(2)}) async-start(), calls=%async_computation | async-start | bytes 4128768 | tf_op jit(solution)/shard_map/all_gather | solution.py:136
  14.4 1.0 copy-start.2
  14.4 2.1 copy-start.3
  16.4 2.6 copy-start.4
  16.4 3.7 %copy-start.5 = (f32[16,32,512]{2,1,0:T(8,128)S(1)}, f32[16,32,512]{2,1,0:T(8,128)}, u32[]{:S(2)}) copy-start(f32[16,32,512]{2,1,0:T(8,128)} %get-tuple-element.502) | copy-start | bytes 3145732
  21.3 1.2 copy-start.1
  21.3 1.1 copy-start.6
  141.0 3.6 %collective-permute-start = (f32[6,32,512]{2,1,0:T(8,128)S(1)}, f32[6,32,512]{2,1,0:T(8,128)S(1)}, u32[]{:S(2)}, u32[]{:S(2)}) collective-permute-start(f32[6,32,512]{2,1,0:T(8,128)S(1)} %slice_bitcast_fusion.5), channel_id=1, source_target_pairs={{4,0},{8,4},{12,8},{16,12},{20,16},{24,20},{28,24},{5,1},{9,5},{13... | collective-permute-start | bytes 1179656 | tf_op jit(solution)/shard_map/ppermute | solution.py:10
  238.1 1.9 copy-start
Sparse Core Ops, SparseCore 0:
  147.6 42.1 all-gather.2
where the time goes:
time: 297 us; the launch traced here: 293 us
  other arithmetic  140 us (47%)
  local copies, waits for them, and re-layouts  54.6 us (18%)
  waiting for transfers between devices  40.3 us (14%)
  blocking collectives  39.6 us (13%)
  between operations  17.5 us (6%)
    dynamic_update_slice x69, other arithmetic, scan_thomas(): lax.scan(forward, zero_state, (lower_band, diagonal, upper_band, rhs_rows))  114 us
    psum x1, blocking collectives, corrected(): lax.psum((partial_flow, partial_weight), ('gz', 'gy'))  39.6 us
    all_gather x1, waiting for transfers between devices, shards(): gathered = lax.all_gather(reduced[None], 'gz', axis=0, tiled=True)  37.9 us
    mul x23, local copies, waits for them, and re-layouts, backward(): current = solved_row - factor[None] * following  28.7 us
    another operation x4, local copies, waits for them, and re-layouts  8.43 us
  transfers between devices with their start and end apart: 2, of which 2 were waited for; matrix products, arithmetic and copies ran while one was open for 1% of the time, Pallas kernels for 0%

commit v1 on v0

v1 whole, which is shorter than its diff:
```python
import functools

import jax
import jax.numpy as jnp
from jax import lax
from jax.experimental import pallas as pl
from jax.experimental.pallas import tpu as pltpu
from jax.sharding import PartitionSpec as P

SUB = 8
LANES = 128
MIB = 1024 * 1024


def height(index_ref, k):
    return 0.5 + 0.25 * index_ref[k].astype(jnp.float32)


def half_sum(index_ref, k):
    return 0.5 * (height(index_ref, k) + height(index_ref, k + 1))


def ladder_kernel(
    cells, blocks, chips,
    index_ref, diffusion_ref, walls_ref, velocity_hbm,
    sums_ref, pair_ref, chip_ref, left_ref, right_ref, ends_ref, tile_ref,
    velocity_ref, through_ref, inverse_ref, sems,
):
    total = cells * blocks
    components = velocity_ref.shape[0]
    copies = [
        pltpu.make_async_copy(velocity_hbm.at[c], velocity_ref.at[c], sems.at[c])
        for c in range(components)
    ]
    for copy in copies:
        copy.start()
    me = lax.axis_index("gz")
    chip = me // 2
    first = chip * 2
    diffusion = diffusion_ref[...]
    inverse_ref[...] = 1.0 / diffusion
    walls = walls_ref[...]
    lower = diffusion * (walls % 2).astype(jnp.float32) * 2.0 / height(index_ref, 0)
    upper = diffusion * (walls // 2).astype(jnp.float32) * 2.0 / height(index_ref, total - 1)

    def forward(block, kappa, keep=None):
        start = block * cells
        inverse = inverse_ref[...]
        flux = height(index_ref, start) + kappa
        value = jnp.ones_like(flux)
        for j in range(cells):
            if keep is not None:
                keep(j, flux, value)
            k = start + j
            if j < cells - 1:
                value = value + (half_sum(index_ref, k) * inverse) * flux
                flux = flux + height(index_ref, k + 1) * value
        k = jnp.minimum(start + cells - 1, total - 2)
        after = 1.0 / (value + (half_sum(index_ref, k) * inverse) * flux)
        return flux * after, after

    def backward(block, kappa, scale=None, keep=None):
        start = block * cells
        inverse = inverse_ref[...]
        flux = height(index_ref, start + cells - 1) + kappa
        value = jnp.ones_like(flux)
        if scale is not None:
            flux, value = flux * scale, scale
        for j in reversed(range(cells)):
            if keep is not None:
                keep(j, flux, value)
            k = start + j
            if j > 0:
                value = value + (half_sum(index_ref, k - 1) * inverse) * flux
                flux = flux + height(index_ref, k - 1) * value
        k = jnp.maximum(start - 1, 0)
        after = 1.0 / (value + (half_sum(index_ref, k) * inverse) * flux)
        return flux * after, after

    def sweep_forward(block, state):
        kappa, product = state
        kappa, after = forward(block, kappa)
        through_ref[block] = after
        return kappa, product * after

    def sweep_backward(step, state):
        block = blocks - 1 - step
        kappa, product = state
        kappa, after = backward(block, kappa)
        through_ref[block] = after
        return kappa, product * after

    ones = jnp.ones_like(diffusion)
    kappa_left, product_left = lax.fori_loop(0, me, sweep_forward, (lower, ones))
    ends = {}

    def keep_left(j, flux, value):
        left_ref[j] = value
        ends["flux"], ends["value"] = flux, value

    kappa, own_forward = forward(me, kappa_left, keep_left)
    ends_ref[0] = kappa
    ends_ref[1] = lower * product_left

    @pl.when(me == first)
    def _():
        _, after = forward(me + 1, kappa)
        pair_ref[0] = after

    @pl.when(me != first)
    def _():
        pair_ref[0] = own_forward
        pair_ref[2] = through_ref[first]

    kappa_right, product_right = lax.fori_loop(
        0, blocks - 1 - me, sweep_backward, (upper, ones)
    )
    scale = 1.0 / (ends["flux"] + kappa_right * ends["value"])

    def keep_right(j, flux, value):
        right_ref[j] = value

    kappa, own_backward = backward(me, kappa_right, scale, keep_right)

    @pl.when(me == first)
    def _():
        pair_ref[1] = own_backward * scale
        pair_ref[2] = through_ref[first + 1]

    @pl.when(me != first)
    def _():
        _, after = backward(me - 1, kappa)
        pair_ref[1] = after

    ends_ref[0] = lower * product_left
    ends_ref[1] = upper * product_right
    for m in range(1, chips):
        other = chip ^ m
        low = jnp.minimum(chip, other)
        high = jnp.maximum(chip, other)
        chip_ref[m - 1] = lax.fori_loop(
            low + 1,
            high,
            lambda r, product: product * (through_ref[2 * r] * through_ref[2 * r + 1]),
            ones,
        )
    for copy in copies:
        copy.wait()
    flow = jnp.zeros((SUB, LANES), jnp.float32)
    weight = jnp.zeros((SUB, LANES), jnp.float32)

    def fold(array):
        parts = [array[:, i * LANES:(i + 1) * LANES] for i in range(array.shape[1] // LANES)]
        return functools.reduce(jnp.add, parts)

    for t in range(diffusion.shape[0] // SUB):
        rows = pl.ds(t * SUB, SUB)
        from_left = [0.0] * components
        from_right = [0.0] * components
        plain = 0.0
        left_total = 0.0
        right_total = 0.0
        extent = 0.0
        for j in range(cells):
            h = height(index_ref, me * cells + j)
            left = h * left_ref[j, rows]
            right = h * right_ref[j, rows]
            extent = extent + h
            left_total = left_total + left
            right_total = right_total + right
            for c in range(components):
                v = velocity_ref[c, j, rows]
                from_left[c] = from_left[c] + left * v
                from_right[c] = from_right[c] + right * v
                if c == 0:
                    plain = plain + h * v
        block_scale = scale[t * SUB:(t + 1) * SUB]
        low_part = ends_ref[0, rows]
        high_part = ends_ref[1, rows] * block_scale
        for c in range(components):
            sums_ref[t, c] = from_left[c] * own_forward[t * SUB:(t + 1) * SUB]
            sums_ref[t, components + c] = from_right[c] * own_backward[t * SUB:(t + 1) * SUB]
        flow = flow + fold(plain - low_part * from_right[0] - high_part * from_left[0])
        weight = weight + fold(extent - low_part * right_total - high_part * left_total)
    tile_ref[0] = flow
    tile_ref[1] = weight


def merge_kernel(chips, components, tiles_count, sums_ref, mate_ref, pair_ref, *rest):
    tile_refs = rest[:tiles_count]
    send_refs = rest[tiles_count:tiles_count + chips - 1]
    column_ref = rest[-1]
    me = lax.axis_index("gz")
    chip = me // 2
    is_first = me == chip * 2
    row_tiles = sums_ref.shape[0]
    column = functools.reduce(jnp.add, [ref[...] for ref in tile_refs])
    column_ref[...] = column
    for ref in send_refs:
        ref[components * row_tiles] = jnp.zeros(ref.shape[1:], jnp.float32)
        ref[components * row_tiles, :, 0:LANES] = column[0]
        ref[components * row_tiles, :, LANES:2 * LANES] = column[1]
    for t in range(row_tiles):
        for c in range(components):
            mine, mate = sums_ref[t, c], mate_ref[t, c]
            first = jnp.where(is_first, mine, mate)
            second = jnp.where(is_first, mate, mine)
            to_right = second + pair_ref[0, t * SUB:(t + 1) * SUB] * first
            mine, mate = sums_ref[t, components + c], mate_ref[t, components + c]
            first = jnp.where(is_first, mine, mate)
            second = jnp.where(is_first, mate, mine)
            to_left = first + pair_ref[1, t * SUB:(t + 1) * SUB] * second
            for m in range(1, chips):
                goes_right = (chip ^ m) > chip
                send_refs[m - 1][t * components + c] = jnp.where(goes_right, to_right, to_left)


def inner_kernel(cells, index_ref, velocity_ref, left_ref, right_ref, base_ref):
    me = lax.axis_index("gz")
    components = velocity_ref.shape[0]
    heights = [height(index_ref, me * cells + j) for j in range(cells)]
    gathered = [jnp.zeros(left_ref.shape[1:], jnp.float32)] * components
    for j in reversed(range(cells)):
        left = left_ref[j]
        right = heights[j] * right_ref[j]
        for c in range(components):
            base_ref[c, j] = left * gathered[c]
            if j > 0:
                gathered[c] = gathered[c] + right * velocity_ref[c, j]
    gathered = [jnp.zeros(left_ref.shape[1:], jnp.float32)] * components
    for j in range(cells):
        left = heights[j] * left_ref[j]
        right = right_ref[j]
        for c in range(components):
            gathered[c] = gathered[c] + left * velocity_ref[c, j]
            base_ref[c, j] = base_ref[c, j] + right * gathered[c]


def finish_kernel(
    cells, blocks, chips, lines,
    index_ref, target_ref, column_ref, base_ref, left_ref, right_ref,
    mate_ref, pair_ref, chip_ref, ends_ref, *rest,
):
    recv_refs = rest[:chips - 1]
    scalar_refs = rest[chips - 1:2 * (chips - 1)]
    out_ref, alpha_ref = rest[-2:]
    me = lax.axis_index("gz")
    chip = me // 2
    is_first = me == chip * 2
    components = base_ref.shape[0]

    @pl.when(pl.program_id(0) == 0)
    def _():
        extent = lax.fori_loop(
            0, cells * blocks, lambda k, total: total + height(index_ref, k), jnp.float32(0.0)
        )
        flow = column_ref[0]
        weight = column_ref[1]
        for ref in scalar_refs:
            flow = flow + ref[0, :, 0:LANES]
            weight = weight + ref[0, :, LANES:2 * LANES]
        flow = jnp.sum(flow, keepdims=True)
        weight = jnp.sum(weight, keepdims=True)
        alpha = (target_ref[0] * (extent * lines) - flow) / weight
        alpha_ref[...] = jnp.broadcast_to(alpha, alpha_ref.shape)

    alpha = alpha_ref[0:1, 0:1]
    scale = right_ref[cells - 1]
    lefts, rights = [], []
    for c in range(components):
        left_in = jnp.zeros(scale.shape, jnp.float32)
        right_in = jnp.zeros(scale.shape, jnp.float32)
        for m in range(1, chips):
            term = chip_ref[m - 1] * recv_refs[m - 1][c]
            from_left = (chip ^ m) < chip
            left_in = left_in + jnp.where(from_left, term, 0.0)
            right_in = right_in + jnp.where(from_left, 0.0, term)
        near = pair_ref[0]
        left_in = jnp.where(is_first, left_in, mate_ref[0, c] + near * left_in)
        right_in = jnp.where(is_first, mate_ref[0, components + c] + near * right_in, right_in)
        if c == 0:
            left_in = left_in - alpha * ends_ref[0]
            right_in = right_in - alpha * ends_ref[1]
        lefts.append(left_in)
        rights.append(right_in * scale)
    for j in range(cells):
        left = left_ref[j]
        right = right_ref[j]
        for c in range(components):
            value = base_ref[c, j] + (right * lefts[c] + left * rights[c])
            out_ref[c, j] = value + alpha if c == 0 else value


def shards(velocity, diffusion, wall_types, stretch_index, bulk_target):
    blocks = lax.axis_size("gz")
    columns = lax.axis_size("gy")
    components, cells, lines_y, lines_x = velocity.shape
    chips = blocks // 2
    row_tiles = lines_y // SUB
    f32 = jnp.float32
    vmem = pl.BlockSpec(memory_space=pltpu.VMEM)
    smem = pl.BlockSpec(memory_space=pltpu.SMEM)
    plane = (lines_y, lines_x)
    sums, pair, chip_coefs, left, right, ends, tile = pl.pallas_call(
        functools.partial(ladder_kernel, cells, blocks, chips),
        out_shape=[
            jax.ShapeDtypeStruct((row_tiles, 2 * components, SUB, lines_x), f32),
            jax.ShapeDtypeStruct((3,) + plane, f32),
            jax.ShapeDtypeStruct((chips - 1,) + plane, f32),
            jax.ShapeDtypeStruct((cells,) + plane, f32),
            jax.ShapeDtypeStruct((cells,) + plane, f32),
            jax.ShapeDtypeStruct((2,) + plane, f32),
            jax.ShapeDtypeStruct((2, SUB, LANES), f32),
        ],
        in_specs=[smem, vmem, vmem, pl.BlockSpec(memory_space=pl.ANY)],
        out_specs=[vmem] * 7,
        scratch_shapes=[
            pltpu.VMEM(velocity.shape, f32),
            pltpu.VMEM((blocks,) + plane, f32),
            pltpu.VMEM(plane, f32),
            pltpu.SemaphoreType.DMA((components,)),
        ],
        compiler_params=pltpu.CompilerParams(vmem_limit_bytes=24 * MIB),
        cost_estimate=pl.CostEstimate(flops=40_000_000, bytes_accessed=6_000_000, transcendentals=0),
        name="ladder",
    )(stretch_index, diffusion, wall_types, velocity)

    def route(partner):
        return [
            (z * columns + y, partner(z, y)[0] * columns + partner(z, y)[1])
            for z in range(blocks)
            for y in range(columns)
        ]

    def send(array, partner):
        return lax.ppermute(array, ("gz", "gy"), route(partner))

    mate = send(sums, lambda z, y: (z ^ 1, y))
    tiles = [tile] + [
        send(tile, lambda z, y: (z ^ flip, (y + shift) % columns))
        for flip in range(2)
        for shift in range(columns)
        if (flip, shift) != (0, 0)
    ]
    outgoing = pl.pallas_call(
        functools.partial(merge_kernel, chips, components, len(tiles)),
        out_shape=[
            jax.ShapeDtypeStruct((components * row_tiles + 1, SUB, lines_x), f32)
            for _ in range(chips - 1)
        ] + [jax.ShapeDtypeStruct((2, SUB, LANES), f32)],
        in_specs=[vmem] * (3 + len(tiles)),
        out_specs=[vmem] * chips,
        compiler_params=pltpu.CompilerParams(vmem_limit_bytes=16 * MIB),
        cost_estimate=pl.CostEstimate(flops=500_000, bytes_accessed=1_600_000, transcendentals=0),
        name="merge",
    )(sums, mate, pair, *tiles)
    column = outgoing[-1]
    incoming = [
        send(outgoing[m - 1], lambda z, y: (z ^ (2 * m), y)) for m in range(1, chips)
    ]

    state = pl.BlockSpec((components, cells, SUB, lines_x), lambda t: (0, 0, t, 0))
    profile = pl.BlockSpec((cells, SUB, lines_x), lambda t: (0, t, 0))
    base = pl.pallas_call(
        functools.partial(inner_kernel, cells),
        grid=(row_tiles,),
        out_shape=jax.ShapeDtypeStruct(velocity.shape, f32),
        in_specs=[smem, state, profile, profile],
        out_specs=state,
        compiler_params=pltpu.CompilerParams(vmem_limit_bytes=16 * MIB),
        cost_estimate=pl.CostEstimate(flops=8_000_000, bytes_accessed=8_000_000, transcendentals=0),
        name="inner",
    )(stretch_index, velocity, left, right)
    one = pl.BlockSpec((1, SUB, lines_x), lambda t: (2, t, 0))
    received = pl.BlockSpec((components, SUB, lines_x), lambda t: (t, 0, 0))
    scalars = pl.BlockSpec((1, SUB, lines_x), lambda t: (components * row_tiles, 0, 0))
    return pl.pallas_call(
        functools.partial(finish_kernel, cells, blocks, chips, float(lines_y * columns * lines_x)),
        grid=(row_tiles,),
        out_shape=jax.ShapeDtypeStruct(velocity.shape, f32),
        in_specs=[
            smem,
            smem,
            vmem,
            state,
            profile,
            profile,
            pl.BlockSpec((1, 2 * components, SUB, lines_x), lambda t: (t, 0, 0, 0)),
            one,
            pl.BlockSpec((chips - 1, SUB, lines_x), lambda t: (0, t, 0)),
            pl.BlockSpec((2, SUB, lines_x), lambda t: (0, t, 0)),
        ] + [received] * (chips - 1) + [scalars] * (chips - 1),
        out_specs=state,
        scratch_shapes=[pltpu.VMEM((SUB, LANES), f32)],
        compiler_params=pltpu.CompilerParams(vmem_limit_bytes=16 * MIB),
        cost_estimate=pl.CostEstimate(flops=4_000_000, bytes_accessed=9_000_000, transcendentals=0),
        name="finish",
    )(stretch_index, bulk_target, column, base, left, right, mate, pair, chip_coefs, ends,
      *incoming, *incoming)


def solution(mesh):
    return jax.shard_map(
        shards,
        mesh=mesh,
        in_specs=(P(None, "gz", "gy", None), P("gy", None), P("gy", None), P(), P()),
        out_specs=P(None, "gz", "gy", None),
        check_vma=False,
    )
```

time: 297 us -> 40.8 us (0.14); the launches traced: 293 us -> 40.6 us
  other arithmetic: 140 us -> 0 us
  local copies, waits for them, and re-layouts: 54.6 us -> 4.22 us
  blocking collectives: 39.6 us -> 0 us
  waiting for transfers between devices: 40.3 us -> 11.3 us
  between operations: 17.5 us -> 0.69 us
  starting transfers between devices: 1.29 us -> 13.6 us
  Pallas kernels: 0 us -> 10.8 us
    dynamic_update_slice x69 -> x0, other arithmetic: 114 us -> none  [scan_thomas(): lax.scan(forward, zero_state, (lower_band, diagonal, upper_band, rhs_rows))]
    psum x1 -> x0, blocking collectives: 39.6 us -> none  [corrected(): lax.psum((partial_flow, partial_weight), ('gz', 'gy'))]
    all_gather x1 -> x0, waiting for transfers between devices: 37.9 us -> none  [shards(): gathered = lax.all_gather(reduced[None], 'gz', axis=0, tiled=True)]
    mul x25 -> x0, local copies, waits for them, and re-layouts: 32.7 us -> none  [the longest x23 28.7 us: backward(): current = solved_row - factor[None] * following]
    ppermute x1 -> x11, starting transfers between devices: 1.29 us -> 13.6 us  [send(): return lax.ppermute(array, ('gz', 'gy'), route(partner))]
    pallas_call x0 -> x4, Pallas kernels: none -> 10.8 us  [the longest x1 4.46 us: shards(): pl.pallas_call(functools.partial(finish_kernel, cells, blocks, chips, flo...]
    mul x6 -> x0, other arithmetic: 8.96 us -> none  [the longest x1 2.55 us: shards(): heights[:, None, None, None] * jnp.moveaxis(velocity, 0, 1)]
    ppermute x1 -> x11, waiting for transfers between devices: 2.32 us -> 11.3 us  [send(): return lax.ppermute(array, ('gz', 'gy'), route(partner))]
  transfers between devices with their start and end apart: 2 -> 11, of which waited for: 2 -> 6; matrix products, arithmetic and copies ran while one was open for 1% -> 0% of each run, Pallas kernels for 0% -> 5%
where the time goes in v1:
time: 40.8 us; the launch traced here: 40.6 us
  starting transfers between devices  13.6 us (33%)
  waiting for transfers between devices  11.3 us (28%)
  Pallas kernels  10.8 us (26%)
  local copies, waits for them, and re-layouts  4.22 us (10%)
  between operations  0.69 us (2%)
    ppermute x11, starting transfers between devices, send(): return lax.ppermute(array, ('gz', 'gy'), route(partner))  13.6 us
    ppermute x11, waiting for transfers between devices, send(): return lax.ppermute(array, ('gz', 'gy'), route(partner))  11.3 us
    pallas_call x1, Pallas kernels, shards(): pl.pallas_call(functools.partial(finish_kernel, cells, blocks, chips, flo...  4.46 us
    unnamed x8, local copies, waits for them, and re-layouts  4.22 us
    pallas_call x1, Pallas kernels, shards(): pl.pallas_call(functools.partial(ladder_kernel, cells, blocks, chips), ou...  4.13 us
    pallas_call x1, Pallas kernels, shards(): pl.pallas_call(functools.partial(inner_kernel, cells), grid=(row_tiles,),...  2.14 us
  transfers between devices with their start and end apart: 11, of which 6 were waited for; matrix products, arithmetic and copies ran while one was open for 0% of the time, Pallas kernels for 5%

profile of v1, /device:TPU:0, one launch (start us, length us, event | category | flops | bytes accessed | tf_op | source)
XLA Modules:
  0.0 40.6 jit_solution(17330942014524087431)
XLA Ops:
  0.0 0.0 copy-start
  0.0 1.9 %copy-done = f32[3,16,32,512]{3,2,1,0:T(8,128)S(1)} copy-done((f32[3,16,32,512]{3,2,1,0:T(8,128)S(1)}, f32[3,16,32,512]{3,2,1,0:T(8,128)}, u32[]{:S(2)}) %copy-start) | copy-done | bytes 3145752
  1.9 0.0 copy-start.1
  1.9 0.8 %copy-done.1 = f32[32,512]{1,0:T(8,128)S(1)} copy-done((f32[32,512]{1,0:T(8,128)S(1)}, f32[32,512]{1,0:T(8,128)}, u32[]{:S(2)}) %copy-start.1) | copy-done | bytes 65560
  2.7 0.0 copy-start.2
  2.7 0.8 %copy-done.2 = s32[32,512]{1,0:T(8,128)S(1)} copy-done((s32[32,512]{1,0:T(8,128)S(1)}, s32[32,512]{1,0:T(8,128)}, u32[]{:S(2)}) %copy-start.2) | copy-done | bytes 65560
  3.6 0.0 copy-start.3
  3.6 0.7 %copy-done.3 = s32[128]{0:T(128)S(1)} copy-done((s32[128]{0:T(128)S(1)}, s32[128]{0:T(128)}, u32[]{:S(2)}) %copy-start.3) | copy-done | bytes 536
  4.2 4.1 %ladder.1 = (f32[4,6,8,512]{3,2,1,0:T(8,128)S(1)}, f32[3,32,512]{2,1,0:T(8,128)S(1)}, f32[3,32,512]{2,1,0:T(8,128)S(1)}, f32[16,32,512]{2,1,0:T(8,128)S(1)}, f32...) custom-call(s32[128]{0:T(128)S(1)} %copy-done.3, f32[32,512]{1,0:T(8,128)S(1)} %copy-done.1, ...), custom_call_target="tpu_custom_call" | custom-call | flops 40000000 | bytes 6000000 | tf_op jit(solution)/shard_map/ladder/pallas_call | solution.py:304
  8.4 0.5 %collective-permute-start = (f32[4,6,8,512]{3,2,1,0:T(8,128)S(1)}, f32[4,6,8,512]{3,2,1,0:T(8,128)S(1)}, u32[]{:S(2)}, u32[]{:S(2)}) collective-permute-start(f32[4,6,8,512]{3,2,1,0:T(8,128)S(1)} %get-tuple-element.16.sums_ref), channel_id=1, source_target_pairs={{0,4},{1,5},{2,6},{3,7},{4,0},{5,1},{6,2},{7,3},{8,12},{9,13},{10,... | collective-permute-start | bytes 1179656 | tf_op jit(solution)/shard_map/ppermute | solution.py:336
  8.9 4.7 %collective-permute-start.7 = (f32[2,8,128]{2,1,0:T(8,128)S(1)}, f32[2,8,128]{2,1,0:T(8,128)S(1)}, u32[]{:S(2)}, u32[]{:S(2)}) collective-permute-start(f32[2,8,128]{2,1,0:T(8,128)S(1)} %get-tuple-element.18.rest_0_), channel_id=1, source_target_pairs={{0,7},{1,4},{2,5},{3,6},{4,3},{5,0},{6,1},{7,2},{8,15},{9,12},{10,... | collective-permute-start | bytes 24584 | tf_op jit(solution)/shard_map/ppermute | solution.py:336
  13.6 0.0 collective-permute-start.6
  13.6 0.7 %collective-permute-start.5 = (f32[2,8,128]{2,1,0:T(8,128)S(1)}, f32[2,8,128]{2,1,0:T(8,128)S(1)}, u32[]{:S(2)}, u32[]{:S(2)}) collective-permute-start(f32[2,8,128]{2,1,0:T(8,128)S(1)} %get-tuple-element.18.rest_0_), channel_id=1, source_target_pairs={{0,5},{1,6},{2,7},{3,4},{4,1},{5,2},{6,3},{7,0},{8,13},{9,14},{10,... | collective-permute-start | bytes 24584 | tf_op jit(solution)/shard_map/ppermute | solution.py:336
  14.3 0.1 collective-permute-start.4
  14.4 0.6 %collective-permute-done.7.rest_7_ = f32[2,8,128]{2,1,0:T(8,128)S(1)} collective-permute-done((f32[2,8,128]{2,1,0:T(8,128)S(1)}, f32[2,8,128]{2,1,0:T(8,128)S(1)}, u32[]{:S(2)}, u32[]{:S(2)}) %collective-permute-start.7) | collective-permute-done | bytes 8224 | tf_op jit(solution)/shard_map/ppermute | solution.py:336
  15.0 3.5 %collective-permute-start.3 = (f32[2,8,128]{2,1,0:T(8,128)S(1)}, f32[2,8,128]{2,1,0:T(8,128)S(1)}, u32[]{:S(2)}, u32[]{:S(2)}) collective-permute-start(f32[2,8,128]{2,1,0:T(8,128)S(1)} %get-tuple-element.18.rest_0_), channel_id=1, source_target_pairs={{0,3},{1,0},{2,1},{3,2},{4,7},{5,4},{6,5},{7,6},{8,11},{9,8},{10,9... | collective-permute-start | bytes 24584 | tf_op jit(solution)/shard_map/ppermute | solution.py:336
  18.4 0.0 collective-permute-done.6.rest_6_
  18.4 0.0 collective-permute-start.2
  18.4 0.0 collective-permute-done.5.rest_5_
  18.5 0.5 %collective-permute-start.1 = (f32[2,8,128]{2,1,0:T(8,128)S(1)}, f32[2,8,128]{2,1,0:T(8,128)S(1)}, u32[]{:S(2)}, u32[]{:S(2)}) collective-permute-start(f32[2,8,128]{2,1,0:T(8,128)S(1)} %get-tuple-element.18.rest_0_), channel_id=1, source_target_pairs={{0,1},{1,2},{2,3},{3,0},{4,5},{5,6},{6,7},{7,4},{8,9},{9,10},{10,1... | collective-permute-start | bytes 24584 | tf_op jit(solution)/shard_map/ppermute | solution.py:336
  19.0 0.0 collective-permute-done.4.rest_4_
  19.0 0.8 %collective-permute-done.3.rest_3_ = f32[2,8,128]{2,1,0:T(8,128)S(1)} collective-permute-done((f32[2,8,128]{2,1,0:T(8,128)S(1)}, f32[2,8,128]{2,1,0:T(8,128)S(1)}, u32[]{:S(2)}, u32[]{:S(2)}) %collective-permute-start.3) | collective-permute-done | bytes 8224 | tf_op jit(solution)/shard_map/ppermute | solution.py:336
  19.8 3.2 %collective-permute-done.2.rest_2_ = f32[2,8,128]{2,1,0:T(8,128)S(1)} collective-permute-done((f32[2,8,128]{2,1,0:T(8,128)S(1)}, f32[2,8,128]{2,1,0:T(8,128)S(1)}, u32[]{:S(2)}, u32[]{:S(2)}) %collective-permute-start.2) | collective-permute-done | bytes 8224 | tf_op jit(solution)/shard_map/ppermute | solution.py:336
  23.0 1.0 %collective-permute-done.1.rest_1_ = f32[2,8,128]{2,1,0:T(8,128)S(1)} collective-permute-done((f32[2,8,128]{2,1,0:T(8,128)S(1)}, f32[2,8,128]{2,1,0:T(8,128)S(1)}, u32[]{:S(2)}, u32[]{:S(2)}) %collective-permute-start.1) | collective-permute-done | bytes 8224 | tf_op jit(solution)/shard_map/ppermute | solution.py:336
  23.9 0.0 collective-permute-done.mate_ref
  23.9 0.1 merge.1
  24.1 1.5 %collective-permute-start.8 = (f32[13,8,512]{2,1,0:T(8,128)S(1)}, f32[13,8,512]{2,1,0:T(8,128)S(1)}, u32[]{:S(2)}, u32[]{:S(2)}) collective-permute-start(f32[13,8,512]{2,1,0:T(8,128)S(1)} %get-tuple-element.24), channel_id=1, source_target_pairs={{0,8},{1,9},{2,10},{3,11},{4,12},{5,13},{6,14},{7,15},{8,0},{9,1},... | collective-permute-start | bytes 638984 | tf_op jit(solution)/shard_map/ppermute | solution.py:336
  25.6 1.5 %collective-permute-start.9 = (f32[13,8,512]{2,1,0:T(8,128)S(1)}, f32[13,8,512]{2,1,0:T(8,128)S(1)}, u32[]{:S(2)}, u32[]{:S(2)}) collective-permute-start(f32[13,8,512]{2,1,0:T(8,128)S(1)} %get-tuple-element.25), channel_id=1, source_target_pairs={{0,16},{1,17},{2,18},{3,19},{4,20},{5,21},{6,22},{7,23},{8,24},{9,... | collective-permute-start | bytes 638984 | tf_op jit(solution)/shard_map/ppermute | solution.py:336
  27.1 0.5 %collective-permute-start.10 = (f32[13,8,512]{2,1,0:T(8,128)S(1)}, f32[13,8,512]{2,1,0:T(8,128)S(1)}, u32[]{:S(2)}, u32[]{:S(2)}) collective-permute-start(f32[13,8,512]{2,1,0:T(8,128)S(1)} %get-tuple-element.26), channel_id=1, source_target_pairs={{0,24},{1,25},{2,26},{3,27},{4,28},{5,29},{6,30},{7,31},{8,16},{9,... | collective-permute-start | bytes 638984 | tf_op jit(solution)/shard_map/ppermute | solution.py:336
  28.3 2.1 %inner.1.base_ref = f32[3,16,32,512]{3,2,1,0:T(8,128)S(1)} custom-call(s32[128]{0:T(128)S(1)} %copy-done.3, f32[3,16,32,512]{3,2,1,0:T(8,128)S(1)} %copy-done, f32[16,32,512]{2,1,0:T(8,128)S(1)} %get-tuple-element.20.left_ref, f32[16,32,512]{2,1,0:T(8,128)S(1)} %get-tuple-element.21.right_ref), custom_call_target="tpu_custom_call" | custom-call | flops 8000000 | bytes 8000000 | tf_op jit(solution)/shard_map/inner/pallas_call | solution.py:364
  30.4 1.9 %collective-permute-done.8.rest_0_.rest_3_ = f32[13,8,512]{2,1,0:T(8,128)S(1)} collective-permute-done((f32[13,8,512]{2,1,0:T(8,128)S(1)}, f32[13,8,512]{2,1,0:T(8,128)S(1)}, u32[]{:S(2)}, u32[]{:S(2)}) %collective-permute-start.8) | collective-permute-done | bytes 213024 | tf_op jit(solution)/shard_map/ppermute | solution.py:336
  32.3 3.8 %collective-permute-done.9.rest_1_.rest_4_ = f32[13,8,512]{2,1,0:T(8,128)S(1)} collective-permute-done((f32[13,8,512]{2,1,0:T(8,128)S(1)}, f32[13,8,512]{2,1,0:T(8,128)S(1)}, u32[]{:S(2)}, u32[]{:S(2)}) %collective-permute-start.9) | collective-permute-done | bytes 213024 | tf_op jit(solution)/shard_map/ppermute | solution.py:336
  36.1 0.0 collective-permute-done.10.rest_2_.rest_5_
  36.1 4.5 %finish.1 = f32[3,16,32,512]{3,2,1,0:T(8,128)} custom-call(s32[128]{0:T(128)S(1)} %copy-done.3, f32[1]{0:T(128)S(6)} %copy.6.target_ref, f32[2,8,128]{2,1,0:T(8,128)S(1)} %get-tuple-element.19.column_ref, f32[3,16,32,512]{3,2,1,0:T(8,128)S(1)} %inner.1.base_ref, f32[16,32,512]{2,1,0:T(8,128)S(1)} %get-tuple-element.20.left_ref, ...), custom_call_target="tpu_custom_call" | custom-call | flops 4000000 | bytes 9000000 | tf_op jit(solution)/shard_map/finish/pallas_call | solution.py:377
Async XLA Ops:
  0.0 1.9 %copy-start = (f32[3,16,32,512]{3,2,1,0:T(8,128)S(1)}, f32[3,16,32,512]{3,2,1,0:T(8,128)}, u32[]{:S(2)}) copy-start(f32[3,16,32,512]{3,2,1,0:T(8,128)} %velocity_ref.1) | copy-start | bytes 9437188
  1.9 0.8 %copy-start.1 = (f32[32,512]{1,0:T(8,128)S(1)}, f32[32,512]{1,0:T(8,128)}, u32[]{:S(2)}) copy-start(f32[32,512]{1,0:T(8,128)} %diffusion_ref.1) | copy-start | bytes 196612
  2.7 0.8 %copy-start.2 = (s32[32,512]{1,0:T(8,128)S(1)}, s32[32,512]{1,0:T(8,128)}, u32[]{:S(2)}) copy-start(s32[32,512]{1,0:T(8,128)} %walls_ref.1) | copy-start | bytes 196612
  3.6 0.7 %copy-start.3 = (s32[128]{0:T(128)S(1)}, s32[128]{0:T(128)}, u32[]{:S(2)}) copy-start(s32[128]{0:T(128)} %index_ref.5) | copy-start | bytes 1540
  8.4 15.6 %collective-permute-start = (f32[4,6,8,512]{3,2,1,0:T(8,128)S(1)}, f32[4,6,8,512]{3,2,1,0:T(8,128)S(1)}, u32[]{:S(2)}, u32[]{:S(2)}) collective-permute-start(f32[4,6,8,512]{3,2,1,0:T(8,128)S(1)} %get-tuple-element.16.sums_ref), channel_id=1, source_target_pairs={{0,4},{1,5},{2,6},{3,7},{4,0},{5,1},{6,2},{7,3},{8,12},{9,13},{10,... | collective-permute-start | bytes 1179656 | tf_op jit(solution)/shard_map/ppermute | solution.py:336
  8.9 6.1 %collective-permute-start.7 = (f32[2,8,128]{2,1,0:T(8,128)S(1)}, f32[2,8,128]{2,1,0:T(8,128)S(1)}, u32[]{:S(2)}, u32[]{:S(2)}) collective-permute-start(f32[2,8,128]{2,1,0:T(8,128)S(1)} %get-tuple-element.18.rest_0_), channel_id=1, source_target_pairs={{0,7},{1,4},{2,5},{3,6},{4,3},{5,0},{6,1},{7,2},{8,15},{9,12},{10,... | collective-permute-start | bytes 24584 | tf_op jit(solution)/shard_map/ppermute | solution.py:336
  13.6 4.8 %collective-permute-start.6 = (f32[2,8,128]{2,1,0:T(8,128)S(1)}, f32[2,8,128]{2,1,0:T(8,128)S(1)}, u32[]{:S(2)}, u32[]{:S(2)}) collective-permute-start(f32[2,8,128]{2,1,0:T(8,128)S(1)} %get-tuple-element.18.rest_0_), channel_id=1, source_target_pairs={{0,6},{1,7},{2,4},{3,5},{4,2},{5,3},{6,0},{7,1},{8,14},{9,15},{10,... | collective-permute-start | bytes 24584 | tf_op jit(solution)/shard_map/ppermute | solution.py:336
  13.6 4.9 %collective-permute-start.5 = (f32[2,8,128]{2,1,0:T(8,128)S(1)}, f32[2,8,128]{2,1,0:T(8,128)S(1)}, u32[]{:S(2)}, u32[]{:S(2)}) collective-permute-start(f32[2,8,128]{2,1,0:T(8,128)S(1)} %get-tuple-element.18.rest_0_), channel_id=1, source_target_pairs={{0,5},{1,6},{2,7},{3,4},{4,1},{5,2},{6,3},{7,0},{8,13},{9,14},{10,... | collective-permute-start | bytes 24584 | tf_op jit(solution)/shard_map/ppermute | solution.py:336
  14.3 4.7 %collective-permute-start.4 = (f32[2,8,128]{2,1,0:T(8,128)S(1)}, f32[2,8,128]{2,1,0:T(8,128)S(1)}, u32[]{:S(2)}, u32[]{:S(2)}) collective-permute-start(f32[2,8,128]{2,1,0:T(8,128)S(1)} %get-tuple-element.18.rest_0_), channel_id=1, source_target_pairs={{0,4},{1,5},{2,6},{3,7},{4,0},{5,1},{6,2},{7,3},{8,12},{9,13},{10,... | collective-permute-start | bytes 24584 | tf_op jit(solution)/shard_map/ppermute | solution.py:336
  15.0 4.8 %collective-permute-start.3 = (f32[2,8,128]{2,1,0:T(8,128)S(1)}, f32[2,8,128]{2,1,0:T(8,128)S(1)}, u32[]{:S(2)}, u32[]{:S(2)}) collective-permute-start(f32[2,8,128]{2,1,0:T(8,128)S(1)} %get-tuple-element.18.rest_0_), channel_id=1, source_target_pairs={{0,3},{1,0},{2,1},{3,2},{4,7},{5,4},{6,5},{7,6},{8,11},{9,8},{10,9... | collective-permute-start | bytes 24584 | tf_op jit(solution)/shard_map/ppermute | solution.py:336
  18.4 4.6 %collective-permute-start.2 = (f32[2,8,128]{2,1,0:T(8,128)S(1)}, f32[2,8,128]{2,1,0:T(8,128)S(1)}, u32[]{:S(2)}, u32[]{:S(2)}) collective-permute-start(f32[2,8,128]{2,1,0:T(8,128)S(1)} %get-tuple-element.18.rest_0_), channel_id=1, source_target_pairs={{0,2},{1,3},{2,0},{3,1},{4,6},{5,7},{6,4},{7,5},{8,10},{9,11},{10,... | collective-permute-start | bytes 24584 | tf_op jit(solution)/shard_map/ppermute | solution.py:336
  18.5 5.5 %collective-permute-start.1 = (f32[2,8,128]{2,1,0:T(8,128)S(1)}, f32[2,8,128]{2,1,0:T(8,128)S(1)}, u32[]{:S(2)}, u32[]{:S(2)}) collective-permute-start(f32[2,8,128]{2,1,0:T(8,128)S(1)} %get-tuple-element.18.rest_0_), channel_id=1, source_target_pairs={{0,1},{1,2},{2,3},{3,0},{4,5},{5,6},{6,7},{7,4},{8,9},{9,10},{10,1... | collective-permute-start | bytes 24584 | tf_op jit(solution)/shard_map/ppermute | solution.py:336
  24.1 8.3 %collective-permute-start.8 = (f32[13,8,512]{2,1,0:T(8,128)S(1)}, f32[13,8,512]{2,1,0:T(8,128)S(1)}, u32[]{:S(2)}, u32[]{:S(2)}) collective-permute-start(f32[13,8,512]{2,1,0:T(8,128)S(1)} %get-tuple-element.24), channel_id=1, source_target_pairs={{0,8},{1,9},{2,10},{3,11},{4,12},{5,13},{6,14},{7,15},{8,0},{9,1},... | collective-permute-start | bytes 638984 | tf_op jit(solution)/shard_map/ppermute | solution.py:336
  25.6 10.5 %collective-permute-start.9 = (f32[13,8,512]{2,1,0:T(8,128)S(1)}, f32[13,8,512]{2,1,0:T(8,128)S(1)}, u32[]{:S(2)}, u32[]{:S(2)}) collective-permute-start(f32[13,8,512]{2,1,0:T(8,128)S(1)} %get-tuple-element.25), channel_id=1, source_target_pairs={{0,16},{1,17},{2,18},{3,19},{4,20},{5,21},{6,22},{7,23},{8,24},{9,... | collective-permute-start | bytes 638984 | tf_op jit(solution)/shard_map/ppermute | solution.py:336
  27.1 9.0 %collective-permute-start.10 = (f32[13,8,512]{2,1,0:T(8,128)S(1)}, f32[13,8,512]{2,1,0:T(8,128)S(1)}, u32[]{:S(2)}, u32[]{:S(2)}) collective-permute-start(f32[13,8,512]{2,1,0:T(8,128)S(1)} %get-tuple-element.26), channel_id=1, source_target_pairs={{0,24},{1,25},{2,26},{3,27},{4,28},{5,29},{6,30},{7,31},{8,16},{9,... | collective-permute-start | bytes 638984 | tf_op jit(solution)/shard_map/ppermute | solution.py:336

commit v2 on v1

v2 whole, which is shorter than its diff:
```python
import functools

import jax
import jax.numpy as jnp
from jax import lax
from jax.experimental import pallas as pl
from jax.experimental.pallas import tpu as pltpu
from jax.sharding import PartitionSpec as P

SUB = 8
LANES = 128
MIB = 1024 * 1024


def row_tile(t):
    return pl.ds(pl.multiple_of(t * SUB, SUB), SUB)


def height(index_ref, k):
    return 0.5 + 0.25 * index_ref[k].astype(jnp.float32)


def half_sum(index_ref, k):
    return 0.5 * (height(index_ref, k) + height(index_ref, k + 1))


def ladder_kernel(
    cells, blocks, chips,
    index_hbm, diffusion_hbm, walls_hbm, velocity_hbm,
    mine_ref, away_ref, pair_ref, chip_ref, left_ref, right_ref, ends_ref,
    index_ref, diffusion_ref, walls_ref, velocity_ref, through_ref, inverse_ref, scale_ref, sems,
):
    total = cells * blocks
    components = velocity_ref.shape[0]
    small = [
        pltpu.make_async_copy(index_hbm, index_ref, sems.at[0]),
        pltpu.make_async_copy(diffusion_hbm, diffusion_ref, sems.at[1]),
        pltpu.make_async_copy(walls_hbm, walls_ref, sems.at[2]),
    ]
    large = [
        pltpu.make_async_copy(velocity_hbm.at[c], velocity_ref.at[c], sems.at[3 + c])
        for c in range(components)
    ]
    for copy in small + large:
        copy.start()
    me = lax.axis_index("gz")
    chip = me // 2
    first = chip * 2
    for copy in small:
        copy.wait()
    diffusion = diffusion_ref[...]
    inverse_ref[...] = 1.0 / diffusion
    walls = walls_ref[...]
    lower = diffusion * (walls % 2).astype(jnp.float32) * 2.0 / height(index_ref, 0)
    upper = diffusion * (walls // 2).astype(jnp.float32) * 2.0 / height(index_ref, total - 1)

    def forward(block, kappa, keep=None):
        start = block * cells
        inverse = inverse_ref[...]
        flux = height(index_ref, start) + kappa
        value = jnp.ones_like(flux)
        for j in range(cells):
            if keep is not None:
                keep(j, flux, value)
            k = start + j
            if j < cells - 1:
                value = value + (half_sum(index_ref, k) * inverse) * flux
                flux = flux + height(index_ref, k + 1) * value
        k = jnp.minimum(start + cells - 1, total - 2)
        after = 1.0 / (value + (half_sum(index_ref, k) * inverse) * flux)
        return flux * after, after

    def backward(block, kappa, scale=None, keep=None):
        start = block * cells
        inverse = inverse_ref[...]
        flux = height(index_ref, start + cells - 1) + kappa
        value = jnp.ones_like(flux)
        if scale is not None:
            flux, value = flux * scale, scale
        for j in reversed(range(cells)):
            if keep is not None:
                keep(j, flux, value)
            k = start + j
            if j > 0:
                value = value + (half_sum(index_ref, k - 1) * inverse) * flux
                flux = flux + height(index_ref, k - 1) * value
        k = jnp.maximum(start - 1, 0)
        after = 1.0 / (value + (half_sum(index_ref, k) * inverse) * flux)
        return flux * after, after

    def sweep_forward(block, state):
        kappa, product = state
        kappa, after = forward(block, kappa)
        through_ref[block] = after
        return kappa, product * after

    def sweep_backward(step, state):
        block = blocks - 1 - step
        kappa, product = state
        kappa, after = backward(block, kappa)
        through_ref[block] = after
        return kappa, product * after

    ones = jnp.ones_like(diffusion)
    kappa_left, product_left = lax.fori_loop(0, me, sweep_forward, (lower, ones))
    ends_ref[0] = lower * product_left
    state = {}

    def keep_left(j, flux, value):
        left_ref[j] = value
        state["flux"], state["value"] = flux, value

    kappa, own_forward = forward(me, kappa_left, keep_left)

    @pl.when(me == first)
    def _():
        pair_ref[2] = own_forward
        _, after = forward(me + 1, kappa)
        pair_ref[0] = after

    @pl.when(me != first)
    def _():
        pair_ref[2] = through_ref[first]
        pair_ref[0] = own_forward

    kappa_right, product_right = lax.fori_loop(
        0, blocks - 1 - me, sweep_backward, (upper, ones)
    )
    ends_ref[1] = upper * product_right
    scale = 1.0 / (state["flux"] + kappa_right * state["value"])
    scale_ref[0] = scale

    def keep_right(j, flux, value):
        right_ref[j] = value

    kappa, own_backward = backward(me, kappa_right, scale, keep_right)
    scale_ref[1] = own_forward
    scale_ref[2] = own_backward

    @pl.when(me == first)
    def _():
        pair_ref[1] = own_backward * scale
        pair_ref[3] = through_ref[first + 1]

    @pl.when(me != first)
    def _():
        pair_ref[3] = own_backward * scale
        _, after = backward(me - 1, kappa)
        pair_ref[1] = after

    for m in range(1, chips):
        other = chip ^ m
        low = jnp.minimum(chip, other)
        high = jnp.maximum(chip, other)
        chip_ref[m - 1] = lax.fori_loop(
            low + 1,
            high,
            lambda r, product: product * (through_ref[2 * r] * through_ref[2 * r + 1]),
            ones,
        )
    for copy in large:
        copy.wait()
    flow = jnp.zeros((SUB, LANES), jnp.float32)
    weight = jnp.zeros((SUB, LANES), jnp.float32)

    def fold(array):
        parts = [array[:, i * LANES:(i + 1) * LANES] for i in range(array.shape[1] // LANES)]
        return functools.reduce(jnp.add, parts)

    half = diffusion.shape[0] // SUB // 2
    heights = [height(index_ref, me * cells + j) for j in range(cells)]
    for ref, whose in ((away_ref, 1 - (me - first)), (mine_ref, me - first)):
        for i in range(half):
            rows = row_tile(whose * half + i)
            from_left = [0.0] * components
            from_right = [0.0] * components
            plain = 0.0
            left_total = 0.0
            right_total = 0.0
            extent = 0.0
            for j in range(cells):
                h = heights[j]
                left = h * left_ref[j, rows]
                right = h * right_ref[j, rows]
                extent = extent + h
                left_total = left_total + left
                right_total = right_total + right
                for c in range(components):
                    v = velocity_ref[c, j, rows]
                    from_left[c] = from_left[c] + left * v
                    from_right[c] = from_right[c] + right * v
                    if c == 0:
                        plain = plain + h * v
            low_part = ends_ref[0, rows]
            high_part = ends_ref[1, rows] * scale_ref[0, rows]
            for c in range(components):
                ref[i * 2 * components + c] = from_left[c] * scale_ref[1, rows]
                ref[i * 2 * components + components + c] = from_right[c] * scale_ref[2, rows]
            flow = flow + fold(plain - low_part * from_right[0] - high_part * from_left[0])
            weight = weight + fold(extent - low_part * right_total - high_part * left_total)
    away_ref[half * 2 * components] = jnp.zeros(away_ref.shape[1:], jnp.float32)
    away_ref[half * 2 * components, :, 0:LANES] = flow
    away_ref[half * 2 * components, :, LANES:2 * LANES] = weight


def merge_kernel(chips, components, mine_ref, away_ref, mate_ref, pair_ref, _, *rest):
    send_refs, tile_ref = rest[:-1], rest[-1]
    me = lax.axis_index("gz")
    chip = me // 2
    is_first = me == chip * 2
    half = mine_ref.shape[0] // (2 * components)
    slot = half * 2 * components
    for i in range(2):
        lanes = slice(i * LANES, (i + 1) * LANES)
        tile_ref[i] = away_ref[slot, :, lanes] + mate_ref[slot, :, lanes]
    for i in range(half):
        rows = row_tile((me - chip * 2) * half + i)
        for c in range(components):
            at = i * 2 * components + c
            mine, mate = mine_ref[at], mate_ref[at]
            first = jnp.where(is_first, mine, mate)
            second = jnp.where(is_first, mate, mine)
            to_right = second + pair_ref[0, rows] * first
            at = at + components
            mine, mate = mine_ref[at], mate_ref[at]
            first = jnp.where(is_first, mine, mate)
            second = jnp.where(is_first, mate, mine)
            to_left = first + pair_ref[1, rows] * second
            for m in range(1, chips):
                goes_right = (chip ^ m) > chip
                send_refs[m - 1][i * components + c] = jnp.where(goes_right, to_right, to_left)


def spread_kernel(chips, components, mine_ref, mate_ref, pair_ref, chip_ref, _, *rest):
    recv_refs, (own_ref, other_ref) = rest[:chips - 1], rest[chips - 1:]
    me = lax.axis_index("gz")
    chip = me // 2
    is_first = me == chip * 2
    half = mine_ref.shape[0] // (2 * components)
    for i in range(half):
        rows = row_tile((me - chip * 2) * half + i)
        coefs = [chip_ref[m, rows] for m in range(chips - 1)]
        for c in range(components):
            left_in = jnp.zeros(mine_ref.shape[1:], jnp.float32)
            right_in = jnp.zeros(mine_ref.shape[1:], jnp.float32)
            for m in range(1, chips):
                term = coefs[m - 1] * recv_refs[m - 1][i * components + c]
                from_left = (chip ^ m) < chip
                left_in = left_in + jnp.where(from_left, term, 0.0)
                right_in = right_in + jnp.where(from_left, 0.0, term)
            at = i * 2 * components + c
            first_out = jnp.where(is_first, mine_ref[at], mate_ref[at])
            left_second = first_out + pair_ref[2, rows] * left_in
            at = at + components
            second_out = jnp.where(is_first, mate_ref[at], mine_ref[at])
            right_first = second_out + pair_ref[3, rows] * right_in
            at = i * 2 * components + c
            own_ref[at] = jnp.where(is_first, left_in, left_second)
            other_ref[at] = jnp.where(is_first, left_second, left_in)
            at = at + components
            own_ref[at] = jnp.where(is_first, right_first, right_in)
            other_ref[at] = jnp.where(is_first, right_in, right_first)


def add_kernel(*refs):
    refs[-1][...] = functools.reduce(jnp.add, [ref[...] for ref in refs[:-1]])


def inner_kernel(cells, index_ref, velocity_ref, left_ref, right_ref, base_ref):
    me = lax.axis_index("gz")
    components = velocity_ref.shape[0]
    heights = [height(index_ref, me * cells + j) for j in range(cells)]
    gathered = [jnp.zeros(left_ref.shape[1:], jnp.float32)] * components
    for j in reversed(range(cells)):
        left = left_ref[j]
        right = heights[j] * right_ref[j]
        for c in range(components):
            base_ref[c, j] = left * gathered[c]
            if j > 0:
                gathered[c] = gathered[c] + right * velocity_ref[c, j]
    gathered = [jnp.zeros(left_ref.shape[1:], jnp.float32)] * components
    for j in range(cells):
        left = heights[j] * left_ref[j]
        right = right_ref[j]
        for c in range(components):
            gathered[c] = gathered[c] + left * velocity_ref[c, j]
            base_ref[c, j] = base_ref[c, j] + right * gathered[c]


def emit(parts, rows, alpha, ends_ref, incoming_ref, at, base_ref, left_ref, right_ref, result_ref):
    cells = left_ref.shape[0]
    components = base_ref.shape[0]
    scale = right_ref[cells - 1, rows]
    lefts, rights = {}, {}
    for c in parts:
        left_in = incoming_ref[at + c]
        right_in = incoming_ref[at + components + c]
        if c == 0:
            left_in = left_in - alpha * ends_ref[0, rows]
            right_in = right_in - alpha * ends_ref[1, rows]
        lefts[c] = left_in
        rights[c] = right_in * scale
    for j in range(cells):
        left = left_ref[j, rows]
        right = right_ref[j, rows]
        for c in parts:
            value = base_ref[c, j, rows] + (right * lefts[c] + left * rights[c])
            result_ref[c, j, rows] = value + alpha if c == 0 else value


def early_kernel(own_ref, base_ref, left_ref, right_ref, out_hbm, result_ref, sems):
    components = base_ref.shape[0]
    half = own_ref.shape[0] // (2 * components)
    me = lax.axis_index("gz")
    copies = []
    for i in range(half):
        rows = row_tile(lax.rem(me, 2) * half + i)
        emit(range(1, components), rows, None, None, own_ref, i * 2 * components,
             base_ref, left_ref, right_ref, result_ref)
        for c in range(1, components):
            copies.append(pltpu.make_async_copy(
                result_ref.at[c, :, rows], out_hbm.at[c, :, rows], sems.at[len(copies)]))
            copies[-1].start()
    for copy in copies:
        copy.wait()


def late_kernel(
    lines, index_ref, target_ref, ends_ref, own_ref, other_ref, base_ref, left_ref, right_ref,
    *rest,
):
    tile_refs, (_, out_hbm, result_ref, sems) = rest[:-4], rest[-4:]
    components = base_ref.shape[0]
    half = own_ref.shape[0] // (2 * components)
    me = lax.axis_index("gz")
    copies = []

    def leave(c, rows):
        copies.append(pltpu.make_async_copy(
            result_ref.at[c, :, rows], out_hbm.at[c, :, rows], sems.at[len(copies)]))
        copies[-1].start()

    for i in range(half):
        rows = row_tile((1 - lax.rem(me, 2)) * half + i)
        emit(range(1, components), rows, None, None, other_ref, i * 2 * components,
             base_ref, left_ref, right_ref, result_ref)
        for c in range(1, components):
            leave(c, rows)
    extent = 0.0
    for k in range(index_ref.shape[0]):
        extent = extent + height(index_ref, k)
    totals = functools.reduce(jnp.add, [ref[...] for ref in tile_refs])
    flow = jnp.sum(totals[0], keepdims=True)
    weight = jnp.sum(totals[1], keepdims=True)
    alpha = (target_ref[0] * (extent * lines) - flow) / weight
    for ref, whose in ((own_ref, lax.rem(me, 2)), (other_ref, 1 - lax.rem(me, 2))):
        for i in range(half):
            rows = row_tile(whose * half + i)
            emit((0,), rows, alpha, ends_ref, ref, i * 2 * components,
                 base_ref, left_ref, right_ref, result_ref)
            leave(0, rows)
    for copy in copies:
        copy.wait()


def shards(velocity, diffusion, wall_types, stretch_index, bulk_target):
    blocks = lax.axis_size("gz")
    columns = lax.axis_size("gy")
    components, cells, lines_y, lines_x = velocity.shape
    chips = blocks // 2
    row_tiles = lines_y // SUB
    half = row_tiles // 2
    f32 = jnp.float32
    vmem = pl.BlockSpec(memory_space=pltpu.VMEM)
    smem = pl.BlockSpec(memory_space=pltpu.SMEM)
    anywhere = pl.BlockSpec(memory_space=pl.ANY)
    plane = (lines_y, lines_x)
    sheet = (SUB, lines_x)
    tile = jax.ShapeDtypeStruct((2, SUB, LANES), f32)

    def shape(*dims):
        return jax.ShapeDtypeStruct(dims, f32)

    def in_hbm(array):
        return pltpu.with_memory_space_constraint(array, pltpu.HBM)

    def options(mib):
        return pltpu.CompilerParams(vmem_limit_bytes=mib * MIB)

    def cost(flops, transferred):
        return pl.CostEstimate(flops=flops, bytes_accessed=transferred, transcendentals=0)

    mine, away, pair, chip_coefs, left, right, ends = pl.pallas_call(
        functools.partial(ladder_kernel, cells, blocks, chips),
        out_shape=[
            shape(half * 2 * components, *sheet),
            shape(half * 2 * components + 1, *sheet),
            shape(4, *plane),
            shape(chips - 1, *plane),
            shape(cells, *plane),
            shape(cells, *plane),
            shape(2, *plane),
        ],
        in_specs=[anywhere] * 4,
        out_specs=[vmem] * 7,
        scratch_shapes=[
            pltpu.SMEM(stretch_index.shape, jnp.int32),
            pltpu.VMEM(plane, f32),
            pltpu.VMEM(plane, jnp.int32),
            pltpu.VMEM(velocity.shape, f32),
            pltpu.VMEM((blocks,) + plane, f32),
            pltpu.VMEM(plane, f32),
            pltpu.VMEM((3,) + plane, f32),
            pltpu.SemaphoreType.DMA((3 + components,)),
        ],
        compiler_params=options(24),
        cost_estimate=cost(40_000_000, 6_000_000),
        name="ladder",
    )(in_hbm(stretch_index), in_hbm(diffusion), in_hbm(wall_types), in_hbm(velocity))

    def send(array, partner):
        pairs = [((z, y), partner(z, y)) for z in range(blocks) for y in range(columns)]
        route = [(a * columns + b, c * columns + d) for (a, b), (c, d) in pairs]
        return lax.ppermute(array, ("gz", "gy"), route)

    def to_mate(array):
        return send(array, lambda z, y: (z ^ 1, y))

    def to_chips(array):
        return [send(array, lambda z, y: (z ^ (2 * m), y)) for m in range(1, chips)]

    mate = to_mate(away)
    state = pl.BlockSpec((components, cells, SUB, lines_x), lambda t: (0, 0, t, 0))
    profile = pl.BlockSpec((cells, SUB, lines_x), lambda t: (0, t, 0))
    base = pl.pallas_call(
        functools.partial(inner_kernel, cells),
        grid=(row_tiles,),
        out_shape=shape(*velocity.shape),
        in_specs=[smem, state, profile, profile],
        out_specs=state,
        compiler_params=options(16),
        cost_estimate=cost(8_000_000, 8_000_000),
        name="inner",
    )(stretch_index, in_hbm(velocity), left, right)
    *outgoing, chip_tile = pl.pallas_call(
        functools.partial(merge_kernel, chips, components),
        out_shape=[shape(half * components, *sheet)] * (chips - 1) + [tile],
        in_specs=[vmem] * 4 + [anywhere],
        out_specs=[vmem] * chips,
        compiler_params=options(16),
        cost_estimate=cost(500_000, 1_600_000),
        name="merge",
    )(mine, away, mate, pair, base)
    incoming = [
        send(outgoing[m - 1], lambda z, y: (z ^ (2 * m), y)) for m in range(1, chips)
    ]
    tiles = [chip_tile] + [
        send(chip_tile, lambda z, y: (z, (y + shift) % columns)) for shift in range(1, columns)
    ]
    column_tile = pl.pallas_call(
        add_kernel,
        out_shape=tile,
        in_specs=[vmem] * len(tiles),
        out_specs=vmem,
        compiler_params=options(16),
        cost_estimate=cost(10_000, 40_000),
        name="column_sum",
    )(*tiles)

    own_in, other_out = pl.pallas_call(
        functools.partial(spread_kernel, chips, components),
        out_shape=[shape(half * 2 * components, *sheet)] * 2,
        in_specs=[vmem] * 4 + [anywhere] + [vmem] * (chips - 1),
        out_specs=[vmem] * 2,
        compiler_params=options(16),
        cost_estimate=cost(500_000, 1_600_000),
        name="spread",
    )(mine, mate, pair, chip_coefs, column_tile, *incoming)
    other_in = to_mate(other_out)
    plane_tiles = [column_tile] + to_chips(column_tile)
    early = pl.pallas_call(
        early_kernel,
        out_shape=shape(*velocity.shape),
        in_specs=[vmem] * 4,
        out_specs=anywhere,
        scratch_shapes=[
            pltpu.VMEM(velocity.shape, f32),
            pltpu.SemaphoreType.DMA(((components - 1) * half,)),
        ],
        compiler_params=options(16),
        cost_estimate=cost(2_000_000, 4_000_000),
        name="early",
    )(own_in, base, left, right)
    return pl.pallas_call(
        functools.partial(late_kernel, float(lines_y * columns * lines_x)),
        out_shape=shape(*velocity.shape),
        in_specs=[smem, smem] + [vmem] * (6 + chips) + [anywhere],
        out_specs=anywhere,
        scratch_shapes=[
            pltpu.VMEM(velocity.shape, f32),
            pltpu.SemaphoreType.DMA(((components + 1) * half,)),
        ],
        input_output_aliases={8 + chips: 0},
        compiler_params=options(16),
        cost_estimate=cost(3_000_000, 6_000_000),
        name="late",
    )(stretch_index, bulk_target, ends, own_in, other_in, base, left, right, *plane_tiles, early)


def solution(mesh):
    return jax.shard_map(
        shards,
        mesh=mesh,
        in_specs=(P(None, "gz", "gy", None), P("gy", None), P("gy", None), P(), P()),
        out_specs=P(None, "gz", "gy", None),
        check_vma=False,
    )
```

time: 40.8 us -> 32.6 us (0.80)
  local copies, waits for them, and re-layouts: 4.22 us -> 0.01 us
  waiting for transfers between devices: 11.3 us -> 8.15 us
  starting transfers between devices: 13.6 us -> 12.6 us
    unnamed x8 -> x2, local copies, waits for them, and re-layouts: 4.22 us -> 0.01 us
    ppermute x11, waiting for transfers between devices: 11.3 us -> 8.15 us  [send(): return lax.ppermute(array, ('gz', 'gy'), route)]
    pallas_call x2 -> x5, Pallas kernels: 4.57 us -> 3.38 us  [the longest x1 2.11 us: shards(): pl.pallas_call(functools.partial(late_kernel, float(lines_y * columns * l...]
    pallas_call x1, Pallas kernels: 2.14 us -> 3.33 us  [shards(): pl.pallas_call(functools.partial(inner_kernel, cells), grid=(row_tiles,),...]
    ppermute x11, starting transfers between devices: 13.6 us -> 12.6 us  [send(): return lax.ppermute(array, ('gz', 'gy'), route)]
  transfers between devices with their start and end apart: 11 -> 11, of which waited for: 6 -> 5; matrix products, arithmetic and copies ran while one was open for 0% -> 0% of each run, Pallas kernels for 5% -> 14%
where the time goes in v2:
time: 32.6 us; the launch traced here: 32.4 us
  starting transfers between devices  12.6 us (39%)
  Pallas kernels  10.9 us (33%)
  waiting for transfers between devices  8.15 us (25%)
  between operations  0.74 us (2%)
    ppermute x11, starting transfers between devices, send(): return lax.ppermute(array, ('gz', 'gy'), route)  12.6 us
    ppermute x11, waiting for transfers between devices, send(): return lax.ppermute(array, ('gz', 'gy'), route)  8.15 us
    pallas_call x1, Pallas kernels, shards(): pl.pallas_call(functools.partial(ladder_kernel, cells, blocks, chips), ou...  4.22 us
    pallas_call x1, Pallas kernels, shards(): pl.pallas_call(functools.partial(inner_kernel, cells), grid=(row_tiles,),...  3.33 us
    pallas_call x1, Pallas kernels, shards(): pl.pallas_call(functools.partial(late_kernel, float(lines_y * columns * l...  2.11 us
    pallas_call x1, Pallas kernels, shards(): pl.pallas_call(early_kernel, out_shape=shape(*velocity.shape), in_specs=[...  1.1 us
  transfers between devices with their start and end apart: 11, of which 5 were waited for; matrix products, arithmetic and copies ran while one was open for 0% of the time, Pallas kernels for 14%

profile of v2, /device:TPU:0, one launch (start us, length us, event | category | flops | bytes accessed | tf_op | source)
XLA Modules:
  0.0 32.4 jit_solution(11627380341959495420)
XLA Ops:
  0.0 0.0 copy-start
  0.0 4.2 %ladder.1 = (f32[12,8,512]{2,1,0:T(8,128)S(1)}, f32[13,8,512]{2,1,0:T(8,128)S(1)}, f32[4,32,512]{2,1,0:T(8,128)S(1)}, f32[3,32,512]{2,1,0:T(8,128)S(1)}, f32[16,...) custom-call(s32[128]{0:T(128)} %index_ref.3, f32[32,512]{1,0:T(8,128)} %diffusion_hbm.1, ...), custom_call_target="tpu_custom_call" | custom-call | flops 40000000 | bytes 6000000 | tf_op jit(solution)/shard_map/ladder/pallas_call | solution.py:393
  4.2 0.5 %collective-permute-start = (f32[13,8,512]{2,1,0:T(8,128)S(1)}, f32[13,8,512]{2,1,0:T(8,128)S(1)}, u32[]{:S(2)}, u32[]{:S(2)}) collective-permute-start(f32[13,8,512]{2,1,0:T(8,128)S(1)} %get-tuple-element.20.away_ref), channel_id=1, source_target_pairs={{0,4},{1,5},{2,6},{3,7},{4,0},{5,1},{6,2},{7,3},{8,12},{9,13},{10,... | collective-permute-start | bytes 638984 | tf_op jit(solution)/shard_map/ppermute | solution.py:424
  4.7 0.0 copy-done
  4.8 3.3 %inner.1._.base_ref = f32[3,16,32,512]{3,2,1,0:T(8,128)S(1)} custom-call(s32[128]{0:T(128)S(1)} %copy-done, f32[3,16,32,512]{3,2,1,0:T(8,128)} %velocity_ref.1, f32[16,32,512]{2,1,0:T(8,128)S(1)} %get-tuple-element.23.left_ref, f32[16,32,512]{2,1,0:T(8,128)S(1)} %get-tuple-element.24.right_ref), custom_call_target="tpu_custom_call" | custom-call | flops 8000000 | bytes 8000000 | tf_op jit(solution)/shard_map/inner/pallas_call | solution.py:435
  8.1 0.0 collective-permute-done.mate_ref
  8.1 0.1 merge.1
  8.2 2.6 %collective-permute-start.4 = (f32[6,8,512]{2,1,0:T(8,128)S(1)}, f32[6,8,512]{2,1,0:T(8,128)S(1)}, u32[]{:S(2)}, u32[]{:S(2)}) collective-permute-start(f32[6,8,512]{2,1,0:T(8,128)S(1)} %get-tuple-element.26), channel_id=1, source_target_pairs={{0,8},{1,9},{2,10},{3,11},{4,12},{5,13},{6,14},{7,15},{8,0},{9,1},... | collective-permute-start | bytes 294920 | tf_op jit(solution)/shard_map/ppermute | solution.py:424
  10.7 1.5 %collective-permute-start.5 = (f32[6,8,512]{2,1,0:T(8,128)S(1)}, f32[6,8,512]{2,1,0:T(8,128)S(1)}, u32[]{:S(2)}, u32[]{:S(2)}) collective-permute-start(f32[6,8,512]{2,1,0:T(8,128)S(1)} %get-tuple-element.27), channel_id=1, source_target_pairs={{0,16},{1,17},{2,18},{3,19},{4,20},{5,21},{6,22},{7,23},{8,24},{9,... | collective-permute-start | bytes 294920 | tf_op jit(solution)/shard_map/ppermute | solution.py:424
  12.3 0.0 collective-permute-start.6
  12.3 4.1 %collective-permute-start.3 = (f32[2,8,128]{2,1,0:T(8,128)S(1)}, f32[2,8,128]{2,1,0:T(8,128)S(1)}, u32[]{:S(2)}, u32[]{:S(2)}) collective-permute-start(f32[2,8,128]{2,1,0:T(8,128)S(1)} %get-tuple-element.25.refs_0_), channel_id=1, source_target_pairs={{0,3},{1,0},{2,1},{3,2},{4,7},{5,4},{6,5},{7,6},{8,11},{9,8},{10,9... | collective-permute-start | bytes 24584 | tf_op jit(solution)/shard_map/ppermute | solution.py:424
  16.4 0.0 collective-permute-start.2
  16.4 1.4 %collective-permute-done.3.refs_3_ = f32[2,8,128]{2,1,0:T(8,128)S(1)} collective-permute-done((f32[2,8,128]{2,1,0:T(8,128)S(1)}, f32[2,8,128]{2,1,0:T(8,128)S(1)}, u32[]{:S(2)}, u32[]{:S(2)}) %collective-permute-start.3) | collective-permute-done | bytes 8224 | tf_op jit(solution)/shard_map/ppermute | solution.py:424
  17.7 0.3 collective-permute-start.1
  18.0 2.9 %collective-permute-done.2.refs_2_ = f32[2,8,128]{2,1,0:T(8,128)S(1)} collective-permute-done((f32[2,8,128]{2,1,0:T(8,128)S(1)}, f32[2,8,128]{2,1,0:T(8,128)S(1)}, u32[]{:S(2)}, u32[]{:S(2)}) %collective-permute-start.2) | collective-permute-done | bytes 8224 | tf_op jit(solution)/shard_map/ppermute | solution.py:424
  20.9 2.5 %collective-permute-done.1.refs_1_ = f32[2,8,128]{2,1,0:T(8,128)S(1)} collective-permute-done((f32[2,8,128]{2,1,0:T(8,128)S(1)}, f32[2,8,128]{2,1,0:T(8,128)S(1)}, u32[]{:S(2)}, u32[]{:S(2)}) %collective-permute-start.1) | collective-permute-done | bytes 8224 | tf_op jit(solution)/shard_map/ppermute | solution.py:424
  23.4 0.0 collective-permute-done.4.rest_0_
  23.4 0.0 collective-permute-done.5.rest_1_
  23.5 0.0 collective-permute-done.6.rest_2_
  23.5 0.1 spread.1
  23.6 0.1 collective-permute-start.7
  23.7 2.5 %collective-permute-start.10 = (f32[2,8,128]{2,1,0:T(8,128)S(1)}, f32[2,8,128]{2,1,0:T(8,128)S(1)}, u32[]{:S(2)}, u32[]{:S(2)}) collective-permute-start(f32[2,8,128]{2,1,0:T(8,128)S(1)} %column_sum.1._.rest_0_), channel_id=1, source_target_pairs={{0,24},{1,25},{2,26},{3,27},{4,28},{5,29},{6,30},{7,31},{8,16},{9,... | collective-permute-start | bytes 24584 | tf_op jit(solution)/shard_map/ppermute | solution.py:424
  26.2 0.5 %collective-permute-start.9 = (f32[2,8,128]{2,1,0:T(8,128)S(1)}, f32[2,8,128]{2,1,0:T(8,128)S(1)}, u32[]{:S(2)}, u32[]{:S(2)}) collective-permute-start(f32[2,8,128]{2,1,0:T(8,128)S(1)} %column_sum.1._.rest_0_), channel_id=1, source_target_pairs={{0,16},{1,17},{2,18},{3,19},{4,20},{5,21},{6,22},{7,23},{8,24},{9,... | collective-permute-start | bytes 24584 | tf_op jit(solution)/shard_map/ppermute | solution.py:424
  26.7 0.6 %collective-permute-start.8 = (f32[2,8,128]{2,1,0:T(8,128)S(1)}, f32[2,8,128]{2,1,0:T(8,128)S(1)}, u32[]{:S(2)}, u32[]{:S(2)}) collective-permute-start(f32[2,8,128]{2,1,0:T(8,128)S(1)} %column_sum.1._.rest_0_), channel_id=1, source_target_pairs={{0,8},{1,9},{2,10},{3,11},{4,12},{5,13},{6,14},{7,15},{8,0},{9,1},... | collective-permute-start | bytes 24584 | tf_op jit(solution)/shard_map/ppermute | solution.py:424
  27.9 1.1 %early.1.rest_4_ = f32[3,16,32,512]{3,2,1,0:T(8,128)} custom-call(f32[12,8,512]{2,1,0:T(8,128)S(1)} %get-tuple-element.29.own_ref, f32[3,16,32,512]{3,2,1,0:T(8,128)S(1)} %inner.1._.base_ref, f32[16,32,512]{2,1,0:T(8,128)S(1)} %get-tuple-element.23.left_ref, f32[16,32,512]{2,1,0:T(8,128)S(1)} %get-tuple-element.24.right_ref), custom_call_target="tpu_custom_call" | custom-call | flops 2000000 | bytes 4000000 | tf_op jit(solution)/shard_map/early/pallas_call | solution.py:481
  29.0 0.0 collective-permute-done.10.rest_3_
  29.0 0.8 %collective-permute-done.9.rest_2_ = f32[2,8,128]{2,1,0:T(8,128)S(1)} collective-permute-done((f32[2,8,128]{2,1,0:T(8,128)S(1)}, f32[2,8,128]{2,1,0:T(8,128)S(1)}, u32[]{:S(2)}, u32[]{:S(2)}) %collective-permute-start.9) | collective-permute-done | bytes 8224 | tf_op jit(solution)/shard_map/ppermute | solution.py:424
  29.8 0.5 %collective-permute-done.8.rest_1_ = f32[2,8,128]{2,1,0:T(8,128)S(1)} collective-permute-done((f32[2,8,128]{2,1,0:T(8,128)S(1)}, f32[2,8,128]{2,1,0:T(8,128)S(1)}, u32[]{:S(2)}, u32[]{:S(2)}) %collective-permute-start.8) | collective-permute-done | bytes 8224 | tf_op jit(solution)/shard_map/ppermute | solution.py:424
  30.3 0.0 collective-permute-done.7.other_ref
  30.3 2.1 %late.1 = f32[3,16,32,512]{3,2,1,0:T(8,128)} custom-call(s32[128]{0:T(128)S(1)} %copy-done, f32[1]{0:T(128)S(6)} %copy.8.target_ref, f32[2,32,512]{2,1,0:T(8,128)S(1)} %get-tuple-element.18.ends_ref, f32[12,8,512]{2,1,0:T(8,128)S(1)} %get-tuple-element.29.own_ref, ...), custom_call_target="tpu_custom_call", output_to_operand_aliasing={{}: (12, {})} | custom-call | flops 3000000 | bytes 6000000 | tf_op jit(solution)/shard_map/late/pallas_call | solution.py:494
  (1 shorter events, 0.0 us)
Async XLA Ops:
  0.0 4.7 %copy-start = (s32[128]{0:T(128)S(1)}, s32[128]{0:T(128)}, u32[]{:S(2)}) copy-start(s32[128]{0:T(128)} %index_ref.3) | copy-start | bytes 1540
  4.2 3.9 %collective-permute-start = (f32[13,8,512]{2,1,0:T(8,128)S(1)}, f32[13,8,512]{2,1,0:T(8,128)S(1)}, u32[]{:S(2)}, u32[]{:S(2)}) collective-permute-start(f32[13,8,512]{2,1,0:T(8,128)S(1)} %get-tuple-element.20.away_ref), channel_id=1, source_target_pairs={{0,4},{1,5},{2,6},{3,7},{4,0},{5,1},{6,2},{7,3},{8,12},{9,13},{10,... | collective-permute-start | bytes 638984 | tf_op jit(solution)/shard_map/ppermute | solution.py:424
  8.2 15.3 %collective-permute-start.4 = (f32[6,8,512]{2,1,0:T(8,128)S(1)}, f32[6,8,512]{2,1,0:T(8,128)S(1)}, u32[]{:S(2)}, u32[]{:S(2)}) collective-permute-start(f32[6,8,512]{2,1,0:T(8,128)S(1)} %get-tuple-element.26), channel_id=1, source_target_pairs={{0,8},{1,9},{2,10},{3,11},{4,12},{5,13},{6,14},{7,15},{8,0},{9,1},... | collective-permute-start | bytes 294920 | tf_op jit(solution)/shard_map/ppermute | solution.py:424
  10.7 12.7 %collective-permute-start.5 = (f32[6,8,512]{2,1,0:T(8,128)S(1)}, f32[6,8,512]{2,1,0:T(8,128)S(1)}, u32[]{:S(2)}, u32[]{:S(2)}) collective-permute-start(f32[6,8,512]{2,1,0:T(8,128)S(1)} %get-tuple-element.27), channel_id=1, source_target_pairs={{0,16},{1,17},{2,18},{3,19},{4,20},{5,21},{6,22},{7,23},{8,24},{9,... | collective-permute-start | bytes 294920 | tf_op jit(solution)/shard_map/ppermute | solution.py:424
  12.3 11.2 %collective-permute-start.6 = (f32[6,8,512]{2,1,0:T(8,128)S(1)}, f32[6,8,512]{2,1,0:T(8,128)S(1)}, u32[]{:S(2)}, u32[]{:S(2)}) collective-permute-start(f32[6,8,512]{2,1,0:T(8,128)S(1)} %get-tuple-element.28), channel_id=1, source_target_pairs={{0,24},{1,25},{2,26},{3,27},{4,28},{5,29},{6,30},{7,31},{8,16},{9,... | collective-permute-start | bytes 294920 | tf_op jit(solution)/shard_map/ppermute | solution.py:424
  12.3 5.4 %collective-permute-start.3 = (f32[2,8,128]{2,1,0:T(8,128)S(1)}, f32[2,8,128]{2,1,0:T(8,128)S(1)}, u32[]{:S(2)}, u32[]{:S(2)}) collective-permute-start(f32[2,8,128]{2,1,0:T(8,128)S(1)} %get-tuple-element.25.refs_0_), channel_id=1, source_target_pairs={{0,3},{1,0},{2,1},{3,2},{4,7},{5,4},{6,5},{7,6},{8,11},{9,8},{10,9... | collective-permute-start | bytes 24584 | tf_op jit(solution)/shard_map/ppermute | solution.py:424
  16.4 4.5 %collective-permute-start.2 = (f32[2,8,128]{2,1,0:T(8,128)S(1)}, f32[2,8,128]{2,1,0:T(8,128)S(1)}, u32[]{:S(2)}, u32[]{:S(2)}) collective-permute-start(f32[2,8,128]{2,1,0:T(8,128)S(1)} %get-tuple-element.25.refs_0_), channel_id=1, source_target_pairs={{0,2},{1,3},{2,0},{3,1},{4,6},{5,7},{6,4},{7,5},{8,10},{9,11},{10,... | collective-permute-start | bytes 24584 | tf_op jit(solution)/shard_map/ppermute | solution.py:424
  17.7 5.7 %collective-permute-start.1 = (f32[2,8,128]{2,1,0:T(8,128)S(1)}, f32[2,8,128]{2,1,0:T(8,128)S(1)}, u32[]{:S(2)}, u32[]{:S(2)}) collective-permute-start(f32[2,8,128]{2,1,0:T(8,128)S(1)} %get-tuple-element.25.refs_0_), channel_id=1, source_target_pairs={{0,1},{1,2},{2,3},{3,0},{4,5},{5,6},{6,7},{7,4},{8,9},{9,10},{10,1... | collective-permute-start | bytes 24584 | tf_op jit(solution)/shard_map/ppermute | solution.py:424
  23.6 6.7 %collective-permute-start.7 = (f32[12,8,512]{2,1,0:T(8,128)S(1)}, f32[12,8,512]{2,1,0:T(8,128)S(1)}, u32[]{:S(2)}, u32[]{:S(2)}) collective-permute-start(f32[12,8,512]{2,1,0:T(8,128)S(1)} %get-tuple-element.30), channel_id=1, source_target_pairs={{0,4},{1,5},{2,6},{3,7},{4,0},{5,1},{6,2},{7,3},{8,12},{9,13},{10,... | collective-permute-start | bytes 589832 | tf_op jit(solution)/shard_map/ppermute | solution.py:424
  23.7 5.3 %collective-permute-start.10 = (f32[2,8,128]{2,1,0:T(8,128)S(1)}, f32[2,8,128]{2,1,0:T(8,128)S(1)}, u32[]{:S(2)}, u32[]{:S(2)}) collective-permute-start(f32[2,8,128]{2,1,0:T(8,128)S(1)} %column_sum.1._.rest_0_), channel_id=1, source_target_pairs={{0,24},{1,25},{2,26},{3,27},{4,28},{5,29},{6,30},{7,31},{8,16},{9,... | collective-permute-start | bytes 24584 | tf_op jit(solution)/shard_map/ppermute | solution.py:424
  26.2 3.7 %collective-permute-start.9 = (f32[2,8,128]{2,1,0:T(8,128)S(1)}, f32[2,8,128]{2,1,0:T(8,128)S(1)}, u32[]{:S(2)}, u32[]{:S(2)}) collective-permute-start(f32[2,8,128]{2,1,0:T(8,128)S(1)} %column_sum.1._.rest_0_), channel_id=1, source_target_pairs={{0,16},{1,17},{2,18},{3,19},{4,20},{5,21},{6,22},{7,23},{8,24},{9,... | collective-permute-start | bytes 24584 | tf_op jit(solution)/shard_map/ppermute | solution.py:424
  26.7 3.7 %collective-permute-start.8 = (f32[2,8,128]{2,1,0:T(8,128)S(1)}, f32[2,8,128]{2,1,0:T(8,128)S(1)}, u32[]{:S(2)}, u32[]{:S(2)}) collective-permute-start(f32[2,8,128]{2,1,0:T(8,128)S(1)} %column_sum.1._.rest_0_), channel_id=1, source_target_pairs={{0,8},{1,9},{2,10},{3,11},{4,12},{5,13},{6,14},{7,15},{8,0},{9,1},... | collective-permute-start | bytes 24584 | tf_op jit(solution)/shard_map/ppermute | solution.py:424

commit v3 on v2

--- a/solution.py
+++ b/solution.py
@@ -27,7 +27,7 @@
 def ladder_kernel(
     cells, blocks, chips,
     index_hbm, diffusion_hbm, walls_hbm, velocity_hbm,
-    mine_ref, away_ref, pair_ref, chip_ref, left_ref, right_ref, ends_ref,
+    mine_ref, away_ref, pair_ref, chip_ref, left_ref, right_ref, ends_ref, tile_ref,
     index_ref, diffusion_ref, walls_ref, velocity_ref, through_ref, inverse_ref, scale_ref, sems,
 ):
     total = cells * blocks
@@ -51,8 +51,8 @@
     diffusion = diffusion_ref[...]
     inverse_ref[...] = 1.0 / diffusion
     walls = walls_ref[...]
-    lower = diffusion * (walls % 2).astype(jnp.float32) * 2.0 / height(index_ref, 0)
-    upper = diffusion * (walls // 2).astype(jnp.float32) * 2.0 / height(index_ref, total - 1)
+    lower = diffusion * (walls & 1).astype(jnp.float32) * 2.0 / height(index_ref, 0)
+    upper = diffusion * (walls >> 1).astype(jnp.float32) * 2.0 / height(index_ref, total - 1)
 
     def forward(block, kappa, keep=None):
         start = block * cells
@@ -160,12 +160,12 @@
         )
     for copy in large:
         copy.wait()
-    flow = jnp.zeros((SUB, LANES), jnp.float32)
-    weight = jnp.zeros((SUB, LANES), jnp.float32)
-
-    def fold(array):
-        parts = [array[:, i * LANES:(i + 1) * LANES] for i in range(array.shape[1] // LANES)]
-        return functools.reduce(jnp.add, parts)
+    flow = [jnp.zeros((SUB, LANES), jnp.float32)] * 2
+    weight = [jnp.zeros((SUB, LANES), jnp.float32)] * 2
+
+    def fold(sums, array):
+        for i in range(array.shape[1] // LANES):
+            sums[i % 2] = sums[i % 2] + array[:, i * LANES:(i + 1) * LANES]
 
     half = diffusion.shape[0] // SUB // 2
     heights = [height(index_ref, me * cells + j) for j in range(cells)]
@@ -196,23 +196,17 @@
             for c in range(components):
                 ref[i * 2 * components + c] = from_left[c] * scale_ref[1, rows]
                 ref[i * 2 * components + components + c] = from_right[c] * scale_ref[2, rows]
-            flow = flow + fold(plain - low_part * from_right[0] - high_part * from_left[0])
-            weight = weight + fold(extent - low_part * right_total - high_part * left_total)
-    away_ref[half * 2 * components] = jnp.zeros(away_ref.shape[1:], jnp.float32)
-    away_ref[half * 2 * components, :, 0:LANES] = flow
-    away_ref[half * 2 * components, :, LANES:2 * LANES] = weight
-
-
-def merge_kernel(chips, components, mine_ref, away_ref, mate_ref, pair_ref, _, *rest):
-    send_refs, tile_ref = rest[:-1], rest[-1]
+            fold(flow, plain - low_part * from_right[0] - high_part * from_left[0])
+            fold(weight, extent - low_part * right_total - high_part * left_total)
+    for i, part in enumerate(flow + weight):
+        tile_ref[i * SUB:(i + 1) * SUB] = part
+
+
+def merge_kernel(chips, components, mine_ref, mate_ref, pair_ref, *send_refs):
     me = lax.axis_index("gz")
     chip = me // 2
     is_first = me == chip * 2
     half = mine_ref.shape[0] // (2 * components)
-    slot = half * 2 * components
-    for i in range(2):
-        lanes = slice(i * LANES, (i + 1) * LANES)
-        tile_ref[i] = away_ref[slot, :, lanes] + mate_ref[slot, :, lanes]
     for i in range(half):
         rows = row_tile((me - chip * 2) * half + i)
         for c in range(components):
@@ -262,11 +256,7 @@
             other_ref[at] = jnp.where(is_first, right_in, right_first)
 
 
-def add_kernel(*refs):
-    refs[-1][...] = functools.reduce(jnp.add, [ref[...] for ref in refs[:-1]])
-
-
-def inner_kernel(cells, index_ref, velocity_ref, left_ref, right_ref, base_ref):
+def inner_kernel(cells, index_ref, velocity_ref, left_ref, right_ref, _, base_ref):
     me = lax.axis_index("gz")
     components = velocity_ref.shape[0]
     heights = [height(index_ref, me * cells + j) for j in range(cells)]
@@ -329,10 +319,12 @@
     lines, index_ref, target_ref, ends_ref, own_ref, other_ref, base_ref, left_ref, right_ref,
     *rest,
 ):
-    tile_refs, (_, out_hbm, result_ref, sems) = rest[:-4], rest[-4:]
+    tiles_hbm, _, out_hbm, result_ref, tiles_ref, sems = rest
     components = base_ref.shape[0]
     half = own_ref.shape[0] // (2 * components)
     me = lax.axis_index("gz")
+    arrival = pltpu.make_async_copy(tiles_hbm, tiles_ref, sems.at[sems.shape[0] - 1])
+    arrival.start()
     copies = []
 
     def leave(c, rows):
@@ -349,9 +341,12 @@
     extent = 0.0
     for k in range(index_ref.shape[0]):
         extent = extent + height(index_ref, k)
-    totals = functools.reduce(jnp.add, [ref[...] for ref in tile_refs])
-    flow = jnp.sum(totals[0], keepdims=True)
-    weight = jnp.sum(totals[1], keepdims=True)
+    arrival.wait()
+    tiles = [tiles_ref[i * SUB:(i + 1) * SUB] for i in range(tiles_ref.shape[0] // SUB)]
+    flow = functools.reduce(jnp.add, tiles[0::4] + tiles[1::4])
+    weight = functools.reduce(jnp.add, tiles[2::4] + tiles[3::4])
+    flow = jnp.sum(flow, keepdims=True)
+    weight = jnp.sum(weight, keepdims=True)
     alpha = (target_ref[0] * (extent * lines) - flow) / weight
     for ref, whose in ((own_ref, lax.rem(me, 2)), (other_ref, 1 - lax.rem(me, 2))):
         for i in range(half):
@@ -376,7 +371,6 @@
     anywhere = pl.BlockSpec(memory_space=pl.ANY)
     plane = (lines_y, lines_x)
     sheet = (SUB, lines_x)
-    tile = jax.ShapeDtypeStruct((2, SUB, LANES), f32)
 
     def shape(*dims):
         return jax.ShapeDtypeStruct(dims, f32)
@@ -390,19 +384,20 @@
     def cost(flops, transferred):
         return pl.CostEstimate(flops=flops, bytes_accessed=transferred, transcendentals=0)
 
-    mine, away, pair, chip_coefs, left, right, ends = pl.pallas_call(
+    mine, away, pair, chip_coefs, left, right, ends, tile = pl.pallas_call(
         functools.partial(ladder_kernel, cells, blocks, chips),
         out_shape=[
             shape(half * 2 * components, *sheet),
-            shape(half * 2 * components + 1, *sheet),
+            shape(half * 2 * components, *sheet),
             shape(4, *plane),
             shape(chips - 1, *plane),
             shape(cells, *plane),
             shape(cells, *plane),
             shape(2, *plane),
+            shape(4 * SUB, LANES),
         ],
         in_specs=[anywhere] * 4,
-        out_specs=[vmem] * 7,
+        out_specs=[vmem] * 8,
         scratch_shapes=[
             pltpu.SMEM(stretch_index.shape, jnp.int32),
             pltpu.VMEM(plane, f32),
@@ -426,58 +421,42 @@
     def to_mate(array):
         return send(array, lambda z, y: (z ^ 1, y))
 
-    def to_chips(array):
-        return [send(array, lambda z, y: (z ^ (2 * m), y)) for m in range(1, chips)]
-
     mate = to_mate(away)
+    outgoing = pl.pallas_call(
+        functools.partial(merge_kernel, chips, components),
+        out_shape=[shape(half * components, *sheet)] * (chips - 1),
+        in_specs=[vmem] * 3,
+        out_specs=[vmem] * (chips - 1),
+        compiler_params=options(16),
+        cost_estimate=cost(500, 1_600),
+        name="merge",
+    )(mine, mate, pair)
+    incoming = [
+        send(outgoing[m - 1], lambda z, y: (z ^ (2 * m), y)) for m in range(1, chips)
+    ]
+    tiles = lax.all_gather(tile, ("gz", "gy"), axis=0, tiled=True)
     state = pl.BlockSpec((components, cells, SUB, lines_x), lambda t: (0, 0, t, 0))
     profile = pl.BlockSpec((cells, SUB, lines_x), lambda t: (0, t, 0))
     base = pl.pallas_call(
         functools.partial(inner_kernel, cells),
         grid=(row_tiles,),
         out_shape=shape(*velocity.shape),
-        in_specs=[smem, state, profile, profile],
+        in_specs=[smem, state, profile, profile, anywhere],
         out_specs=state,
         compiler_params=options(16),
-        cost_estimate=cost(8_000_000, 8_000_000),
+        cost_estimate=cost(800, 800),
         name="inner",
-    )(stretch_index, in_hbm(velocity), left, right)
-    *outgoing, chip_tile = pl.pallas_call(
-        functools.partial(merge_kernel, chips, components),
-        out_shape=[shape(half * components, *sheet)] * (chips - 1) + [tile],
-        in_specs=[vmem] * 4 + [anywhere],
-        out_specs=[vmem] * chips,
-        compiler_params=options(16),
-        cost_estimate=cost(500_000, 1_600_000),
-        name="merge",
-    )(mine, away, mate, pair, base)
-    incoming = [
-        send(outgoing[m - 1], lambda z, y: (z ^ (2 * m), y)) for m in range(1, chips)
-    ]
-    tiles = [chip_tile] + [
-        send(chip_tile, lambda z, y: (z, (y + shift) % columns)) for shift in range(1, columns)
-    ]
-    column_tile = pl.pallas_call(
-        add_kernel,
-        out_shape=tile,
-        in_specs=[vmem] * len(tiles),
-        out_specs=vmem,
-        compiler_params=options(16),
-        cost_estimate=cost(10_000, 40_000),
-        name="column_sum",
-    )(*tiles)
-
+    )(stretch_index, in_hbm(velocity), left, right, outgoing[0])
     own_in, other_out = pl.pallas_call(
         functools.partial(spread_kernel, chips, components),
         out_shape=[shape(half * 2 * components, *sheet)] * 2,
         in_specs=[vmem] * 4 + [anywhere] + [vmem] * (chips - 1),
         out_specs=[vmem] * 2,
         compiler_params=options(16),
-        cost_estimate=cost(500_000, 1_600_000),
+        cost_estimate=cost(500, 1_600),
         name="spread",
-    )(mine, mate, pair, chip_coefs, column_tile, *incoming)
+    )(mine, mate, pair, chip_coefs, base, *incoming)
     other_in = to_mate(other_out)
-    plane_tiles = [column_tile] + to_chips(column_tile)
     early = pl.pallas_call(
         early_kernel,
         out_shape=shape(*velocity.shape),
@@ -488,23 +467,24 @@
             pltpu.SemaphoreType.DMA(((components - 1) * half,)),
         ],
         compiler_params=options(16),
-        cost_estimate=cost(2_000_000, 4_000_000),
+        cost_estimate=cost(500, 500),
         name="early",
     )(own_in, base, left, right)
     return pl.pallas_call(
         functools.partial(late_kernel, float(lines_y * columns * lines_x)),
         out_shape=shape(*velocity.shape),
-        in_specs=[smem, smem] + [vmem] * (6 + chips) + [anywhere],
+        in_specs=[smem, smem] + [vmem] * 6 + [anywhere] * 2,
         out_specs=anywhere,
         scratch_shapes=[
             pltpu.VMEM(velocity.shape, f32),
-            pltpu.SemaphoreType.DMA(((components + 1) * half,)),
+            pltpu.VMEM(tiles.shape, f32),
+            pltpu.SemaphoreType.DMA(((2 * components) * half + 1,)),
         ],
-        input_output_aliases={8 + chips: 0},
+        input_output_aliases={9: 0},
         compiler_params=options(16),
-        cost_estimate=cost(3_000_000, 6_000_000),
+        cost_estimate=cost(500, 500),
         name="late",
-    )(stretch_index, bulk_target, ends, own_in, other_in, base, left, right, *plane_tiles, early)
+    )(stretch_index, bulk_target, ends, own_in, other_in, base, left, right, in_hbm(tiles), early)
 
 
 def solution(mesh):

time: 32.6 us -> 98.1 us (3.01)
  blocking collectives: 0 us -> 78.2 us
  starting transfers between devices: 12.6 us -> 5.06 us
  waiting for transfers between devices: 8.15 us -> 2.01 us
  Pallas kernels: 10.9 us -> 11.9 us
    all_gather x0 -> x1, blocking collectives: none -> 78.2 us  [shards(): tiles = lax.all_gather(tile, ('gz', 'gy'), axis=0, tiled=True)]
    ppermute x11 -> x5, starting transfers between devices: 12.6 us -> 5.06 us  [send(): return lax.ppermute(array, ('gz', 'gy'), route)]
    ppermute x11 -> x5, waiting for transfers between devices: 8.15 us -> 2.01 us  [send(): return lax.ppermute(array, ('gz', 'gy'), route)]
  transfers between devices with their start and end apart: 11 -> 5, of which waited for: 5 -> 3; matrix products, arithmetic and copies ran while one was open for 0% -> 0% of each run, Pallas kernels for 14% -> 5%
where the time goes in v3:
time: 98.1 us; the launch traced here: 97.8 us
  blocking collectives  78.2 us (80%)
  Pallas kernels  11.9 us (12%)
  starting transfers between devices  5.06 us (5%)
  waiting for transfers between devices  2.01 us (2%)
    all_gather x1, blocking collectives, shards(): tiles = lax.all_gather(tile, ('gz', 'gy'), axis=0, tiled=True)  78.2 us
    ppermute x5, starting transfers between devices, send(): return lax.ppermute(array, ('gz', 'gy'), route)  5.06 us
    pallas_call x1, Pallas kernels, shards(): pl.pallas_call(functools.partial(ladder_kernel, cells, blocks, chips), ou...  4.26 us
    pallas_call x1, Pallas kernels, shards(): pl.pallas_call(functools.partial(inner_kernel, cells), grid=(row_tiles,),...  3.35 us
    pallas_call x1, Pallas kernels, shards(): pl.pallas_call(functools.partial(late_kernel, float(lines_y * columns * l...  3.06 us
    ppermute x5, waiting for transfers between devices, send(): return lax.ppermute(array, ('gz', 'gy'), route)  2.01 us
  transfers between devices with their start and end apart: 5, of which 3 were waited for; matrix products, arithmetic and copies ran while one was open for 0% of the time, Pallas kernels for 5%

profile of v3, /device:TPU:0, one launch (start us, length us, event | category | flops | bytes accessed | tf_op | source)
XLA Modules:
  0.0 97.8 jit_solution(13910282447684810942)
XLA Ops:
  0.0 0.0 copy-start
  0.0 4.3 %ladder.1 = (f32[12,8,512]{2,1,0:T(8,128)S(1)}, f32[12,8,512]{2,1,0:T(8,128)S(1)}, f32[4,32,512]{2,1,0:T(8,128)S(1)}, f32[3,32,512]{2,1,0:T(8,128)S(1)}, f32[16,...) custom-call(s32[128]{0:T(128)} %index_ref.3, ...), custom_call_target="tpu_custom_call" | custom-call | flops 40000000 | bytes 6000000 | tf_op jit(solution)/shard_map/ladder/pallas_call | solution.py:387
  4.3 0.5 collective-permute-start
  4.8 1.1 %collective-permute-done.mate_ref = f32[12,8,512]{2,1,0:T(8,128)S(1)} collective-permute-done((f32[12,8,512]{2,1,0:T(8,128)S(1)}, f32[12,8,512]{2,1,0:T(8,128)S(1)}, u32[]{:S(2)}, u32[]{:S(2)}) %collective-permute-start) | collective-permute-done | bytes 196640 | tf_op jit(solution)/shard_map/ppermute | solution.py:419
  5.9 2.9 %collective-permute-start.2 = (f32[6,8,512]{2,1,0:T(8,128)S(1)}, f32[6,8,512]{2,1,0:T(8,128)S(1)}, u32[]{:S(2)}, u32[]{:S(2)}) collective-permute-start(f32[6,8,512]{2,1,0:T(8,128)S(1)} %get-tuple-element.26), channel_id=1, source_target_pairs={{0,16},{1,17},{2,18},{3,19},{4,20},{5,21},{6,22},{7,23},{8,24},{9,... | collective-permute-start | bytes 294920 | tf_op jit(solution)/shard_map/ppermute | solution.py:419
  8.8 1.4 %collective-permute-start.3 = (f32[6,8,512]{2,1,0:T(8,128)S(1)}, f32[6,8,512]{2,1,0:T(8,128)S(1)}, u32[]{:S(2)}, u32[]{:S(2)}) collective-permute-start(f32[6,8,512]{2,1,0:T(8,128)S(1)} %get-tuple-element.27), channel_id=1, source_target_pairs={{0,24},{1,25},{2,26},{3,27},{4,28},{5,29},{6,30},{7,31},{8,16},{9,... | collective-permute-start | bytes 294920 | tf_op jit(solution)/shard_map/ppermute | solution.py:419
  10.3 0.1 collective-permute-start.1
  11.0 0.0 copy-done
  11.0 3.4 %inner.1._.base_ref = f32[3,16,32,512]{3,2,1,0:T(8,128)S(1)} custom-call(s32[128]{0:T(128)S(1)} %copy-done, f32[3,16,32,512]{3,2,1,0:T(8,128)} %velocity_ref.1, f32[16,32,512]{2,1,0:T(8,128)S(1)} %get-tuple-element.23.left_ref, f32[16,32,512]{2,1,0:T(8,128)S(1)} %get-tuple-element.24.right_ref, f32[6,8,512]{2,1,0:T(8,128)S(1)} %get-tuple-element.25._), custom_call_target="tpu_custom_call" | custom-call | flops 800 | bytes 800 | tf_op jit(solution)/shard_map/inner/pallas_call | solution.py:440
  14.4 0.0 collective-permute-done.2.rest_1_
  14.4 0.9 collective-permute-done.3.rest_2_
  15.3 0.1 collective-permute-done.1.rest_0_
  15.3 0.1 spread.1
  15.4 0.1 collective-permute-start.4
  15.5 78.2 %all_gather.3.rest_0_ = f32[1024,128]{1,0:T(8,128)} all-gather(f32[32,128]{1,0:T(8,128)S(1)} %get-tuple-element.30), channel_id=1, replica_groups=mesh['gz'=8,'gy'=4] {'gz','gy'}, dimensions={0}, use_global_device_ids=true | all-gather | bytes 540672 | tf_op jit(solution)/shard_map/all_gather | solution.py:437
  93.7 1.1 %early.1.rest_1_ = f32[3,16,32,512]{3,2,1,0:T(8,128)} custom-call(f32[12,8,512]{2,1,0:T(8,128)S(1)} %get-tuple-element.28.own_ref, f32[3,16,32,512]{3,2,1,0:T(8,128)S(1)} %inner.1._.base_ref, f32[16,32,512]{2,1,0:T(8,128)S(1)} %get-tuple-element.23.left_ref, f32[16,32,512]{2,1,0:T(8,128)S(1)} %get-tuple-element.24.right_ref), custom_call_target="tpu_custom_call" | custom-call | flops 500 | bytes 500 | tf_op jit(solution)/shard_map/early/pallas_call | solution.py:460
  94.8 0.0 collective-permute-done.4.other_ref
  94.8 3.1 %late.1 = f32[3,16,32,512]{3,2,1,0:T(8,128)} custom-call(s32[128]{0:T(128)S(1)} %copy-done, f32[1]{0:T(128)S(6)} %copy.8.target_ref, f32[2,32,512]{2,1,0:T(8,128)S(1)} %get-tuple-element.18.ends_ref, f32[12,8,512]{2,1,0:T(8,128)S(1)} %get-tuple-element.28.own_ref, ...), custom_call_target="tpu_custom_call", output_to_operand_aliasing={{}: (9, {})} | custom-call | flops 500 | bytes 500 | tf_op jit(solution)/shard_map/late/pallas_call | solution.py:473
  (1 shorter events, 0.0 us)
Async XLA Ops:
  0.0 11.0 %copy-start = (s32[128]{0:T(128)S(1)}, s32[128]{0:T(128)}, u32[]{:S(2)}) copy-start(s32[128]{0:T(128)} %index_ref.3) | copy-start | bytes 1540
  4.3 1.6 %collective-permute-start = (f32[12,8,512]{2,1,0:T(8,128)S(1)}, f32[12,8,512]{2,1,0:T(8,128)S(1)}, u32[]{:S(2)}, u32[]{:S(2)}) collective-permute-start(f32[12,8,512]{2,1,0:T(8,128)S(1)} %get-tuple-element.20), channel_id=1, source_target_pairs={{0,4},{1,5},{2,6},{3,7},{4,0},{5,1},{6,2},{7,3},{8,12},{9,13},{10,... | collective-permute-start | bytes 589832 | tf_op jit(solution)/shard_map/ppermute | solution.py:419
  5.9 8.5 %collective-permute-start.2 = (f32[6,8,512]{2,1,0:T(8,128)S(1)}, f32[6,8,512]{2,1,0:T(8,128)S(1)}, u32[]{:S(2)}, u32[]{:S(2)}) collective-permute-start(f32[6,8,512]{2,1,0:T(8,128)S(1)} %get-tuple-element.26), channel_id=1, source_target_pairs={{0,16},{1,17},{2,18},{3,19},{4,20},{5,21},{6,22},{7,23},{8,24},{9,... | collective-permute-start | bytes 294920 | tf_op jit(solution)/shard_map/ppermute | solution.py:419
  8.8 6.4 %collective-permute-start.3 = (f32[6,8,512]{2,1,0:T(8,128)S(1)}, f32[6,8,512]{2,1,0:T(8,128)S(1)}, u32[]{:S(2)}, u32[]{:S(2)}) collective-permute-start(f32[6,8,512]{2,1,0:T(8,128)S(1)} %get-tuple-element.27), channel_id=1, source_target_pairs={{0,24},{1,25},{2,26},{3,27},{4,28},{5,29},{6,30},{7,31},{8,16},{9,... | collective-permute-start | bytes 294920 | tf_op jit(solution)/shard_map/ppermute | solution.py:419
  10.3 5.1 %collective-permute-start.1 = (f32[6,8,512]{2,1,0:T(8,128)S(1)}, f32[6,8,512]{2,1,0:T(8,128)S(1)}, u32[]{:S(2)}, u32[]{:S(2)}) collective-permute-start(f32[6,8,512]{2,1,0:T(8,128)S(1)} %get-tuple-element.25._), channel_id=1, source_target_pairs={{0,8},{1,9},{2,10},{3,11},{4,12},{5,13},{6,14},{7,15},{8,0},{9,1},... | collective-permute-start | bytes 294920 | tf_op jit(solution)/shard_map/ppermute | solution.py:419
  15.4 79.3 %collective-permute-start.4 = (f32[12,8,512]{2,1,0:T(8,128)S(1)}, f32[12,8,512]{2,1,0:T(8,128)S(1)}, u32[]{:S(2)}, u32[]{:S(2)}) collective-permute-start(f32[12,8,512]{2,1,0:T(8,128)S(1)} %get-tuple-element.29), channel_id=1, source_target_pairs={{0,4},{1,5},{2,6},{3,7},{4,0},{5,1},{6,2},{7,3},{8,12},{9,13},{10,... | collective-permute-start | bytes 589832 | tf_op jit(solution)/shard_map/ppermute | solution.py:419

commit v4 on v3

v4 whole, which is shorter than its diff:
```python
import functools

import jax
import jax.numpy as jnp
from jax import lax
from jax.experimental import pallas as pl
from jax.experimental.pallas import tpu as pltpu
from jax.sharding import PartitionSpec as P

SUB = 8
STRETCHES = 7
LANES = 128
MIB = 1024 * 1024


def row_tile(t):
    return pl.ds(pl.multiple_of(t * SUB, SUB), SUB)


def height(index_ref, k):
    return 0.5 + 0.25 * index_ref[k].astype(jnp.float32)


def half_sum(index_ref, k):
    return 0.5 * (height(index_ref, k) + height(index_ref, k + 1))


def ladder_kernel(
    cells, blocks, chips, lines,
    index_hbm, diffusion_hbm, walls_hbm, velocity_hbm,
    mine_ref, away_ref, pair_ref, chip_ref, left_ref, right_ref, left_h_ref, right_h_ref,
    ends_ref, tile_ref, volume_ref, velocity_ref,
    index_ref, diffusion_ref, walls_ref, through_ref, table_ref, held_ref, sems,
):
    total = cells * blocks
    components = velocity_ref.shape[0]
    row_tiles = diffusion_ref.shape[0] // SUB
    small = [
        pltpu.make_async_copy(index_hbm, index_ref, sems.at[0]),
        pltpu.make_async_copy(diffusion_hbm, diffusion_ref, sems.at[1]),
        pltpu.make_async_copy(walls_hbm, walls_ref, sems.at[2]),
    ]
    large = [
        pltpu.make_async_copy(velocity_hbm.at[c], velocity_ref.at[c], sems.at[3 + c])
        for c in range(components)
    ]
    for copy in small + large:
        copy.start()
    me = lax.axis_index("gz")
    chip = me // 2
    first = chip * 2
    for copy in small:
        copy.wait()
    diffusion = diffusion_ref[...]
    inverse = 1.0 / diffusion
    for i in range(STRETCHES):
        table_ref[i] = (0.5 + 0.25 * i) * inverse
    walls = walls_ref[...]

    def wall(bits, k):
        face = 1.0 / jnp.full((SUB, diffusion.shape[1]), 0.5 * height(index_ref, k))
        return bits.astype(jnp.float32) * jnp.concatenate([face] * row_tiles, axis=0)

    lower = wall(walls & 1, 0)
    upper = wall(walls >> 1, total - 1)

    def forward(block, kappa, keep=None):
        start = block * cells
        flux = table_ref[index_ref[start]] + kappa
        value = jnp.ones_like(flux)
        for j in range(cells):
            if keep is not None:
                keep(j, flux, value)
            k = start + j
            if j < cells - 1:
                value = value + half_sum(index_ref, k) * flux
                flux = flux + table_ref[index_ref[k + 1]] * value
        k = jnp.minimum(start + cells - 1, total - 2)
        after = 1.0 / (value + half_sum(index_ref, k) * flux)
        return flux * after, after

    def backward(block, kappa, scale=None, keep=None):
        start = block * cells
        flux = table_ref[index_ref[start + cells - 1]] + kappa
        value = jnp.ones_like(flux)
        if scale is not None:
            flux, value = flux * scale, scale
        for j in reversed(range(cells)):
            if keep is not None:
                keep(j, flux, value)
            k = start + j
            if j > 0:
                value = value + half_sum(index_ref, k - 1) * flux
                flux = flux + table_ref[index_ref[k - 1]] * value
        k = jnp.maximum(start - 1, 0)
        after = 1.0 / (value + half_sum(index_ref, k) * flux)
        return flux * after, after

    def thickness(block):
        parts = [height(index_ref, block * cells + j) for j in range(cells)]
        return functools.reduce(jnp.add, parts)

    def sweep_forward(block, state):
        kappa, product, extent = state
        kappa, after = forward(block, kappa)
        through_ref[block] = after
        return kappa, product * after, extent + thickness(block)

    def sweep_backward(step, state):
        block = blocks - 1 - step
        kappa, product, extent = state
        kappa, after = backward(block, kappa)
        through_ref[block] = after
        return kappa, product * after, extent + thickness(block)

    ones = jnp.ones_like(diffusion)
    kappa_left, product, extent = lax.fori_loop(
        0, me, sweep_forward, (lower, ones, thickness(me))
    )
    ends_ref[0] = diffusion * lower * product
    state = {}

    def keep_left(j, flux, value):
        left_ref[j] = value
        left_h_ref[j] = height(index_ref, me * cells + j) * value
        state["flux"], state["value"] = flux, value

    kappa, own_forward = forward(me, kappa_left, keep_left)
    held_ref[1] = own_forward
    held_ref[3] = state["flux"]
    held_ref[4] = state["value"]
    held_ref[5] = state["flux"] - kappa_left

    @pl.when(me == first)
    def _():
        pair_ref[2] = own_forward
        _, after = forward(me + 1, kappa)
        pair_ref[0] = after

    @pl.when(me != first)
    def _():
        pair_ref[2] = through_ref[first]
        pair_ref[0] = own_forward

    kappa_right, product, extent = lax.fori_loop(
        0, blocks - 1 - me, sweep_backward, (upper, ones, extent)
    )
    ends_ref[1] = diffusion_ref[...] * upper * product
    scale = 1.0 / (diffusion_ref[...] * (held_ref[3] + kappa_right * held_ref[4]))
    held_ref[0] = scale

    def keep_right(j, flux, value):
        right_ref[j] = value
        right_h_ref[j] = height(index_ref, me * cells + j) * value
        state["flux"] = flux

    kappa, own_backward = backward(me, kappa_right, scale, keep_right)
    held_ref[2] = own_backward
    held_ref[6] = state["flux"] - kappa_right * scale

    @pl.when(me == first)
    def _():
        pair_ref[1] = own_backward * held_ref[0]
        pair_ref[3] = through_ref[first + 1]

    @pl.when(me != first)
    def _():
        pair_ref[3] = own_backward * held_ref[0]
        _, after = backward(me - 1, kappa)
        pair_ref[1] = after

    for m in range(1, chips):
        other = chip ^ m
        low = jnp.minimum(chip, other)
        high = jnp.maximum(chip, other)
        chip_ref[m - 1] = lax.fori_loop(
            low + 1,
            high,
            lambda r, product: product * (through_ref[2 * r] * through_ref[2 * r + 1]),
            ones,
        )
    flow = jnp.zeros((SUB, LANES), jnp.float32)
    weight = jnp.zeros((SUB, LANES), jnp.float32)

    def fold(array):
        parts = [array[:, i * LANES:(i + 1) * LANES] for i in range(array.shape[1] // LANES)]
        return functools.reduce(jnp.add, parts)

    for copy in large:
        copy.wait()
    volume_ref[...] = jnp.full(volume_ref.shape, extent * lines)
    half = row_tiles // 2
    own_extent = thickness(me)
    heights = [height(index_ref, me * cells + j) for j in range(cells)]
    for ref, whose in ((away_ref, 1 - (me - first)), (mine_ref, me - first)):
        for i in range(half):
            rows = row_tile(whose * half + i)
            from_left = [0.0] * components
            from_right = [0.0] * components
            plain = 0.0
            for j in range(cells):
                left = left_h_ref[j, rows]
                right = right_h_ref[j, rows]
                for c in range(components):
                    v = velocity_ref[c, j, rows]
                    from_left[c] = from_left[c] + left * v
                    from_right[c] = from_right[c] + right * v
                    if c == 0:
                        plain = plain + heights[j] * v
            for c in range(components):
                ref[i * 2 * components + c] = from_left[c] * held_ref[1, rows]
                ref[i * 2 * components + components + c] = from_right[c] * held_ref[2, rows]
            low_part = ends_ref[0, rows]
            high_part = ends_ref[1, rows] * held_ref[0, rows]
            flow = flow + fold(plain - low_part * from_right[0] - high_part * from_left[0])
            totals = low_part * held_ref[6, rows] + high_part * held_ref[5, rows]
            weight = weight + fold(own_extent - diffusion_ref[rows] * totals)
    middle = SUB // 2
    for i in range(tile_ref.shape[0]):
        tile_ref[i, 0:middle] = flow[0:middle] + flow[middle:]
        tile_ref[i, middle:] = weight[0:middle] + weight[middle:]


def merge_kernel(chips, components, mine_ref, mate_ref, pair_ref, *send_refs):
    me = lax.axis_index("gz")
    chip = me // 2
    is_first = me == chip * 2
    half = mine_ref.shape[0] // (2 * components)
    for i in range(half):
        rows = row_tile((me - chip * 2) * half + i)
        for c in range(components):
            at = i * 2 * components + c
            mine, mate = mine_ref[at], mate_ref[at]
            first = jnp.where(is_first, mine, mate)
            second = jnp.where(is_first, mate, mine)
            to_right = second + pair_ref[0, rows] * first
            at = at + components
            mine, mate = mine_ref[at], mate_ref[at]
            first = jnp.where(is_first, mine, mate)
            second = jnp.where(is_first, mate, mine)
            to_left = first + pair_ref[1, rows] * second
            for m in range(1, chips):
                goes_right = (chip ^ m) > chip
                send_refs[m - 1][i * components + c] = jnp.where(goes_right, to_right, to_left)


def spread_kernel(chips, components, mine_ref, mate_ref, pair_ref, chip_ref, _, *rest):
    recv_refs, (own_ref, other_ref) = rest[:chips - 1], rest[chips - 1:]
    me = lax.axis_index("gz")
    chip = me // 2
    is_first = me == chip * 2
    half = mine_ref.shape[0] // (2 * components)
    for i in range(half):
        rows = row_tile((me - chip * 2) * half + i)
        coefs = [chip_ref[m, rows] for m in range(chips - 1)]
        for c in range(components):
            left_in = jnp.zeros(mine_ref.shape[1:], jnp.float32)
            right_in = jnp.zeros(mine_ref.shape[1:], jnp.float32)
            for m in range(1, chips):
                term = coefs[m - 1] * recv_refs[m - 1][i * components + c]
                from_left = (chip ^ m) < chip
                left_in = left_in + jnp.where(from_left, term, 0.0)
                right_in = right_in + jnp.where(from_left, 0.0, term)
            at = i * 2 * components + c
            first_out = jnp.where(is_first, mine_ref[at], mate_ref[at])
            left_second = first_out + pair_ref[2, rows] * left_in
            at = at + components
            second_out = jnp.where(is_first, mate_ref[at], mine_ref[at])
            right_first = second_out + pair_ref[3, rows] * right_in
            at = i * 2 * components + c
            own_ref[at] = jnp.where(is_first, left_in, left_second)
            other_ref[at] = jnp.where(is_first, left_second, left_in)
            at = at + components
            own_ref[at] = jnp.where(is_first, right_first, right_in)
            other_ref[at] = jnp.where(is_first, right_in, right_first)


def inner_kernel(velocity_ref, left_ref, right_ref, left_h_ref, right_h_ref, *rest):
    base_ref = rest[-1]
    components, cells, lines_y, lines_x = velocity_ref.shape
    for t in range(lines_y // SUB):
        rows = row_tile(t)
        gathered = [jnp.zeros((SUB, lines_x), jnp.float32)] * components
        for j in reversed(range(cells)):
            left = left_ref[j, rows]
            right = right_h_ref[j, rows]
            for c in range(components):
                base_ref[c, j, rows] = left * gathered[c]
                if j > 0:
                    gathered[c] = gathered[c] + right * velocity_ref[c, j, rows]
        gathered = [jnp.zeros((SUB, lines_x), jnp.float32)] * components
        for j in range(cells):
            left = left_h_ref[j, rows]
            right = right_ref[j, rows]
            for c in range(components):
                gathered[c] = gathered[c] + left * velocity_ref[c, j, rows]
                base_ref[c, j, rows] = base_ref[c, j, rows] + right * gathered[c]


def emit(parts, rows, alpha, ends_ref, incoming_ref, at, base_ref, left_ref, right_ref, result_ref):
    cells = left_ref.shape[0]
    components = base_ref.shape[0]
    scale = right_ref[cells - 1, rows]
    lefts, rights = {}, {}
    for c in parts:
        left_in = incoming_ref[at + c]
        right_in = incoming_ref[at + components + c]
        if c == 0:
            left_in = left_in - alpha * ends_ref[0, rows]
            right_in = right_in - alpha * ends_ref[1, rows]
        lefts[c] = left_in
        rights[c] = right_in * scale
    for j in range(cells):
        left = left_ref[j, rows]
        right = right_ref[j, rows]
        for c in parts:
            value = base_ref[c, j, rows] + (right * lefts[c] + left * rights[c])
            result_ref[c, j, rows] = value + alpha if c == 0 else value


def early_kernel(own_ref, base_ref, left_ref, right_ref, out_hbm, result_ref, sems):
    components = base_ref.shape[0]
    half = own_ref.shape[0] // (2 * components)
    me = lax.axis_index("gz")
    copies = []
    for i in range(half):
        rows = row_tile(lax.rem(me, 2) * half + i)
        emit(range(1, components), rows, None, None, own_ref, i * 2 * components,
             base_ref, left_ref, right_ref, result_ref)
        for c in range(1, components):
            copies.append(pltpu.make_async_copy(
                result_ref.at[c, :, rows], out_hbm.at[c, :, rows], sems.at[len(copies)]))
            copies[-1].start()
    for copy in copies:
        copy.wait()


def late_kernel(
    target_ref, volume_ref, ends_ref, own_ref, other_ref, base_ref, left_ref, right_ref, *rest
):
    tiles_ref, _, out_hbm, result_ref, sems = rest
    components = base_ref.shape[0]
    half = own_ref.shape[0] // (2 * components)
    me = lax.axis_index("gz")
    copies = []

    def leave(c, rows):
        copies.append(pltpu.make_async_copy(
            result_ref.at[c, :, rows], out_hbm.at[c, :, rows], sems.at[len(copies)]))
        copies[-1].start()

    for i in range(half):
        rows = row_tile((1 - lax.rem(me, 2)) * half + i)
        emit(range(1, components), rows, None, None, other_ref, i * 2 * components,
             base_ref, left_ref, right_ref, result_ref)
        for c in range(1, components):
            leave(c, rows)
    totals = functools.reduce(jnp.add, [tiles_ref[i] for i in range(tiles_ref.shape[0])])
    flow = jnp.sum(totals[0:SUB // 2], keepdims=True)
    weight = jnp.sum(totals[SUB // 2:], keepdims=True)
    alpha = (target_ref[...] * volume_ref[0:1, 0:1] - flow) / weight
    for ref, whose in ((own_ref, lax.rem(me, 2)), (other_ref, 1 - lax.rem(me, 2))):
        for i in range(half):
            rows = row_tile(whose * half + i)
            emit((0,), rows, alpha, ends_ref, ref, i * 2 * components,
                 base_ref, left_ref, right_ref, result_ref)
            leave(0, rows)
    for copy in copies:
        copy.wait()


def shards(velocity, diffusion, wall_types, stretch_index, bulk_target):
    blocks = lax.axis_size("gz")
    columns = lax.axis_size("gy")
    components, cells, lines_y, lines_x = velocity.shape
    chips = blocks // 2
    row_tiles = lines_y // SUB
    half = row_tiles // 2
    f32 = jnp.float32
    vmem = pl.BlockSpec(memory_space=pltpu.VMEM)
    anywhere = pl.BlockSpec(memory_space=pl.ANY)
    plane = (lines_y, lines_x)
    sheet = (SUB, lines_x)

    def shape(*dims):
        return jax.ShapeDtypeStruct(dims, f32)

    def in_hbm(array):
        return pltpu.with_memory_space_constraint(array, pltpu.HBM)

    def options(mib):
        return pltpu.CompilerParams(vmem_limit_bytes=mib * MIB)

    def cost(flops, transferred):
        return pl.CostEstimate(flops=flops, bytes_accessed=transferred, transcendentals=0)

    def send(array, partner):
        pairs = [((z, y), partner(z, y)) for z in range(blocks) for y in range(columns)]
        route = [(a * columns + b, c * columns + d) for (a, b), (c, d) in pairs]
        return lax.ppermute(array, ("gz", "gy"), route)

    def to_mate(array):
        return send(array, lambda z, y: (z ^ 1, y))

    def to_chip(array, m):
        return send(array, lambda z, y: (z ^ (2 * m), y))

    lines = float(lines_y * columns * lines_x)
    (mine, away, pair, chip_coefs, left, right, left_h, right_h, ends, tile, volume,
     near_velocity) = pl.pallas_call(
        functools.partial(ladder_kernel, cells, blocks, chips, lines),
        out_shape=[
            shape(half * 2 * components, *sheet),
            shape(half * 2 * components, *sheet),
            shape(4, *plane),
            shape(chips - 1, *plane),
            shape(cells, *plane),
            shape(cells, *plane),
            shape(cells, *plane),
            shape(cells, *plane),
            shape(2, *plane),
            shape(blocks * columns, SUB, LANES),
            shape(SUB, LANES),
            shape(*velocity.shape),
        ],
        in_specs=[anywhere] * 4,
        out_specs=[vmem] * 12,
        scratch_shapes=[
            pltpu.SMEM(stretch_index.shape, jnp.int32),
            pltpu.VMEM(plane, f32),
            pltpu.VMEM(plane, jnp.int32),
            pltpu.VMEM((blocks,) + plane, f32),
            pltpu.VMEM((STRETCHES,) + plane, f32),
            pltpu.VMEM((7,) + plane, f32),
            pltpu.SemaphoreType.DMA((3 + components,)),
        ],
        compiler_params=options(24),
        cost_estimate=cost(40_000_000, 6_000_000),
        name="ladder",
    )(in_hbm(stretch_index), in_hbm(diffusion), in_hbm(wall_types), in_hbm(velocity))

    mate = to_mate(away)
    tiles = lax.all_to_all(tile, ("gz", "gy"), 0, 0, tiled=True)
    outgoing = pl.pallas_call(
        functools.partial(merge_kernel, chips, components),
        out_shape=[shape(half * components, *sheet)] * (chips - 1),
        in_specs=[vmem] * 3,
        out_specs=[vmem] * (chips - 1),
        compiler_params=options(16),
        cost_estimate=cost(500_000, 1_600_000),
        name="merge",
    )(mine, mate, pair)
    incoming = [to_chip(outgoing[m - 1], m) for m in range(1, chips)]
    base = pl.pallas_call(
        inner_kernel,
        out_shape=shape(*velocity.shape),
        in_specs=[vmem] * 5 + [anywhere],
        out_specs=vmem,
        compiler_params=options(16),
        cost_estimate=cost(8_000_000, 8_000_000),
        name="inner",
    )(near_velocity, left, right, left_h, right_h, outgoing[0])
    own_in, other_out = pl.pallas_call(
        functools.partial(spread_kernel, chips, components),
        out_shape=[shape(half * 2 * components, *sheet)] * 2,
        in_specs=[vmem] * 4 + [anywhere] + [vmem] * (chips - 1),
        out_specs=[vmem] * 2,
        compiler_params=options(16),
        cost_estimate=cost(500_000, 1_600_000),
        name="spread",
    )(mine, mate, pair, chip_coefs, base, *incoming)
    other_in = to_mate(other_out)
    early = pl.pallas_call(
        early_kernel,
        out_shape=shape(*velocity.shape),
        in_specs=[vmem] * 4,
        out_specs=anywhere,
        scratch_shapes=[
            pltpu.VMEM(velocity.shape, f32),
            pltpu.SemaphoreType.DMA(((components - 1) * half,)),
        ],
        compiler_params=options(16),
        cost_estimate=cost(2_000_000, 4_000_000),
        name="early",
    )(own_in, base, left, right)
    return pl.pallas_call(
        late_kernel,
        out_shape=shape(*velocity.shape),
        in_specs=[vmem] * 9 + [anywhere],
        out_specs=anywhere,
        scratch_shapes=[
            pltpu.VMEM(velocity.shape, f32),
            pltpu.SemaphoreType.DMA(((components + 1) * half,)),
        ],
        input_output_aliases={9: 0},
        compiler_params=options(16),
        cost_estimate=cost(3_000_000, 6_000_000),
        name="late",
    )(bulk_target.reshape(1, 1), volume, ends, own_in, other_in, base, left, right, tiles, early)


def solution(mesh):
    return jax.shard_map(
        shards,
        mesh=mesh,
        in_specs=(P(None, "gz", "gy", None), P("gy", None), P("gy", None), P(), P()),
        out_specs=P(None, "gz", "gy", None),
        check_vma=False,
    )
```

time: 98.1 us -> 42.2 us (0.43)
  blocking collectives: 78.2 us -> 0 us
  local copies, waits for them, and re-layouts: 0.01 us -> 18.3 us
  starting transfers between devices: 5.06 us -> 11.4 us
  Pallas kernels: 11.9 us -> 10.1 us
    all_gather x1 -> x0, blocking collectives: 78.2 us -> none  [shards(): tiles = lax.all_gather(tile, ('gz', 'gy'), axis=0, tiled=True)]
    unnamed x2 -> x46, local copies, waits for them, and re-layouts: 0.01 us -> 18.3 us
    all_to_all x0 -> x1, starting transfers between devices: none -> 6.31 us  [shards(): tiles = lax.all_to_all(tile, ('gz', 'gy'), 0, 0, tiled=True)]
    pallas_call x3, Pallas kernels: 10.7 us -> 6.47 us  [the longest x1 4.15 us: shards(): pl.pallas_call(functools.partial(ladder_kernel, cells, blocks, chips, lin...]
    pallas_call x1, Pallas kernels: 0.09 us -> 1.75 us  [shards(): pl.pallas_call(functools.partial(spread_kernel, chips, components), out_s...]
  transfers between devices with their start and end apart: 5 -> 6, of which waited for: 3 -> 1; matrix products, arithmetic and copies ran while one was open for 0% -> 0% of each run, Pallas kernels for 5% -> 9%
where the time goes in v4:
time: 42.2 us; the launch traced here: 41.7 us
  local copies, waits for them, and re-layouts  18.3 us (43%)
  starting transfers between devices  11.4 us (27%)
  Pallas kernels  10.1 us (24%)
  waiting for transfers between devices  1.08 us (3%)
  between operations  0.77 us (2%)
    unnamed x46, local copies, waits for them, and re-layouts  18.3 us
    all_to_all x1, starting transfers between devices, shards(): tiles = lax.all_to_all(tile, ('gz', 'gy'), 0, 0, tiled=True)  6.31 us
    ppermute x5, starting transfers between devices, send(): return lax.ppermute(array, ('gz', 'gy'), route)  5.11 us
    pallas_call x1, Pallas kernels, shards(): pl.pallas_call(functools.partial(ladder_kernel, cells, blocks, chips, lin...  4.15 us
    pallas_call x1, Pallas kernels, shards(): pl.pallas_call(functools.partial(spread_kernel, chips, components), out_s...  1.75 us
    pallas_call x1, Pallas kernels, shards(): pl.pallas_call(late_kernel, out_shape=shape(*velocity.shape), in_specs=[v...  1.56 us
    pallas_call x1, Pallas kernels, shards(): pl.pallas_call(early_kernel, out_shape=shape(*velocity.shape), in_specs=[...  1.08 us
    ppermute x5, waiting for transfers between devices, send(): return lax.ppermute(array, ('gz', 'gy'), route)  1.08 us
  transfers between devices with their start and end apart: 6, of which 1 were waited for; matrix products, arithmetic and copies ran while one was open for 0% of the time, Pallas kernels for 9%

profile of v4, /device:TPU:0, one launch (start us, length us, event | category | flops | bytes accessed | tf_op | source)
XLA Modules:
  0.0 41.7 jit_solution(15081727539605082847)
XLA Ops:
  0.0 4.1 %ladder.1 = (f32[12,8,512]{2,1,0:T(8,128)S(1)}, f32[12,8,512]{2,1,0:T(8,128)S(1)}, f32[4,32,512]{2,1,0:T(8,128)S(1)}, f32[3,32,512]{2,1,0:T(8,128)S(1)}, f32[16,...) custom-call(s32[128]{0:T(128)} %index_hbm.1, ...), custom_call_target="tpu_custom_call" | custom-call | flops 40000000 | bytes 6000000 | tf_op jit(solution)/shard_map/ladder/pallas_call | solution.py:410
  4.2 0.0 copy-start
  4.2 1.0 %copy-done = f32[16,32,512]{2,1,0:T(8,128)} copy-done((f32[16,32,512]{2,1,0:T(8,128)}, f32[16,32,512]{2,1,0:T(8,128)S(1)}, u32[]{:S(2)}) %copy-start) | copy-done | bytes 1048600
  5.1 0.0 copy-start.4
  5.1 1.0 %copy-done.4 = f32[16,32,512]{2,1,0:T(8,128)} copy-done((f32[16,32,512]{2,1,0:T(8,128)}, f32[16,32,512]{2,1,0:T(8,128)S(1)}, u32[]{:S(2)}) %copy-start.4) | copy-done | bytes 1048600
  6.1 0.0 copy-start.7
  6.1 1.7 %copy-done.7 = f32[3,16,32,512]{3,2,1,0:T(8,128)} copy-done((f32[3,16,32,512]{3,2,1,0:T(8,128)}, f32[3,16,32,512]{3,2,1,0:T(8,128)S(1)}, u32[]{:S(2)}) %copy-start.7) | copy-done | bytes 3145752
  7.8 0.0 copy-start.9
  7.8 1.0 %copy-done.9 = f32[16,32,512]{2,1,0:T(8,128)} copy-done((f32[16,32,512]{2,1,0:T(8,128)}, f32[16,32,512]{2,1,0:T(8,128)S(1)}, u32[]{:S(2)}) %copy-start.9) | copy-done | bytes 1048600
  8.8 1.0 %copy-done.11 = f32[16,32,512]{2,1,0:T(8,128)} copy-done((f32[16,32,512]{2,1,0:T(8,128)}, f32[16,32,512]{2,1,0:T(8,128)S(1)}, u32[]{:S(2)}) %copy-start.11) | copy-done | bytes 1048600
  9.7 0.5 %collective-permute-start = (f32[12,8,512]{2,1,0:T(8,128)S(1)}, f32[12,8,512]{2,1,0:T(8,128)S(1)}, u32[]{:S(2)}, u32[]{:S(2)}) collective-permute-start(f32[12,8,512]{2,1,0:T(8,128)S(1)} %get-tuple-element.25), channel_id=1, source_target_pairs={{0,4},{1,5},{2,6},{3,7},{4,0},{5,1},{6,2},{7,3},{8,12},{9,13},{10,... | collective-permute-start | bytes 589832 | tf_op jit(solution)/shard_map/ppermute | solution.py:400
  10.2 1.1 %collective-permute-done.mate_ref = f32[12,8,512]{2,1,0:T(8,128)S(1)} collective-permute-done((f32[12,8,512]{2,1,0:T(8,128)S(1)}, f32[12,8,512]{2,1,0:T(8,128)S(1)}, u32[]{:S(2)}, u32[]{:S(2)}) %collective-permute-start) | collective-permute-done | bytes 196640 | tf_op jit(solution)/shard_map/ppermute | solution.py:400
  11.3 0.8 %merge.1 = (f32[6,8,512]{2,1,0:T(8,128)}, f32[6,8,512]{2,1,0:T(8,128)}, f32[6,8,512]{2,1,0:T(8,128)}) custom-call(f32[12,8,512]{2,1,0:T(8,128)S(1)} %get-tuple-element.24.mine_ref, f32[12,8,512]{2,1,0:T(8,128)S(1)} %collective-permute-done.mate_ref, f32[4,32,512]{2,1,0:T(8,128)S(1)} %get-tuple-element.26.pair_ref), custom_call_target="tpu_custom_call" | custom-call | flops 500000 | bytes 1600000 | tf_op jit(solution)/shard_map/merge/pallas_call | solution.py:444
  12.1 0.0 copy-done.15
  12.1 0.7 %copy-done.13 = f32[12,8,512]{2,1,0:T(8,128)} copy-done((f32[12,8,512]{2,1,0:T(8,128)}, f32[12,8,512]{2,1,0:T(8,128)S(1)}, u32[]{:S(2)}) %copy-start.13) | copy-done | bytes 196632
  12.8 0.0 copy-done.19
  12.8 2.9 %collective-permute-start.2 = (f32[6,8,512]{2,1,0:T(8,128)}, f32[6,8,512]{2,1,0:T(8,128)}, u32[]{:S(2)}, u32[]{:S(2)}) collective-permute-start(f32[6,8,512]{2,1,0:T(8,128)} %get-tuple-element.34), channel_id=1, source_target_pairs={{0,16},{1,17},{2,18},{3,19},{4,20},{5,21},{6,22},{7,23},{8,24},{9,... | collective-permute-start | bytes 294920 | tf_op jit(solution)/shard_map/ppermute | solution.py:400
  15.6 0.0 copy-done.21
  15.6 1.4 %collective-permute-start.3 = (f32[6,8,512]{2,1,0:T(8,128)}, f32[6,8,512]{2,1,0:T(8,128)}, u32[]{:S(2)}, u32[]{:S(2)}) collective-permute-start(f32[6,8,512]{2,1,0:T(8,128)} %get-tuple-element.35), channel_id=1, source_target_pairs={{0,24},{1,25},{2,26},{3,27},{4,28},{5,29},{6,30},{7,31},{8,16},{9,... | collective-permute-start | bytes 294920 | tf_op jit(solution)/shard_map/ppermute | solution.py:400
  17.1 0.1 collective-permute-start.1
  17.2 6.3 %all-to-all-start = ((f32[32,8,128]{2,1,0:T(8,128)}), f32[32,8,128]{2,1,0:T(8,128)S(1)}, u32[]{:S(2)}, u32[]{:S(2)}) async-start(f32[32,8,128]{2,1,0:T(8,128)} %get-tuple-element.38), calls=%async_computation | async-start | bytes 262144 | tf_op jit(solution)/shard_map/all_to_all | solution.py:443
  23.5 0.0 copy-start.1
  23.5 1.2 %copy-done.1 = f32[16,32,512]{2,1,0:T(8,128)S(1)} copy-done((f32[16,32,512]{2,1,0:T(8,128)S(1)}, f32[16,32,512]{2,1,0:T(8,128)}, u32[]{:S(2)}) %copy-start.1) | copy-done | bytes 1048600
  24.7 1.2 %copy-done.5 = f32[16,32,512]{2,1,0:T(8,128)S(1)} copy-done((f32[16,32,512]{2,1,0:T(8,128)S(1)}, f32[16,32,512]{2,1,0:T(8,128)}, u32[]{:S(2)}) %copy-start.5) | copy-done | bytes 1048600
  25.9 1.9 %copy-done.8 = f32[3,16,32,512]{3,2,1,0:T(8,128)S(1)} copy-done((f32[3,16,32,512]{3,2,1,0:T(8,128)S(1)}, f32[3,16,32,512]{3,2,1,0:T(8,128)}, u32[]{:S(2)}) %copy-start.8) | copy-done | bytes 3145752
  27.8 1.2 %copy-done.10 = f32[16,32,512]{2,1,0:T(8,128)S(1)} copy-done((f32[16,32,512]{2,1,0:T(8,128)S(1)}, f32[16,32,512]{2,1,0:T(8,128)}, u32[]{:S(2)}) %copy-start.10) | copy-done | bytes 1048600
  29.1 1.2 %copy-done.12 = f32[16,32,512]{2,1,0:T(8,128)S(1)} copy-done((f32[16,32,512]{2,1,0:T(8,128)S(1)}, f32[16,32,512]{2,1,0:T(8,128)}, u32[]{:S(2)}) %copy-start.12) | copy-done | bytes 1048600
  30.3 0.8 %inner.1._.base_ref = f32[3,16,32,512]{3,2,1,0:T(8,128)S(1)} custom-call(f32[3,16,32,512]{3,2,1,0:T(8,128)S(1)} %copy-done.8, f32[16,32,512]{2,1,0:T(8,128)S(1)} %copy-done.1, f32[16,32,512]{2,1,0:T(8,128)S(1)} %copy-done.5, f32[16,32,512]{2,1,0:T(8,128)S(1)} %copy-done.10, f32[16,32,512]{2,1,0:T(8,128)S(1)} %copy-done.12, ...), custom_call_target="tpu_custom_call" | custom-call | flops 8000000 | bytes 8000000 | tf_op jit(solution)/shard_map/inner/pallas_call | solution.py:454
  31.1 0.0 copy-start.2
  31.1 0.0 collective-permute-done.2.rest_1_
  31.1 0.0 collective-permute-done.3.rest_2_
  31.1 0.0 collective-permute-done.1.rest_0_
  31.1 0.1 copy-done.14
  31.2 0.1 copy-done.16
  31.3 0.1 copy-done.20
  31.4 1.7 %spread.1 = (f32[12,8,512]{2,1,0:T(8,128)S(1)}, f32[12,8,512]{2,1,0:T(8,128)}) custom-call(f32[12,8,512]{2,1,0:T(8,128)S(1)} %copy-done.14, f32[12,8,512]{2,1,0:T(8,128)S(1)} %copy-done.16, f32[4,32,512]{2,1,0:T(8,128)S(1)} %get-tuple-element.26.pair_ref, f32[3,32,512]{2,1,0:T(8,128)S(1)} %copy-done.20, f32[3,16,32,512]{3,2,1,0:T(8,128)S(1)} %inner.1._.base_ref, ...), custom_call_target="tpu_custom_call" | custom-call | flops 500000 | bytes 1600000 | tf_op jit(solution)/shard_map/spread/pallas_call | solution.py:463
  33.1 0.3 collective-permute-start.4
  34.1 0.0 copy-done.2
  34.1 1.1 %early.1.rest_1_ = f32[3,16,32,512]{3,2,1,0:T(8,128)} custom-call(f32[12,8,512]{2,1,0:T(8,128)S(1)} %get-tuple-element.36.own_ref, f32[3,16,32,512]{3,2,1,0:T(8,128)S(1)} %inner.1._.base_ref, f32[16,32,512]{2,1,0:T(8,128)S(1)} %copy-done.2, f32[16,32,512]{2,1,0:T(8,128)S(1)} %copy-done.5), custom_call_target="tpu_custom_call" | custom-call | flops 2000000 | bytes 4000000 | tf_op jit(solution)/shard_map/early/pallas_call | solution.py:473
  35.2 0.0 copy-start.17
  35.2 0.7 %copy-done.17 = f32[12,8,512]{2,1,0:T(8,128)} copy-done((f32[12,8,512]{2,1,0:T(8,128)}, f32[12,8,512]{2,1,0:T(8,128)S(1)}, u32[]{:S(2)}) %copy-start.17) | copy-done | bytes 196632
  35.8 0.0 all-to-all-done.rest_0_
  35.8 0.0 collective-permute-done.4.other_ref
  35.8 1.2 %copy-done.3 = f32[16,32,512]{2,1,0:T(8,128)S(1)} copy-done((f32[16,32,512]{2,1,0:T(8,128)S(1)}, f32[16,32,512]{2,1,0:T(8,128)}, u32[]{:S(2)}) %copy-start.3) | copy-done | bytes 1048600
  37.1 1.2 %copy-done.6 = f32[16,32,512]{2,1,0:T(8,128)S(1)} copy-done((f32[16,32,512]{2,1,0:T(8,128)S(1)}, f32[16,32,512]{2,1,0:T(8,128)}, u32[]{:S(2)}) %copy-start.6) | copy-done | bytes 1048600
  38.3 0.9 %copy-done.18 = f32[12,8,512]{2,1,0:T(8,128)S(1)} copy-done((f32[12,8,512]{2,1,0:T(8,128)S(1)}, f32[12,8,512]{2,1,0:T(8,128)}, u32[]{:S(2)}) %copy-start.18) | copy-done | bytes 196632
  39.2 0.9 %copy-done.22 = f32[2,32,512]{2,1,0:T(8,128)S(1)} copy-done((f32[2,32,512]{2,1,0:T(8,128)S(1)}, f32[2,32,512]{2,1,0:T(8,128)}, u32[]{:S(2)}) %copy-start.22) | copy-done | bytes 131096
  40.1 1.6 %late.1 = f32[3,16,32,512]{3,2,1,0:T(8,128)} custom-call(f32[1,1]{1,0:T(1,128)} %bitcast.1.target_ref, f32[8,128]{1,0:T(8,128)S(1)} %get-tuple-element.22.volume_ref, f32[2,32,512]{2,1,0:T(8,128)S(1)} %copy-done.22, f32[12,8,512]{2,1,0:T(8,128)S(1)} %copy-done.18, ...), custom_call_target="tpu_custom_call", output_to_operand_aliasing={{}: (9, {})} | custom-call | flops 3000000 | bytes 6000000 | tf_op jit(solution)/shard_map/late/pallas_call | solution.py:486
  (16 shorter events, 0.0 us)
Async XLA Ops:
  4.2 1.0 %copy-start = (f32[16,32,512]{2,1,0:T(8,128)}, f32[16,32,512]{2,1,0:T(8,128)S(1)}, u32[]{:S(2)}) copy-start(f32[16,32,512]{2,1,0:T(8,128)S(1)} %get-tuple-element.29.left_ref) | copy-start | bytes 3145732
  5.1 1.0 %copy-start.4 = (f32[16,32,512]{2,1,0:T(8,128)}, f32[16,32,512]{2,1,0:T(8,128)S(1)}, u32[]{:S(2)}) copy-start(f32[16,32,512]{2,1,0:T(8,128)S(1)} %get-tuple-element.30.right_ref) | copy-start | bytes 3145732
  6.1 1.7 %copy-start.7 = (f32[3,16,32,512]{3,2,1,0:T(8,128)}, f32[3,16,32,512]{3,2,1,0:T(8,128)S(1)}, u32[]{:S(2)}) copy-start(f32[3,16,32,512]{3,2,1,0:T(8,128)S(1)} %get-tuple-element.28.velocity_ref) | copy-start | bytes 9437188
  7.8 1.0 %copy-start.9 = (f32[16,32,512]{2,1,0:T(8,128)}, f32[16,32,512]{2,1,0:T(8,128)S(1)}, u32[]{:S(2)}) copy-start(f32[16,32,512]{2,1,0:T(8,128)S(1)} %get-tuple-element.31.left_h_ref) | copy-start | bytes 3145732
  8.8 1.0 %copy-start.11 = (f32[16,32,512]{2,1,0:T(8,128)}, f32[16,32,512]{2,1,0:T(8,128)S(1)}, u32[]{:S(2)}) copy-start(f32[16,32,512]{2,1,0:T(8,128)S(1)} %get-tuple-element.32.right_h_ref) | copy-start | bytes 3145732
  9.7 3.0 %copy-start.19 = (f32[3,32,512]{2,1,0:T(8,128)}, f32[3,32,512]{2,1,0:T(8,128)S(1)}, u32[]{:S(2)}) copy-start(f32[3,32,512]{2,1,0:T(8,128)S(1)} %get-tuple-element.27.chip_ref) | copy-start | bytes 589828
  9.7 5.9 %copy-start.21 = (f32[2,32,512]{2,1,0:T(8,128)}, f32[2,32,512]{2,1,0:T(8,128)S(1)}, u32[]{:S(2)}) copy-start(f32[2,32,512]{2,1,0:T(8,128)S(1)} %get-tuple-element.23.ends_ref) | copy-start | bytes 393220
  9.7 1.5 %collective-permute-start = (f32[12,8,512]{2,1,0:T(8,128)S(1)}, f32[12,8,512]{2,1,0:T(8,128)S(1)}, u32[]{:S(2)}, u32[]{:S(2)}) collective-permute-start(f32[12,8,512]{2,1,0:T(8,128)S(1)} %get-tuple-element.25), channel_id=1, source_target_pairs={{0,4},{1,5},{2,6},{3,7},{4,0},{5,1},{6,2},{7,3},{8,12},{9,13},{10,... | collective-permute-start | bytes 589832 | tf_op jit(solution)/shard_map/ppermute | solution.py:400
  11.3 0.8 %copy-start.15 = (f32[12,8,512]{2,1,0:T(8,128)}, f32[12,8,512]{2,1,0:T(8,128)S(1)}, u32[]{:S(2)}) copy-start(f32[12,8,512]{2,1,0:T(8,128)S(1)} %collective-permute-done.mate_ref) | copy-start | bytes 589828
  12.1 0.7 %copy-start.13 = (f32[12,8,512]{2,1,0:T(8,128)}, f32[12,8,512]{2,1,0:T(8,128)S(1)}, u32[]{:S(2)}) copy-start(f32[12,8,512]{2,1,0:T(8,128)S(1)} %get-tuple-element.24.mine_ref) | copy-start | bytes 589828
  12.8 18.3 %collective-permute-start.2 = (f32[6,8,512]{2,1,0:T(8,128)}, f32[6,8,512]{2,1,0:T(8,128)}, u32[]{:S(2)}, u32[]{:S(2)}) collective-permute-start(f32[6,8,512]{2,1,0:T(8,128)} %get-tuple-element.34), channel_id=1, source_target_pairs={{0,16},{1,17},{2,18},{3,19},{4,20},{5,21},{6,22},{7,23},{8,24},{9,... | collective-permute-start | bytes 294920 | tf_op jit(solution)/shard_map/ppermute | solution.py:400
  15.6 15.4 %collective-permute-start.3 = (f32[6,8,512]{2,1,0:T(8,128)}, f32[6,8,512]{2,1,0:T(8,128)}, u32[]{:S(2)}, u32[]{:S(2)}) collective-permute-start(f32[6,8,512]{2,1,0:T(8,128)} %get-tuple-element.35), channel_id=1, source_target_pairs={{0,24},{1,25},{2,26},{3,27},{4,28},{5,29},{6,30},{7,31},{8,16},{9,... | collective-permute-start | bytes 294920 | tf_op jit(solution)/shard_map/ppermute | solution.py:400
  17.1 14.0 %collective-permute-start.1 = (f32[6,8,512]{2,1,0:T(8,128)}, f32[6,8,512]{2,1,0:T(8,128)}, u32[]{:S(2)}, u32[]{:S(2)}) collective-permute-start(f32[6,8,512]{2,1,0:T(8,128)} %get-tuple-element.33.rest_0_), channel_id=1, source_target_pairs={{0,8},{1,9},{2,10},{3,11},{4,12},{5,13},{6,14},{7,15},{8,0},{9,1},... | collective-permute-start | bytes 294920 | tf_op jit(solution)/shard_map/ppermute | solution.py:400
  17.2 18.7 %all-to-all-start = ((f32[32,8,128]{2,1,0:T(8,128)}), f32[32,8,128]{2,1,0:T(8,128)S(1)}, u32[]{:S(2)}, u32[]{:S(2)}) async-start(f32[32,8,128]{2,1,0:T(8,128)} %get-tuple-element.38), calls=%async_computation | async-start | bytes 262144 | tf_op jit(solution)/shard_map/all_to_all | solution.py:443
  23.5 1.2 %copy-start.1 = (f32[16,32,512]{2,1,0:T(8,128)S(1)}, f32[16,32,512]{2,1,0:T(8,128)}, u32[]{:S(2)}) copy-start(f32[16,32,512]{2,1,0:T(8,128)} %copy-done) | copy-start | bytes 3145732
  24.7 1.2 %copy-start.5 = (f32[16,32,512]{2,1,0:T(8,128)S(1)}, f32[16,32,512]{2,1,0:T(8,128)}, u32[]{:S(2)}) copy-start(f32[16,32,512]{2,1,0:T(8,128)} %copy-done.4) | copy-start | bytes 3145732
  25.9 1.9 %copy-start.8 = (f32[3,16,32,512]{3,2,1,0:T(8,128)S(1)}, f32[3,16,32,512]{3,2,1,0:T(8,128)}, u32[]{:S(2)}) copy-start(f32[3,16,32,512]{3,2,1,0:T(8,128)} %copy-done.7) | copy-start | bytes 9437188
  27.8 1.2 %copy-start.10 = (f32[16,32,512]{2,1,0:T(8,128)S(1)}, f32[16,32,512]{2,1,0:T(8,128)}, u32[]{:S(2)}) copy-start(f32[16,32,512]{2,1,0:T(8,128)} %copy-done.9) | copy-start | bytes 3145732
  29.1 1.2 %copy-start.12 = (f32[16,32,512]{2,1,0:T(8,128)S(1)}, f32[16,32,512]{2,1,0:T(8,128)}, u32[]{:S(2)}) copy-start(f32[16,32,512]{2,1,0:T(8,128)} %copy-done.11) | copy-start | bytes 3145732
  30.3 0.9 %copy-start.14 = (f32[12,8,512]{2,1,0:T(8,128)S(1)}, f32[12,8,512]{2,1,0:T(8,128)}, u32[]{:S(2)}) copy-start(f32[12,8,512]{2,1,0:T(8,128)} %copy-done.13) | copy-start | bytes 589828
  30.3 1.0 %copy-start.16 = (f32[12,8,512]{2,1,0:T(8,128)S(1)}, f32[12,8,512]{2,1,0:T(8,128)}, u32[]{:S(2)}) copy-start(f32[12,8,512]{2,1,0:T(8,128)} %copy-done.15) | copy-start | bytes 589828
  30.3 1.1 %copy-start.20 = (f32[3,32,512]{2,1,0:T(8,128)S(1)}, f32[3,32,512]{2,1,0:T(8,128)}, u32[]{:S(2)}) copy-start(f32[3,32,512]{2,1,0:T(8,128)} %copy-done.19) | copy-start | bytes 589828
  31.1 3.0 %copy-start.2 = (f32[16,32,512]{2,1,0:T(8,128)S(1)}, f32[16,32,512]{2,1,0:T(8,128)}, u32[]{:S(2)}) copy-start(f32[16,32,512]{2,1,0:T(8,128)} %copy-done) | copy-start | bytes 3145732
  33.1 2.7 %collective-permute-start.4 = (f32[12,8,512]{2,1,0:T(8,128)}, f32[12,8,512]{2,1,0:T(8,128)S(1)}, u32[]{:S(2)}, u32[]{:S(2)}) collective-permute-start(f32[12,8,512]{2,1,0:T(8,128)} %get-tuple-element.37), channel_id=1, source_target_pairs={{0,4},{1,5},{2,6},{3,7},{4,0},{5,1},{6,2},{7,3},{8,12},{9,13},{10,... | collective-permute-start | bytes 589832 | tf_op jit(solution)/shard_map/ppermute | solution.py:400
  35.2 0.7 %copy-start.17 = (f32[12,8,512]{2,1,0:T(8,128)}, f32[12,8,512]{2,1,0:T(8,128)S(1)}, u32[]{:S(2)}) copy-start(f32[12,8,512]{2,1,0:T(8,128)S(1)} %get-tuple-element.36.own_ref) | copy-start | bytes 589828
  35.8 1.2 %copy-start.3 = (f32[16,32,512]{2,1,0:T(8,128)S(1)}, f32[16,32,512]{2,1,0:T(8,128)}, u32[]{:S(2)}) copy-start(f32[16,32,512]{2,1,0:T(8,128)} %copy-done) | copy-start | bytes 3145732
  37.1 1.2 %copy-start.6 = (f32[16,32,512]{2,1,0:T(8,128)S(1)}, f32[16,32,512]{2,1,0:T(8,128)}, u32[]{:S(2)}) copy-start(f32[16,32,512]{2,1,0:T(8,128)} %copy-done.4) | copy-start | bytes 3145732
  38.3 0.9 %copy-start.18 = (f32[12,8,512]{2,1,0:T(8,128)S(1)}, f32[12,8,512]{2,1,0:T(8,128)}, u32[]{:S(2)}) copy-start(f32[12,8,512]{2,1,0:T(8,128)} %copy-done.17) | copy-start | bytes 589828
  39.2 0.9 %copy-start.22 = (f32[2,32,512]{2,1,0:T(8,128)S(1)}, f32[2,32,512]{2,1,0:T(8,128)}, u32[]{:S(2)}) copy-start(f32[2,32,512]{2,1,0:T(8,128)} %copy-done.21) | copy-start | bytes 393220

commit v5 on v4

--- a/solution.py
+++ b/solution.py
@@ -28,8 +28,8 @@
 def ladder_kernel(
     cells, blocks, chips, lines,
     index_hbm, diffusion_hbm, walls_hbm, velocity_hbm,
-    mine_ref, away_ref, pair_ref, chip_ref, left_ref, right_ref, left_h_ref, right_h_ref,
-    ends_ref, tile_ref, volume_ref, velocity_ref,
+    mine_ref, away_ref, pair_ref, chip_ref, ends_ref, state_ref, volume_ref,
+    left_h_ref, right_h_ref, velocity_ref,
     index_ref, diffusion_ref, walls_ref, through_ref, table_ref, held_ref, sems,
 ):
     total = cells * blocks
@@ -118,10 +118,10 @@
         0, me, sweep_forward, (lower, ones, thickness(me))
     )
     ends_ref[0] = diffusion * lower * product
+    state_ref[0] = kappa_left
     state = {}
 
     def keep_left(j, flux, value):
-        left_ref[j] = value
         left_h_ref[j] = height(index_ref, me * cells + j) * value
         state["flux"], state["value"] = flux, value
 
@@ -149,8 +149,10 @@
     scale = 1.0 / (diffusion_ref[...] * (held_ref[3] + kappa_right * held_ref[4]))
     held_ref[0] = scale
 
+    state_ref[1] = kappa_right
+    state_ref[2] = scale
+
     def keep_right(j, flux, value):
-        right_ref[j] = value
         right_h_ref[j] = height(index_ref, me * cells + j) * value
         state["flux"] = flux
 
@@ -169,15 +171,14 @@
         _, after = backward(me - 1, kappa)
         pair_ref[1] = after
 
-    for m in range(1, chips):
-        other = chip ^ m
+    for other in range(chips):
         low = jnp.minimum(chip, other)
         high = jnp.maximum(chip, other)
-        chip_ref[m - 1] = lax.fori_loop(
+        chip_ref[other] = lax.fori_loop(
             low + 1,
             high,
             lambda r, product: product * (through_ref[2 * r] * through_ref[2 * r + 1]),
-            ones,
+            jnp.where(chip == other, 0.0, ones),
         )
     flow = jnp.zeros((SUB, LANES), jnp.float32)
     weight = jnp.zeros((SUB, LANES), jnp.float32)
@@ -215,17 +216,20 @@
             flow = flow + fold(plain - low_part * from_right[0] - high_part * from_left[0])
             totals = low_part * held_ref[6, rows] + high_part * held_ref[5, rows]
             weight = weight + fold(own_extent - diffusion_ref[rows] * totals)
-    middle = SUB // 2
-    for i in range(tile_ref.shape[0]):
-        tile_ref[i, 0:middle] = flow[0:middle] + flow[middle:]
-        tile_ref[i, middle:] = weight[0:middle] + weight[middle:]
-
-
-def merge_kernel(chips, components, mine_ref, mate_ref, pair_ref, *send_refs):
+    slot = half * 2 * components
+    away_ref[slot] = jnp.zeros(away_ref.shape[1:], jnp.float32)
+    away_ref[slot, :, 0:LANES] = flow
+    away_ref[slot, :, LANES:2 * LANES] = weight
+
+
+def merge_kernel(chips, components, mine_ref, away_ref, mate_ref, pair_ref, send_ref):
     me = lax.axis_index("gz")
     chip = me // 2
     is_first = me == chip * 2
     half = mine_ref.shape[0] // (2 * components)
+    tile = away_ref[half * 2 * components] + mate_ref[half * 2 * components]
+    for other in range(chips):
+        send_ref[other, half * components] = tile
     for i in range(half):
         rows = row_tile((me - chip * 2) * half + i)
         for c in range(components):
@@ -239,28 +243,32 @@
             first = jnp.where(is_first, mine, mate)
             second = jnp.where(is_first, mate, mine)
             to_left = first + pair_ref[1, rows] * second
-            for m in range(1, chips):
-                goes_right = (chip ^ m) > chip
-                send_refs[m - 1][i * components + c] = jnp.where(goes_right, to_right, to_left)
-
-
-def spread_kernel(chips, components, mine_ref, mate_ref, pair_ref, chip_ref, _, *rest):
-    recv_refs, (own_ref, other_ref) = rest[:chips - 1], rest[chips - 1:]
+            for other in range(chips):
+                send_ref[other, i * components + c] = jnp.where(other > chip, to_right, to_left)
+
+
+def spread_kernel(
+    chips, components, mine_ref, mate_ref, pair_ref, chip_ref, recv_ref, own_ref, other_ref, tile_ref
+):
     me = lax.axis_index("gz")
     chip = me // 2
     is_first = me == chip * 2
     half = mine_ref.shape[0] // (2 * components)
+    slot = half * components
+    tile = functools.reduce(jnp.add, [recv_ref[k, slot, :, 0:2 * LANES] for k in range(chips)])
+    for y in range(tile_ref.shape[0]):
+        tile_ref[y, 0] = tile[:, 0:LANES]
+        tile_ref[y, 1] = tile[:, LANES:]
     for i in range(half):
         rows = row_tile((me - chip * 2) * half + i)
-        coefs = [chip_ref[m, rows] for m in range(chips - 1)]
+        coefs = [chip_ref[k, rows] for k in range(chips)]
         for c in range(components):
             left_in = jnp.zeros(mine_ref.shape[1:], jnp.float32)
             right_in = jnp.zeros(mine_ref.shape[1:], jnp.float32)
-            for m in range(1, chips):
-                term = coefs[m - 1] * recv_refs[m - 1][i * components + c]
-                from_left = (chip ^ m) < chip
-                left_in = left_in + jnp.where(from_left, term, 0.0)
-                right_in = right_in + jnp.where(from_left, 0.0, term)
+            for k in range(chips):
+                term = coefs[k] * recv_ref[k, i * components + c]
+                left_in = left_in + jnp.where(k < chip, term, 0.0)
+                right_in = right_in + jnp.where(k < chip, 0.0, term)
             at = i * 2 * components + c
             first_out = jnp.where(is_first, mine_ref[at], mate_ref[at])
             left_second = first_out + pair_ref[2, rows] * left_in
@@ -275,96 +283,158 @@
             other_ref[at] = jnp.where(is_first, right_in, right_first)
 
 
-def inner_kernel(velocity_ref, left_ref, right_ref, left_h_ref, right_h_ref, *rest):
-    base_ref = rest[-1]
+def leave(copies, source, target, sems):
+    copies.append(pltpu.make_async_copy(source, target, sems.at[len(copies)]))
+    copies[-1].start()
+
+
+def early_kernel(
+    index_hbm, diffusion_hbm, velocity_hbm, state_ref, ends_ref, own_ref,
+    out_hbm, plain_ref, unit_ref, base_ref, left_ref, right_ref,
+    index_ref, diffusion_ref, velocity_ref, near_ref, far_ref, result_ref, in_sems, out_sems,
+):
     components, cells, lines_y, lines_x = velocity_ref.shape
-    for t in range(lines_y // SUB):
-        rows = row_tile(t)
-        gathered = [jnp.zeros((SUB, lines_x), jnp.float32)] * components
+    half = lines_y // SUB // 2
+    middle = half * SUB
+    me = lax.axis_index("gz")
+    starts = [lax.rem(me, 2) * middle, (1 - lax.rem(me, 2)) * middle]
+    parts = [pl.ds(pl.multiple_of(start, SUB), middle) for start in starts]
+    small = [
+        pltpu.make_async_copy(index_hbm, index_ref, in_sems.at[0]),
+        pltpu.make_async_copy(diffusion_hbm, diffusion_ref, in_sems.at[1]),
+    ]
+    large = [
+        pltpu.make_async_copy(
+            velocity_hbm.at[:, :, part], velocity_ref.at[:, :, part], in_sems.at[2 + i])
+        for i, part in enumerate(parts)
+    ]
+    for copy in small + large:
+        copy.start()
+    for copy in small:
+        copy.wait()
+    heights = [height(index_ref, me * cells + j) for j in range(cells)]
+    for part, low_ref, high_ref in ((parts[0], near_ref, far_ref), (parts[1], left_ref, right_ref)):
+        inverse = 1.0 / diffusion_ref[part]
+        flux = heights[0] * inverse + state_ref[0, part]
+        value = jnp.ones_like(flux)
+        for j in range(cells):
+            low_ref[j] = value
+            if j < cells - 1:
+                value = value + (0.5 * (heights[j] + heights[j + 1])) * flux
+                flux = flux + (heights[j + 1] * inverse) * value
+        scale = state_ref[2, part]
+        flux = (heights[cells - 1] * inverse + state_ref[1, part]) * scale
+        value = scale
         for j in reversed(range(cells)):
-            left = left_ref[j, rows]
-            right = right_h_ref[j, rows]
+            high_ref[j] = value
+            if j > 0:
+                value = value + (0.5 * (heights[j] + heights[j - 1])) * flux
+                flux = flux + (heights[j - 1] * inverse) * value
+    copies = []
+    for side, (low_ref, high_ref) in enumerate(((near_ref, far_ref), (left_ref, right_ref))):
+        large[side].wait()
+        for i in range(half):
+            rows = row_tile(starts[side] // SUB + i)
+            near = slice(i * SUB, (i + 1) * SUB)
+            scale = high_ref[cells - 1, near]
+            below, above = [], []
             for c in range(components):
-                base_ref[c, j, rows] = left * gathered[c]
-                if j > 0:
-                    gathered[c] = gathered[c] + right * velocity_ref[c, j, rows]
-        gathered = [jnp.zeros((SUB, lines_x), jnp.float32)] * components
-        for j in range(cells):
-            left = left_h_ref[j, rows]
-            right = right_ref[j, rows]
-            for c in range(components):
-                gathered[c] = gathered[c] + left * velocity_ref[c, j, rows]
-                base_ref[c, j, rows] = base_ref[c, j, rows] + right * gathered[c]
-
-
-def emit(parts, rows, alpha, ends_ref, incoming_ref, at, base_ref, left_ref, right_ref, result_ref):
-    cells = left_ref.shape[0]
-    components = base_ref.shape[0]
-    scale = right_ref[cells - 1, rows]
-    lefts, rights = {}, {}
-    for c in parts:
-        left_in = incoming_ref[at + c]
-        right_in = incoming_ref[at + components + c]
-        if c == 0:
-            left_in = left_in - alpha * ends_ref[0, rows]
-            right_in = right_in - alpha * ends_ref[1, rows]
-        lefts[c] = left_in
-        rights[c] = right_in * scale
-    for j in range(cells):
-        left = left_ref[j, rows]
-        right = right_ref[j, rows]
-        for c in parts:
-            value = base_ref[c, j, rows] + (right * lefts[c] + left * rights[c])
-            result_ref[c, j, rows] = value + alpha if c == 0 else value
-
-
-def early_kernel(own_ref, base_ref, left_ref, right_ref, out_hbm, result_ref, sems):
-    components = base_ref.shape[0]
-    half = own_ref.shape[0] // (2 * components)
+                if side == 0:
+                    below.append(own_ref[i * 2 * components + c])
+                    above.append(own_ref[i * 2 * components + components + c] * scale)
+                else:
+                    below.append(jnp.zeros((SUB, lines_x), jnp.float32))
+                    above.append(jnp.zeros((SUB, lines_x), jnp.float32))
+
+            def place(c, j):
+                if side == 1:
+                    return base_ref, (c, j, near)
+                if c == 0:
+                    return plain_ref, (j, near)
+                return result_ref, (c - 1, j, near)
+
+            for j in reversed(range(cells)):
+                low = low_ref[j, near]
+                high = heights[j] * high_ref[j, near]
+                for c in range(components):
+                    ref, at = place(c, j)
+                    ref[at] = low * above[c]
+                    if j > 0:
+                        above[c] = above[c] + high * velocity_ref[c, j, rows]
+            for j in range(cells):
+                low = heights[j] * low_ref[j, near]
+                high = high_ref[j, near]
+                for c in range(components):
+                    below[c] = below[c] + low * velocity_ref[c, j, rows]
+                    ref, at = place(c, j)
+                    ref[at] = ref[at] + high * below[c]
+            if side == 0:
+                low_part = ends_ref[0, rows]
+                high_part = ends_ref[1, rows] * scale
+                for j in range(cells):
+                    unit_ref[j, near] = 1.0 - (
+                        low_part * high_ref[j, near] + high_part * low_ref[j, near])
+                for c in range(1, components):
+                    leave(copies, result_ref.at[c - 1, :, near], out_hbm.at[c, :, rows], out_sems)
+    for copy in copies:
+        copy.wait()
+
+
+def late_kernel(
+    ends_ref, other_ref, base_ref, left_ref, right_ref, _,
+    out_hbm, plain_ref, unit_ref, result_ref, sems,
+):
+    components, cells, middle, _ = base_ref.shape
+    half = middle // SUB
     me = lax.axis_index("gz")
     copies = []
     for i in range(half):
-        rows = row_tile(lax.rem(me, 2) * half + i)
-        emit(range(1, components), rows, None, None, own_ref, i * 2 * components,
-             base_ref, left_ref, right_ref, result_ref)
+        rows = row_tile((1 - lax.rem(me, 2)) * half + i)
+        near = slice(i * SUB, (i + 1) * SUB)
+        scale = right_ref[cells - 1, near]
+        lefts = [other_ref[i * 2 * components + c] for c in range(components)]
+        rights = [other_ref[i * 2 * components + components + c] * scale for c in range(components)]
+        low_part = ends_ref[0, rows]
+        high_part = ends_ref[1, rows] * scale
+        for j in range(cells):
+            left = left_ref[j, near]
+            right = right_ref[j, near]
+            unit_ref[j, near] = 1.0 - (low_part * right + high_part * left)
+            for c in range(components):
+                value = base_ref[c, j, near] + (right * lefts[c] + left * rights[c])
+                if c == 0:
+                    plain_ref[j, near] = value
+                else:
+                    result_ref[c - 1, j, near] = value
         for c in range(1, components):
-            copies.append(pltpu.make_async_copy(
-                result_ref.at[c, :, rows], out_hbm.at[c, :, rows], sems.at[len(copies)]))
-            copies[-1].start()
+            leave(copies, result_ref.at[c - 1, :, near], out_hbm.at[c, :, rows], sems)
     for copy in copies:
         copy.wait()
 
 
-def late_kernel(
-    target_ref, volume_ref, ends_ref, own_ref, other_ref, base_ref, left_ref, right_ref, *rest
+def correct_kernel(
+    target_ref, volume_ref, tiles_ref, own_plain_ref, own_unit_ref, other_plain_ref, other_unit_ref,
+    _, out_hbm, result_ref, sems,
 ):
-    tiles_ref, _, out_hbm, result_ref, sems = rest
-    components = base_ref.shape[0]
-    half = own_ref.shape[0] // (2 * components)
+    totals = functools.reduce(jnp.add, [tiles_ref[y] for y in range(tiles_ref.shape[0])])
+    flow = jnp.sum(totals[0], keepdims=True)
+    weight = jnp.sum(totals[1], keepdims=True)
+    alpha = (target_ref[...] * volume_ref[0:1, 0:1] - flow) / weight
+    cells, middle, _ = own_plain_ref.shape
+    half = middle // SUB
     me = lax.axis_index("gz")
+    sides = (
+        (lax.rem(me, 2), own_plain_ref, own_unit_ref),
+        (1 - lax.rem(me, 2), other_plain_ref, other_unit_ref),
+    )
     copies = []
-
-    def leave(c, rows):
-        copies.append(pltpu.make_async_copy(
-            result_ref.at[c, :, rows], out_hbm.at[c, :, rows], sems.at[len(copies)]))
-        copies[-1].start()
-
-    for i in range(half):
-        rows = row_tile((1 - lax.rem(me, 2)) * half + i)
-        emit(range(1, components), rows, None, None, other_ref, i * 2 * components,
-             base_ref, left_ref, right_ref, result_ref)
-        for c in range(1, components):
-            leave(c, rows)
-    totals = functools.reduce(jnp.add, [tiles_ref[i] for i in range(tiles_ref.shape[0])])
-    flow = jnp.sum(totals[0:SUB // 2], keepdims=True)
-    weight = jnp.sum(totals[SUB // 2:], keepdims=True)
-    alpha = (target_ref[...] * volume_ref[0:1, 0:1] - flow) / weight
-    for ref, whose in ((own_ref, lax.rem(me, 2)), (other_ref, 1 - lax.rem(me, 2))):
+    for whose, plain_ref, unit_ref in sides:
         for i in range(half):
             rows = row_tile(whose * half + i)
-            emit((0,), rows, alpha, ends_ref, ref, i * 2 * components,
-                 base_ref, left_ref, right_ref, result_ref)
-            leave(0, rows)
+            near = slice(i * SUB, (i + 1) * SUB)
+            for j in range(cells):
+                result_ref[j, rows] = plain_ref[j, near] + alpha * unit_ref[j, near]
+            leave(copies, result_ref.at[:, rows], out_hbm.at[0, :, rows], sems)
     for copy in copies:
         copy.wait()
 
@@ -402,30 +472,25 @@
     def to_mate(array):
         return send(array, lambda z, y: (z ^ 1, y))
 
-    def to_chip(array, m):
-        return send(array, lambda z, y: (z ^ (2 * m), y))
-
+    middle = half * SUB
     lines = float(lines_y * columns * lines_x)
-    (mine, away, pair, chip_coefs, left, right, left_h, right_h, ends, tile, volume,
-     near_velocity) = pl.pallas_call(
+    mine, away, pair, chip_coefs, ends, state, volume = pl.pallas_call(
         functools.partial(ladder_kernel, cells, blocks, chips, lines),
         out_shape=[
             shape(half * 2 * components, *sheet),
-            shape(half * 2 * components, *sheet),
+            shape(half * 2 * components + 1, *sheet),
             shape(4, *plane),
-            shape(chips - 1, *plane),
-            shape(cells, *plane),
-            shape(cells, *plane),
-            shape(cells, *plane),
-            shape(cells, *plane),
+            shape(chips, *plane),
             shape(2, *plane),
-            shape(blocks * columns, SUB, LANES),
+            shape(3, *plane),
             shape(SUB, LANES),
-            shape(*velocity.shape),
         ],
         in_specs=[anywhere] * 4,
-        out_specs=[vmem] * 12,
+        out_specs=[vmem] * 7,
         scratch_shapes=[
+            pltpu.VMEM((cells,) + plane, f32),
+            pltpu.VMEM((cells,) + plane, f32),
+            pltpu.VMEM(velocity.shape, f32),
             pltpu.SMEM(stretch_index.shape, jnp.int32),
             pltpu.VMEM(plane, f32),
             pltpu.VMEM(plane, jnp.int32),
@@ -440,63 +505,88 @@
     )(in_hbm(stretch_index), in_hbm(diffusion), in_hbm(wall_types), in_hbm(velocity))
 
     mate = to_mate(away)
-    tiles = lax.all_to_all(tile, ("gz", "gy"), 0, 0, tiled=True)
     outgoing = pl.pallas_call(
         functools.partial(merge_kernel, chips, components),
-        out_shape=[shape(half * components, *sheet)] * (chips - 1),
-        in_specs=[vmem] * 3,
-        out_specs=[vmem] * (chips - 1),
+        out_shape=shape(chips, half * components + 1, *sheet),
+        in_specs=[vmem] * 4,
+        out_specs=vmem,
         compiler_params=options(16),
         cost_estimate=cost(500_000, 1_600_000),
         name="merge",
-    )(mine, mate, pair)
-    incoming = [to_chip(outgoing[m - 1], m) for m in range(1, chips)]
-    base = pl.pallas_call(
-        inner_kernel,
-        out_shape=shape(*velocity.shape),
-        in_specs=[vmem] * 5 + [anywhere],
-        out_specs=vmem,
-        compiler_params=options(16),
-        cost_estimate=cost(8_000_000, 8_000_000),
-        name="inner",
-    )(near_velocity, left, right, left_h, right_h, outgoing[0])
-    own_in, other_out = pl.pallas_call(
+    )(mine, away, mate, pair)
+    same_core = [[2 * k + core for k in range(chips)] for core in range(2)]
+    incoming = lax.all_to_all(
+        outgoing, "gz", 0, 0, axis_index_groups=same_core, tiled=True
+    )
+    own_in, other_out, tile = pl.pallas_call(
         functools.partial(spread_kernel, chips, components),
-        out_shape=[shape(half * 2 * components, *sheet)] * 2,
-        in_specs=[vmem] * 4 + [anywhere] + [vmem] * (chips - 1),
-        out_specs=[vmem] * 2,
+        out_shape=[shape(half * 2 * components, *sheet)] * 2 + [shape(columns, 2, SUB, LANES)],
+        in_specs=[vmem] * 5,
+        out_specs=[vmem] * 3,
         compiler_params=options(16),
         cost_estimate=cost(500_000, 1_600_000),
         name="spread",
-    )(mine, mate, pair, chip_coefs, base, *incoming)
+    )(mine, mate, pair, chip_coefs, incoming)
     other_in = to_mate(other_out)
-    early = pl.pallas_call(
+    tiles = lax.all_to_all(tile, "gy", 0, 0, tiled=True)
+    partial, own_plain, own_unit, base, left, right = pl.pallas_call(
         early_kernel,
-        out_shape=shape(*velocity.shape),
-        in_specs=[vmem] * 4,
-        out_specs=anywhere,
+        out_shape=[
+            shape(*velocity.shape),
+            shape(cells, middle, lines_x),
+            shape(cells, middle, lines_x),
+            shape(components, cells, middle, lines_x),
+            shape(cells, middle, lines_x),
+            shape(cells, middle, lines_x),
+        ],
+        in_specs=[anywhere] * 3 + [vmem] * 3,
+        out_specs=[anywhere] + [vmem] * 5,
         scratch_shapes=[
+            pltpu.SMEM(stretch_index.shape, jnp.int32),
+            pltpu.VMEM(plane, f32),
             pltpu.VMEM(velocity.shape, f32),
+            pltpu.VMEM((cells, middle, lines_x), f32),
+            pltpu.VMEM((cells, middle, lines_x), f32),
+            pltpu.VMEM((components - 1, cells, middle, lines_x), f32),
+            pltpu.SemaphoreType.DMA((4,)),
             pltpu.SemaphoreType.DMA(((components - 1) * half,)),
         ],
-        compiler_params=options(16),
-        cost_estimate=cost(2_000_000, 4_000_000),
+        compiler_params=options(24),
+        cost_estimate=cost(8_000_000, 8_000_000),
         name="early",
-    )(own_in, base, left, right)
-    return pl.pallas_call(
+    )(in_hbm(stretch_index), in_hbm(diffusion), in_hbm(velocity), state, ends, own_in)
+    partial, other_plain, other_unit = pl.pallas_call(
         late_kernel,
-        out_shape=shape(*velocity.shape),
-        in_specs=[vmem] * 9 + [anywhere],
-        out_specs=anywhere,
+        out_shape=[
+            shape(*velocity.shape),
+            shape(cells, middle, lines_x),
+            shape(cells, middle, lines_x),
+        ],
+        in_specs=[vmem] * 5 + [anywhere],
+        out_specs=[anywhere] + [vmem] * 2,
         scratch_shapes=[
-            pltpu.VMEM(velocity.shape, f32),
-            pltpu.SemaphoreType.DMA(((components + 1) * half,)),
-        ],
-        input_output_aliases={9: 0},
+            pltpu.VMEM((components - 1, cells, middle, lines_x), f32),
+            pltpu.SemaphoreType.DMA(((components - 1) * half,)),
+        ],
+        input_output_aliases={5: 0},
         compiler_params=options(16),
         cost_estimate=cost(3_000_000, 6_000_000),
         name="late",
-    )(bulk_target.reshape(1, 1), volume, ends, own_in, other_in, base, left, right, tiles, early)
+    )(ends, other_in, base, left, right, partial)
+    return pl.pallas_call(
+        correct_kernel,
+        out_shape=shape(*velocity.shape),
+        in_specs=[vmem] * 7 + [anywhere],
+        out_specs=anywhere,
+        scratch_shapes=[
+            pltpu.VMEM((cells,) + plane, f32),
+            pltpu.SemaphoreType.DMA((row_tiles,)),
+        ],
+        input_output_aliases={7: 0},
+        compiler_params=options(16),
+        cost_estimate=cost(500_000, 1_600_000),
+        name="correct",
+    )(bulk_target.reshape(1, 1), volume, tiles, own_plain, own_unit, other_plain, other_unit, partial)
 
 
 def solution(mesh):

time: 42.2 us -> 31.3 us (0.74)
  local copies, waits for them, and re-layouts: 18.3 us -> 0 us
  blocking collectives: 0 us -> 13.2 us
  starting transfers between devices: 11.4 us -> 5.4 us
  waiting for transfers between devices: 1.08 us -> 2.22 us
  Pallas kernels: 10.1 us -> 9.47 us
    unnamed x46 -> x0, local copies, waits for them, and re-layouts: 18.3 us -> none
    all_to_all x0 -> x1, blocking collectives: none -> 13.2 us  [shards(): lax.all_to_all(outgoing, 'gz', 0, 0, axis_index_groups=same_core, tiled=T...]
    ppermute x5 -> x2, starting transfers between devices: 5.11 us -> 0.53 us  [send(): return lax.ppermute(array, ('gz', 'gy'), route)]
    pallas_call x3, Pallas kernels: 3.41 us -> 5.08 us  [the longest x1 2.78 us: shards(): pl.pallas_call(early_kernel, out_shape=[shape(*velocity.shape), shape(cel...]
    all_to_all x1, starting transfers between devices: 6.31 us -> 4.87 us  [shards(): tiles = lax.all_to_all(tile, 'gy', 0, 0, tiled=True)]
    all_to_all x1, waiting for transfers between devices: 0.01 us -> 1.12 us  [shards(): tiles = lax.all_to_all(tile, 'gy', 0, 0, tiled=True)]
    pallas_call x1, Pallas kernels: 1.75 us -> 0.63 us  [shards(): pl.pallas_call(functools.partial(spread_kernel, chips, components), out_s...]
    pallas_call x1, Pallas kernels: 0.8 us -> 0.05 us  [shards(): pl.pallas_call(functools.partial(merge_kernel, chips, components), out_sh...]
  transfers between devices with their start and end apart: 6 -> 3, of which waited for: 1 -> 2; matrix products, arithmetic and copies ran while one was open for 0% -> 0% of each run, Pallas kernels for 9% -> 12%
where the time goes in v5:
time: 31.3 us; the launch traced here: 31 us
  blocking collectives  13.2 us (42%)
  Pallas kernels  9.47 us (30%)
  starting transfers between devices  5.4 us (17%)
  waiting for transfers between devices  2.22 us (7%)
  between operations  0.69 us (2%)
    all_to_all x1, blocking collectives, shards(): lax.all_to_all(outgoing, 'gz', 0, 0, axis_index_groups=same_core, tiled=T...  13.2 us
    all_to_all x1, starting transfers between devices, shards(): tiles = lax.all_to_all(tile, 'gy', 0, 0, tiled=True)  4.87 us
    pallas_call x1, Pallas kernels, shards(): pl.pallas_call(functools.partial(ladder_kernel, cells, blocks, chips, lin...  3.7 us
    pallas_call x1, Pallas kernels, shards(): pl.pallas_call(early_kernel, out_shape=[shape(*velocity.shape), shape(cel...  2.78 us
    pallas_call x1, Pallas kernels, shards(): pl.pallas_call(correct_kernel, out_shape=shape(*velocity.shape), in_specs...  1.23 us
    all_to_all x1, waiting for transfers between devices, shards(): tiles = lax.all_to_all(tile, 'gy', 0, 0, tiled=True)  1.12 us
    ppermute x2, waiting for transfers between devices, send(): return lax.ppermute(array, ('gz', 'gy'), route)  1.09 us
    pallas_call x1, Pallas kernels, shards(): pl.pallas_call(late_kernel, out_shape=[shape(*velocity.shape), shape(cell...  1.07 us
  transfers between devices with their start and end apart: 3, of which 2 were waited for; matrix products, arithmetic and copies ran while one was open for 0% of the time, Pallas kernels for 12%

profile of v5, /device:TPU:0, one launch (start us, length us, event | category | flops | bytes accessed | tf_op | source)
XLA Modules:
  0.0 31.0 jit_solution(3786925482006711048)
XLA Ops:
  0.0 3.7 %ladder.1 = (f32[12,8,512]{2,1,0:T(8,128)S(1)}, f32[13,8,512]{2,1,0:T(8,128)S(1)}, f32[4,32,512]{2,1,0:T(8,128)S(1)}, f32[4,32,512]{2,1,0:T(8,128)S(1)}, f32[2,3...) custom-call(s32[128]{0:T(128)} %index_hbm.3, f32[32,512]{1,0:T(8,128)} %diffusion_hbm.3, ...), custom_call_target="tpu_custom_call" | custom-call | flops 40000000 | bytes 6000000 | tf_op jit(solution)/shard_map/ladder/pallas_call | solution.py:477
  3.7 0.5 %collective-permute-start = (f32[13,8,512]{2,1,0:T(8,128)S(1)}, f32[13,8,512]{2,1,0:T(8,128)S(1)}, u32[]{:S(2)}, u32[]{:S(2)}) collective-permute-start(f32[13,8,512]{2,1,0:T(8,128)S(1)} %get-tuple-element.26.away_ref), channel_id=1, source_target_pairs={{0,4},{1,5},{2,6},{3,7},{4,0},{5,1},{6,2},{7,3},{8,12},{9,13},{10,... | collective-permute-start | bytes 638984 | tf_op jit(solution)/shard_map/ppermute | solution.py:470
  4.2 1.1 %collective-permute-done.mate_ref = f32[13,8,512]{2,1,0:T(8,128)S(1)} collective-permute-done((f32[13,8,512]{2,1,0:T(8,128)S(1)}, f32[13,8,512]{2,1,0:T(8,128)S(1)}, u32[]{:S(2)}, u32[]{:S(2)}) %collective-permute-start) | collective-permute-done | bytes 213024 | tf_op jit(solution)/shard_map/ppermute | solution.py:470
  5.3 0.1 merge.1
  5.4 13.2 %all_to_all.10.recv_ref = f32[4,7,8,512]{3,2,1,0:T(8,128)S(1)} all-to-all(f32[4,7,8,512]{3,2,1,0:T(8,128)S(1)} %merge.1), channel_id=1, replica_groups={{0,8,16,24},{4,12,20,28},{1,9,17,25},{5,13,21,29},{2,10,18,26},{6,14,22..., dimensions={0} | all-to-all | bytes 917504 | tf_op jit(solution)/shard_map/all_to_all | solution.py:518
  18.6 0.6 %spread.1 = (f32[12,8,512]{2,1,0:T(8,128)S(1)}, f32[12,8,512]{2,1,0:T(8,128)S(1)}, f32[4,2,8,128]{3,2,1,0:T(8,128)}) custom-call(f32[12,8,512]{2,1,0:T(8,128)S(1)} %get-tuple-element.25.mine_ref, f32[13,8,512]{2,1,0:T(8,128)S(1)} %collective-permute-done.mate_ref, f32[4,32,512]{2,1,0:T(8,128)S(1)} %get-tuple-element.27.pair_ref, ...), custom_call_target="tpu_custom_call" | custom-call | flops 500000 | bytes 1600000 | tf_op jit(solution)/shard_map/spread/pallas_call | solution.py:521
  19.2 0.0 collective-permute-start.1
  19.2 4.9 %all-to-all-start.1 = ((f32[4,2,8,128]{3,2,1,0:T(8,128)}), f32[4,2,8,128]{3,2,1,0:T(8,128)S(1)}, u32[]{:S(2)}, u32[]{:S(2)}) async-start(f32[4,2,8,128]{3,2,1,0:T(8,128)} %get-tuple-element.29), calls=%async_computation.1 | async-start | bytes 65536 | tf_op jit(solution)/shard_map/all_to_all | solution.py:531
  24.7 2.8 %early.1 = (f32[3,16,32,512]{3,2,1,0:T(8,128)}, f32[16,16,512]{2,1,0:T(8,128)S(1)}, f32[16,16,512]{2,1,0:T(8,128)S(1)}, f32[3,16,16,512]{3,2,1,0:T(8,128)S(1)}, ...) custom-call(s32[128]{0:T(128)} %index_hbm.3, f32[32,512]{1,0:T(8,128)} %diffusion_hbm.3, ...), custom_call_target="tpu_custom_call" | custom-call | flops 8000000 | bytes 8000000 | tf_op jit(solution)/shard_map/early/pallas_call | solution.py:532
  27.5 0.0 collective-permute-done.1.other_ref
  27.5 1.1 %late.1 = (f32[3,16,32,512]{3,2,1,0:T(8,128)}, f32[16,16,512]{2,1,0:T(8,128)S(1)}, f32[16,16,512]{2,1,0:T(8,128)S(1)}) custom-call(f32[2,32,512]{2,1,0:T(8,128)S(1)} %get-tuple-element.31.ends_ref, f32[12,8,512]{2,1,0:T(8,128)S(1)} %collective-permute-done.1.other_ref, ...), custom_call_target="tpu_custom_call", output_to_operand_aliasing={{0}: (5, {})} | custom-call | flops 3000000 | bytes 6000000 | tf_op jit(solution)/shard_map/late/pallas_call | solution.py:558
  28.6 1.1 %all-to-all-done.1.tiles_ref = f32[4,2,8,128]{3,2,1,0:T(8,128)S(1)} async-done(((f32[4,2,8,128]{3,2,1,0:T(8,128)}), f32[4,2,8,128]{3,2,1,0:T(8,128)S(1)}, u32[]{:S(2)}, u32[]{:S(2)}) %all-to-all-start.1) | async-done | bytes 32800 | tf_op jit(solution)/shard_map/all_to_all | solution.py:531
  29.7 1.2 %correct.1 = f32[3,16,32,512]{3,2,1,0:T(8,128)} custom-call(f32[1,1]{1,0:T(1,128)} %bitcast.1.target_ref, f32[8,128]{1,0:T(8,128)S(1)} %get-tuple-element.24.volume_ref, f32[4,2,8,128]{3,2,1,0:T(8,128)S(1)} %all-to-all-done.1.tiles_ref, f32[16,16,512]{2,1,0:T(8,128)S(1)} %get-tuple-element.33.own_plain_ref, ...), custom_call_target="tpu_custom_call", output_to_operand_aliasing={{}: (7, {})} | custom-call | flops 500000 | bytes 1600000 | tf_op jit(solution)/shard_map/correct/pallas_call | solution.py:576
Async XLA Ops:
  3.7 1.6 %collective-permute-start = (f32[13,8,512]{2,1,0:T(8,128)S(1)}, f32[13,8,512]{2,1,0:T(8,128)S(1)}, u32[]{:S(2)}, u32[]{:S(2)}) collective-permute-start(f32[13,8,512]{2,1,0:T(8,128)S(1)} %get-tuple-element.26.away_ref), channel_id=1, source_target_pairs={{0,4},{1,5},{2,6},{3,7},{4,0},{5,1},{6,2},{7,3},{8,12},{9,13},{10,... | collective-permute-start | bytes 638984 | tf_op jit(solution)/shard_map/ppermute | solution.py:470
  19.2 8.3 %collective-permute-start.1 = (f32[12,8,512]{2,1,0:T(8,128)S(1)}, f32[12,8,512]{2,1,0:T(8,128)S(1)}, u32[]{:S(2)}, u32[]{:S(2)}) collective-permute-start(f32[12,8,512]{2,1,0:T(8,128)S(1)} %get-tuple-element.35), channel_id=1, source_target_pairs={{0,4},{1,5},{2,6},{3,7},{4,0},{5,1},{6,2},{7,3},{8,12},{9,13},{10,... | collective-permute-start | bytes 589832 | tf_op jit(solution)/shard_map/ppermute | solution.py:470
  19.2 10.5 %all-to-all-start.1 = ((f32[4,2,8,128]{3,2,1,0:T(8,128)}), f32[4,2,8,128]{3,2,1,0:T(8,128)S(1)}, u32[]{:S(2)}, u32[]{:S(2)}) async-start(f32[4,2,8,128]{3,2,1,0:T(8,128)} %get-tuple-element.29), calls=%async_computation.1 | async-start | bytes 65536 | tf_op jit(solution)/shard_map/all_to_all | solution.py:531

commit v6 on v4

v6 whole, which is shorter than its diff:
```python
import functools

import jax
import jax.numpy as jnp
from jax import lax
from jax.experimental import pallas as pl
from jax.experimental.pallas import tpu as pltpu
from jax.sharding import PartitionSpec as P

SUB = 8
STRETCHES = 7
LANES = 128
MIB = 1024 * 1024


def row_tile(t):
    return pl.ds(pl.multiple_of(t * SUB, SUB), SUB)


def wide(tile, lines_x):
    return jnp.concatenate([tile] * (lines_x // LANES), axis=1)


def height(index_ref, k):
    return 0.5 + 0.25 * index_ref[k].astype(jnp.float32)


def half_sum(index_ref, k):
    return 0.5 * (height(index_ref, k) + height(index_ref, k + 1))


def ladder_kernel(
    cells, blocks, chips, lines,
    index_hbm, diffusion_hbm, walls_hbm, velocity_hbm,
    mine_ref, away_ref, pair_ref, chip_ref, ends_ref, state_ref, heights_ref, near_velocity_ref,
    tile_ref, volume_ref,
    left_h_ref, right_h_ref, far_velocity_ref,
    index_ref, diffusion_ref, walls_ref, through_ref, table_ref, held_ref, sems,
):
    total = cells * blocks
    components = near_velocity_ref.shape[0]
    row_tiles = diffusion_ref.shape[0] // SUB
    half = row_tiles // 2
    me = lax.axis_index("gz")
    chip = me // 2
    first = chip * 2
    sides = ((away_ref, far_velocity_ref, 1 - (me - first)), (mine_ref, near_velocity_ref, me - first))
    small = [
        pltpu.make_async_copy(index_hbm, index_ref, sems.at[0]),
        pltpu.make_async_copy(diffusion_hbm, diffusion_ref, sems.at[1]),
        pltpu.make_async_copy(walls_hbm, walls_ref, sems.at[2]),
    ]
    large = [
        pltpu.make_async_copy(
            velocity_hbm.at[:, :, pl.ds(pl.multiple_of(whose * half * SUB, SUB), half * SUB)],
            ref, sems.at[3 + i])
        for i, (_, ref, whose) in enumerate(sides)
    ]
    for copy in small + large:
        copy.start()
    for copy in small:
        copy.wait()
    diffusion = diffusion_ref[...]
    inverse = 1.0 / diffusion
    state_ref[3] = inverse
    for i in range(STRETCHES):
        table_ref[i] = (0.5 + 0.25 * i) * inverse
    walls = walls_ref[...]

    def wall(bits, k):
        face = 1.0 / jnp.full((SUB, diffusion.shape[1]), 0.5 * height(index_ref, k))
        return bits.astype(jnp.float32) * jnp.concatenate([face] * row_tiles, axis=0)

    lower = wall(walls & 1, 0)
    upper = wall(walls >> 1, total - 1)

    def forward(block, kappa, keep=None):
        start = block * cells
        flux = table_ref[index_ref[start]] + kappa
        value = jnp.ones_like(flux)
        for j in range(cells):
            if keep is not None:
                keep(j, flux, value)
            k = start + j
            if j < cells - 1:
                value = value + half_sum(index_ref, k) * flux
                flux = flux + table_ref[index_ref[k + 1]] * value
        k = jnp.minimum(start + cells - 1, total - 2)
        after = 1.0 / (value + half_sum(index_ref, k) * flux)
        return flux * after, after

    def backward(block, kappa, scale=None, keep=None):
        start = block * cells
        flux = table_ref[index_ref[start + cells - 1]] + kappa
        value = jnp.ones_like(flux)
        if scale is not None:
            flux, value = flux * scale, scale
        for j in reversed(range(cells)):
            if keep is not None:
                keep(j, flux, value)
            k = start + j
            if j > 0:
                value = value + half_sum(index_ref, k - 1) * flux
                flux = flux + table_ref[index_ref[k - 1]] * value
        k = jnp.maximum(start - 1, 0)
        after = 1.0 / (value + half_sum(index_ref, k) * flux)
        return flux * after, after

    def thickness(block):
        parts = [height(index_ref, block * cells + j) for j in range(cells)]
        return functools.reduce(jnp.add, parts)

    def sweep_forward(block, state):
        kappa, product, extent = state
        kappa, after = forward(block, kappa)
        through_ref[block] = after
        return kappa, product * after, extent + thickness(block)

    def sweep_backward(step, state):
        block = blocks - 1 - step
        kappa, product, extent = state
        kappa, after = backward(block, kappa)
        through_ref[block] = after
        return kappa, product * after, extent + thickness(block)

    ones = jnp.ones_like(diffusion)
    kappa_left, product, extent = lax.fori_loop(
        0, me, sweep_forward, (lower, ones, thickness(me))
    )
    ends_ref[0] = diffusion * lower * product
    state_ref[0] = kappa_left
    state = {}

    def keep_left(j, flux, value):
        left_h_ref[j] = height(index_ref, me * cells + j) * value
        state["flux"], state["value"] = flux, value

    kappa, own_forward = forward(me, kappa_left, keep_left)
    held_ref[1] = own_forward
    held_ref[3] = state["flux"]
    held_ref[4] = state["value"]
    held_ref[5] = state["flux"] - kappa_left

    @pl.when(me == first)
    def _():
        pair_ref[2] = own_forward
        _, after = forward(me + 1, kappa)
        pair_ref[0] = after

    @pl.when(me != first)
    def _():
        pair_ref[2] = through_ref[first]
        pair_ref[0] = own_forward

    kappa_right, product, extent = lax.fori_loop(
        0, blocks - 1 - me, sweep_backward, (upper, ones, extent)
    )
    ends_ref[1] = diffusion_ref[...] * upper * product
    scale = 1.0 / (diffusion_ref[...] * (held_ref[3] + kappa_right * held_ref[4]))
    held_ref[0] = scale

    state_ref[1] = kappa_right
    state_ref[2] = scale

    def keep_right(j, flux, value):
        right_h_ref[j] = height(index_ref, me * cells + j) * value
        state["flux"] = flux

    kappa, own_backward = backward(me, kappa_right, scale, keep_right)
    held_ref[2] = own_backward
    held_ref[6] = state["flux"] - kappa_right * scale

    @pl.when(me == first)
    def _():
        pair_ref[1] = own_backward * held_ref[0]
        pair_ref[3] = through_ref[first + 1]

    @pl.when(me != first)
    def _():
        pair_ref[3] = own_backward * held_ref[0]
        _, after = backward(me - 1, kappa)
        pair_ref[1] = after

    for m in range(1, chips):
        other = chip ^ m
        low = jnp.minimum(chip, other)
        high = jnp.maximum(chip, other)
        chip_ref[m - 1] = lax.fori_loop(
            low + 1,
            high,
            lambda r, product: product * (through_ref[2 * r] * through_ref[2 * r + 1]),
            ones,
        )
    flow = jnp.zeros((SUB, LANES), jnp.float32)
    weight = jnp.zeros((SUB, LANES), jnp.float32)

    def fold(array):
        parts = [array[:, i * LANES:(i + 1) * LANES] for i in range(array.shape[1] // LANES)]
        return functools.reduce(jnp.add, parts)

    for copy in large:
        copy.wait()
    volume_ref[...] = jnp.full(volume_ref.shape, extent * lines)
    own_extent = thickness(me)
    heights = [height(index_ref, me * cells + j) for j in range(cells)]
    for j in range(cells):
        heights_ref[j] = jnp.full((SUB, LANES), heights[j])
    for ref, velocity_ref, whose in sides:
        for i in range(half):
            rows = row_tile(whose * half + i)
            near = slice(i * SUB, (i + 1) * SUB)
            from_left = [0.0] * components
            from_right = [0.0] * components
            plain = 0.0
            for j in range(cells):
                left = left_h_ref[j, rows]
                right = right_h_ref[j, rows]
                for c in range(components):
                    v = velocity_ref[c, j, near]
                    from_left[c] = from_left[c] + left * v
                    from_right[c] = from_right[c] + right * v
                    if c == 0:
                        plain = plain + heights[j] * v
            for c in range(components):
                ref[i * 2 * components + c] = from_left[c] * held_ref[1, rows]
                ref[i * 2 * components + components + c] = from_right[c] * held_ref[2, rows]
            low_part = ends_ref[0, rows]
            high_part = ends_ref[1, rows] * held_ref[0, rows]
            flow = flow + fold(plain - low_part * from_right[0] - high_part * from_left[0])
            totals = low_part * held_ref[6, rows] + high_part * held_ref[5, rows]
            weight = weight + fold(own_extent - diffusion_ref[rows] * totals)
    middle = SUB // 2
    tile_ref[0:middle] = flow[0:middle] + flow[middle:]
    tile_ref[middle:] = weight[0:middle] + weight[middle:]


def copies_kernel(tile_ref, volume_ref, target_ref, tiles_ref, goal_ref):
    tile = tile_ref[...]
    for i in range(tiles_ref.shape[0]):
        tiles_ref[i] = tile
    goal_ref[...] = target_ref[...] * volume_ref[...]


def merge_kernel(chips, components, mine_ref, mate_ref, pair_ref, *rest):
    send_refs, near_ref = rest[1:-1], rest[-1]
    me = lax.axis_index("gz")
    chip = me // 2
    is_first = me == chip * 2
    half = mine_ref.shape[0] // (2 * components)
    for i in range(half):
        rows = row_tile((me - chip * 2) * half + i)
        for c in range(components):
            at = i * 2 * components + c
            mine, mate = mine_ref[at], mate_ref[at]
            first = jnp.where(is_first, mine, mate)
            second = jnp.where(is_first, mate, mine)
            near_ref[at] = first
            to_right = second + pair_ref[0, rows] * first
            at = at + components
            mine, mate = mine_ref[at], mate_ref[at]
            first = jnp.where(is_first, mine, mate)
            second = jnp.where(is_first, mate, mine)
            near_ref[at] = second
            to_left = first + pair_ref[1, rows] * second
            for m in range(1, chips):
                goes_right = (chip ^ m) > chip
                send_refs[m - 1][i * components + c] = jnp.where(goes_right, to_right, to_left)


def spread_kernel(chips, components, near_ref, pair_ref, chip_ref, *rest):
    recv_refs, (own_ref, other_ref) = rest[:chips - 1], rest[chips - 1:]
    me = lax.axis_index("gz")
    chip = me // 2
    is_first = me == chip * 2
    half = near_ref.shape[0] // (2 * components)
    for i in range(half):
        rows = row_tile((me - chip * 2) * half + i)
        coefs = [chip_ref[m, rows] for m in range(chips - 1)]
        for c in range(components):
            left_in = jnp.zeros(near_ref.shape[1:], jnp.float32)
            right_in = jnp.zeros(near_ref.shape[1:], jnp.float32)
            for m in range(1, chips):
                term = coefs[m - 1] * recv_refs[m - 1][i * components + c]
                from_left = (chip ^ m) < chip
                left_in = left_in + jnp.where(from_left, term, 0.0)
                right_in = right_in + jnp.where(from_left, 0.0, term)
            at = i * 2 * components + c
            left_second = near_ref[at] + pair_ref[2, rows] * left_in
            right_first = near_ref[at + components] + pair_ref[3, rows] * right_in
            own_ref[at] = jnp.where(is_first, left_in, left_second)
            other_ref[at] = jnp.where(is_first, left_second, left_in)
            at = at + components
            own_ref[at] = jnp.where(is_first, right_first, right_in)
            other_ref[at] = jnp.where(is_first, right_in, right_first)


def leave(copies, source, target, sems):
    copies.append(pltpu.make_async_copy(source, target, sems.at[len(copies)]))
    copies[-1].start()


def finish(i, rows, incoming_ref, ends_ref, heights_ref, velocity_ref, low_ref, high_ref,
           plain_ref, unit_ref, result_ref):
    components, cells, _, lines_x = velocity_ref.shape
    near = slice(i * SUB, (i + 1) * SUB)
    scale = high_ref[cells - 1, near]

    def place(c):
        return (plain_ref, ()) if c == 0 else (result_ref, (c - 1,))

    below = [incoming_ref[i * 2 * components + c] for c in range(components)]
    above = [
        incoming_ref[i * 2 * components + components + c] * scale for c in range(components)
    ]
    for j in reversed(range(cells)):
        low = low_ref[j, near]
        high = wide(heights_ref[j], lines_x) * high_ref[j, near]
        for c in range(components):
            ref, at = place(c)
            ref[at + (j, near)] = low * above[c]
            if j > 0:
                above[c] = above[c] + high * velocity_ref[c, j, near]
    low_part = ends_ref[0, rows]
    high_part = ends_ref[1, rows] * scale
    for j in range(cells):
        low = low_ref[j, near]
        high = high_ref[j, near]
        weighted = wide(heights_ref[j], lines_x) * low
        for c in range(components):
            below[c] = below[c] + weighted * velocity_ref[c, j, near]
            ref, at = place(c)
            ref[at + (j, near)] = ref[at + (j, near)] + high * below[c]
        unit_ref[j, near] = 1.0 - (low_part * high + high_part * low)


def profiles(part, heights_ref, state_ref, low_ref, high_ref):
    cells, middle, lines_x = low_ref.shape
    heights = [
        jnp.concatenate([wide(heights_ref[j], lines_x)] * (middle // SUB), axis=0)
        for j in range(cells)
    ]
    inverse = state_ref[3, part]
    flux = heights[0] * inverse + state_ref[0, part]
    value = jnp.ones_like(flux)
    for j in range(cells):
        low_ref[j] = value
        if j < cells - 1:
            value = value + (0.5 * (heights[j] + heights[j + 1])) * flux
            flux = flux + (heights[j + 1] * inverse) * value
    scale = state_ref[2, part]
    flux = (heights[cells - 1] * inverse + state_ref[1, part]) * scale
    value = scale
    for j in reversed(range(cells)):
        high_ref[j] = value
        if j > 0:
            value = value + (0.5 * (heights[j] + heights[j - 1])) * flux
            flux = flux + (heights[j - 1] * inverse) * value


def early_kernel(
    velocity_hbm, near_velocity_ref, heights_ref, state_ref, ends_ref, own_ref,
    out_hbm, plain_ref, unit_ref, far_velocity_ref, left_ref, right_ref,
    low_ref, high_ref, result_ref, arrival, sems,
):
    components, cells, middle, _ = near_velocity_ref.shape
    half = middle // SUB
    me = lax.axis_index("gz")
    starts = [lax.rem(me, 2) * middle, (1 - lax.rem(me, 2)) * middle]
    parts = [pl.ds(pl.multiple_of(start, SUB), middle) for start in starts]
    load = pltpu.make_async_copy(velocity_hbm.at[:, :, parts[1]], far_velocity_ref, arrival)
    load.start()
    copies = []
    profiles(parts[0], heights_ref, state_ref, low_ref, high_ref)
    for i in range(half):
        rows = row_tile(lax.rem(me, 2) * half + i)
        finish(i, rows, own_ref, ends_ref, heights_ref, near_velocity_ref, low_ref, high_ref,
               plain_ref, unit_ref, result_ref)
        for c in range(1, components):
            leave(copies, result_ref.at[c - 1, :, i * SUB:(i + 1) * SUB],
                  out_hbm.at[c, :, rows], sems)
    profiles(parts[1], heights_ref, state_ref, left_ref, right_ref)
    load.wait()
    for copy in copies:
        copy.wait()


def late_kernel(
    heights_ref, ends_ref, other_ref, far_velocity_ref, left_ref, right_ref, _,
    out_hbm, plain_ref, unit_ref, result_ref, sems,
):
    components, cells, middle, _ = far_velocity_ref.shape
    half = middle // SUB
    me = lax.axis_index("gz")
    copies = []
    for i in range(half):
        rows = row_tile((1 - lax.rem(me, 2)) * half + i)
        finish(i, rows, other_ref, ends_ref, heights_ref, far_velocity_ref, left_ref, right_ref,
               plain_ref, unit_ref, result_ref)
        for c in range(1, components):
            leave(copies, result_ref.at[c - 1, :, i * SUB:(i + 1) * SUB],
                  out_hbm.at[c, :, rows], sems)
    for copy in copies:
        copy.wait()


def correct_kernel(
    goal_ref, tiles_ref, own_plain_ref, own_unit_ref, other_plain_ref, other_unit_ref,
    _, out_hbm, result_ref, sems,
):
    totals = functools.reduce(jnp.add, [tiles_ref[i] for i in range(tiles_ref.shape[0])])
    flow = jnp.sum(totals[0:SUB // 2], keepdims=True)
    weight = jnp.sum(totals[SUB // 2:], keepdims=True)
    alpha = (goal_ref[0:1, 0:1] - flow) / weight
    cells, middle, _ = own_plain_ref.shape
    half = middle // SUB
    me = lax.axis_index("gz")
    sides = (
        (lax.rem(me, 2), own_plain_ref, own_unit_ref),
        (1 - lax.rem(me, 2), other_plain_ref, other_unit_ref),
    )
    copies = []
    for whose, plain_ref, unit_ref in sides:
        for i in range(half):
            rows = row_tile(whose * half + i)
            near = slice(i * SUB, (i + 1) * SUB)
            for j in range(cells):
                result_ref[j, rows] = plain_ref[j, near] + alpha * unit_ref[j, near]
            leave(copies, result_ref.at[:, rows], out_hbm.at[0, :, rows], sems)
    for copy in copies:
        copy.wait()


def shards(velocity, diffusion, wall_types, stretch_index, bulk_target):
    blocks = lax.axis_size("gz")
    columns = lax.axis_size("gy")
    components, cells, lines_y, lines_x = velocity.shape
    chips = blocks // 2
    row_tiles = lines_y // SUB
    half = row_tiles // 2
    f32 = jnp.float32
    vmem = pl.BlockSpec(memory_space=pltpu.VMEM)
    anywhere = pl.BlockSpec(memory_space=pl.ANY)
    plane = (lines_y, lines_x)
    sheet = (SUB, lines_x)

    def shape(*dims):
        return jax.ShapeDtypeStruct(dims, f32)

    def in_hbm(array):
        return pltpu.with_memory_space_constraint(array, pltpu.HBM)

    def options(mib):
        return pltpu.CompilerParams(vmem_limit_bytes=mib * MIB)

    def cost(flops, transferred):
        return pl.CostEstimate(flops=flops, bytes_accessed=transferred, transcendentals=0)

    def send(array, partner):
        pairs = [((z, y), partner(z, y)) for z in range(blocks) for y in range(columns)]
        route = [(a * columns + b, c * columns + d) for (a, b), (c, d) in pairs]
        return lax.ppermute(array, ("gz", "gy"), route)

    def to_mate(array):
        return send(array, lambda z, y: (z ^ 1, y))

    middle = half * SUB
    lines = float(lines_y * columns * lines_x)
    (mine, away, pair, chip_coefs, ends, state, heights, near_velocity, tile,
     volume) = pl.pallas_call(
        functools.partial(ladder_kernel, cells, blocks, chips, lines),
        out_shape=[
            shape(half * 2 * components, *sheet),
            shape(half * 2 * components, *sheet),
            shape(4, *plane),
            shape(chips - 1, *plane),
            shape(2, *plane),
            shape(4, *plane),
            shape(cells, SUB, LANES),
            shape(components, cells, middle, lines_x),
            shape(SUB, LANES),
            shape(SUB, LANES),
        ],
        in_specs=[anywhere] * 4,
        out_specs=[vmem] * 10,
        scratch_shapes=[
            pltpu.VMEM((cells,) + plane, f32),
            pltpu.VMEM((cells,) + plane, f32),
            pltpu.VMEM((components, cells, middle, lines_x), f32),
            pltpu.SMEM(stretch_index.shape, jnp.int32),
            pltpu.VMEM(plane, f32),
            pltpu.VMEM(plane, jnp.int32),
            pltpu.VMEM((blocks,) + plane, f32),
            pltpu.VMEM((STRETCHES,) + plane, f32),
            pltpu.VMEM((7,) + plane, f32),
            pltpu.SemaphoreType.DMA((5,)),
        ],
        compiler_params=options(24),
        cost_estimate=cost(40_000_000, 6_000_000),
        name="ladder",
    )(in_hbm(stretch_index), in_hbm(diffusion), in_hbm(wall_types), in_hbm(velocity))

    mate = to_mate(away)
    tile_copies, goal = pl.pallas_call(
        copies_kernel,
        out_shape=[shape(blocks * columns, SUB, LANES), shape(SUB, LANES)],
        in_specs=[vmem] * 3,
        out_specs=[vmem] * 2,
        compiler_params=options(16),
        cost_estimate=cost(10_000, 200_000),
        name="copies",
    )(tile, volume, bulk_target.reshape(1, 1))
    tiles = lax.all_to_all(tile_copies, ("gz", "gy"), 0, 0, tiled=True)
    *outgoing, near = pl.pallas_call(
        functools.partial(merge_kernel, chips, components),
        out_shape=[shape(half * components, *sheet)] * (chips - 1)
        + [shape(half * 2 * components, *sheet)],
        in_specs=[vmem] * 3 + [anywhere],
        out_specs=[vmem] * chips,
        compiler_params=options(16),
        cost_estimate=cost(500_000, 1_600_000),
        name="merge",
    )(mine, mate, pair, goal)
    incoming = [
        send(outgoing[m - 1], lambda z, y: (z ^ (2 * m), y)) for m in range(1, chips)
    ]
    own_in, other_out = pl.pallas_call(
        functools.partial(spread_kernel, chips, components),
        out_shape=[shape(half * 2 * components, *sheet)] * 2,
        in_specs=[vmem] * (3 + chips - 1),
        out_specs=[vmem] * 2,
        compiler_params=options(16),
        cost_estimate=cost(500_000, 1_600_000),
        name="spread",
    )(near, pair, chip_coefs, *incoming)
    other_in = to_mate(other_out)
    part = (components, cells, middle, lines_x)
    profile = shape(cells, middle, lines_x)
    partial, own_plain, own_unit, far_velocity, left, right = pl.pallas_call(
        early_kernel,
        out_shape=[shape(*velocity.shape), profile, profile, shape(*part), profile, profile],
        in_specs=[anywhere] + [vmem] * 5,
        out_specs=[anywhere] + [vmem] * 5,
        scratch_shapes=[
            pltpu.VMEM((cells, middle, lines_x), f32),
            pltpu.VMEM((cells, middle, lines_x), f32),
            pltpu.VMEM((components - 1, cells, middle, lines_x), f32),
            pltpu.SemaphoreType.DMA,
            pltpu.SemaphoreType.DMA(((components - 1) * half,)),
        ],
        compiler_params=options(24),
        cost_estimate=cost(8_000_000, 8_000_000),
        name="early",
    )(in_hbm(velocity), near_velocity, heights, state, ends, own_in)
    partial, other_plain, other_unit = pl.pallas_call(
        late_kernel,
        out_shape=[shape(*velocity.shape), profile, profile],
        in_specs=[vmem] * 6 + [anywhere],
        out_specs=[anywhere] + [vmem] * 2,
        scratch_shapes=[
            pltpu.VMEM((components - 1, cells, middle, lines_x), f32),
            pltpu.SemaphoreType.DMA(((components - 1) * half,)),
        ],
        input_output_aliases={6: 0},
        compiler_params=options(16),
        cost_estimate=cost(3_000_000, 6_000_000),
        name="late",
    )(heights, ends, other_in, far_velocity, left, right, partial)
    return pl.pallas_call(
        correct_kernel,
        out_shape=shape(*velocity.shape),
        in_specs=[vmem] * 6 + [anywhere],
        out_specs=anywhere,
        scratch_shapes=[
            pltpu.VMEM((cells,) + plane, f32),
            pltpu.SemaphoreType.DMA((row_tiles,)),
        ],
        input_output_aliases={6: 0},
        compiler_params=options(16),
        cost_estimate=cost(500_000, 1_600_000),
        name="correct",
    )(goal, tiles, own_plain, own_unit, other_plain, other_unit, partial)


def solution(mesh):
    return jax.shard_map(
        shards,
        mesh=mesh,
        in_specs=(P(None, "gz", "gy", None), P("gy", None), P("gy", None), P(), P()),
        out_specs=P(None, "gz", "gy", None),
        check_vma=False,
    )
```

time: 42.2 us -> 26 us (0.62)
  local copies, waits for them, and re-layouts: 18.3 us -> 0 us
  waiting for transfers between devices: 1.08 us -> 4.37 us
  Pallas kernels: 10.1 us -> 9.28 us
    unnamed x46 -> x0, local copies, waits for them, and re-layouts: 18.3 us -> none
    all_to_all x1, waiting for transfers between devices: 0.01 us -> 4.36 us  [shards(): tiles = lax.all_to_all(tile_copies, ('gz', 'gy'), 0, 0, tiled=True)]
    pallas_call x3 -> x4, Pallas kernels: 3.41 us -> 5.45 us  [the longest x1 2.23 us: shards(): pl.pallas_call(early_kernel, out_shape=[shape(*velocity.shape), profile,...]
    pallas_call x1, Pallas kernels: 1.75 us -> 0.09 us  [shards(): pl.pallas_call(functools.partial(spread_kernel, chips, components), out_s...]
    ppermute x5, waiting for transfers between devices: 1.08 us -> 0.01 us  [send(): return lax.ppermute(array, ('gz', 'gy'), route)]
    pallas_call x1, Pallas kernels: 0.8 us -> 0.05 us  [shards(): pl.pallas_call(functools.partial(merge_kernel, chips, components), out_sh...]
    pallas_call x1, Pallas kernels: 4.15 us -> 3.69 us  [shards(): pl.pallas_call(functools.partial(ladder_kernel, cells, blocks, chips, lin...]
  transfers between devices with their start and end apart: 6 -> 6, of which waited for: 1 -> 1; matrix products, arithmetic and copies ran while one was open for 0% -> 0% of each run, Pallas kernels for 9% -> 17%
where the time goes in v6:
time: 26 us; the launch traced here: 25.8 us
  starting transfers between devices  11.4 us (44%)
  Pallas kernels  9.28 us (36%)
  waiting for transfers between devices  4.37 us (17%)
  between operations  0.73 us (3%)
    all_to_all x1, starting transfers between devices, shards(): tiles = lax.all_to_all(tile_copies, ('gz', 'gy'), 0, 0, tiled=True)  6.32 us
    ppermute x5, starting transfers between devices, send(): return lax.ppermute(array, ('gz', 'gy'), route)  5.07 us
    all_to_all x1, waiting for transfers between devices, shards(): tiles = lax.all_to_all(tile_copies, ('gz', 'gy'), 0, 0, tiled=True)  4.36 us
    pallas_call x1, Pallas kernels, shards(): pl.pallas_call(functools.partial(ladder_kernel, cells, blocks, chips, lin...  3.69 us
    pallas_call x1, Pallas kernels, shards(): pl.pallas_call(early_kernel, out_shape=[shape(*velocity.shape), profile,...  2.23 us
    pallas_call x1, Pallas kernels, shards(): pl.pallas_call(late_kernel, out_shape=[shape(*velocity.shape), profile, p...  1.33 us
    pallas_call x1, Pallas kernels, shards(): pl.pallas_call(correct_kernel, out_shape=shape(*velocity.shape), in_specs...  1.21 us
    pallas_call x1, Pallas kernels, shards(): pl.pallas_call(copies_kernel, out_shape=[shape(blocks * columns, SUB, LAN...  0.67 us
  transfers between devices with their start and end apart: 6, of which 1 were waited for; matrix products, arithmetic and copies ran while one was open for 0% of the time, Pallas kernels for 17%

profile of v6, /device:TPU:0, one launch (start us, length us, event | category | flops | bytes accessed | tf_op | source)
XLA Modules:
  0.0 25.8 jit_solution(14918710821577568233)
XLA Ops:
  0.0 3.7 %ladder.1 = (f32[12,8,512]{2,1,0:T(8,128)S(1)}, f32[12,8,512]{2,1,0:T(8,128)S(1)}, f32[4,32,512]{2,1,0:T(8,128)S(1)}, f32[3,32,512]{2,1,0:T(8,128)S(1)}, f32[2,3...) custom-call(s32[128]{0:T(128)} %index_hbm.1, ...), custom_call_target="tpu_custom_call" | custom-call | flops 40000000 | bytes 6000000 | tf_op jit(solution)/shard_map/ladder/pallas_call | solution.py:469
  3.7 0.5 %collective-permute-start = (f32[12,8,512]{2,1,0:T(8,128)S(1)}, f32[12,8,512]{2,1,0:T(8,128)S(1)}, u32[]{:S(2)}, u32[]{:S(2)}) collective-permute-start(f32[12,8,512]{2,1,0:T(8,128)S(1)} %get-tuple-element.41), channel_id=1, source_target_pairs={{0,4},{1,5},{2,6},{3,7},{4,0},{5,1},{6,2},{7,3},{8,12},{9,13},{10,... | collective-permute-start | bytes 589832 | tf_op jit(solution)/shard_map/ppermute | solution.py:461
  4.9 0.7 %copies.1 = (f32[32,8,128]{2,1,0:T(8,128)}, f32[8,128]{1,0:T(8,128)S(1)}) custom-call(f32[8,128]{1,0:T(8,128)S(1)} %get-tuple-element.32.tile_ref, f32[8,128]{1,0:T(8,128)S(1)} %get-tuple-element.33.volume_ref, f32[1,1]{1,0:T(1,128)} %bitcast.1.target_ref), custom_call_target="tpu_custom_call" | custom-call | flops 10000 | bytes 200000 | tf_op jit(solution)/shard_map/copies/pallas_call | solution.py:503
  5.5 0.0 collective-permute-done.mate_ref
  5.5 0.1 merge.1
  5.6 2.7 %collective-permute-start.1 = (f32[6,8,512]{2,1,0:T(8,128)S(1)}, f32[6,8,512]{2,1,0:T(8,128)S(1)}, u32[]{:S(2)}, u32[]{:S(2)}) collective-permute-start(f32[6,8,512]{2,1,0:T(8,128)S(1)} %get-tuple-element.45), channel_id=1, source_target_pairs={{0,8},{1,9},{2,10},{3,11},{4,12},{5,13},{6,14},{7,15},{8,0},{9,1},... | collective-permute-start | bytes 294920 | tf_op jit(solution)/shard_map/ppermute | solution.py:461
  8.3 1.5 %collective-permute-start.2 = (f32[6,8,512]{2,1,0:T(8,128)S(1)}, f32[6,8,512]{2,1,0:T(8,128)S(1)}, u32[]{:S(2)}, u32[]{:S(2)}) collective-permute-start(f32[6,8,512]{2,1,0:T(8,128)S(1)} %get-tuple-element.46), channel_id=1, source_target_pairs={{0,16},{1,17},{2,18},{3,19},{4,20},{5,21},{6,22},{7,23},{8,24},{9,... | collective-permute-start | bytes 294920 | tf_op jit(solution)/shard_map/ppermute | solution.py:461
  9.8 0.0 collective-permute-start.3
  9.8 6.3 %all-to-all-start = ((f32[32,8,128]{2,1,0:T(8,128)}), f32[32,8,128]{2,1,0:T(8,128)S(1)}, u32[]{:S(2)}, u32[]{:S(2)}) async-start(f32[32,8,128]{2,1,0:T(8,128)} %get-tuple-element.35), calls=%async_computation | async-start | bytes 262144 | tf_op jit(solution)/shard_map/all_to_all | solution.py:512
  16.2 0.0 collective-permute-done.1.rest_0_
  16.2 0.0 collective-permute-done.2.rest_1_
  16.2 0.0 collective-permute-done.3.rest_2_
  16.2 0.1 spread.1
  16.3 0.3 %collective-permute-start.4 = (f32[12,8,512]{2,1,0:T(8,128)S(1)}, f32[12,8,512]{2,1,0:T(8,128)S(1)}, u32[]{:S(2)}, u32[]{:S(2)}) collective-permute-start(f32[12,8,512]{2,1,0:T(8,128)S(1)} %get-tuple-element.51), channel_id=1, source_target_pairs={{0,4},{1,5},{2,6},{3,7},{4,0},{5,1},{6,2},{7,3},{8,12},{9,13},{10,... | collective-permute-start | bytes 589832 | tf_op jit(solution)/shard_map/ppermute | solution.py:461
  16.6 2.2 %early.1 = (f32[3,16,32,512]{3,2,1,0:T(8,128)}, f32[16,16,512]{2,1,0:T(8,128)S(1)}, f32[16,16,512]{2,1,0:T(8,128)S(1)}, f32[3,16,16,512]{3,2,1,0:T(8,128)S(1)}, ...) custom-call(f32[3,16,32,512]{3,2,1,0:T(8,128)} %velocity_hbm.3, ...), custom_call_target="tpu_custom_call" | custom-call | flops 8000000 | bytes 8000000 | tf_op jit(solution)/shard_map/early/pallas_call | solution.py:538
  18.8 0.0 collective-permute-done.4.other_ref
  18.9 1.3 %late.1 = (f32[3,16,32,512]{3,2,1,0:T(8,128)}, f32[16,16,512]{2,1,0:T(8,128)S(1)}, f32[16,16,512]{2,1,0:T(8,128)S(1)}) custom-call(f32[16,8,128]{2,1,0:T(8,128)S(1)} %get-tuple-element.37.heights_ref, f32[2,32,512]{2,1,0:T(8,128)S(1)} %get-tuple-element.39.ends_ref, ...), custom_call_target="tpu_custom_call", output_to_operand_aliasing={{0}: (6, {})} | custom-call | flops 3000000 | bytes 6000000 | tf_op jit(solution)/shard_map/late/pallas_call | solution.py:554
  20.2 4.4 %all-to-all-done.tiles_ref = f32[32,8,128]{2,1,0:T(8,128)S(1)} async-done(((f32[32,8,128]{2,1,0:T(8,128)}), f32[32,8,128]{2,1,0:T(8,128)S(1)}, u32[]{:S(2)}, u32[]{:S(2)}) %all-to-all-start) | async-done | bytes 131104 | tf_op jit(solution)/shard_map/all_to_all | solution.py:512
  24.6 1.2 %correct.1 = f32[3,16,32,512]{3,2,1,0:T(8,128)} custom-call(f32[8,128]{1,0:T(8,128)S(1)} %get-tuple-element.34.rest_0_.goal_ref, f32[32,8,128]{2,1,0:T(8,128)S(1)} %all-to-all-done.tiles_ref, f32[16,16,512]{2,1,0:T(8,128)S(1)} %get-tuple-element.49.own_plain_ref, f32[16,16,512]{2,1,0:T(8,128)S(1)} %get-tuple-element.50.own_unit_ref, ...), custom_call_target="tpu_custom_call", output_to_operand_aliasing={{}: (6, {})} | custom-call | flops 500000 | bytes 1600000 | tf_op jit(solution)/shard_map/correct/pallas_call | solution.py:568
Async XLA Ops:
  3.7 1.8 %collective-permute-start = (f32[12,8,512]{2,1,0:T(8,128)S(1)}, f32[12,8,512]{2,1,0:T(8,128)S(1)}, u32[]{:S(2)}, u32[]{:S(2)}) collective-permute-start(f32[12,8,512]{2,1,0:T(8,128)S(1)} %get-tuple-element.41), channel_id=1, source_target_pairs={{0,4},{1,5},{2,6},{3,7},{4,0},{5,1},{6,2},{7,3},{8,12},{9,13},{10,... | collective-permute-start | bytes 589832 | tf_op jit(solution)/shard_map/ppermute | solution.py:461
  5.6 10.6 %collective-permute-start.1 = (f32[6,8,512]{2,1,0:T(8,128)S(1)}, f32[6,8,512]{2,1,0:T(8,128)S(1)}, u32[]{:S(2)}, u32[]{:S(2)}) collective-permute-start(f32[6,8,512]{2,1,0:T(8,128)S(1)} %get-tuple-element.45), channel_id=1, source_target_pairs={{0,8},{1,9},{2,10},{3,11},{4,12},{5,13},{6,14},{7,15},{8,0},{9,1},... | collective-permute-start | bytes 294920 | tf_op jit(solution)/shard_map/ppermute | solution.py:461
  8.3 7.9 %collective-permute-start.2 = (f32[6,8,512]{2,1,0:T(8,128)S(1)}, f32[6,8,512]{2,1,0:T(8,128)S(1)}, u32[]{:S(2)}, u32[]{:S(2)}) collective-permute-start(f32[6,8,512]{2,1,0:T(8,128)S(1)} %get-tuple-element.46), channel_id=1, source_target_pairs={{0,16},{1,17},{2,18},{3,19},{4,20},{5,21},{6,22},{7,23},{8,24},{9,... | collective-permute-start | bytes 294920 | tf_op jit(solution)/shard_map/ppermute | solution.py:461
  9.8 6.4 %collective-permute-start.3 = (f32[6,8,512]{2,1,0:T(8,128)S(1)}, f32[6,8,512]{2,1,0:T(8,128)S(1)}, u32[]{:S(2)}, u32[]{:S(2)}) collective-permute-start(f32[6,8,512]{2,1,0:T(8,128)S(1)} %get-tuple-element.47), channel_id=1, source_target_pairs={{0,24},{1,25},{2,26},{3,27},{4,28},{5,29},{6,30},{7,31},{8,16},{9,... | collective-permute-start | bytes 294920 | tf_op jit(solution)/shard_map/ppermute | solution.py:461
  9.8 14.7 %all-to-all-start = ((f32[32,8,128]{2,1,0:T(8,128)}), f32[32,8,128]{2,1,0:T(8,128)S(1)}, u32[]{:S(2)}, u32[]{:S(2)}) async-start(f32[32,8,128]{2,1,0:T(8,128)} %get-tuple-element.35), calls=%async_computation | async-start | bytes 262144 | tf_op jit(solution)/shard_map/all_to_all | solution.py:512
  16.3 2.6 %collective-permute-start.4 = (f32[12,8,512]{2,1,0:T(8,128)S(1)}, f32[12,8,512]{2,1,0:T(8,128)S(1)}, u32[]{:S(2)}, u32[]{:S(2)}) collective-permute-start(f32[12,8,512]{2,1,0:T(8,128)S(1)} %get-tuple-element.51), channel_id=1, source_target_pairs={{0,4},{1,5},{2,6},{3,7},{4,0},{5,1},{6,2},{7,3},{8,12},{9,13},{10,... | collective-permute-start | bytes 589832 | tf_op jit(solution)/shard_map/ppermute | solution.py:461

commit v7 on v4

--- a/solution.py
+++ b/solution.py
@@ -29,7 +29,7 @@
     cells, blocks, chips, lines,
     index_hbm, diffusion_hbm, walls_hbm, velocity_hbm,
     mine_ref, away_ref, pair_ref, chip_ref, left_ref, right_ref, left_h_ref, right_h_ref,
-    ends_ref, tile_ref, volume_ref, velocity_ref,
+    ends_ref, volume_ref, velocity_ref,
     index_ref, diffusion_ref, walls_ref, through_ref, table_ref, held_ref, sems,
 ):
     total = cells * blocks
@@ -215,17 +215,23 @@
             flow = flow + fold(plain - low_part * from_right[0] - high_part * from_left[0])
             totals = low_part * held_ref[6, rows] + high_part * held_ref[5, rows]
             weight = weight + fold(own_extent - diffusion_ref[rows] * totals)
-    middle = SUB // 2
-    for i in range(tile_ref.shape[0]):
-        tile_ref[i, 0:middle] = flow[0:middle] + flow[middle:]
-        tile_ref[i, middle:] = weight[0:middle] + weight[middle:]
-
-
-def merge_kernel(chips, components, mine_ref, mate_ref, pair_ref, *send_refs):
+    slot = half * 2 * components
+    away_ref[slot] = jnp.zeros(away_ref.shape[1:], jnp.float32)
+    away_ref[slot, :, 0:LANES] = flow
+    away_ref[slot, :, LANES:2 * LANES] = weight
+
+
+def merge_kernel(chips, components, mine_ref, away_ref, mate_ref, pair_ref, *rest):
+    send_refs, near_ref = rest[:-1], rest[-1]
     me = lax.axis_index("gz")
     chip = me // 2
     is_first = me == chip * 2
     half = mine_ref.shape[0] // (2 * components)
+    slot = half * 2 * components
+    tile = away_ref[slot] + mate_ref[slot]
+    near_ref[slot] = tile
+    for ref in send_refs:
+        ref[half * components] = tile
     for i in range(half):
         rows = row_tile((me - chip * 2) * half + i)
         for c in range(components):
@@ -233,41 +239,44 @@
             mine, mate = mine_ref[at], mate_ref[at]
             first = jnp.where(is_first, mine, mate)
             second = jnp.where(is_first, mate, mine)
+            near_ref[at] = first
             to_right = second + pair_ref[0, rows] * first
             at = at + components
             mine, mate = mine_ref[at], mate_ref[at]
             first = jnp.where(is_first, mine, mate)
             second = jnp.where(is_first, mate, mine)
+            near_ref[at] = second
             to_left = first + pair_ref[1, rows] * second
             for m in range(1, chips):
                 goes_right = (chip ^ m) > chip
                 send_refs[m - 1][i * components + c] = jnp.where(goes_right, to_right, to_left)
 
 
-def spread_kernel(chips, components, mine_ref, mate_ref, pair_ref, chip_ref, _, *rest):
-    recv_refs, (own_ref, other_ref) = rest[:chips - 1], rest[chips - 1:]
+def spread_kernel(chips, components, near_ref, pair_ref, chip_ref, *rest):
+    recv_refs, (own_ref, other_ref, tile_ref) = rest[1:chips], rest[chips:]
     me = lax.axis_index("gz")
     chip = me // 2
     is_first = me == chip * 2
-    half = mine_ref.shape[0] // (2 * components)
+    half = near_ref.shape[0] // (2 * components)
+    tile = near_ref[half * 2 * components]
+    for ref in recv_refs:
+        tile = tile + ref[half * components]
+    tile_ref[0] = tile[:, 0:LANES]
+    tile_ref[1] = tile[:, LANES:2 * LANES]
     for i in range(half):
         rows = row_tile((me - chip * 2) * half + i)
         coefs = [chip_ref[m, rows] for m in range(chips - 1)]
         for c in range(components):
-            left_in = jnp.zeros(mine_ref.shape[1:], jnp.float32)
-            right_in = jnp.zeros(mine_ref.shape[1:], jnp.float32)
+            left_in = jnp.zeros(near_ref.shape[1:], jnp.float32)
+            right_in = jnp.zeros(near_ref.shape[1:], jnp.float32)
             for m in range(1, chips):
                 term = coefs[m - 1] * recv_refs[m - 1][i * components + c]
                 from_left = (chip ^ m) < chip
                 left_in = left_in + jnp.where(from_left, term, 0.0)
                 right_in = right_in + jnp.where(from_left, 0.0, term)
             at = i * 2 * components + c
-            first_out = jnp.where(is_first, mine_ref[at], mate_ref[at])
-            left_second = first_out + pair_ref[2, rows] * left_in
-            at = at + components
-            second_out = jnp.where(is_first, mate_ref[at], mine_ref[at])
-            right_first = second_out + pair_ref[3, rows] * right_in
-            at = i * 2 * components + c
+            left_second = near_ref[at] + pair_ref[2, rows] * left_in
+            right_first = near_ref[at + components] + pair_ref[3, rows] * right_in
             own_ref[at] = jnp.where(is_first, left_in, left_second)
             other_ref[at] = jnp.where(is_first, left_second, left_in)
             at = at + components
@@ -275,9 +284,17 @@
             other_ref[at] = jnp.where(is_first, right_in, right_first)
 
 
-def inner_kernel(velocity_ref, left_ref, right_ref, left_h_ref, right_h_ref, *rest):
-    base_ref = rest[-1]
+def leave(copies, source, target, sems):
+    copies.append(pltpu.make_async_copy(source, target, sems.at[len(copies)]))
+    copies[-1].start()
+
+
+def inner_kernel(
+    velocity_ref, left_ref, right_ref, left_h_ref, right_h_ref, ends_ref, volume_ref, target_ref,
+    _, base_ref, unit_ref, goal_ref,
+):
     components, cells, lines_y, lines_x = velocity_ref.shape
+    goal_ref[...] = target_ref[...] * volume_ref[...]
     for t in range(lines_y // SUB):
         rows = row_tile(t)
         gathered = [jnp.zeros((SUB, lines_x), jnp.float32)] * components
@@ -289,82 +306,63 @@
                 if j > 0:
                     gathered[c] = gathered[c] + right * velocity_ref[c, j, rows]
         gathered = [jnp.zeros((SUB, lines_x), jnp.float32)] * components
+        low_part = ends_ref[0, rows]
+        high_part = ends_ref[1, rows] * right_ref[cells - 1, rows]
         for j in range(cells):
             left = left_h_ref[j, rows]
             right = right_ref[j, rows]
+            unit_ref[j, rows] = 1.0 - (low_part * right + high_part * left_ref[j, rows])
             for c in range(components):
                 gathered[c] = gathered[c] + left * velocity_ref[c, j, rows]
                 base_ref[c, j, rows] = base_ref[c, j, rows] + right * gathered[c]
 
 
-def emit(parts, rows, alpha, ends_ref, incoming_ref, at, base_ref, left_ref, right_ref, result_ref):
-    cells = left_ref.shape[0]
-    components = base_ref.shape[0]
-    scale = right_ref[cells - 1, rows]
-    lefts, rights = {}, {}
-    for c in parts:
-        left_in = incoming_ref[at + c]
-        right_in = incoming_ref[at + components + c]
-        if c == 0:
-            left_in = left_in - alpha * ends_ref[0, rows]
-            right_in = right_in - alpha * ends_ref[1, rows]
-        lefts[c] = left_in
-        rights[c] = right_in * scale
-    for j in range(cells):
-        left = left_ref[j, rows]
-        right = right_ref[j, rows]
-        for c in parts:
-            value = base_ref[c, j, rows] + (right * lefts[c] + left * rights[c])
-            result_ref[c, j, rows] = value + alpha if c == 0 else value
-
-
-def early_kernel(own_ref, base_ref, left_ref, right_ref, out_hbm, result_ref, sems):
-    components = base_ref.shape[0]
-    half = own_ref.shape[0] // (2 * components)
+def finish_kernel(side, incoming_ref, base_ref, left_ref, right_ref, *rest):
+    out_hbm, plain_ref, result_ref, sems = rest[-4:]
+    components, cells, _, _ = base_ref.shape
+    half = incoming_ref.shape[0] // (2 * components)
     me = lax.axis_index("gz")
     copies = []
     for i in range(half):
-        rows = row_tile(lax.rem(me, 2) * half + i)
-        emit(range(1, components), rows, None, None, own_ref, i * 2 * components,
-             base_ref, left_ref, right_ref, result_ref)
+        rows = row_tile(lax.rem(me + side, 2) * half + i)
+        near = slice(i * SUB, (i + 1) * SUB)
+        scale = right_ref[cells - 1, rows]
+        at = i * 2 * components
+        lefts = [incoming_ref[at + c] for c in range(components)]
+        rights = [incoming_ref[at + components + c] * scale for c in range(components)]
+        for j in range(cells):
+            left = left_ref[j, rows]
+            right = right_ref[j, rows]
+            for c in range(components):
+                value = base_ref[c, j, rows] + (right * lefts[c] + left * rights[c])
+                if c == 0:
+                    plain_ref[j, near] = value
+                else:
+                    result_ref[c - 1, j, near] = value
         for c in range(1, components):
-            copies.append(pltpu.make_async_copy(
-                result_ref.at[c, :, rows], out_hbm.at[c, :, rows], sems.at[len(copies)]))
-            copies[-1].start()
+            leave(copies, result_ref.at[c - 1, :, near], out_hbm.at[c, :, rows], sems)
     for copy in copies:
         copy.wait()
 
 
-def late_kernel(
-    target_ref, volume_ref, ends_ref, own_ref, other_ref, base_ref, left_ref, right_ref, *rest
-):
-    tiles_ref, _, out_hbm, result_ref, sems = rest
-    components = base_ref.shape[0]
-    half = own_ref.shape[0] // (2 * components)
+def correct_kernel(columns, goal_ref, unit_ref, *rest):
+    tile_refs, plain_refs = rest[:columns], rest[columns:columns + 2]
+    out_hbm, result_ref, sems = rest[-3:]
+    totals = functools.reduce(jnp.add, [ref[...] for ref in tile_refs])
+    flow = jnp.sum(totals[0], keepdims=True)
+    weight = jnp.sum(totals[1], keepdims=True)
+    alpha = (goal_ref[0:1, 0:1] - flow) / weight
+    cells, middle, _ = plain_refs[0].shape
+    half = middle // SUB
     me = lax.axis_index("gz")
     copies = []
-
-    def leave(c, rows):
-        copies.append(pltpu.make_async_copy(
-            result_ref.at[c, :, rows], out_hbm.at[c, :, rows], sems.at[len(copies)]))
-        copies[-1].start()
-
-    for i in range(half):
-        rows = row_tile((1 - lax.rem(me, 2)) * half + i)
-        emit(range(1, components), rows, None, None, other_ref, i * 2 * components,
-             base_ref, left_ref, right_ref, result_ref)
-        for c in range(1, components):
-            leave(c, rows)
-    totals = functools.reduce(jnp.add, [tiles_ref[i] for i in range(tiles_ref.shape[0])])
-    flow = jnp.sum(totals[0:SUB // 2], keepdims=True)
-    weight = jnp.sum(totals[SUB // 2:], keepdims=True)
-    alpha = (target_ref[...] * volume_ref[0:1, 0:1] - flow) / weight
-    for ref, whose in ((own_ref, lax.rem(me, 2)), (other_ref, 1 - lax.rem(me, 2))):
+    for side, plain_ref in enumerate(plain_refs):
         for i in range(half):
-            rows = row_tile(whose * half + i)
-            emit((0,), rows, alpha, ends_ref, ref, i * 2 * components,
-                 base_ref, left_ref, right_ref, result_ref)
-            leave(0, rows)
+            rows = row_tile(lax.rem(me + side, 2) * half + i)
+            for j in range(cells):
+                plain = plain_ref[j, i * SUB:(i + 1) * SUB]
+                result_ref[j, rows] = plain + alpha * unit_ref[j, rows]
+            leave(copies, result_ref.at[:, rows], out_hbm.at[0, :, rows], sems)
     for copy in copies:
         copy.wait()
 
@@ -402,16 +400,14 @@
     def to_mate(array):
         return send(array, lambda z, y: (z ^ 1, y))
 
-    def to_chip(array, m):
-        return send(array, lambda z, y: (z ^ (2 * m), y))
-
+    middle = half * SUB
     lines = float(lines_y * columns * lines_x)
-    (mine, away, pair, chip_coefs, left, right, left_h, right_h, ends, tile, volume,
+    (mine, away, pair, chip_coefs, left, right, left_h, right_h, ends, volume,
      near_velocity) = pl.pallas_call(
         functools.partial(ladder_kernel, cells, blocks, chips, lines),
         out_shape=[
             shape(half * 2 * components, *sheet),
-            shape(half * 2 * components, *sheet),
+            shape(half * 2 * components + 1, *sheet),
             shape(4, *plane),
             shape(chips - 1, *plane),
             shape(cells, *plane),
@@ -419,12 +415,11 @@
             shape(cells, *plane),
             shape(cells, *plane),
             shape(2, *plane),
-            shape(blocks * columns, SUB, LANES),
             shape(SUB, LANES),
             shape(*velocity.shape),
         ],
         in_specs=[anywhere] * 4,
-        out_specs=[vmem] * 12,
+        out_specs=[vmem] * 11,
         scratch_shapes=[
             pltpu.SMEM(stretch_index.shape, jnp.int32),
             pltpu.VMEM(plane, f32),
@@ -440,63 +435,76 @@
     )(in_hbm(stretch_index), in_hbm(diffusion), in_hbm(wall_types), in_hbm(velocity))
 
     mate = to_mate(away)
-    tiles = lax.all_to_all(tile, ("gz", "gy"), 0, 0, tiled=True)
-    outgoing = pl.pallas_call(
+    *outgoing, near = pl.pallas_call(
         functools.partial(merge_kernel, chips, components),
-        out_shape=[shape(half * components, *sheet)] * (chips - 1),
-        in_specs=[vmem] * 3,
-        out_specs=[vmem] * (chips - 1),
+        out_shape=[shape(half * components + 1, *sheet)] * (chips - 1)
+        + [shape(half * 2 * components + 1, *sheet)],
+        in_specs=[vmem] * 4,
+        out_specs=[vmem] * chips,
         compiler_params=options(16),
         cost_estimate=cost(500_000, 1_600_000),
         name="merge",
-    )(mine, mate, pair)
-    incoming = [to_chip(outgoing[m - 1], m) for m in range(1, chips)]
-    base = pl.pallas_call(
+    )(mine, away, mate, pair)
+    incoming = [
+        send(outgoing[m - 1], lambda z, y: (z ^ (2 * m), y)) for m in range(1, chips)
+    ]
+    profile = shape(cells, *plane)
+    base, unit, goal = pl.pallas_call(
         inner_kernel,
-        out_shape=shape(*velocity.shape),
-        in_specs=[vmem] * 5 + [anywhere],
-        out_specs=vmem,
+        out_shape=[shape(*velocity.shape), profile, shape(SUB, LANES)],
+        in_specs=[vmem] * 8 + [anywhere],
+        out_specs=[vmem] * 3,
         compiler_params=options(16),
         cost_estimate=cost(8_000_000, 8_000_000),
         name="inner",
-    )(near_velocity, left, right, left_h, right_h, outgoing[0])
-    own_in, other_out = pl.pallas_call(
+    )(near_velocity, left, right, left_h, right_h, ends, volume, bulk_target.reshape(1, 1),
+      outgoing[0])
+    own_in, other_out, tile = pl.pallas_call(
         functools.partial(spread_kernel, chips, components),
-        out_shape=[shape(half * 2 * components, *sheet)] * 2,
-        in_specs=[vmem] * 4 + [anywhere] + [vmem] * (chips - 1),
-        out_specs=[vmem] * 2,
+        out_shape=[shape(half * 2 * components, *sheet)] * 2 + [shape(2, SUB, LANES)],
+        in_specs=[vmem] * 3 + [anywhere] + [vmem] * (chips - 1),
+        out_specs=[vmem] * 3,
         compiler_params=options(16),
         cost_estimate=cost(500_000, 1_600_000),
         name="spread",
-    )(mine, mate, pair, chip_coefs, base, *incoming)
+    )(near, pair, chip_coefs, base, *incoming)
     other_in = to_mate(other_out)
-    early = pl.pallas_call(
-        early_kernel,
+    tiles = [tile] + [
+        send(tile, lambda z, y: (z, (y + shift) % columns)) for shift in range(1, columns)
+    ]
+
+    def finish(side, arrived, *before):
+        return pl.pallas_call(
+            functools.partial(finish_kernel, side),
+            out_shape=[shape(*velocity.shape), shape(cells, middle, lines_x)],
+            in_specs=[vmem] * 4 + [anywhere] * len(before),
+            out_specs=[anywhere, vmem],
+            scratch_shapes=[
+                pltpu.VMEM((components - 1, cells, middle, lines_x), f32),
+                pltpu.SemaphoreType.DMA(((components - 1) * half,)),
+            ],
+            input_output_aliases={4: 0} if before else {},
+            compiler_params=options(16),
+            cost_estimate=cost(3_000_000, 6_000_000),
+            name="finish" + str(side),
+        )(arrived, base, left, right, *before)
+
+    partial, own_plain = finish(0, own_in)
+    partial, other_plain = finish(1, other_in, partial)
+    return pl.pallas_call(
+        functools.partial(correct_kernel, columns),
         out_shape=shape(*velocity.shape),
-        in_specs=[vmem] * 4,
+        in_specs=[vmem] * (4 + columns) + [anywhere],
         out_specs=anywhere,
         scratch_shapes=[
-            pltpu.VMEM(velocity.shape, f32),
-            pltpu.SemaphoreType.DMA(((components - 1) * half,)),
+            pltpu.VMEM((cells,) + plane, f32),
+            pltpu.SemaphoreType.DMA((row_tiles,)),
         ],
+        input_output_aliases={4 + columns: 0},
         compiler_params=options(16),
-        cost_estimate=cost(2_000_000, 4_000_000),
-        name="early",
-    )(own_in, base, left, right)
-    return pl.pallas_call(
-        late_kernel,
-        out_shape=shape(*velocity.shape),
-        in_specs=[vmem] * 9 + [anywhere],
-        out_specs=anywhere,
-        scratch_shapes=[
-            pltpu.VMEM(velocity.shape, f32),
-            pltpu.SemaphoreType.DMA(((components + 1) * half,)),
-        ],
-        input_output_aliases={9: 0},
-        compiler_params=options(16),
-        cost_estimate=cost(3_000_000, 6_000_000),
-        name="late",
-    )(bulk_target.reshape(1, 1), volume, ends, own_in, other_in, base, left, right, tiles, early)
+        cost_estimate=cost(500_000, 1_600_000),
+        name="correct",
+    )(goal, unit, *tiles, own_plain, other_plain, partial)
 
 
 def solution(mesh):

time: 42.2 us -> 25.2 us (0.60)
  local copies, waits for them, and re-layouts: 18.3 us -> 0 us
  waiting for transfers between devices: 1.08 us -> 5.37 us
  Pallas kernels: 10.1 us -> 8.38 us
  starting transfers between devices: 11.4 us -> 10.6 us
    unnamed x46 -> x0, local copies, waits for them, and re-layouts: 18.3 us -> none
    all_to_all x1 -> x0, starting transfers between devices: 6.31 us -> none  [shards(): tiles = lax.all_to_all(tile, ('gz', 'gy'), 0, 0, tiled=True)]
    ppermute x5 -> x8, starting transfers between devices: 5.11 us -> 10.6 us  [send(): return lax.ppermute(array, ('gz', 'gy'), route)]
    ppermute x5 -> x8, waiting for transfers between devices: 1.08 us -> 5.37 us  [send(): return lax.ppermute(array, ('gz', 'gy'), route)]
    pallas_call x1, Pallas kernels: 1.75 us -> 0.09 us  [shards(): pl.pallas_call(functools.partial(spread_kernel, chips, components), out_s...]
    pallas_call x3 -> x4, Pallas kernels: 3.41 us -> 4.34 us  [the longest x2 2.17 us: finish(): pl.pallas_call(functools.partial(finish_kernel, side), out_shape=[shape(*...]
    pallas_call x1, Pallas kernels: 0.8 us -> 0.05 us  [shards(): pl.pallas_call(functools.partial(merge_kernel, chips, components), out_sh...]
  transfers between devices with their start and end apart: 6 -> 8, of which waited for: 1 -> 4; matrix products, arithmetic and copies ran while one was open for 0% -> 0% of each run, Pallas kernels for 9% -> 13%
where the time goes in v7:
time: 25.2 us; the launch traced here: 25.1 us
  starting transfers between devices  10.6 us (42%)
  Pallas kernels  8.38 us (33%)
  waiting for transfers between devices  5.37 us (21%)
  between operations  0.73 us (3%)
    ppermute x8, starting transfers between devices, send(): return lax.ppermute(array, ('gz', 'gy'), route)  10.6 us
    ppermute x8, waiting for transfers between devices, send(): return lax.ppermute(array, ('gz', 'gy'), route)  5.37 us
    pallas_call x1, Pallas kernels, shards(): pl.pallas_call(functools.partial(ladder_kernel, cells, blocks, chips, lin...  3.89 us
    pallas_call x2, Pallas kernels, finish(): pl.pallas_call(functools.partial(finish_kernel, side), out_shape=[shape(*...  2.17 us
    pallas_call x1, Pallas kernels, shards(): pl.pallas_call(functools.partial(correct_kernel, columns), out_shape=shap...  1.19 us
    pallas_call x1, Pallas kernels, shards(): pl.pallas_call(inner_kernel, out_shape=[shape(*velocity.shape), profile,...  0.98 us
  transfers between devices with their start and end apart: 8, of which 4 were waited for; matrix products, arithmetic and copies ran while one was open for 0% of the time, Pallas kernels for 13%

profile of v7, /device:TPU:0, one launch (start us, length us, event | category | flops | bytes accessed | tf_op | source)
XLA Modules:
  0.0 25.1 jit_solution(14223236176714184505)
XLA Ops:
  0.0 3.9 %ladder.1 = (f32[12,8,512]{2,1,0:T(8,128)S(1)}, f32[13,8,512]{2,1,0:T(8,128)S(1)}, f32[4,32,512]{2,1,0:T(8,128)S(1)}, f32[3,32,512]{2,1,0:T(8,128)S(1)}, f32[16,...) custom-call(s32[128]{0:T(128)} %index_hbm.1, ...), custom_call_target="tpu_custom_call" | custom-call | flops 40000000 | bytes 6000000 | tf_op jit(solution)/shard_map/ladder/pallas_call | solution.py:406
  3.9 0.5 %collective-permute-start = (f32[13,8,512]{2,1,0:T(8,128)S(1)}, f32[13,8,512]{2,1,0:T(8,128)S(1)}, u32[]{:S(2)}, u32[]{:S(2)}) collective-permute-start(f32[13,8,512]{2,1,0:T(8,128)S(1)} %get-tuple-element.38.away_ref), channel_id=1, source_target_pairs={{0,4},{1,5},{2,6},{3,7},{4,0},{5,1},{6,2},{7,3},{8,12},{9,13},{10,... | collective-permute-start | bytes 638984 | tf_op jit(solution)/shard_map/ppermute | solution.py:398
  4.4 1.1 %collective-permute-done.mate_ref = f32[13,8,512]{2,1,0:T(8,128)S(1)} collective-permute-done((f32[13,8,512]{2,1,0:T(8,128)S(1)}, f32[13,8,512]{2,1,0:T(8,128)S(1)}, u32[]{:S(2)}, u32[]{:S(2)}) %collective-permute-start) | collective-permute-done | bytes 213024 | tf_op jit(solution)/shard_map/ppermute | solution.py:398
  5.5 0.1 merge.1
  5.6 2.9 %collective-permute-start.1 = (f32[7,8,512]{2,1,0:T(8,128)S(1)}, f32[7,8,512]{2,1,0:T(8,128)S(1)}, u32[]{:S(2)}, u32[]{:S(2)}) collective-permute-start(f32[7,8,512]{2,1,0:T(8,128)S(1)} %get-tuple-element.40._), channel_id=1, source_target_pairs={{0,8},{1,9},{2,10},{3,11},{4,12},{5,13},{6,14},{7,15},{8,0},{9,1},... | collective-permute-start | bytes 344072 | tf_op jit(solution)/shard_map/ppermute | solution.py:398
  8.5 1.5 %collective-permute-start.2 = (f32[7,8,512]{2,1,0:T(8,128)S(1)}, f32[7,8,512]{2,1,0:T(8,128)S(1)}, u32[]{:S(2)}, u32[]{:S(2)}) collective-permute-start(f32[7,8,512]{2,1,0:T(8,128)S(1)} %get-tuple-element.46), channel_id=1, source_target_pairs={{0,16},{1,17},{2,18},{3,19},{4,20},{5,21},{6,22},{7,23},{8,24},{9,... | collective-permute-start | bytes 344072 | tf_op jit(solution)/shard_map/ppermute | solution.py:398
  10.0 0.0 collective-permute-start.3
  10.7 1.0 %inner.1 = (f32[3,16,32,512]{3,2,1,0:T(8,128)S(1)}, f32[16,32,512]{2,1,0:T(8,128)S(1)}, f32[8,128]{1,0:T(8,128)S(1)}) custom-call(f32[3,16,32,512]{3,2,1,0:T(8,128)S(1)} %get-tuple-element.30.velocity_ref, f32[16,32,512]{2,1,0:T(8,128)S(1)} %get-tuple-element.31.left_ref, f32[16,32,512]{2,1,0:T(8,128)S(1)} %get-tuple-element.32.right_ref, ...), custom_call_target="tpu_custom_call" | custom-call | flops 8000000 | bytes 8000000 | tf_op jit(solution)/shard_map/inner/pallas_call | solution.py:452
  11.7 0.3 %collective-permute-done.1.rest_1_ = f32[7,8,512]{2,1,0:T(8,128)S(1)} collective-permute-done((f32[7,8,512]{2,1,0:T(8,128)S(1)}, f32[7,8,512]{2,1,0:T(8,128)S(1)}, u32[]{:S(2)}, u32[]{:S(2)}) %collective-permute-start.1) | collective-permute-done | bytes 114720 | tf_op jit(solution)/shard_map/ppermute | solution.py:398
  12.0 3.9 %collective-permute-done.2.rest_2_ = f32[7,8,512]{2,1,0:T(8,128)S(1)} collective-permute-done((f32[7,8,512]{2,1,0:T(8,128)S(1)}, f32[7,8,512]{2,1,0:T(8,128)S(1)}, u32[]{:S(2)}, u32[]{:S(2)}) %collective-permute-start.2) | collective-permute-done | bytes 114720 | tf_op jit(solution)/shard_map/ppermute | solution.py:398
  15.8 0.0 collective-permute-done.3.rest_3_
  15.8 0.1 spread.1
  15.9 0.1 collective-permute-start.7
  16.0 1.6 %collective-permute-start.4 = (f32[2,8,128]{2,1,0:T(8,128)S(1)}, f32[2,8,128]{2,1,0:T(8,128)S(1)}, u32[]{:S(2)}, u32[]{:S(2)}) collective-permute-start(f32[2,8,128]{2,1,0:T(8,128)S(1)} %get-tuple-element.48.rest_0_), channel_id=1, source_target_pairs={{0,1},{1,2},{2,3},{3,0},{4,5},{5,6},{6,7},{7,4},{8,9},{9,10},{10,1... | collective-permute-start | bytes 24584 | tf_op jit(solution)/shard_map/ppermute | solution.py:398
  17.7 2.6 %collective-permute-start.5 = (f32[2,8,128]{2,1,0:T(8,128)S(1)}, f32[2,8,128]{2,1,0:T(8,128)S(1)}, u32[]{:S(2)}, u32[]{:S(2)}) collective-permute-start(f32[2,8,128]{2,1,0:T(8,128)S(1)} %get-tuple-element.48.rest_0_), channel_id=1, source_target_pairs={{0,2},{1,3},{2,0},{3,1},{4,6},{5,7},{6,4},{7,5},{8,10},{9,11},{10,... | collective-permute-start | bytes 24584 | tf_op jit(solution)/shard_map/ppermute | solution.py:398
  20.2 1.3 %collective-permute-start.6 = (f32[2,8,128]{2,1,0:T(8,128)S(1)}, f32[2,8,128]{2,1,0:T(8,128)S(1)}, u32[]{:S(2)}, u32[]{:S(2)}) collective-permute-start(f32[2,8,128]{2,1,0:T(8,128)S(1)} %get-tuple-element.48.rest_0_), channel_id=1, source_target_pairs={{0,3},{1,0},{2,1},{3,2},{4,7},{5,4},{6,5},{7,6},{8,11},{9,8},{10,9... | collective-permute-start | bytes 24584 | tf_op jit(solution)/shard_map/ppermute | solution.py:398
  21.6 1.1 %finish0.1 = (f32[3,16,32,512]{3,2,1,0:T(8,128)}, f32[16,16,512]{2,1,0:T(8,128)S(1)}) custom-call(f32[12,8,512]{2,1,0:T(8,128)S(1)} %get-tuple-element.49.incoming_ref, f32[3,16,32,512]{3,2,1,0:T(8,128)S(1)} %get-tuple-element.45.rest_0_.base_ref, f32[16,32,512]{2,1,0:T(8,128)S(1)} %get-tuple-element.31.left_ref, f32[16,32,512]{2,1,0:T(8,128)S(1)} %get-tuple-element.32.right_ref), custom_call_target="tpu_custom_call" | custom-call | flops 3000000 | bytes 6000000 | tf_op jit(solution)/shard_map/finish0/pallas_call | solution.py:477
  22.7 0.0 collective-permute-done.7.incoming_ref
  22.7 1.1 %finish1.1 = (f32[3,16,32,512]{3,2,1,0:T(8,128)}, f32[16,16,512]{2,1,0:T(8,128)S(1)}) custom-call(f32[12,8,512]{2,1,0:T(8,128)S(1)} %collective-permute-done.7.incoming_ref, f32[3,16,32,512]{3,2,1,0:T(8,128)S(1)} %get-tuple-element.45.rest_0_.base_ref, f32[16,32,512]{2,1,0:T(8,128)S(1)} %get-tuple-element.31.left_ref, ...), custom_call_target="tpu_custom_call", output_to_operand_aliasing={{0}: (4, {})} | custom-call | flops 3000000 | bytes 6000000 | tf_op jit(solution)/shard_map/finish1/pallas_call | solution.py:477
  23.8 0.0 collective-permute-done.4.rest_1_
  23.8 0.0 collective-permute-done.5.rest_2_
  23.8 0.1 collective-permute-done.6.rest_3_
  23.9 1.2 %correct.1 = f32[3,16,32,512]{3,2,1,0:T(8,128)} custom-call(f32[8,128]{1,0:T(8,128)S(1)} %get-tuple-element.41.goal_ref, f32[16,32,512]{2,1,0:T(8,128)S(1)} %get-tuple-element.42.unit_ref, f32[2,8,128]{2,1,0:T(8,128)S(1)} %get-tuple-element.48.rest_0_, f32[2,8,128]{2,1,0:T(8,128)S(1)} %collective-permute-done.4.rest_1_, ...), custom_call_target="tpu_custom_call", output_to_operand_aliasing={{}: (8, {})} | custom-call | flops 500000 | bytes 1600000 | tf_op jit(solution)/shard_map/correct/pallas_call | solution.py:494
Async XLA Ops:
  3.9 1.6 %collective-permute-start = (f32[13,8,512]{2,1,0:T(8,128)S(1)}, f32[13,8,512]{2,1,0:T(8,128)S(1)}, u32[]{:S(2)}, u32[]{:S(2)}) collective-permute-start(f32[13,8,512]{2,1,0:T(8,128)S(1)} %get-tuple-element.38.away_ref), channel_id=1, source_target_pairs={{0,4},{1,5},{2,6},{3,7},{4,0},{5,1},{6,2},{7,3},{8,12},{9,13},{10,... | collective-permute-start | bytes 638984 | tf_op jit(solution)/shard_map/ppermute | solution.py:398
  5.6 6.4 %collective-permute-start.1 = (f32[7,8,512]{2,1,0:T(8,128)S(1)}, f32[7,8,512]{2,1,0:T(8,128)S(1)}, u32[]{:S(2)}, u32[]{:S(2)}) collective-permute-start(f32[7,8,512]{2,1,0:T(8,128)S(1)} %get-tuple-element.40._), channel_id=1, source_target_pairs={{0,8},{1,9},{2,10},{3,11},{4,12},{5,13},{6,14},{7,15},{8,0},{9,1},... | collective-permute-start | bytes 344072 | tf_op jit(solution)/shard_map/ppermute | solution.py:398
  8.5 7.4 %collective-permute-start.2 = (f32[7,8,512]{2,1,0:T(8,128)S(1)}, f32[7,8,512]{2,1,0:T(8,128)S(1)}, u32[]{:S(2)}, u32[]{:S(2)}) collective-permute-start(f32[7,8,512]{2,1,0:T(8,128)S(1)} %get-tuple-element.46), channel_id=1, source_target_pairs={{0,16},{1,17},{2,18},{3,19},{4,20},{5,21},{6,22},{7,23},{8,24},{9,... | collective-permute-start | bytes 344072 | tf_op jit(solution)/shard_map/ppermute | solution.py:398
  10.0 5.8 %collective-permute-start.3 = (f32[7,8,512]{2,1,0:T(8,128)S(1)}, f32[7,8,512]{2,1,0:T(8,128)S(1)}, u32[]{:S(2)}, u32[]{:S(2)}) collective-permute-start(f32[7,8,512]{2,1,0:T(8,128)S(1)} %get-tuple-element.47), channel_id=1, source_target_pairs={{0,24},{1,25},{2,26},{3,27},{4,28},{5,29},{6,30},{7,31},{8,16},{9,... | collective-permute-start | bytes 344072 | tf_op jit(solution)/shard_map/ppermute | solution.py:398
  15.9 6.7 %collective-permute-start.7 = (f32[12,8,512]{2,1,0:T(8,128)S(1)}, f32[12,8,512]{2,1,0:T(8,128)S(1)}, u32[]{:S(2)}, u32[]{:S(2)}) collective-permute-start(f32[12,8,512]{2,1,0:T(8,128)S(1)} %get-tuple-element.51), channel_id=1, source_target_pairs={{0,4},{1,5},{2,6},{3,7},{4,0},{5,1},{6,2},{7,3},{8,12},{9,13},{10,... | collective-permute-start | bytes 589832 | tf_op jit(solution)/shard_map/ppermute | solution.py:398
  16.0 7.8 %collective-permute-start.4 = (f32[2,8,128]{2,1,0:T(8,128)S(1)}, f32[2,8,128]{2,1,0:T(8,128)S(1)}, u32[]{:S(2)}, u32[]{:S(2)}) collective-permute-start(f32[2,8,128]{2,1,0:T(8,128)S(1)} %get-tuple-element.48.rest_0_), channel_id=1, source_target_pairs={{0,1},{1,2},{2,3},{3,0},{4,5},{5,6},{6,7},{7,4},{8,9},{9,10},{10,1... | collective-permute-start | bytes 24584 | tf_op jit(solution)/shard_map/ppermute | solution.py:398
  17.7 6.1 %collective-permute-start.5 = (f32[2,8,128]{2,1,0:T(8,128)S(1)}, f32[2,8,128]{2,1,0:T(8,128)S(1)}, u32[]{:S(2)}, u32[]{:S(2)}) collective-permute-start(f32[2,8,128]{2,1,0:T(8,128)S(1)} %get-tuple-element.48.rest_0_), channel_id=1, source_target_pairs={{0,2},{1,3},{2,0},{3,1},{4,6},{5,7},{6,4},{7,5},{8,10},{9,11},{10,... | collective-permute-start | bytes 24584 | tf_op jit(solution)/shard_map/ppermute | solution.py:398
  20.2 3.7 %collective-permute-start.6 = (f32[2,8,128]{2,1,0:T(8,128)S(1)}, f32[2,8,128]{2,1,0:T(8,128)S(1)}, u32[]{:S(2)}, u32[]{:S(2)}) collective-permute-start(f32[2,8,128]{2,1,0:T(8,128)S(1)} %get-tuple-element.48.rest_0_), channel_id=1, source_target_pairs={{0,3},{1,0},{2,1},{3,2},{4,7},{5,4},{6,5},{7,6},{8,11},{9,8},{10,9... | collective-permute-start | bytes 24584 | tf_op jit(solution)/shard_map/ppermute | solution.py:398

commit v8 on v7

--- a/solution.py
+++ b/solution.py
@@ -15,6 +15,16 @@
 
 def row_tile(t):
     return pl.ds(pl.multiple_of(t * SUB, SUB), SUB)
+
+
+def put(ref, at, sheet):
+    count = sheet.shape[1] // LANES
+    for i in range(count):
+        ref[at * count + i] = sheet[:, i * LANES:(i + 1) * LANES]
+
+
+def get(ref, at, count):
+    return jnp.concatenate([ref[at * count + i] for i in range(count)], axis=1)
 
 
 def height(index_ref, k):
@@ -208,17 +218,17 @@
                     if c == 0:
                         plain = plain + heights[j] * v
             for c in range(components):
-                ref[i * 2 * components + c] = from_left[c] * held_ref[1, rows]
-                ref[i * 2 * components + components + c] = from_right[c] * held_ref[2, rows]
+                at = i * 2 * components + c
+                put(ref, at, from_left[c] * held_ref[1, rows])
+                put(ref, at + components, from_right[c] * held_ref[2, rows])
             low_part = ends_ref[0, rows]
             high_part = ends_ref[1, rows] * held_ref[0, rows]
             flow = flow + fold(plain - low_part * from_right[0] - high_part * from_left[0])
             totals = low_part * held_ref[6, rows] + high_part * held_ref[5, rows]
             weight = weight + fold(own_extent - diffusion_ref[rows] * totals)
-    slot = half * 2 * components
-    away_ref[slot] = jnp.zeros(away_ref.shape[1:], jnp.float32)
-    away_ref[slot, :, 0:LANES] = flow
-    away_ref[slot, :, LANES:2 * LANES] = weight
+    slot, middle = away_ref.shape[0] - 1, SUB // 2
+    away_ref[slot, 0:middle] = flow[0:middle] + flow[middle:]
+    away_ref[slot, middle:] = weight[0:middle] + weight[middle:]
 
 
 def merge_kernel(chips, components, mine_ref, away_ref, mate_ref, pair_ref, *rest):
@@ -226,57 +236,57 @@
     me = lax.axis_index("gz")
     chip = me // 2
     is_first = me == chip * 2
-    half = mine_ref.shape[0] // (2 * components)
-    slot = half * 2 * components
+    count = pair_ref.shape[2] // LANES
+    half = mine_ref.shape[0] // (2 * components * count)
+    slot = away_ref.shape[0] - 1
     tile = away_ref[slot] + mate_ref[slot]
     near_ref[slot] = tile
     for ref in send_refs:
-        ref[half * components] = tile
+        ref[ref.shape[0] - 1] = tile
     for i in range(half):
         rows = row_tile((me - chip * 2) * half + i)
         for c in range(components):
             at = i * 2 * components + c
-            mine, mate = mine_ref[at], mate_ref[at]
+            mine, mate = get(mine_ref, at, count), get(mate_ref, at, count)
             first = jnp.where(is_first, mine, mate)
             second = jnp.where(is_first, mate, mine)
-            near_ref[at] = first
+            put(near_ref, at, first)
             to_right = second + pair_ref[0, rows] * first
             at = at + components
-            mine, mate = mine_ref[at], mate_ref[at]
+            mine, mate = get(mine_ref, at, count), get(mate_ref, at, count)
             first = jnp.where(is_first, mine, mate)
             second = jnp.where(is_first, mate, mine)
-            near_ref[at] = second
+            put(near_ref, at, second)
             to_left = first + pair_ref[1, rows] * second
             for m in range(1, chips):
                 goes_right = (chip ^ m) > chip
-                send_refs[m - 1][i * components + c] = jnp.where(goes_right, to_right, to_left)
-
-
-def spread_kernel(chips, components, near_ref, pair_ref, chip_ref, *rest):
-    recv_refs, (own_ref, other_ref, tile_ref) = rest[1:chips], rest[chips:]
+                sheet = jnp.where(goes_right, to_right, to_left)
+                put(send_refs[m - 1], i * components + c, sheet)
+
+
+def spread_kernel(order, components, near_ref, pair_ref, chip_ref, *rest):
+    recv_refs, (own_ref, other_ref, tile_ref) = rest[1:-3], rest[-3:]
     me = lax.axis_index("gz")
     chip = me // 2
     is_first = me == chip * 2
-    half = near_ref.shape[0] // (2 * components)
-    tile = near_ref[half * 2 * components]
-    for ref in recv_refs:
-        tile = tile + ref[half * components]
-    tile_ref[0] = tile[:, 0:LANES]
-    tile_ref[1] = tile[:, LANES:2 * LANES]
+    count = pair_ref.shape[2] // LANES
+    half = near_ref.shape[0] // (2 * components * count)
+    tiles = [ref[ref.shape[0] - 1] for ref in (near_ref, *recv_refs)]
+    tile_ref[...] = functools.reduce(jnp.add, tiles)
     for i in range(half):
         rows = row_tile((me - chip * 2) * half + i)
-        coefs = [chip_ref[m, rows] for m in range(chips - 1)]
+        coefs = [chip_ref[m - 1, rows] for m in order]
         for c in range(components):
-            left_in = jnp.zeros(near_ref.shape[1:], jnp.float32)
-            right_in = jnp.zeros(near_ref.shape[1:], jnp.float32)
-            for m in range(1, chips):
-                term = coefs[m - 1] * recv_refs[m - 1][i * components + c]
+            left_in = jnp.zeros(own_ref.shape[1:], jnp.float32)
+            right_in = jnp.zeros(own_ref.shape[1:], jnp.float32)
+            for m, coef, ref in zip(order, coefs, recv_refs):
+                term = coef * get(ref, i * components + c, count)
                 from_left = (chip ^ m) < chip
                 left_in = left_in + jnp.where(from_left, term, 0.0)
                 right_in = right_in + jnp.where(from_left, 0.0, term)
             at = i * 2 * components + c
-            left_second = near_ref[at] + pair_ref[2, rows] * left_in
-            right_first = near_ref[at + components] + pair_ref[3, rows] * right_in
+            left_second = get(near_ref, at, count) + pair_ref[2, rows] * left_in
+            right_first = get(near_ref, at + components, count) + pair_ref[3, rows] * right_in
             own_ref[at] = jnp.where(is_first, left_in, left_second)
             other_ref[at] = jnp.where(is_first, left_second, left_in)
             at = at + components
@@ -349,8 +359,8 @@
     tile_refs, plain_refs = rest[:columns], rest[columns:columns + 2]
     out_hbm, result_ref, sems = rest[-3:]
     totals = functools.reduce(jnp.add, [ref[...] for ref in tile_refs])
-    flow = jnp.sum(totals[0], keepdims=True)
-    weight = jnp.sum(totals[1], keepdims=True)
+    flow = jnp.sum(totals[0:SUB // 2], keepdims=True)
+    weight = jnp.sum(totals[SUB // 2:], keepdims=True)
     alpha = (goal_ref[0:1, 0:1] - flow) / weight
     cells, middle, _ = plain_refs[0].shape
     half = middle // SUB
@@ -401,13 +411,14 @@
         return send(array, lambda z, y: (z ^ 1, y))
 
     middle = half * SUB
+    count = lines_x // LANES
     lines = float(lines_y * columns * lines_x)
     (mine, away, pair, chip_coefs, left, right, left_h, right_h, ends, volume,
      near_velocity) = pl.pallas_call(
         functools.partial(ladder_kernel, cells, blocks, chips, lines),
         out_shape=[
-            shape(half * 2 * components, *sheet),
-            shape(half * 2 * components + 1, *sheet),
+            shape(half * 2 * components * count, SUB, LANES),
+            shape(half * 2 * components * count + 1, SUB, LANES),
             shape(4, *plane),
             shape(chips - 1, *plane),
             shape(cells, *plane),
@@ -437,17 +448,16 @@
     mate = to_mate(away)
     *outgoing, near = pl.pallas_call(
         functools.partial(merge_kernel, chips, components),
-        out_shape=[shape(half * components + 1, *sheet)] * (chips - 1)
-        + [shape(half * 2 * components + 1, *sheet)],
+        out_shape=[shape(half * components * count + 1, SUB, LANES)] * (chips - 1)
+        + [shape(half * 2 * components * count + 1, SUB, LANES)],
         in_specs=[vmem] * 4,
         out_specs=[vmem] * chips,
         compiler_params=options(16),
         cost_estimate=cost(500_000, 1_600_000),
         name="merge",
     )(mine, away, mate, pair)
-    incoming = [
-        send(outgoing[m - 1], lambda z, y: (z ^ (2 * m), y)) for m in range(1, chips)
-    ]
+    order = sorted(range(1, chips), key=lambda m: -m.bit_count())
+    incoming = [send(outgoing[m - 1], lambda z, y: (z ^ (2 * m), y)) for m in order]
     profile = shape(cells, *plane)
     base, unit, goal = pl.pallas_call(
         inner_kernel,
@@ -460,8 +470,8 @@
     )(near_velocity, left, right, left_h, right_h, ends, volume, bulk_target.reshape(1, 1),
       outgoing[0])
     own_in, other_out, tile = pl.pallas_call(
-        functools.partial(spread_kernel, chips, components),
-        out_shape=[shape(half * 2 * components, *sheet)] * 2 + [shape(2, SUB, LANES)],
+        functools.partial(spread_kernel, order, components),
+        out_shape=[shape(half * 2 * components, *sheet)] * 2 + [shape(SUB, LANES)],
         in_specs=[vmem] * 3 + [anywhere] + [vmem] * (chips - 1),
         out_specs=[vmem] * 3,
         compiler_params=options(16),
@@ -470,7 +480,7 @@
     )(near, pair, chip_coefs, base, *incoming)
     other_in = to_mate(other_out)
     tiles = [tile] + [
-        send(tile, lambda z, y: (z, (y + shift) % columns)) for shift in range(1, columns)
+        send(tile, lambda z, y: (z, y ^ other)) for other in reversed(range(1, columns))
     ]
 
     def finish(side, arrived, *before):

time: 25.2 us -> 26.2 us (1.040)
  waiting for transfers between devices: 5.37 us -> 7.43 us
  starting transfers between devices: 10.6 us -> 9.5 us
    ppermute x8, waiting for transfers between devices: 5.37 us -> 7.43 us  [send(): return lax.ppermute(array, ('gz', 'gy'), route)]
    ppermute x8, starting transfers between devices: 10.6 us -> 9.5 us  [send(): return lax.ppermute(array, ('gz', 'gy'), route)]
  transfers between devices with their start and end apart: 8 -> 8, of which waited for: 4 -> 5; matrix products, arithmetic and copies ran while one was open for 0% -> 0% of each run, Pallas kernels for 13% -> 12%
where the time goes in v8:
time: 26.2 us; the launch traced here: 26.1 us
  starting transfers between devices  9.5 us (36%)
  Pallas kernels  8.41 us (32%)
  waiting for transfers between devices  7.43 us (28%)
  between operations  0.72 us (3%)
    ppermute x8, starting transfers between devices, send(): return lax.ppermute(array, ('gz', 'gy'), route)  9.5 us
    ppermute x8, waiting for transfers between devices, send(): return lax.ppermute(array, ('gz', 'gy'), route)  7.43 us
    pallas_call x1, Pallas kernels, shards(): pl.pallas_call(functools.partial(ladder_kernel, cells, blocks, chips, lin...  3.94 us
    pallas_call x2, Pallas kernels, finish(): pl.pallas_call(functools.partial(finish_kernel, side), out_shape=[shape(*...  2.17 us
    pallas_call x1, Pallas kernels, shards(): pl.pallas_call(functools.partial(correct_kernel, columns), out_shape=shap...  1.18 us
    pallas_call x1, Pallas kernels, shards(): pl.pallas_call(inner_kernel, out_shape=[shape(*velocity.shape), profile,...  0.98 us
  transfers between devices with their start and end apart: 8, of which 5 were waited for; matrix products, arithmetic and copies ran while one was open for 0% of the time, Pallas kernels for 12%

profile of v8, /device:TPU:0, one launch (start us, length us, event | category | flops | bytes accessed | tf_op | source)
XLA Modules:
  0.0 26.1 jit_solution(3405407120004546805)
XLA Ops:
  0.0 3.9 %ladder.1 = (f32[48,8,128]{2,1,0:T(8,128)S(1)}, f32[49,8,128]{2,1,0:T(8,128)S(1)}, f32[4,32,512]{2,1,0:T(8,128)S(1)}, f32[3,32,512]{2,1,0:T(8,128)S(1)}, f32[16,...) custom-call(s32[128]{0:T(128)} %index_hbm.1, ...), custom_call_target="tpu_custom_call" | custom-call | flops 40000000 | bytes 6000000 | tf_op jit(solution)/shard_map/ladder/pallas_call | solution.py:417
  4.0 0.5 %collective-permute-start = (f32[49,8,128]{2,1,0:T(8,128)S(1)}, f32[49,8,128]{2,1,0:T(8,128)S(1)}, u32[]{:S(2)}, u32[]{:S(2)}) collective-permute-start(f32[49,8,128]{2,1,0:T(8,128)S(1)} %get-tuple-element.38.away_ref), channel_id=1, source_target_pairs={{0,4},{1,5},{2,6},{3,7},{4,0},{5,1},{6,2},{7,3},{8,12},{9,13},{10,... | collective-permute-start | bytes 602120 | tf_op jit(solution)/shard_map/ppermute | solution.py:408
  4.5 1.1 %collective-permute-done.mate_ref = f32[49,8,128]{2,1,0:T(8,128)S(1)} collective-permute-done((f32[49,8,128]{2,1,0:T(8,128)S(1)}, f32[49,8,128]{2,1,0:T(8,128)S(1)}, u32[]{:S(2)}, u32[]{:S(2)}) %collective-permute-start) | collective-permute-done | bytes 200736 | tf_op jit(solution)/shard_map/ppermute | solution.py:408
  5.5 0.1 merge.1
  5.6 2.9 %collective-permute-start.2 = (f32[25,8,128]{2,1,0:T(8,128)S(1)}, f32[25,8,128]{2,1,0:T(8,128)S(1)}, u32[]{:S(2)}, u32[]{:S(2)}) collective-permute-start(f32[25,8,128]{2,1,0:T(8,128)S(1)} %get-tuple-element.40._), channel_id=1, source_target_pairs={{0,8},{1,9},{2,10},{3,11},{4,12},{5,13},{6,14},{7,15},{8,0},{9,1},... | collective-permute-start | bytes 307208 | tf_op jit(solution)/shard_map/ppermute | solution.py:408
  8.5 1.5 %collective-permute-start.1 = (f32[25,8,128]{2,1,0:T(8,128)S(1)}, f32[25,8,128]{2,1,0:T(8,128)S(1)}, u32[]{:S(2)}, u32[]{:S(2)}) collective-permute-start(f32[25,8,128]{2,1,0:T(8,128)S(1)} %get-tuple-element.46), channel_id=1, source_target_pairs={{0,24},{1,25},{2,26},{3,27},{4,28},{5,29},{6,30},{7,31},{8,16},{9,... | collective-permute-start | bytes 307208 | tf_op jit(solution)/shard_map/ppermute | solution.py:408
  10.0 0.1 collective-permute-start.3
  10.7 1.0 %inner.1 = (f32[3,16,32,512]{3,2,1,0:T(8,128)S(1)}, f32[16,32,512]{2,1,0:T(8,128)S(1)}, f32[8,128]{1,0:T(8,128)S(1)}) custom-call(f32[3,16,32,512]{3,2,1,0:T(8,128)S(1)} %get-tuple-element.30.velocity_ref, f32[16,32,512]{2,1,0:T(8,128)S(1)} %get-tuple-element.31.left_ref, f32[16,32,512]{2,1,0:T(8,128)S(1)} %get-tuple-element.32.right_ref, ...), custom_call_target="tpu_custom_call" | custom-call | flops 8000000 | bytes 8000000 | tf_op jit(solution)/shard_map/inner/pallas_call | solution.py:462
  11.7 0.1 collective-permute-done.2.rest_2_
  11.8 3.4 %collective-permute-done.1.rest_1_ = f32[25,8,128]{2,1,0:T(8,128)S(1)} collective-permute-done((f32[25,8,128]{2,1,0:T(8,128)S(1)}, f32[25,8,128]{2,1,0:T(8,128)S(1)}, u32[]{:S(2)}, u32[]{:S(2)}) %collective-permute-start.1) | collective-permute-done | bytes 102432 | tf_op jit(solution)/shard_map/ppermute | solution.py:408
  15.2 1.3 %collective-permute-done.3.rest_3_ = f32[25,8,128]{2,1,0:T(8,128)S(1)} collective-permute-done((f32[25,8,128]{2,1,0:T(8,128)S(1)}, f32[25,8,128]{2,1,0:T(8,128)S(1)}, u32[]{:S(2)}, u32[]{:S(2)}) %collective-permute-start.3) | collective-permute-done | bytes 102432 | tf_op jit(solution)/shard_map/ppermute | solution.py:408
  16.5 0.1 spread.1
  16.6 0.1 collective-permute-start.7
  16.7 3.7 %collective-permute-start.4 = (f32[8,128]{1,0:T(8,128)S(1)}, f32[8,128]{1,0:T(8,128)S(1)}, u32[]{:S(2)}, u32[]{:S(2)}) collective-permute-start(f32[8,128]{1,0:T(8,128)S(1)} %get-tuple-element.48.rest_0_), channel_id=1, source_target_pairs={{0,3},{1,2},{2,1},{3,0},{4,7},{5,6},{6,5},{7,4},{8,11},{9,10},{10,... | collective-permute-start | bytes 12296 | tf_op jit(solution)/shard_map/ppermute | solution.py:408
  20.4 0.0 collective-permute-start.5
  20.4 0.8 %collective-permute-start.6 = (f32[8,128]{1,0:T(8,128)S(1)}, f32[8,128]{1,0:T(8,128)S(1)}, u32[]{:S(2)}, u32[]{:S(2)}) collective-permute-start(f32[8,128]{1,0:T(8,128)S(1)} %get-tuple-element.48.rest_0_), channel_id=1, source_target_pairs={{0,1},{1,0},{2,3},{3,2},{4,5},{5,4},{6,7},{7,6},{8,9},{9,8},{10,11... | collective-permute-start | bytes 12296 | tf_op jit(solution)/shard_map/ppermute | solution.py:408
  21.1 1.1 %finish0.1 = (f32[3,16,32,512]{3,2,1,0:T(8,128)}, f32[16,16,512]{2,1,0:T(8,128)S(1)}) custom-call(f32[12,8,512]{2,1,0:T(8,128)S(1)} %get-tuple-element.49.incoming_ref, f32[3,16,32,512]{3,2,1,0:T(8,128)S(1)} %get-tuple-element.45.rest_0_.base_ref, f32[16,32,512]{2,1,0:T(8,128)S(1)} %get-tuple-element.31.left_ref, f32[16,32,512]{2,1,0:T(8,128)S(1)} %get-tuple-element.32.right_ref), custom_call_target="tpu_custom_call" | custom-call | flops 3000000 | bytes 6000000 | tf_op jit(solution)/shard_map/finish0/pallas_call | solution.py:487
  22.2 0.0 collective-permute-done.7.incoming_ref
  22.2 1.1 %finish1.1 = (f32[3,16,32,512]{3,2,1,0:T(8,128)}, f32[16,16,512]{2,1,0:T(8,128)S(1)}) custom-call(f32[12,8,512]{2,1,0:T(8,128)S(1)} %collective-permute-done.7.incoming_ref, f32[3,16,32,512]{3,2,1,0:T(8,128)S(1)} %get-tuple-element.45.rest_0_.base_ref, f32[16,32,512]{2,1,0:T(8,128)S(1)} %get-tuple-element.31.left_ref, ...), custom_call_target="tpu_custom_call", output_to_operand_aliasing={{0}: (4, {})} | custom-call | flops 3000000 | bytes 6000000 | tf_op jit(solution)/shard_map/finish1/pallas_call | solution.py:487
  23.3 0.0 collective-permute-done.4.rest_1_
  23.3 1.5 %collective-permute-done.5.rest_2_ = f32[8,128]{1,0:T(8,128)S(1)} collective-permute-done((f32[8,128]{1,0:T(8,128)S(1)}, f32[8,128]{1,0:T(8,128)S(1)}, u32[]{:S(2)}, u32[]{:S(2)}) %collective-permute-start.5) | collective-permute-done | bytes 4128 | tf_op jit(solution)/shard_map/ppermute | solution.py:408
  24.9 0.0 collective-permute-done.6.rest_3_
  24.9 1.2 %correct.1 = f32[3,16,32,512]{3,2,1,0:T(8,128)} custom-call(f32[8,128]{1,0:T(8,128)S(1)} %get-tuple-element.41.goal_ref, f32[16,32,512]{2,1,0:T(8,128)S(1)} %get-tuple-element.42.unit_ref, f32[8,128]{1,0:T(8,128)S(1)} %get-tuple-element.48.rest_0_, f32[8,128]{1,0:T(8,128)S(1)} %collective-permute-done.4.rest_1_, ...), custom_call_target="tpu_custom_call", output_to_operand_aliasing={{}: (8, {})} | custom-call | flops 500000 | bytes 1600000 | tf_op jit(solution)/shard_map/correct/pallas_call | solution.py:504
Async XLA Ops:
  4.0 1.6 %collective-permute-start = (f32[49,8,128]{2,1,0:T(8,128)S(1)}, f32[49,8,128]{2,1,0:T(8,128)S(1)}, u32[]{:S(2)}, u32[]{:S(2)}) collective-permute-start(f32[49,8,128]{2,1,0:T(8,128)S(1)} %get-tuple-element.38.away_ref), channel_id=1, source_target_pairs={{0,4},{1,5},{2,6},{3,7},{4,0},{5,1},{6,2},{7,3},{8,12},{9,13},{10,... | collective-permute-start | bytes 602120 | tf_op jit(solution)/shard_map/ppermute | solution.py:408
  5.6 6.1 %collective-permute-start.2 = (f32[25,8,128]{2,1,0:T(8,128)S(1)}, f32[25,8,128]{2,1,0:T(8,128)S(1)}, u32[]{:S(2)}, u32[]{:S(2)}) collective-permute-start(f32[25,8,128]{2,1,0:T(8,128)S(1)} %get-tuple-element.40._), channel_id=1, source_target_pairs={{0,8},{1,9},{2,10},{3,11},{4,12},{5,13},{6,14},{7,15},{8,0},{9,1},... | collective-permute-start | bytes 307208 | tf_op jit(solution)/shard_map/ppermute | solution.py:408
  8.5 6.7 %collective-permute-start.1 = (f32[25,8,128]{2,1,0:T(8,128)S(1)}, f32[25,8,128]{2,1,0:T(8,128)S(1)}, u32[]{:S(2)}, u32[]{:S(2)}) collective-permute-start(f32[25,8,128]{2,1,0:T(8,128)S(1)} %get-tuple-element.46), channel_id=1, source_target_pairs={{0,24},{1,25},{2,26},{3,27},{4,28},{5,29},{6,30},{7,31},{8,16},{9,... | collective-permute-start | bytes 307208 | tf_op jit(solution)/shard_map/ppermute | solution.py:408
  10.0 6.5 %collective-permute-start.3 = (f32[25,8,128]{2,1,0:T(8,128)S(1)}, f32[25,8,128]{2,1,0:T(8,128)S(1)}, u32[]{:S(2)}, u32[]{:S(2)}) collective-permute-start(f32[25,8,128]{2,1,0:T(8,128)S(1)} %get-tuple-element.47), channel_id=1, source_target_pairs={{0,16},{1,17},{2,18},{3,19},{4,20},{5,21},{6,22},{7,23},{8,24},{9,... | collective-permute-start | bytes 307208 | tf_op jit(solution)/shard_map/ppermute | solution.py:408
  16.6 5.6 %collective-permute-start.7 = (f32[12,8,512]{2,1,0:T(8,128)S(1)}, f32[12,8,512]{2,1,0:T(8,128)S(1)}, u32[]{:S(2)}, u32[]{:S(2)}) collective-permute-start(f32[12,8,512]{2,1,0:T(8,128)S(1)} %get-tuple-element.51), channel_id=1, source_target_pairs={{0,4},{1,5},{2,6},{3,7},{4,0},{5,1},{6,2},{7,3},{8,12},{9,13},{10,... | collective-permute-start | bytes 589832 | tf_op jit(solution)/shard_map/ppermute | solution.py:408
  16.7 6.6 %collective-permute-start.4 = (f32[8,128]{1,0:T(8,128)S(1)}, f32[8,128]{1,0:T(8,128)S(1)}, u32[]{:S(2)}, u32[]{:S(2)}) collective-permute-start(f32[8,128]{1,0:T(8,128)S(1)} %get-tuple-element.48.rest_0_), channel_id=1, source_target_pairs={{0,3},{1,2},{2,1},{3,0},{4,7},{5,6},{6,5},{7,4},{8,11},{9,10},{10,... | collective-permute-start | bytes 12296 | tf_op jit(solution)/shard_map/ppermute | solution.py:408
  20.4 4.5 %collective-permute-start.5 = (f32[8,128]{1,0:T(8,128)S(1)}, f32[8,128]{1,0:T(8,128)S(1)}, u32[]{:S(2)}, u32[]{:S(2)}) collective-permute-start(f32[8,128]{1,0:T(8,128)S(1)} %get-tuple-element.48.rest_0_), channel_id=1, source_target_pairs={{0,2},{1,3},{2,0},{3,1},{4,6},{5,7},{6,4},{7,5},{8,10},{9,11},{10,... | collective-permute-start | bytes 12296 | tf_op jit(solution)/shard_map/ppermute | solution.py:408
  20.4 4.5 %collective-permute-start.6 = (f32[8,128]{1,0:T(8,128)S(1)}, f32[8,128]{1,0:T(8,128)S(1)}, u32[]{:S(2)}, u32[]{:S(2)}) collective-permute-start(f32[8,128]{1,0:T(8,128)S(1)} %get-tuple-element.48.rest_0_), channel_id=1, source_target_pairs={{0,1},{1,0},{2,3},{3,2},{4,5},{5,4},{6,7},{7,6},{8,9},{9,8},{10,11... | collective-permute-start | bytes 12296 | tf_op jit(solution)/shard_map/ppermute | solution.py:408

commit v9 on v8

--- a/solution.py
+++ b/solution.py
@@ -242,7 +242,8 @@
     tile = away_ref[slot] + mate_ref[slot]
     near_ref[slot] = tile
     for ref in send_refs:
-        ref[ref.shape[0] - 1] = tile
+        for at in range(half * components * count, ref.shape[0]):
+            ref[at] = tile
     for i in range(half):
         rows = row_tile((me - chip * 2) * half + i)
         for c in range(components):
@@ -448,8 +449,9 @@
     mate = to_mate(away)
     *outgoing, near = pl.pallas_call(
         functools.partial(merge_kernel, chips, components),
-        out_shape=[shape(half * components * count + 1, SUB, LANES)] * (chips - 1)
-        + [shape(half * 2 * components * count + 1, SUB, LANES)],
+        out_shape=[
+            shape(half * components * count + m.bit_count(), SUB, LANES) for m in range(1, chips)
+        ] + [shape(half * 2 * components * count + 1, SUB, LANES)],
         in_specs=[vmem] * 4,
         out_specs=[vmem] * chips,
         compiler_params=options(16),

time: 26.2 us -> 24.9 us (0.950)
  waiting for transfers between devices: 7.43 us -> 6.01 us
    ppermute x8, waiting for transfers between devices: 7.43 us -> 6.01 us  [send(): return lax.ppermute(array, ('gz', 'gy'), route)]
  transfers between devices with their start and end apart: 8 -> 8, of which waited for: 5 -> 3; matrix products, arithmetic and copies ran while one was open for 0% -> 0% of each run, Pallas kernels for 12% -> 13%
where the time goes in v9:
time: 24.9 us; the launch traced here: 24.7 us
  starting transfers between devices  9.57 us (38%)
  Pallas kernels  8.43 us (34%)
  waiting for transfers between devices  6.01 us (24%)
  between operations  0.72 us (3%)
    ppermute x8, starting transfers between devices, send(): return lax.ppermute(array, ('gz', 'gy'), route)  9.57 us
    ppermute x8, waiting for transfers between devices, send(): return lax.ppermute(array, ('gz', 'gy'), route)  6.01 us
    pallas_call x1, Pallas kernels, shards(): pl.pallas_call(functools.partial(ladder_kernel, cells, blocks, chips, lin...  3.95 us
    pallas_call x2, Pallas kernels, finish(): pl.pallas_call(functools.partial(finish_kernel, side), out_shape=[shape(*...  2.17 us
    pallas_call x1, Pallas kernels, shards(): pl.pallas_call(functools.partial(correct_kernel, columns), out_shape=shap...  1.18 us
    pallas_call x1, Pallas kernels, shards(): pl.pallas_call(inner_kernel, out_shape=[shape(*velocity.shape), profile,...  0.99 us
  transfers between devices with their start and end apart: 8, of which 3 were waited for; matrix products, arithmetic and copies ran while one was open for 0% of the time, Pallas kernels for 13%

profile of v9, /device:TPU:0, one launch (start us, length us, event | category | flops | bytes accessed | tf_op | source)
XLA Modules:
  0.0 24.7 jit_solution(1338814849118464399)
XLA Ops:
  0.0 3.9 %ladder.1 = (f32[48,8,128]{2,1,0:T(8,128)S(1)}, f32[49,8,128]{2,1,0:T(8,128)S(1)}, f32[4,32,512]{2,1,0:T(8,128)S(1)}, f32[3,32,512]{2,1,0:T(8,128)S(1)}, f32[16,...) custom-call(s32[128]{0:T(128)} %index_hbm.1, ...), custom_call_target="tpu_custom_call" | custom-call | flops 40000000 | bytes 6000000 | tf_op jit(solution)/shard_map/ladder/pallas_call | solution.py:418
  4.0 0.5 %collective-permute-start = (f32[49,8,128]{2,1,0:T(8,128)S(1)}, f32[49,8,128]{2,1,0:T(8,128)S(1)}, u32[]{:S(2)}, u32[]{:S(2)}) collective-permute-start(f32[49,8,128]{2,1,0:T(8,128)S(1)} %get-tuple-element.38.away_ref), channel_id=1, source_target_pairs={{0,4},{1,5},{2,6},{3,7},{4,0},{5,1},{6,2},{7,3},{8,12},{9,13},{10,... | collective-permute-start | bytes 602120 | tf_op jit(solution)/shard_map/ppermute | solution.py:409
  4.5 1.1 %collective-permute-done.mate_ref = f32[49,8,128]{2,1,0:T(8,128)S(1)} collective-permute-done((f32[49,8,128]{2,1,0:T(8,128)S(1)}, f32[49,8,128]{2,1,0:T(8,128)S(1)}, u32[]{:S(2)}, u32[]{:S(2)}) %collective-permute-start) | collective-permute-done | bytes 200736 | tf_op jit(solution)/shard_map/ppermute | solution.py:409
  5.6 0.1 merge.1
  5.6 3.9 %collective-permute-start.1 = (f32[26,8,128]{2,1,0:T(8,128)S(1)}, f32[26,8,128]{2,1,0:T(8,128)S(1)}, u32[]{:S(2)}, u32[]{:S(2)}) collective-permute-start(f32[26,8,128]{2,1,0:T(8,128)S(1)} %get-tuple-element.46), channel_id=1, source_target_pairs={{0,24},{1,25},{2,26},{3,27},{4,28},{5,29},{6,30},{7,31},{8,16},{9,... | collective-permute-start | bytes 319496 | tf_op jit(solution)/shard_map/ppermute | solution.py:409
  9.5 0.5 %collective-permute-start.2 = (f32[25,8,128]{2,1,0:T(8,128)S(1)}, f32[25,8,128]{2,1,0:T(8,128)S(1)}, u32[]{:S(2)}, u32[]{:S(2)}) collective-permute-start(f32[25,8,128]{2,1,0:T(8,128)S(1)} %get-tuple-element.40._), channel_id=1, source_target_pairs={{0,8},{1,9},{2,10},{3,11},{4,12},{5,13},{6,14},{7,15},{8,0},{9,1},... | collective-permute-start | bytes 307208 | tf_op jit(solution)/shard_map/ppermute | solution.py:409
  10.0 0.1 collective-permute-start.3
  10.8 1.0 %inner.1 = (f32[3,16,32,512]{3,2,1,0:T(8,128)S(1)}, f32[16,32,512]{2,1,0:T(8,128)S(1)}, f32[8,128]{1,0:T(8,128)S(1)}) custom-call(f32[3,16,32,512]{3,2,1,0:T(8,128)S(1)} %get-tuple-element.30.velocity_ref, f32[16,32,512]{2,1,0:T(8,128)S(1)} %get-tuple-element.31.left_ref, f32[16,32,512]{2,1,0:T(8,128)S(1)} %get-tuple-element.32.right_ref, ...), custom_call_target="tpu_custom_call" | custom-call | flops 8000000 | bytes 8000000 | tf_op jit(solution)/shard_map/inner/pallas_call | solution.py:464
  11.8 3.4 %collective-permute-done.2.rest_2_ = f32[25,8,128]{2,1,0:T(8,128)S(1)} collective-permute-done((f32[25,8,128]{2,1,0:T(8,128)S(1)}, f32[25,8,128]{2,1,0:T(8,128)S(1)}, u32[]{:S(2)}, u32[]{:S(2)}) %collective-permute-start.2) | collective-permute-done | bytes 102432 | tf_op jit(solution)/shard_map/ppermute | solution.py:409
  15.2 0.0 collective-permute-done.3.rest_3_
  15.2 0.0 collective-permute-done.1.rest_1_
  15.2 0.1 spread.1
  15.3 0.1 collective-permute-start.7
  15.4 3.7 %collective-permute-start.4 = (f32[8,128]{1,0:T(8,128)S(1)}, f32[8,128]{1,0:T(8,128)S(1)}, u32[]{:S(2)}, u32[]{:S(2)}) collective-permute-start(f32[8,128]{1,0:T(8,128)S(1)} %get-tuple-element.48.rest_0_), channel_id=1, source_target_pairs={{0,3},{1,2},{2,1},{3,0},{4,7},{5,6},{6,5},{7,4},{8,11},{9,10},{10,... | collective-permute-start | bytes 12296 | tf_op jit(solution)/shard_map/ppermute | solution.py:409
  19.0 0.0 collective-permute-start.5
  19.0 0.8 %collective-permute-start.6 = (f32[8,128]{1,0:T(8,128)S(1)}, f32[8,128]{1,0:T(8,128)S(1)}, u32[]{:S(2)}, u32[]{:S(2)}) collective-permute-start(f32[8,128]{1,0:T(8,128)S(1)} %get-tuple-element.48.rest_0_), channel_id=1, source_target_pairs={{0,1},{1,0},{2,3},{3,2},{4,5},{5,4},{6,7},{7,6},{8,9},{9,8},{10,11... | collective-permute-start | bytes 12296 | tf_op jit(solution)/shard_map/ppermute | solution.py:409
  19.8 1.1 %finish0.1 = (f32[3,16,32,512]{3,2,1,0:T(8,128)}, f32[16,16,512]{2,1,0:T(8,128)S(1)}) custom-call(f32[12,8,512]{2,1,0:T(8,128)S(1)} %get-tuple-element.49.incoming_ref, f32[3,16,32,512]{3,2,1,0:T(8,128)S(1)} %get-tuple-element.45.rest_0_.base_ref, f32[16,32,512]{2,1,0:T(8,128)S(1)} %get-tuple-element.31.left_ref, f32[16,32,512]{2,1,0:T(8,128)S(1)} %get-tuple-element.32.right_ref), custom_call_target="tpu_custom_call" | custom-call | flops 3000000 | bytes 6000000 | tf_op jit(solution)/shard_map/finish0/pallas_call | solution.py:489
  20.9 0.0 collective-permute-done.7.incoming_ref
  20.9 1.1 %finish1.1 = (f32[3,16,32,512]{3,2,1,0:T(8,128)}, f32[16,16,512]{2,1,0:T(8,128)S(1)}) custom-call(f32[12,8,512]{2,1,0:T(8,128)S(1)} %collective-permute-done.7.incoming_ref, f32[3,16,32,512]{3,2,1,0:T(8,128)S(1)} %get-tuple-element.45.rest_0_.base_ref, f32[16,32,512]{2,1,0:T(8,128)S(1)} %get-tuple-element.31.left_ref, ...), custom_call_target="tpu_custom_call", output_to_operand_aliasing={{0}: (4, {})} | custom-call | flops 3000000 | bytes 6000000 | tf_op jit(solution)/shard_map/finish1/pallas_call | solution.py:489
  22.0 0.0 collective-permute-done.4.rest_1_
  22.0 1.5 %collective-permute-done.5.rest_2_ = f32[8,128]{1,0:T(8,128)S(1)} collective-permute-done((f32[8,128]{1,0:T(8,128)S(1)}, f32[8,128]{1,0:T(8,128)S(1)}, u32[]{:S(2)}, u32[]{:S(2)}) %collective-permute-start.5) | collective-permute-done | bytes 4128 | tf_op jit(solution)/shard_map/ppermute | solution.py:409
  23.5 0.0 collective-permute-done.6.rest_3_
  23.5 1.2 %correct.1 = f32[3,16,32,512]{3,2,1,0:T(8,128)} custom-call(f32[8,128]{1,0:T(8,128)S(1)} %get-tuple-element.41.goal_ref, f32[16,32,512]{2,1,0:T(8,128)S(1)} %get-tuple-element.42.unit_ref, f32[8,128]{1,0:T(8,128)S(1)} %get-tuple-element.48.rest_0_, f32[8,128]{1,0:T(8,128)S(1)} %collective-permute-done.4.rest_1_, ...), custom_call_target="tpu_custom_call", output_to_operand_aliasing={{}: (8, {})} | custom-call | flops 500000 | bytes 1600000 | tf_op jit(solution)/shard_map/correct/pallas_call | solution.py:506
Async XLA Ops:
  4.0 1.6 %collective-permute-start = (f32[49,8,128]{2,1,0:T(8,128)S(1)}, f32[49,8,128]{2,1,0:T(8,128)S(1)}, u32[]{:S(2)}, u32[]{:S(2)}) collective-permute-start(f32[49,8,128]{2,1,0:T(8,128)S(1)} %get-tuple-element.38.away_ref), channel_id=1, source_target_pairs={{0,4},{1,5},{2,6},{3,7},{4,0},{5,1},{6,2},{7,3},{8,12},{9,13},{10,... | collective-permute-start | bytes 602120 | tf_op jit(solution)/shard_map/ppermute | solution.py:409
  5.6 9.6 %collective-permute-start.1 = (f32[26,8,128]{2,1,0:T(8,128)S(1)}, f32[26,8,128]{2,1,0:T(8,128)S(1)}, u32[]{:S(2)}, u32[]{:S(2)}) collective-permute-start(f32[26,8,128]{2,1,0:T(8,128)S(1)} %get-tuple-element.46), channel_id=1, source_target_pairs={{0,24},{1,25},{2,26},{3,27},{4,28},{5,29},{6,30},{7,31},{8,16},{9,... | collective-permute-start | bytes 319496 | tf_op jit(solution)/shard_map/ppermute | solution.py:409
  9.5 5.7 %collective-permute-start.2 = (f32[25,8,128]{2,1,0:T(8,128)S(1)}, f32[25,8,128]{2,1,0:T(8,128)S(1)}, u32[]{:S(2)}, u32[]{:S(2)}) collective-permute-start(f32[25,8,128]{2,1,0:T(8,128)S(1)} %get-tuple-element.40._), channel_id=1, source_target_pairs={{0,8},{1,9},{2,10},{3,11},{4,12},{5,13},{6,14},{7,15},{8,0},{9,1},... | collective-permute-start | bytes 307208 | tf_op jit(solution)/shard_map/ppermute | solution.py:409
  10.0 5.2 %collective-permute-start.3 = (f32[25,8,128]{2,1,0:T(8,128)S(1)}, f32[25,8,128]{2,1,0:T(8,128)S(1)}, u32[]{:S(2)}, u32[]{:S(2)}) collective-permute-start(f32[25,8,128]{2,1,0:T(8,128)S(1)} %get-tuple-element.47), channel_id=1, source_target_pairs={{0,16},{1,17},{2,18},{3,19},{4,20},{5,21},{6,22},{7,23},{8,24},{9,... | collective-permute-start | bytes 307208 | tf_op jit(solution)/shard_map/ppermute | solution.py:409
  15.3 5.6 %collective-permute-start.7 = (f32[12,8,512]{2,1,0:T(8,128)S(1)}, f32[12,8,512]{2,1,0:T(8,128)S(1)}, u32[]{:S(2)}, u32[]{:S(2)}) collective-permute-start(f32[12,8,512]{2,1,0:T(8,128)S(1)} %get-tuple-element.51), channel_id=1, source_target_pairs={{0,4},{1,5},{2,6},{3,7},{4,0},{5,1},{6,2},{7,3},{8,12},{9,13},{10,... | collective-permute-start | bytes 589832 | tf_op jit(solution)/shard_map/ppermute | solution.py:409
  15.4 6.7 %collective-permute-start.4 = (f32[8,128]{1,0:T(8,128)S(1)}, f32[8,128]{1,0:T(8,128)S(1)}, u32[]{:S(2)}, u32[]{:S(2)}) collective-permute-start(f32[8,128]{1,0:T(8,128)S(1)} %get-tuple-element.48.rest_0_), channel_id=1, source_target_pairs={{0,3},{1,2},{2,1},{3,0},{4,7},{5,6},{6,5},{7,4},{8,11},{9,10},{10,... | collective-permute-start | bytes 12296 | tf_op jit(solution)/shard_map/ppermute | solution.py:409
  19.0 4.5 %collective-permute-start.5 = (f32[8,128]{1,0:T(8,128)S(1)}, f32[8,128]{1,0:T(8,128)S(1)}, u32[]{:S(2)}, u32[]{:S(2)}) collective-permute-start(f32[8,128]{1,0:T(8,128)S(1)} %get-tuple-element.48.rest_0_), channel_id=1, source_target_pairs={{0,2},{1,3},{2,0},{3,1},{4,6},{5,7},{6,4},{7,5},{8,10},{9,11},{10,... | collective-permute-start | bytes 12296 | tf_op jit(solution)/shard_map/ppermute | solution.py:409
  19.0 4.5 %collective-permute-start.6 = (f32[8,128]{1,0:T(8,128)S(1)}, f32[8,128]{1,0:T(8,128)S(1)}, u32[]{:S(2)}, u32[]{:S(2)}) collective-permute-start(f32[8,128]{1,0:T(8,128)S(1)} %get-tuple-element.48.rest_0_), channel_id=1, source_target_pairs={{0,1},{1,0},{2,3},{3,2},{4,5},{5,4},{6,7},{7,6},{8,9},{9,8},{10,11... | collective-permute-start | bytes 12296 | tf_op jit(solution)/shard_map/ppermute | solution.py:409

commit v10 on v9

--- a/solution.py
+++ b/solution.py
@@ -482,7 +482,7 @@
     )(near, pair, chip_coefs, base, *incoming)
     other_in = to_mate(other_out)
     tiles = [tile] + [
-        send(tile, lambda z, y: (z, y ^ other)) for other in reversed(range(1, columns))
+        send(tile, lambda z, y: (z, (y + shift) % columns)) for shift in range(1, columns)
     ]
 
     def finish(side, arrived, *before):

time: 24.9 us -> 24.5 us (0.984)
  waiting for transfers between devices: 6.01 us -> 4.54 us
  starting transfers between devices: 9.57 us -> 10.7 us
    ppermute x8, waiting for transfers between devices: 6.01 us -> 4.54 us  [send(): return lax.ppermute(array, ('gz', 'gy'), route)]
    ppermute x8, starting transfers between devices: 9.57 us -> 10.7 us  [send(): return lax.ppermute(array, ('gz', 'gy'), route)]
  transfers between devices with their start and end apart: 8 -> 8, of which waited for: 3 -> 2; matrix products, arithmetic and copies ran while one was open for 0% -> 0% of each run, Pallas kernels for 13% -> 13%
where the time goes in v10:
time: 24.5 us; the launch traced here: 24.4 us
  starting transfers between devices  10.7 us (44%)
  Pallas kernels  8.43 us (34%)
  waiting for transfers between devices  4.54 us (19%)
  between operations  0.72 us (3%)
    ppermute x8, starting transfers between devices, send(): return lax.ppermute(array, ('gz', 'gy'), route)  10.7 us
    ppermute x8, waiting for transfers between devices, send(): return lax.ppermute(array, ('gz', 'gy'), route)  4.54 us
    pallas_call x1, Pallas kernels, shards(): pl.pallas_call(functools.partial(ladder_kernel, cells, blocks, chips, lin...  3.95 us
    pallas_call x2, Pallas kernels, finish(): pl.pallas_call(functools.partial(finish_kernel, side), out_shape=[shape(*...  2.17 us
    pallas_call x1, Pallas kernels, shards(): pl.pallas_call(functools.partial(correct_kernel, columns), out_shape=shap...  1.18 us
    pallas_call x1, Pallas kernels, shards(): pl.pallas_call(inner_kernel, out_shape=[shape(*velocity.shape), profile,...  0.99 us
  transfers between devices with their start and end apart: 8, of which 2 were waited for; matrix products, arithmetic and copies ran while one was open for 0% of the time, Pallas kernels for 13%

profile of v10, /device:TPU:0, one launch (start us, length us, event | category | flops | bytes accessed | tf_op | source)
XLA Modules:
  0.0 24.4 jit_solution(11536201102040842284)
XLA Ops:
  0.0 3.9 %ladder.1 = (f32[48,8,128]{2,1,0:T(8,128)S(1)}, f32[49,8,128]{2,1,0:T(8,128)S(1)}, f32[4,32,512]{2,1,0:T(8,128)S(1)}, f32[3,32,512]{2,1,0:T(8,128)S(1)}, f32[16,...) custom-call(s32[128]{0:T(128)} %index_hbm.1, ...), custom_call_target="tpu_custom_call" | custom-call | flops 40000000 | bytes 6000000 | tf_op jit(solution)/shard_map/ladder/pallas_call | solution.py:418
  4.0 0.5 %collective-permute-start = (f32[49,8,128]{2,1,0:T(8,128)S(1)}, f32[49,8,128]{2,1,0:T(8,128)S(1)}, u32[]{:S(2)}, u32[]{:S(2)}) collective-permute-start(f32[49,8,128]{2,1,0:T(8,128)S(1)} %get-tuple-element.38.away_ref), channel_id=1, source_target_pairs={{0,4},{1,5},{2,6},{3,7},{4,0},{5,1},{6,2},{7,3},{8,12},{9,13},{10,... | collective-permute-start | bytes 602120 | tf_op jit(solution)/shard_map/ppermute | solution.py:409
  4.5 1.1 %collective-permute-done.mate_ref = f32[49,8,128]{2,1,0:T(8,128)S(1)} collective-permute-done((f32[49,8,128]{2,1,0:T(8,128)S(1)}, f32[49,8,128]{2,1,0:T(8,128)S(1)}, u32[]{:S(2)}, u32[]{:S(2)}) %collective-permute-start) | collective-permute-done | bytes 200736 | tf_op jit(solution)/shard_map/ppermute | solution.py:409
  5.6 0.1 merge.1
  5.6 3.9 %collective-permute-start.1 = (f32[26,8,128]{2,1,0:T(8,128)S(1)}, f32[26,8,128]{2,1,0:T(8,128)S(1)}, u32[]{:S(2)}, u32[]{:S(2)}) collective-permute-start(f32[26,8,128]{2,1,0:T(8,128)S(1)} %get-tuple-element.46), channel_id=1, source_target_pairs={{0,24},{1,25},{2,26},{3,27},{4,28},{5,29},{6,30},{7,31},{8,16},{9,... | collective-permute-start | bytes 319496 | tf_op jit(solution)/shard_map/ppermute | solution.py:409
  9.5 0.5 %collective-permute-start.2 = (f32[25,8,128]{2,1,0:T(8,128)S(1)}, f32[25,8,128]{2,1,0:T(8,128)S(1)}, u32[]{:S(2)}, u32[]{:S(2)}) collective-permute-start(f32[25,8,128]{2,1,0:T(8,128)S(1)} %get-tuple-element.40._), channel_id=1, source_target_pairs={{0,8},{1,9},{2,10},{3,11},{4,12},{5,13},{6,14},{7,15},{8,0},{9,1},... | collective-permute-start | bytes 307208 | tf_op jit(solution)/shard_map/ppermute | solution.py:409
  10.0 0.1 collective-permute-start.3
  10.8 1.0 %inner.1 = (f32[3,16,32,512]{3,2,1,0:T(8,128)S(1)}, f32[16,32,512]{2,1,0:T(8,128)S(1)}, f32[8,128]{1,0:T(8,128)S(1)}) custom-call(f32[3,16,32,512]{3,2,1,0:T(8,128)S(1)} %get-tuple-element.30.velocity_ref, f32[16,32,512]{2,1,0:T(8,128)S(1)} %get-tuple-element.31.left_ref, f32[16,32,512]{2,1,0:T(8,128)S(1)} %get-tuple-element.32.right_ref, ...), custom_call_target="tpu_custom_call" | custom-call | flops 8000000 | bytes 8000000 | tf_op jit(solution)/shard_map/inner/pallas_call | solution.py:464
  11.8 3.4 %collective-permute-done.2.rest_2_ = f32[25,8,128]{2,1,0:T(8,128)S(1)} collective-permute-done((f32[25,8,128]{2,1,0:T(8,128)S(1)}, f32[25,8,128]{2,1,0:T(8,128)S(1)}, u32[]{:S(2)}, u32[]{:S(2)}) %collective-permute-start.2) | collective-permute-done | bytes 102432 | tf_op jit(solution)/shard_map/ppermute | solution.py:409
  15.2 0.0 collective-permute-done.3.rest_3_
  15.2 0.0 collective-permute-done.1.rest_1_
  15.2 0.1 spread.1
  15.3 0.1 collective-permute-start.7
  15.4 1.6 %collective-permute-start.4 = (f32[8,128]{1,0:T(8,128)S(1)}, f32[8,128]{1,0:T(8,128)S(1)}, u32[]{:S(2)}, u32[]{:S(2)}) collective-permute-start(f32[8,128]{1,0:T(8,128)S(1)} %get-tuple-element.48.rest_0_), channel_id=1, source_target_pairs={{0,1},{1,2},{2,3},{3,0},{4,5},{5,6},{6,7},{7,4},{8,9},{9,10},{10,1... | collective-permute-start | bytes 12296 | tf_op jit(solution)/shard_map/ppermute | solution.py:409
  17.0 2.6 %collective-permute-start.5 = (f32[8,128]{1,0:T(8,128)S(1)}, f32[8,128]{1,0:T(8,128)S(1)}, u32[]{:S(2)}, u32[]{:S(2)}) collective-permute-start(f32[8,128]{1,0:T(8,128)S(1)} %get-tuple-element.48.rest_0_), channel_id=1, source_target_pairs={{0,2},{1,3},{2,0},{3,1},{4,6},{5,7},{6,4},{7,5},{8,10},{9,11},{10,... | collective-permute-start | bytes 12296 | tf_op jit(solution)/shard_map/ppermute | solution.py:409
  19.6 1.3 %collective-permute-start.6 = (f32[8,128]{1,0:T(8,128)S(1)}, f32[8,128]{1,0:T(8,128)S(1)}, u32[]{:S(2)}, u32[]{:S(2)}) collective-permute-start(f32[8,128]{1,0:T(8,128)S(1)} %get-tuple-element.48.rest_0_), channel_id=1, source_target_pairs={{0,3},{1,0},{2,1},{3,2},{4,7},{5,4},{6,5},{7,6},{8,11},{9,8},{10,9... | collective-permute-start | bytes 12296 | tf_op jit(solution)/shard_map/ppermute | solution.py:409
  20.9 1.1 %finish0.1 = (f32[3,16,32,512]{3,2,1,0:T(8,128)}, f32[16,16,512]{2,1,0:T(8,128)S(1)}) custom-call(f32[12,8,512]{2,1,0:T(8,128)S(1)} %get-tuple-element.49.incoming_ref, f32[3,16,32,512]{3,2,1,0:T(8,128)S(1)} %get-tuple-element.45.rest_0_.base_ref, f32[16,32,512]{2,1,0:T(8,128)S(1)} %get-tuple-element.31.left_ref, f32[16,32,512]{2,1,0:T(8,128)S(1)} %get-tuple-element.32.right_ref), custom_call_target="tpu_custom_call" | custom-call | flops 3000000 | bytes 6000000 | tf_op jit(solution)/shard_map/finish0/pallas_call | solution.py:489
  22.0 0.0 collective-permute-done.7.incoming_ref
  22.0 1.1 %finish1.1 = (f32[3,16,32,512]{3,2,1,0:T(8,128)}, f32[16,16,512]{2,1,0:T(8,128)S(1)}) custom-call(f32[12,8,512]{2,1,0:T(8,128)S(1)} %collective-permute-done.7.incoming_ref, f32[3,16,32,512]{3,2,1,0:T(8,128)S(1)} %get-tuple-element.45.rest_0_.base_ref, f32[16,32,512]{2,1,0:T(8,128)S(1)} %get-tuple-element.31.left_ref, ...), custom_call_target="tpu_custom_call", output_to_operand_aliasing={{0}: (4, {})} | custom-call | flops 3000000 | bytes 6000000 | tf_op jit(solution)/shard_map/finish1/pallas_call | solution.py:489
  23.1 0.0 collective-permute-done.4.rest_1_
  23.1 0.0 collective-permute-done.5.rest_2_
  23.1 0.0 collective-permute-done.6.rest_3_
  23.2 1.2 %correct.1 = f32[3,16,32,512]{3,2,1,0:T(8,128)} custom-call(f32[8,128]{1,0:T(8,128)S(1)} %get-tuple-element.41.goal_ref, f32[16,32,512]{2,1,0:T(8,128)S(1)} %get-tuple-element.42.unit_ref, f32[8,128]{1,0:T(8,128)S(1)} %get-tuple-element.48.rest_0_, f32[8,128]{1,0:T(8,128)S(1)} %collective-permute-done.4.rest_1_, ...), custom_call_target="tpu_custom_call", output_to_operand_aliasing={{}: (8, {})} | custom-call | flops 500000 | bytes 1600000 | tf_op jit(solution)/shard_map/correct/pallas_call | solution.py:506
Async XLA Ops:
  4.0 1.6 %collective-permute-start = (f32[49,8,128]{2,1,0:T(8,128)S(1)}, f32[49,8,128]{2,1,0:T(8,128)S(1)}, u32[]{:S(2)}, u32[]{:S(2)}) collective-permute-start(f32[49,8,128]{2,1,0:T(8,128)S(1)} %get-tuple-element.38.away_ref), channel_id=1, source_target_pairs={{0,4},{1,5},{2,6},{3,7},{4,0},{5,1},{6,2},{7,3},{8,12},{9,13},{10,... | collective-permute-start | bytes 602120 | tf_op jit(solution)/shard_map/ppermute | solution.py:409
  5.6 9.6 %collective-permute-start.1 = (f32[26,8,128]{2,1,0:T(8,128)S(1)}, f32[26,8,128]{2,1,0:T(8,128)S(1)}, u32[]{:S(2)}, u32[]{:S(2)}) collective-permute-start(f32[26,8,128]{2,1,0:T(8,128)S(1)} %get-tuple-element.46), channel_id=1, source_target_pairs={{0,24},{1,25},{2,26},{3,27},{4,28},{5,29},{6,30},{7,31},{8,16},{9,... | collective-permute-start | bytes 319496 | tf_op jit(solution)/shard_map/ppermute | solution.py:409
  9.5 5.7 %collective-permute-start.2 = (f32[25,8,128]{2,1,0:T(8,128)S(1)}, f32[25,8,128]{2,1,0:T(8,128)S(1)}, u32[]{:S(2)}, u32[]{:S(2)}) collective-permute-start(f32[25,8,128]{2,1,0:T(8,128)S(1)} %get-tuple-element.40._), channel_id=1, source_target_pairs={{0,8},{1,9},{2,10},{3,11},{4,12},{5,13},{6,14},{7,15},{8,0},{9,1},... | collective-permute-start | bytes 307208 | tf_op jit(solution)/shard_map/ppermute | solution.py:409
  10.0 5.2 %collective-permute-start.3 = (f32[25,8,128]{2,1,0:T(8,128)S(1)}, f32[25,8,128]{2,1,0:T(8,128)S(1)}, u32[]{:S(2)}, u32[]{:S(2)}) collective-permute-start(f32[25,8,128]{2,1,0:T(8,128)S(1)} %get-tuple-element.47), channel_id=1, source_target_pairs={{0,16},{1,17},{2,18},{3,19},{4,20},{5,21},{6,22},{7,23},{8,24},{9,... | collective-permute-start | bytes 307208 | tf_op jit(solution)/shard_map/ppermute | solution.py:409
  15.3 6.7 %collective-permute-start.7 = (f32[12,8,512]{2,1,0:T(8,128)S(1)}, f32[12,8,512]{2,1,0:T(8,128)S(1)}, u32[]{:S(2)}, u32[]{:S(2)}) collective-permute-start(f32[12,8,512]{2,1,0:T(8,128)S(1)} %get-tuple-element.51), channel_id=1, source_target_pairs={{0,4},{1,5},{2,6},{3,7},{4,0},{5,1},{6,2},{7,3},{8,12},{9,13},{10,... | collective-permute-start | bytes 589832 | tf_op jit(solution)/shard_map/ppermute | solution.py:409
  15.4 7.8 %collective-permute-start.4 = (f32[8,128]{1,0:T(8,128)S(1)}, f32[8,128]{1,0:T(8,128)S(1)}, u32[]{:S(2)}, u32[]{:S(2)}) collective-permute-start(f32[8,128]{1,0:T(8,128)S(1)} %get-tuple-element.48.rest_0_), channel_id=1, source_target_pairs={{0,1},{1,2},{2,3},{3,0},{4,5},{5,6},{6,7},{7,4},{8,9},{9,10},{10,1... | collective-permute-start | bytes 12296 | tf_op jit(solution)/shard_map/ppermute | solution.py:409
  17.0 6.1 %collective-permute-start.5 = (f32[8,128]{1,0:T(8,128)S(1)}, f32[8,128]{1,0:T(8,128)S(1)}, u32[]{:S(2)}, u32[]{:S(2)}) collective-permute-start(f32[8,128]{1,0:T(8,128)S(1)} %get-tuple-element.48.rest_0_), channel_id=1, source_target_pairs={{0,2},{1,3},{2,0},{3,1},{4,6},{5,7},{6,4},{7,5},{8,10},{9,11},{10,... | collective-permute-start | bytes 12296 | tf_op jit(solution)/shard_map/ppermute | solution.py:409
  19.6 3.6 %collective-permute-start.6 = (f32[8,128]{1,0:T(8,128)S(1)}, f32[8,128]{1,0:T(8,128)S(1)}, u32[]{:S(2)}, u32[]{:S(2)}) collective-permute-start(f32[8,128]{1,0:T(8,128)S(1)} %get-tuple-element.48.rest_0_), channel_id=1, source_target_pairs={{0,3},{1,0},{2,1},{3,2},{4,7},{5,4},{6,5},{7,6},{8,11},{9,8},{10,9... | collective-permute-start | bytes 12296 | tf_op jit(solution)/shard_map/ppermute | solution.py:409

commit v11 on v10

--- a/solution.py
+++ b/solution.py
@@ -9,6 +9,10 @@
 
 SUB = 8
 STRETCHES = 7
+TILES_TO_CHIPS = 3
+TILES_TO_MATE = 22
+TILES_ALONG_GY = 2
+TILES_BACK = 47
 LANES = 128
 MIB = 1024 * 1024
 
@@ -39,7 +43,7 @@
     cells, blocks, chips, lines,
     index_hbm, diffusion_hbm, walls_hbm, velocity_hbm,
     mine_ref, away_ref, pair_ref, chip_ref, left_ref, right_ref, left_h_ref, right_h_ref,
-    ends_ref, volume_ref, velocity_ref,
+    ends_ref, volume_ref, velocity_ref, tile_ref,
     index_ref, diffusion_ref, walls_ref, through_ref, table_ref, held_ref, sems,
 ):
     total = cells * blocks
@@ -226,24 +230,22 @@
             flow = flow + fold(plain - low_part * from_right[0] - high_part * from_left[0])
             totals = low_part * held_ref[6, rows] + high_part * held_ref[5, rows]
             weight = weight + fold(own_extent - diffusion_ref[rows] * totals)
-    slot, middle = away_ref.shape[0] - 1, SUB // 2
-    away_ref[slot, 0:middle] = flow[0:middle] + flow[middle:]
-    away_ref[slot, middle:] = weight[0:middle] + weight[middle:]
-
-
-def merge_kernel(chips, components, mine_ref, away_ref, mate_ref, pair_ref, *rest):
+    middle = SUB // 2
+    for i in range(tile_ref.shape[0]):
+        tile_ref[i, 0:middle] = flow[0:middle] + flow[middle:]
+        tile_ref[i, middle:] = weight[0:middle] + weight[middle:]
+
+
+def merge_kernel(chips, components, mine_ref, mate_ref, pair_ref, *rest):
     send_refs, near_ref = rest[:-1], rest[-1]
     me = lax.axis_index("gz")
     chip = me // 2
     is_first = me == chip * 2
     count = pair_ref.shape[2] // LANES
     half = mine_ref.shape[0] // (2 * components * count)
-    slot = away_ref.shape[0] - 1
-    tile = away_ref[slot] + mate_ref[slot]
-    near_ref[slot] = tile
     for ref in send_refs:
         for at in range(half * components * count, ref.shape[0]):
-            ref[at] = tile
+            ref[at] = jnp.zeros((SUB, LANES), jnp.float32)
     for i in range(half):
         rows = row_tile((me - chip * 2) * half + i)
         for c in range(components):
@@ -266,14 +268,12 @@
 
 
 def spread_kernel(order, components, near_ref, pair_ref, chip_ref, *rest):
-    recv_refs, (own_ref, other_ref, tile_ref) = rest[1:-3], rest[-3:]
+    recv_refs, (own_ref, other_ref) = rest[1:-2], rest[-2:]
     me = lax.axis_index("gz")
     chip = me // 2
     is_first = me == chip * 2
     count = pair_ref.shape[2] // LANES
     half = near_ref.shape[0] // (2 * components * count)
-    tiles = [ref[ref.shape[0] - 1] for ref in (near_ref, *recv_refs)]
-    tile_ref[...] = functools.reduce(jnp.add, tiles)
     for i in range(half):
         rows = row_tile((me - chip * 2) * half + i)
         coefs = [chip_ref[m - 1, rows] for m in order]
@@ -298,6 +298,12 @@
 def leave(copies, source, target, sems):
     copies.append(pltpu.make_async_copy(source, target, sems.at[len(copies)]))
     copies[-1].start()
+
+
+def add_kernel(*refs):
+    total = functools.reduce(jnp.add, [ref[0] for ref in refs[:-1]])
+    for i in range(refs[-1].shape[0]):
+        refs[-1][i] = total
 
 
 def inner_kernel(
@@ -328,52 +334,49 @@
                 base_ref[c, j, rows] = base_ref[c, j, rows] + right * gathered[c]
 
 
-def finish_kernel(side, incoming_ref, base_ref, left_ref, right_ref, *rest):
-    out_hbm, plain_ref, result_ref, sems = rest[-4:]
+def finish_kernel(
+    own_ref, other_ref, base_ref, left_ref, right_ref, out_hbm, plain_ref, result_ref, sems
+):
     components, cells, _, _ = base_ref.shape
-    half = incoming_ref.shape[0] // (2 * components)
+    half = own_ref.shape[0] // (2 * components)
     me = lax.axis_index("gz")
     copies = []
-    for i in range(half):
-        rows = row_tile(lax.rem(me + side, 2) * half + i)
-        near = slice(i * SUB, (i + 1) * SUB)
-        scale = right_ref[cells - 1, rows]
-        at = i * 2 * components
-        lefts = [incoming_ref[at + c] for c in range(components)]
-        rights = [incoming_ref[at + components + c] * scale for c in range(components)]
-        for j in range(cells):
-            left = left_ref[j, rows]
-            right = right_ref[j, rows]
-            for c in range(components):
-                value = base_ref[c, j, rows] + (right * lefts[c] + left * rights[c])
-                if c == 0:
-                    plain_ref[j, near] = value
-                else:
-                    result_ref[c - 1, j, near] = value
-        for c in range(1, components):
-            leave(copies, result_ref.at[c - 1, :, near], out_hbm.at[c, :, rows], sems)
+    for side, incoming_ref in enumerate((own_ref, other_ref)):
+        for i in range(half):
+            rows = row_tile(lax.rem(me + side, 2) * half + i)
+            scale = right_ref[cells - 1, rows]
+            at = i * 2 * components
+            lefts = [incoming_ref[at + c] for c in range(components)]
+            rights = [incoming_ref[at + components + c] * scale for c in range(components)]
+            for j in range(cells):
+                left = left_ref[j, rows]
+                right = right_ref[j, rows]
+                for c in range(components):
+                    value = base_ref[c, j, rows] + (right * lefts[c] + left * rights[c])
+                    if c == 0:
+                        plain_ref[j, rows] = value
+                    else:
+                        result_ref[c - 1, j, rows] = value
+            for c in range(1, components):
+                leave(copies, result_ref.at[c - 1, :, rows], out_hbm.at[c, :, rows], sems)
     for copy in copies:
         copy.wait()
 
 
-def correct_kernel(columns, goal_ref, unit_ref, *rest):
-    tile_refs, plain_refs = rest[:columns], rest[columns:columns + 2]
-    out_hbm, result_ref, sems = rest[-3:]
-    totals = functools.reduce(jnp.add, [ref[...] for ref in tile_refs])
+def correct_kernel(
+    goal_ref, unit_ref, tile_ref, plain_ref, _, out_hbm, result_ref, sems
+):
+    totals = tile_ref[0]
     flow = jnp.sum(totals[0:SUB // 2], keepdims=True)
     weight = jnp.sum(totals[SUB // 2:], keepdims=True)
     alpha = (goal_ref[0:1, 0:1] - flow) / weight
-    cells, middle, _ = plain_refs[0].shape
-    half = middle // SUB
-    me = lax.axis_index("gz")
+    cells, lines_y, _ = plain_ref.shape
     copies = []
-    for side, plain_ref in enumerate(plain_refs):
-        for i in range(half):
-            rows = row_tile(lax.rem(me + side, 2) * half + i)
-            for j in range(cells):
-                plain = plain_ref[j, i * SUB:(i + 1) * SUB]
-                result_ref[j, rows] = plain + alpha * unit_ref[j, rows]
-            leave(copies, result_ref.at[:, rows], out_hbm.at[0, :, rows], sems)
+    for t in range(lines_y // SUB):
+        rows = row_tile(t)
+        for j in range(cells):
+            result_ref[j, rows] = plain_ref[j, rows] + alpha * unit_ref[j, rows]
+        leave(copies, result_ref.at[:, rows], out_hbm.at[0, :, rows], sems)
     for copy in copies:
         copy.wait()
 
@@ -411,15 +414,28 @@
     def to_mate(array):
         return send(array, lambda z, y: (z ^ 1, y))
 
-    middle = half * SUB
+    def to_chip(array, m):
+        return send(array, lambda z, y: (z ^ (2 * m), y))
+
+    def add(tiles, *arrays):
+        return pl.pallas_call(
+            add_kernel,
+            out_shape=shape(tiles, SUB, LANES),
+            in_specs=[vmem] * len(arrays),
+            out_specs=vmem,
+            compiler_params=options(16),
+            cost_estimate=cost(10_000, 40_000),
+            name="add",
+        )(*arrays)
+
     count = lines_x // LANES
     lines = float(lines_y * columns * lines_x)
     (mine, away, pair, chip_coefs, left, right, left_h, right_h, ends, volume,
-     near_velocity) = pl.pallas_call(
+     near_velocity, tile) = pl.pallas_call(
         functools.partial(ladder_kernel, cells, blocks, chips, lines),
         out_shape=[
             shape(half * 2 * components * count, SUB, LANES),
-            shape(half * 2 * components * count + 1, SUB, LANES),
+            shape(half * 2 * components * count, SUB, LANES),
             shape(4, *plane),
             shape(chips - 1, *plane),
             shape(cells, *plane),
@@ -429,9 +445,10 @@
             shape(2, *plane),
             shape(SUB, LANES),
             shape(*velocity.shape),
+            shape(TILES_TO_CHIPS, SUB, LANES),
         ],
         in_specs=[anywhere] * 4,
-        out_specs=[vmem] * 11,
+        out_specs=[vmem] * 12,
         scratch_shapes=[
             pltpu.SMEM(stretch_index.shape, jnp.int32),
             pltpu.VMEM(plane, f32),
@@ -447,19 +464,25 @@
     )(in_hbm(stretch_index), in_hbm(diffusion), in_hbm(wall_types), in_hbm(velocity))
 
     mate = to_mate(away)
+    order = sorted(range(1, chips), key=lambda m: -m.bit_count())
+    core_tile = add(TILES_TO_MATE, tile, *[to_chip(tile, m) for m in order])
+    plane_tile = add(TILES_ALONG_GY, core_tile, to_mate(core_tile))
+    gathered = [
+        send(plane_tile, lambda z, y: (z, (y + shift) % columns)) for shift in range(1, columns)
+    ]
+    whole_tile = to_mate(add(TILES_BACK, plane_tile, *gathered))
     *outgoing, near = pl.pallas_call(
         functools.partial(merge_kernel, chips, components),
         out_shape=[
-            shape(half * components * count + m.bit_count(), SUB, LANES) for m in range(1, chips)
-        ] + [shape(half * 2 * components * count + 1, SUB, LANES)],
-        in_specs=[vmem] * 4,
+            shape(half * components * count + m.bit_count() - 1, SUB, LANES) for m in range(1, chips)
+        ] + [shape(half * 2 * components * count, SUB, LANES)],
+        in_specs=[vmem] * 3,
         out_specs=[vmem] * chips,
         compiler_params=options(16),
         cost_estimate=cost(500_000, 1_600_000),
         name="merge",
-    )(mine, away, mate, pair)
-    order = sorted(range(1, chips), key=lambda m: -m.bit_count())
-    incoming = [send(outgoing[m - 1], lambda z, y: (z ^ (2 * m), y)) for m in order]
+    )(mine, mate, pair)
+    incoming = [to_chip(outgoing[m - 1], m) for m in order]
     profile = shape(cells, *plane)
     base, unit, goal = pl.pallas_call(
         inner_kernel,
@@ -471,52 +494,43 @@
         name="inner",
     )(near_velocity, left, right, left_h, right_h, ends, volume, bulk_target.reshape(1, 1),
       outgoing[0])
-    own_in, other_out, tile = pl.pallas_call(
+    own_in, other_out = pl.pallas_call(
         functools.partial(spread_kernel, order, components),
-        out_shape=[shape(half * 2 * components, *sheet)] * 2 + [shape(SUB, LANES)],
+        out_shape=[shape(half * 2 * components, *sheet)] * 2,
         in_specs=[vmem] * 3 + [anywhere] + [vmem] * (chips - 1),
-        out_specs=[vmem] * 3,
+        out_specs=[vmem] * 2,
         compiler_params=options(16),
         cost_estimate=cost(500_000, 1_600_000),
         name="spread",
     )(near, pair, chip_coefs, base, *incoming)
     other_in = to_mate(other_out)
-    tiles = [tile] + [
-        send(tile, lambda z, y: (z, (y + shift) % columns)) for shift in range(1, columns)
-    ]
-
-    def finish(side, arrived, *before):
-        return pl.pallas_call(
-            functools.partial(finish_kernel, side),
-            out_shape=[shape(*velocity.shape), shape(cells, middle, lines_x)],
-            in_specs=[vmem] * 4 + [anywhere] * len(before),
-            out_specs=[anywhere, vmem],
-            scratch_shapes=[
-                pltpu.VMEM((components - 1, cells, middle, lines_x), f32),
-                pltpu.SemaphoreType.DMA(((components - 1) * half,)),
-            ],
-            input_output_aliases={4: 0} if before else {},
-            compiler_params=options(16),
-            cost_estimate=cost(3_000_000, 6_000_000),
-            name="finish" + str(side),
-        )(arrived, base, left, right, *before)
-
-    partial, own_plain = finish(0, own_in)
-    partial, other_plain = finish(1, other_in, partial)
+    partial, plain = pl.pallas_call(
+        finish_kernel,
+        out_shape=[shape(*velocity.shape), profile],
+        in_specs=[vmem] * 5,
+        out_specs=[anywhere, vmem],
+        scratch_shapes=[
+            pltpu.VMEM((components - 1, cells) + plane, f32),
+            pltpu.SemaphoreType.DMA(((components - 1) * row_tiles,)),
+        ],
+        compiler_params=options(16),
+        cost_estimate=cost(3_000_000, 6_000_000),
+        name="finish",
+    )(own_in, other_in, base, left, right)
     return pl.pallas_call(
-        functools.partial(correct_kernel, columns),
+        correct_kernel,
         out_shape=shape(*velocity.shape),
-        in_specs=[vmem] * (4 + columns) + [anywhere],
+        in_specs=[vmem] * 4 + [anywhere],
         out_specs=anywhere,
         scratch_shapes=[
             pltpu.VMEM((cells,) + plane, f32),
             pltpu.SemaphoreType.DMA((row_tiles,)),
         ],
-        input_output_aliases={4 + columns: 0},
+        input_output_aliases={4: 0},
         compiler_params=options(16),
         cost_estimate=cost(500_000, 1_600_000),
         name="correct",
-    )(goal, unit, *tiles, own_plain, other_plain, partial)
+    )(goal, unit, whole_tile, plain, partial)
 
 
 def solution(mesh):

time: 24.5 us -> 26.4 us (1.078)
  starting transfers between devices: 10.7 us -> 14.3 us
  waiting for transfers between devices: 4.54 us -> 3.45 us
  Pallas kernels: 8.43 us -> 7.76 us
    ppermute x8 -> x13, starting transfers between devices: 10.7 us -> 14.3 us  [send(): return lax.ppermute(array, ('gz', 'gy'), route)]
    ppermute x8 -> x13, waiting for transfers between devices: 4.54 us -> 3.45 us  [send(): return lax.ppermute(array, ('gz', 'gy'), route)]
    pallas_call x3 -> x5, Pallas kernels: 3.35 us -> 2.69 us  [the longest x1 1.47 us: shards(): pl.pallas_call(finish_kernel, out_shape=[shape(*velocity.shape), profile]...]
  transfers between devices with their start and end apart: 8 -> 13, of which waited for: 2 -> 3; matrix products, arithmetic and copies ran while one was open for 0% -> 0% of each run, Pallas kernels for 13% -> 10%
where the time goes in v11:
time: 26.4 us; the launch traced here: 26.3 us
  starting transfers between devices  14.3 us (54%)
  Pallas kernels  7.76 us (29%)
  waiting for transfers between devices  3.45 us (13%)
  between operations  0.76 us (3%)
    ppermute x13, starting transfers between devices, send(): return lax.ppermute(array, ('gz', 'gy'), route)  14.3 us
    pallas_call x1, Pallas kernels, shards(): pl.pallas_call(functools.partial(ladder_kernel, cells, blocks, chips, lin...  3.87 us
    ppermute x13, waiting for transfers between devices, send(): return lax.ppermute(array, ('gz', 'gy'), route)  3.45 us
    pallas_call x1, Pallas kernels, shards(): pl.pallas_call(finish_kernel, out_shape=[shape(*velocity.shape), profile]...  1.47 us
    pallas_call x1, Pallas kernels, shards(): pl.pallas_call(correct_kernel, out_shape=shape(*velocity.shape), in_specs...  1.19 us
    pallas_call x1, Pallas kernels, shards(): pl.pallas_call(inner_kernel, out_shape=[shape(*velocity.shape), profile,...  1.05 us
  transfers between devices with their start and end apart: 13, of which 3 were waited for; matrix products, arithmetic and copies ran while one was open for 0% of the time, Pallas kernels for 10%

profile of v11, /device:TPU:0, one launch (start us, length us, event | category | flops | bytes accessed | tf_op | source)
XLA Modules:
  0.0 26.3 jit_solution(13497158364905025214)
XLA Ops:
  0.0 3.9 %ladder.1 = (f32[48,8,128]{2,1,0:T(8,128)S(1)}, f32[48,8,128]{2,1,0:T(8,128)S(1)}, f32[4,32,512]{2,1,0:T(8,128)S(1)}, f32[3,32,512]{2,1,0:T(8,128)S(1)}, f32[16,...) custom-call(s32[128]{0:T(128)} %index_hbm.1, ...), custom_call_target="tpu_custom_call" | custom-call | flops 40000000 | bytes 6000000 | tf_op jit(solution)/shard_map/ladder/pallas_call | solution.py:434
  3.9 0.5 %collective-permute-start = (f32[48,8,128]{2,1,0:T(8,128)S(1)}, f32[48,8,128]{2,1,0:T(8,128)S(1)}, u32[]{:S(2)}, u32[]{:S(2)}) collective-permute-start(f32[48,8,128]{2,1,0:T(8,128)S(1)} %get-tuple-element.36), channel_id=1, source_target_pairs={{0,4},{1,5},{2,6},{3,7},{4,0},{5,1},{6,2},{7,3},{8,12},{9,13},{10,... | collective-permute-start | bytes 589832 | tf_op jit(solution)/shard_map/ppermute | solution.py:412
  4.4 3.5 %collective-permute-start.1 = (f32[3,8,128]{2,1,0:T(8,128)S(1)}, f32[3,8,128]{2,1,0:T(8,128)S(1)}, u32[]{:S(2)}, u32[]{:S(2)}) collective-permute-start(f32[3,8,128]{2,1,0:T(8,128)S(1)} %get-tuple-element.41.refs_0_), channel_id=1, source_target_pairs={{0,24},{1,25},{2,26},{3,27},{4,28},{5,29},{6,30},{7,31},{8,16},{9,... | collective-permute-start | bytes 36872 | tf_op jit(solution)/shard_map/ppermute | solution.py:412
  7.9 0.5 %collective-permute-start.2 = (f32[3,8,128]{2,1,0:T(8,128)S(1)}, f32[3,8,128]{2,1,0:T(8,128)S(1)}, u32[]{:S(2)}, u32[]{:S(2)}) collective-permute-start(f32[3,8,128]{2,1,0:T(8,128)S(1)} %get-tuple-element.41.refs_0_), channel_id=1, source_target_pairs={{0,8},{1,9},{2,10},{3,11},{4,12},{5,13},{6,14},{7,15},{8,0},{9,1},... | collective-permute-start | bytes 36872 | tf_op jit(solution)/shard_map/ppermute | solution.py:412
  8.4 0.1 collective-permute-start.3
  8.6 0.0 collective-permute-done.mate_ref
  8.6 0.1 merge.1
  8.6 2.9 %collective-permute-start.9 = (f32[25,8,128]{2,1,0:T(8,128)S(1)}, f32[25,8,128]{2,1,0:T(8,128)S(1)}, u32[]{:S(2)}, u32[]{:S(2)}) collective-permute-start(f32[25,8,128]{2,1,0:T(8,128)S(1)} %get-tuple-element.45), channel_id=1, source_target_pairs={{0,24},{1,25},{2,26},{3,27},{4,28},{5,29},{6,30},{7,31},{8,16},{9,... | collective-permute-start | bytes 307208 | tf_op jit(solution)/shard_map/ppermute | solution.py:412
  11.5 0.5 %collective-permute-start.10 = (f32[24,8,128]{2,1,0:T(8,128)S(1)}, f32[24,8,128]{2,1,0:T(8,128)S(1)}, u32[]{:S(2)}, u32[]{:S(2)}) collective-permute-start(f32[24,8,128]{2,1,0:T(8,128)S(1)} %get-tuple-element.38._), channel_id=1, source_target_pairs={{0,8},{1,9},{2,10},{3,11},{4,12},{5,13},{6,14},{7,15},{8,0},{9,1},... | collective-permute-start | bytes 294920 | tf_op jit(solution)/shard_map/ppermute | solution.py:412
  12.1 0.0 collective-permute-done.1.refs_1_
  12.1 0.1 collective-permute-start.11
  12.2 0.0 collective-permute-done.2.refs_2_
  12.2 1.3 %collective-permute-done.3.refs_3_ = f32[3,8,128]{2,1,0:T(8,128)S(1)} collective-permute-done((f32[3,8,128]{2,1,0:T(8,128)S(1)}, f32[3,8,128]{2,1,0:T(8,128)S(1)}, u32[]{:S(2)}, u32[]{:S(2)}) %collective-permute-start.3) | collective-permute-done | bytes 12320 | tf_op jit(solution)/shard_map/ppermute | solution.py:412
  13.5 0.1 collective-permute-start.4
  13.6 1.3 %collective-permute-done.4.refs_1_ = f32[22,8,128]{2,1,0:T(8,128)S(1)} collective-permute-done((f32[22,8,128]{2,1,0:T(8,128)S(1)}, f32[22,8,128]{2,1,0:T(8,128)S(1)}, u32[]{:S(2)}, u32[]{:S(2)}) %collective-permute-start.4) | collective-permute-done | bytes 90144 | tf_op jit(solution)/shard_map/ppermute | solution.py:412
  14.9 0.6 %collective-permute-start.5 = (f32[2,8,128]{2,1,0:T(8,128)S(1)}, f32[2,8,128]{2,1,0:T(8,128)S(1)}, u32[]{:S(2)}, u32[]{:S(2)}) collective-permute-start(f32[2,8,128]{2,1,0:T(8,128)S(1)} %add.4.refs_0_), channel_id=1, source_target_pairs={{0,1},{1,2},{2,3},{3,0},{4,5},{5,6},{6,7},{7,4},{8,9},{9,10},{10,1... | collective-permute-start | bytes 24584 | tf_op jit(solution)/shard_map/ppermute | solution.py:412
  15.5 2.6 %collective-permute-start.6 = (f32[2,8,128]{2,1,0:T(8,128)S(1)}, f32[2,8,128]{2,1,0:T(8,128)S(1)}, u32[]{:S(2)}, u32[]{:S(2)}) collective-permute-start(f32[2,8,128]{2,1,0:T(8,128)S(1)} %add.4.refs_0_), channel_id=1, source_target_pairs={{0,2},{1,3},{2,0},{3,1},{4,6},{5,7},{6,4},{7,5},{8,10},{9,11},{10,... | collective-permute-start | bytes 24584 | tf_op jit(solution)/shard_map/ppermute | solution.py:412
  18.1 0.0 collective-permute-done.10.rest_2_
  18.1 2.1 %collective-permute-start.7 = (f32[2,8,128]{2,1,0:T(8,128)S(1)}, f32[2,8,128]{2,1,0:T(8,128)S(1)}, u32[]{:S(2)}, u32[]{:S(2)}) collective-permute-start(f32[2,8,128]{2,1,0:T(8,128)S(1)} %add.4.refs_0_), channel_id=1, source_target_pairs={{0,3},{1,0},{2,1},{3,2},{4,7},{5,4},{6,5},{7,6},{8,11},{9,8},{10,9... | collective-permute-start | bytes 24584 | tf_op jit(solution)/shard_map/ppermute | solution.py:412
  20.9 1.0 %inner.1 = (f32[3,16,32,512]{3,2,1,0:T(8,128)S(1)}, f32[16,32,512]{2,1,0:T(8,128)S(1)}, f32[8,128]{1,0:T(8,128)S(1)}) custom-call(f32[3,16,32,512]{3,2,1,0:T(8,128)S(1)} %get-tuple-element.28.velocity_ref, f32[16,32,512]{2,1,0:T(8,128)S(1)} %get-tuple-element.29.left_ref, f32[16,32,512]{2,1,0:T(8,128)S(1)} %get-tuple-element.30.right_ref, ...), custom_call_target="tpu_custom_call" | custom-call | flops 8000000 | bytes 8000000 | tf_op jit(solution)/shard_map/inner/pallas_call | solution.py:487
  22.0 0.0 collective-permute-done.11.rest_3_
  22.0 0.0 collective-permute-done.9.rest_1_
  22.0 0.1 spread.1
  22.1 0.1 collective-permute-start.12
  22.2 0.0 collective-permute-done.5.refs_1_
  22.2 0.0 collective-permute-done.6.refs_2_
  22.2 0.0 collective-permute-done.7.refs_3_
  22.2 0.5 %collective-permute-start.8 = (f32[47,8,128]{2,1,0:T(8,128)S(1)}, f32[47,8,128]{2,1,0:T(8,128)S(1)}, u32[]{:S(2)}, u32[]{:S(2)}) collective-permute-start(f32[47,8,128]{2,1,0:T(8,128)S(1)} %add.5), channel_id=1, source_target_pairs={{0,4},{1,5},{2,6},{3,7},{4,0},{5,1},{6,2},{7,3},{8,12},{9,13},{10,... | collective-permute-start | bytes 577544 | tf_op jit(solution)/shard_map/ppermute | solution.py:412
  22.8 0.8 %collective-permute-done.12.other_ref = f32[12,8,512]{2,1,0:T(8,128)S(1)} collective-permute-done((f32[12,8,512]{2,1,0:T(8,128)S(1)}, f32[12,8,512]{2,1,0:T(8,128)S(1)}, u32[]{:S(2)}, u32[]{:S(2)}) %collective-permute-start.12) | collective-permute-done | bytes 196640 | tf_op jit(solution)/shard_map/ppermute | solution.py:412
  23.6 1.5 %finish.1 = (f32[3,16,32,512]{3,2,1,0:T(8,128)}, f32[16,32,512]{2,1,0:T(8,128)S(1)}) custom-call(f32[12,8,512]{2,1,0:T(8,128)S(1)} %get-tuple-element.47.own_ref, f32[12,8,512]{2,1,0:T(8,128)S(1)} %collective-permute-done.12.other_ref, f32[3,16,32,512]{3,2,1,0:T(8,128)S(1)} %get-tuple-element.44.rest_0_.base_ref, ...), custom_call_target="tpu_custom_call" | custom-call | flops 3000000 | bytes 6000000 | tf_op jit(solution)/shard_map/finish/pallas_call | solution.py:507
  25.1 0.0 collective-permute-done.8.tile_ref
  25.1 1.2 %correct.1 = f32[3,16,32,512]{3,2,1,0:T(8,128)} custom-call(f32[8,128]{1,0:T(8,128)S(1)} %get-tuple-element.39.goal_ref, f32[16,32,512]{2,1,0:T(8,128)S(1)} %get-tuple-element.40.unit_ref, f32[47,8,128]{2,1,0:T(8,128)S(1)} %collective-permute-done.8.tile_ref, f32[16,32,512]{2,1,0:T(8,128)S(1)} %get-tuple-element.49.plain_ref, ...), custom_call_target="tpu_custom_call", output_to_operand_aliasing={{}: (4, {})} | custom-call | flops 500000 | bytes 1600000 | tf_op jit(solution)/shard_map/correct/pallas_call | solution.py:520
  (3 shorter events, 0.0 us)
Async XLA Ops:
  3.9 4.7 %collective-permute-start = (f32[48,8,128]{2,1,0:T(8,128)S(1)}, f32[48,8,128]{2,1,0:T(8,128)S(1)}, u32[]{:S(2)}, u32[]{:S(2)}) collective-permute-start(f32[48,8,128]{2,1,0:T(8,128)S(1)} %get-tuple-element.36), channel_id=1, source_target_pairs={{0,4},{1,5},{2,6},{3,7},{4,0},{5,1},{6,2},{7,3},{8,12},{9,13},{10,... | collective-permute-start | bytes 589832 | tf_op jit(solution)/shard_map/ppermute | solution.py:412
  4.4 7.7 %collective-permute-start.1 = (f32[3,8,128]{2,1,0:T(8,128)S(1)}, f32[3,8,128]{2,1,0:T(8,128)S(1)}, u32[]{:S(2)}, u32[]{:S(2)}) collective-permute-start(f32[3,8,128]{2,1,0:T(8,128)S(1)} %get-tuple-element.41.refs_0_), channel_id=1, source_target_pairs={{0,24},{1,25},{2,26},{3,27},{4,28},{5,29},{6,30},{7,31},{8,16},{9,... | collective-permute-start | bytes 36872 | tf_op jit(solution)/shard_map/ppermute | solution.py:412
  7.9 4.3 %collective-permute-start.2 = (f32[3,8,128]{2,1,0:T(8,128)S(1)}, f32[3,8,128]{2,1,0:T(8,128)S(1)}, u32[]{:S(2)}, u32[]{:S(2)}) collective-permute-start(f32[3,8,128]{2,1,0:T(8,128)S(1)} %get-tuple-element.41.refs_0_), channel_id=1, source_target_pairs={{0,8},{1,9},{2,10},{3,11},{4,12},{5,13},{6,14},{7,15},{8,0},{9,1},... | collective-permute-start | bytes 36872 | tf_op jit(solution)/shard_map/ppermute | solution.py:412
  8.4 5.1 %collective-permute-start.3 = (f32[3,8,128]{2,1,0:T(8,128)S(1)}, f32[3,8,128]{2,1,0:T(8,128)S(1)}, u32[]{:S(2)}, u32[]{:S(2)}) collective-permute-start(f32[3,8,128]{2,1,0:T(8,128)S(1)} %get-tuple-element.41.refs_0_), channel_id=1, source_target_pairs={{0,16},{1,17},{2,18},{3,19},{4,20},{5,21},{6,22},{7,23},{8,24},{9,... | collective-permute-start | bytes 36872 | tf_op jit(solution)/shard_map/ppermute | solution.py:412
  8.6 13.4 %collective-permute-start.9 = (f32[25,8,128]{2,1,0:T(8,128)S(1)}, f32[25,8,128]{2,1,0:T(8,128)S(1)}, u32[]{:S(2)}, u32[]{:S(2)}) collective-permute-start(f32[25,8,128]{2,1,0:T(8,128)S(1)} %get-tuple-element.45), channel_id=1, source_target_pairs={{0,24},{1,25},{2,26},{3,27},{4,28},{5,29},{6,30},{7,31},{8,16},{9,... | collective-permute-start | bytes 307208 | tf_op jit(solution)/shard_map/ppermute | solution.py:412
  11.5 6.6 %collective-permute-start.10 = (f32[24,8,128]{2,1,0:T(8,128)S(1)}, f32[24,8,128]{2,1,0:T(8,128)S(1)}, u32[]{:S(2)}, u32[]{:S(2)}) collective-permute-start(f32[24,8,128]{2,1,0:T(8,128)S(1)} %get-tuple-element.38._), channel_id=1, source_target_pairs={{0,8},{1,9},{2,10},{3,11},{4,12},{5,13},{6,14},{7,15},{8,0},{9,1},... | collective-permute-start | bytes 294920 | tf_op jit(solution)/shard_map/ppermute | solution.py:412
  12.1 9.9 %collective-permute-start.11 = (f32[24,8,128]{2,1,0:T(8,128)S(1)}, f32[24,8,128]{2,1,0:T(8,128)S(1)}, u32[]{:S(2)}, u32[]{:S(2)}) collective-permute-start(f32[24,8,128]{2,1,0:T(8,128)S(1)} %get-tuple-element.46), channel_id=1, source_target_pairs={{0,16},{1,17},{2,18},{3,19},{4,20},{5,21},{6,22},{7,23},{8,24},{9,... | collective-permute-start | bytes 294920 | tf_op jit(solution)/shard_map/ppermute | solution.py:412
  13.5 1.4 %collective-permute-start.4 = (f32[22,8,128]{2,1,0:T(8,128)S(1)}, f32[22,8,128]{2,1,0:T(8,128)S(1)}, u32[]{:S(2)}, u32[]{:S(2)}) collective-permute-start(f32[22,8,128]{2,1,0:T(8,128)S(1)} %add.3.refs_0_), channel_id=1, source_target_pairs={{0,4},{1,5},{2,6},{3,7},{4,0},{5,1},{6,2},{7,3},{8,12},{9,13},{10,... | collective-permute-start | bytes 270344 | tf_op jit(solution)/shard_map/ppermute | solution.py:412
  14.9 7.3 %collective-permute-start.5 = (f32[2,8,128]{2,1,0:T(8,128)S(1)}, f32[2,8,128]{2,1,0:T(8,128)S(1)}, u32[]{:S(2)}, u32[]{:S(2)}) collective-permute-start(f32[2,8,128]{2,1,0:T(8,128)S(1)} %add.4.refs_0_), channel_id=1, source_target_pairs={{0,1},{1,2},{2,3},{3,0},{4,5},{5,6},{6,7},{7,4},{8,9},{9,10},{10,1... | collective-permute-start | bytes 24584 | tf_op jit(solution)/shard_map/ppermute | solution.py:412
  15.5 6.7 %collective-permute-start.6 = (f32[2,8,128]{2,1,0:T(8,128)S(1)}, f32[2,8,128]{2,1,0:T(8,128)S(1)}, u32[]{:S(2)}, u32[]{:S(2)}) collective-permute-start(f32[2,8,128]{2,1,0:T(8,128)S(1)} %add.4.refs_0_), channel_id=1, source_target_pairs={{0,2},{1,3},{2,0},{3,1},{4,6},{5,7},{6,4},{7,5},{8,10},{9,11},{10,... | collective-permute-start | bytes 24584 | tf_op jit(solution)/shard_map/ppermute | solution.py:412
  18.1 4.1 %collective-permute-start.7 = (f32[2,8,128]{2,1,0:T(8,128)S(1)}, f32[2,8,128]{2,1,0:T(8,128)S(1)}, u32[]{:S(2)}, u32[]{:S(2)}) collective-permute-start(f32[2,8,128]{2,1,0:T(8,128)S(1)} %add.4.refs_0_), channel_id=1, source_target_pairs={{0,3},{1,0},{2,1},{3,2},{4,7},{5,4},{6,5},{7,6},{8,11},{9,8},{10,9... | collective-permute-start | bytes 24584 | tf_op jit(solution)/shard_map/ppermute | solution.py:412
  22.1 1.5 %collective-permute-start.12 = (f32[12,8,512]{2,1,0:T(8,128)S(1)}, f32[12,8,512]{2,1,0:T(8,128)S(1)}, u32[]{:S(2)}, u32[]{:S(2)}) collective-permute-start(f32[12,8,512]{2,1,0:T(8,128)S(1)} %get-tuple-element.48), channel_id=1, source_target_pairs={{0,4},{1,5},{2,6},{3,7},{4,0},{5,1},{6,2},{7,3},{8,12},{9,13},{10,... | collective-permute-start | bytes 589832 | tf_op jit(solution)/shard_map/ppermute | solution.py:412
  22.2 2.9 %collective-permute-start.8 = (f32[47,8,128]{2,1,0:T(8,128)S(1)}, f32[47,8,128]{2,1,0:T(8,128)S(1)}, u32[]{:S(2)}, u32[]{:S(2)}) collective-permute-start(f32[47,8,128]{2,1,0:T(8,128)S(1)} %add.5), channel_id=1, source_target_pairs={{0,4},{1,5},{2,6},{3,7},{4,0},{5,1},{6,2},{7,3},{8,12},{9,13},{10,... | collective-permute-start | bytes 577544 | tf_op jit(solution)/shard_map/ppermute | solution.py:412

commit v12 on v11

--- a/solution.py
+++ b/solution.py
@@ -9,10 +9,6 @@
 
 SUB = 8
 STRETCHES = 7
-TILES_TO_CHIPS = 3
-TILES_TO_MATE = 22
-TILES_ALONG_GY = 2
-TILES_BACK = 47
 LANES = 128
 MIB = 1024 * 1024
 
@@ -43,7 +39,7 @@
     cells, blocks, chips, lines,
     index_hbm, diffusion_hbm, walls_hbm, velocity_hbm,
     mine_ref, away_ref, pair_ref, chip_ref, left_ref, right_ref, left_h_ref, right_h_ref,
-    ends_ref, volume_ref, velocity_ref, tile_ref,
+    ends_ref, volume_ref, velocity_ref,
     index_ref, diffusion_ref, walls_ref, through_ref, table_ref, held_ref, sems,
 ):
     total = cells * blocks
@@ -139,22 +135,11 @@
         left_h_ref[j] = height(index_ref, me * cells + j) * value
         state["flux"], state["value"] = flux, value
 
-    kappa, own_forward = forward(me, kappa_left, keep_left)
+    _, own_forward = forward(me, kappa_left, keep_left)
     held_ref[1] = own_forward
     held_ref[3] = state["flux"]
     held_ref[4] = state["value"]
     held_ref[5] = state["flux"] - kappa_left
-
-    @pl.when(me == first)
-    def _():
-        pair_ref[2] = own_forward
-        _, after = forward(me + 1, kappa)
-        pair_ref[0] = after
-
-    @pl.when(me != first)
-    def _():
-        pair_ref[2] = through_ref[first]
-        pair_ref[0] = own_forward
 
     kappa_right, product, extent = lax.fori_loop(
         0, blocks - 1 - me, sweep_backward, (upper, ones, extent)
@@ -168,21 +153,15 @@
         right_h_ref[j] = height(index_ref, me * cells + j) * value
         state["flux"] = flux
 
-    kappa, own_backward = backward(me, kappa_right, scale, keep_right)
+    _, own_backward = backward(me, kappa_right, scale, keep_right)
     held_ref[2] = own_backward
     held_ref[6] = state["flux"] - kappa_right * scale
 
-    @pl.when(me == first)
-    def _():
-        pair_ref[1] = own_backward * held_ref[0]
-        pair_ref[3] = through_ref[first + 1]
-
-    @pl.when(me != first)
-    def _():
-        pair_ref[3] = own_backward * held_ref[0]
-        _, after = backward(me - 1, kappa)
-        pair_ref[1] = after
-
+    is_first = me == first
+    forth, back = held_ref[1], own_backward * held_ref[0]
+    pair_ref[0] = jnp.where(is_first, back, forth)
+    pair_ref[1] = jnp.where(is_first, forth, through_ref[first])
+    pair_ref[2] = jnp.where(is_first, through_ref[first + 1], back)
     for m in range(1, chips):
         other = chip ^ m
         low = jnp.minimum(chip, other)
@@ -193,8 +172,6 @@
             lambda r, product: product * (through_ref[2 * r] * through_ref[2 * r + 1]),
             ones,
         )
-    flow = jnp.zeros((SUB, LANES), jnp.float32)
-    weight = jnp.zeros((SUB, LANES), jnp.float32)
 
     def fold(array):
         parts = [array[:, i * LANES:(i + 1) * LANES] for i in range(array.shape[1] // LANES)]
@@ -206,8 +183,10 @@
     half = row_tiles // 2
     own_extent = thickness(me)
     heights = [height(index_ref, me * cells + j) for j in range(cells)]
-    for ref, whose in ((away_ref, 1 - (me - first)), (mine_ref, me - first)):
-        for i in range(half):
+
+    def sums(ref, whose):
+        def of_tile(i, state):
+            flow, weight = state
             rows = row_tile(whose * half + i)
             from_left = [0.0] * components
             from_right = [0.0] * components
@@ -227,40 +206,56 @@
                 put(ref, at + components, from_right[c] * held_ref[2, rows])
             low_part = ends_ref[0, rows]
             high_part = ends_ref[1, rows] * held_ref[0, rows]
-            flow = flow + fold(plain - low_part * from_right[0] - high_part * from_left[0])
             totals = low_part * held_ref[6, rows] + high_part * held_ref[5, rows]
-            weight = weight + fold(own_extent - diffusion_ref[rows] * totals)
-    middle = SUB // 2
-    for i in range(tile_ref.shape[0]):
-        tile_ref[i, 0:middle] = flow[0:middle] + flow[middle:]
-        tile_ref[i, middle:] = weight[0:middle] + weight[middle:]
-
-
-def merge_kernel(chips, components, mine_ref, mate_ref, pair_ref, *rest):
+            return (
+                flow + fold(plain - low_part * from_right[0] - high_part * from_left[0]),
+                weight + fold(own_extent - diffusion_ref[rows] * totals),
+            )
+
+        return of_tile
+
+    state = (jnp.zeros((SUB, LANES), jnp.float32),) * 2
+    mates = 1 - (me - first)
+    state = lax.fori_loop(0, half, sums(away_ref, mates), state)
+    flow, weight = lax.fori_loop(0, half, sums(mine_ref, me - first), state)
+    for i in range(half):
+        put(away_ref, half * 2 * components + i, pair_ref[0, row_tile(mates * half + i)])
+    slot, middle = away_ref.shape[0] - 1, SUB // 2
+    away_ref[slot, 0:middle] = flow[0:middle] + flow[middle:]
+    away_ref[slot, middle:] = weight[0:middle] + weight[middle:]
+
+
+def merge_kernel(chips, components, mine_ref, away_ref, mate_ref, pair_ref, *rest):
     send_refs, near_ref = rest[:-1], rest[-1]
     me = lax.axis_index("gz")
     chip = me // 2
     is_first = me == chip * 2
     count = pair_ref.shape[2] // LANES
     half = mine_ref.shape[0] // (2 * components * count)
+    slot = away_ref.shape[0] - 1
+    tile = away_ref[slot] + mate_ref[slot]
+    near_ref[near_ref.shape[0] - 1] = tile
     for ref in send_refs:
         for at in range(half * components * count, ref.shape[0]):
-            ref[at] = jnp.zeros((SUB, LANES), jnp.float32)
+            ref[at] = tile
     for i in range(half):
         rows = row_tile((me - chip * 2) * half + i)
+        mine, mate = pair_ref[0, rows], get(mate_ref, half * 2 * components + i, count)
+        forth = jnp.where(is_first, mate, mine)
+        back = jnp.where(is_first, mine, mate)
         for c in range(components):
             at = i * 2 * components + c
             mine, mate = get(mine_ref, at, count), get(mate_ref, at, count)
             first = jnp.where(is_first, mine, mate)
             second = jnp.where(is_first, mate, mine)
             put(near_ref, at, first)
-            to_right = second + pair_ref[0, rows] * first
+            to_right = second + forth * first
             at = at + components
             mine, mate = get(mine_ref, at, count), get(mate_ref, at, count)
             first = jnp.where(is_first, mine, mate)
             second = jnp.where(is_first, mate, mine)
             put(near_ref, at, second)
-            to_left = first + pair_ref[1, rows] * second
+            to_left = first + back * second
             for m in range(1, chips):
                 goes_right = (chip ^ m) > chip
                 sheet = jnp.where(goes_right, to_right, to_left)
@@ -268,12 +263,18 @@
 
 
 def spread_kernel(order, components, near_ref, pair_ref, chip_ref, *rest):
-    recv_refs, (own_ref, other_ref) = rest[1:-2], rest[-2:]
+    recv_refs = rest[1:len(order) + 1]
+    own_ref, other_ref, *tile_refs = rest[len(order) + 1:]
     me = lax.axis_index("gz")
     chip = me // 2
     is_first = me == chip * 2
     count = pair_ref.shape[2] // LANES
     half = near_ref.shape[0] // (2 * components * count)
+    tiles = [ref[ref.shape[0] - 1] for ref in (near_ref, *recv_refs)]
+    tile = functools.reduce(jnp.add, tiles)
+    for ref in tile_refs:
+        for i in range(ref.shape[0]):
+            ref[i] = tile
     for i in range(half):
         rows = row_tile((me - chip * 2) * half + i)
         coefs = [chip_ref[m - 1, rows] for m in order]
@@ -286,24 +287,13 @@
                 left_in = left_in + jnp.where(from_left, term, 0.0)
                 right_in = right_in + jnp.where(from_left, 0.0, term)
             at = i * 2 * components + c
-            left_second = get(near_ref, at, count) + pair_ref[2, rows] * left_in
-            right_first = get(near_ref, at + components, count) + pair_ref[3, rows] * right_in
+            left_second = get(near_ref, at, count) + pair_ref[1, rows] * left_in
+            right_first = get(near_ref, at + components, count) + pair_ref[2, rows] * right_in
             own_ref[at] = jnp.where(is_first, left_in, left_second)
             other_ref[at] = jnp.where(is_first, left_second, left_in)
             at = at + components
             own_ref[at] = jnp.where(is_first, right_first, right_in)
             other_ref[at] = jnp.where(is_first, right_in, right_first)
-
-
-def leave(copies, source, target, sems):
-    copies.append(pltpu.make_async_copy(source, target, sems.at[len(copies)]))
-    copies[-1].start()
-
-
-def add_kernel(*refs):
-    total = functools.reduce(jnp.add, [ref[0] for ref in refs[:-1]])
-    for i in range(refs[-1].shape[0]):
-        refs[-1][i] = total
 
 
 def inner_kernel(
@@ -312,7 +302,8 @@
 ):
     components, cells, lines_y, lines_x = velocity_ref.shape
     goal_ref[...] = target_ref[...] * volume_ref[...]
-    for t in range(lines_y // SUB):
+
+    def of_tile(t, _):
         rows = row_tile(t)
         gathered = [jnp.zeros((SUB, lines_x), jnp.float32)] * components
         for j in reversed(range(cells)):
@@ -332,18 +323,30 @@
             for c in range(components):
                 gathered[c] = gathered[c] + left * velocity_ref[c, j, rows]
                 base_ref[c, j, rows] = base_ref[c, j, rows] + right * gathered[c]
+        return 0
+
+    lax.fori_loop(0, lines_y // SUB, of_tile, 0)
 
 
 def finish_kernel(
     own_ref, other_ref, base_ref, left_ref, right_ref, out_hbm, plain_ref, result_ref, sems
 ):
-    components, cells, _, _ = base_ref.shape
+    components, cells, lines_y, _ = base_ref.shape
     half = own_ref.shape[0] // (2 * components)
     me = lax.axis_index("gz")
-    copies = []
-    for side, incoming_ref in enumerate((own_ref, other_ref)):
-        for i in range(half):
-            rows = row_tile(lax.rem(me + side, 2) * half + i)
+
+    def copies(t):
+        rows = row_tile(t)
+        return [
+            pltpu.make_async_copy(
+                result_ref.at[c - 1, :, rows], out_hbm.at[c, :, rows], sems.at[t, c - 1])
+            for c in range(1, components)
+        ]
+
+    def half_of(incoming_ref, side):
+        def of_tile(i, _):
+            t = lax.rem(me + side, 2) * half + i
+            rows = row_tile(t)
             scale = right_ref[cells - 1, rows]
             at = i * 2 * components
             lefts = [incoming_ref[at + c] for c in range(components)]
@@ -357,28 +360,42 @@
                         plain_ref[j, rows] = value
                     else:
                         result_ref[c - 1, j, rows] = value
-            for c in range(1, components):
-                leave(copies, result_ref.at[c - 1, :, rows], out_hbm.at[c, :, rows], sems)
-    for copy in copies:
-        copy.wait()
-
-
-def correct_kernel(
-    goal_ref, unit_ref, tile_ref, plain_ref, _, out_hbm, result_ref, sems
-):
-    totals = tile_ref[0]
+            for copy in copies(t):
+                copy.start()
+            return 0
+
+        lax.fori_loop(0, half, of_tile, 0)
+
+    half_of(own_ref, 0)
+    half_of(other_ref, 1)
+    for t in range(lines_y // SUB):
+        for copy in copies(t):
+            copy.wait()
+
+
+def correct_kernel(columns, goal_ref, unit_ref, *rest):
+    tile_refs = rest[:columns]
+    plain_ref, _, out_hbm, result_ref, sems = rest[columns:]
+    totals = functools.reduce(jnp.add, [ref[0] for ref in tile_refs])
     flow = jnp.sum(totals[0:SUB // 2], keepdims=True)
     weight = jnp.sum(totals[SUB // 2:], keepdims=True)
     alpha = (goal_ref[0:1, 0:1] - flow) / weight
     cells, lines_y, _ = plain_ref.shape
-    copies = []
-    for t in range(lines_y // SUB):
+
+    def copy(t):
+        rows = row_tile(t)
+        return pltpu.make_async_copy(result_ref.at[:, rows], out_hbm.at[0, :, rows], sems.at[t])
+
+    def of_tile(t, _):
         rows = row_tile(t)
         for j in range(cells):
             result_ref[j, rows] = plain_ref[j, rows] + alpha * unit_ref[j, rows]
-        leave(copies, result_ref.at[:, rows], out_hbm.at[0, :, rows], sems)
-    for copy in copies:
-        copy.wait()
+        copy(t).start()
+        return 0
+
+    lax.fori_loop(0, lines_y // SUB, of_tile, 0)
+    for t in range(lines_y // SUB):
+        copy(t).wait()
 
 
 def shards(velocity, diffusion, wall_types, stretch_index, bulk_target):
@@ -414,29 +431,15 @@
     def to_mate(array):
         return send(array, lambda z, y: (z ^ 1, y))
 
-    def to_chip(array, m):
-        return send(array, lambda z, y: (z ^ (2 * m), y))
-
-    def add(tiles, *arrays):
-        return pl.pallas_call(
-            add_kernel,
-            out_shape=shape(tiles, SUB, LANES),
-            in_specs=[vmem] * len(arrays),
-            out_specs=vmem,
-            compiler_params=options(16),
-            cost_estimate=cost(10_000, 40_000),
-            name="add",
-        )(*arrays)
-
     count = lines_x // LANES
     lines = float(lines_y * columns * lines_x)
     (mine, away, pair, chip_coefs, left, right, left_h, right_h, ends, volume,
-     near_velocity, tile) = pl.pallas_call(
+     near_velocity) = pl.pallas_call(
         functools.partial(ladder_kernel, cells, blocks, chips, lines),
         out_shape=[
             shape(half * 2 * components * count, SUB, LANES),
-            shape(half * 2 * components * count, SUB, LANES),
-            shape(4, *plane),
+            shape(half * (2 * components + 1) * count + 1, SUB, LANES),
+            shape(3, *plane),
             shape(chips - 1, *plane),
             shape(cells, *plane),
             shape(cells, *plane),
@@ -445,10 +448,9 @@
             shape(2, *plane),
             shape(SUB, LANES),
             shape(*velocity.shape),
-            shape(TILES_TO_CHIPS, SUB, LANES),
         ],
         in_specs=[anywhere] * 4,
-        out_specs=[vmem] * 12,
+        out_specs=[vmem] * 11,
         scratch_shapes=[
             pltpu.SMEM(stretch_index.shape, jnp.int32),
             pltpu.VMEM(plane, f32),
@@ -464,25 +466,19 @@
     )(in_hbm(stretch_index), in_hbm(diffusion), in_hbm(wall_types), in_hbm(velocity))
 
     mate = to_mate(away)
-    order = sorted(range(1, chips), key=lambda m: -m.bit_count())
-    core_tile = add(TILES_TO_MATE, tile, *[to_chip(tile, m) for m in order])
-    plane_tile = add(TILES_ALONG_GY, core_tile, to_mate(core_tile))
-    gathered = [
-        send(plane_tile, lambda z, y: (z, (y + shift) % columns)) for shift in range(1, columns)
-    ]
-    whole_tile = to_mate(add(TILES_BACK, plane_tile, *gathered))
     *outgoing, near = pl.pallas_call(
         functools.partial(merge_kernel, chips, components),
         out_shape=[
-            shape(half * components * count + m.bit_count() - 1, SUB, LANES) for m in range(1, chips)
-        ] + [shape(half * 2 * components * count, SUB, LANES)],
-        in_specs=[vmem] * 3,
+            shape(half * components * count + m.bit_count(), SUB, LANES) for m in range(1, chips)
+        ] + [shape(half * 2 * components * count + 1, SUB, LANES)],
+        in_specs=[vmem] * 4,
         out_specs=[vmem] * chips,
         compiler_params=options(16),
         cost_estimate=cost(500_000, 1_600_000),
         name="merge",
-    )(mine, mate, pair)
-    incoming = [to_chip(outgoing[m - 1], m) for m in order]
+    )(mine, away, mate, pair)
+    order = sorted(range(1, chips), key=lambda m: -m.bit_count())
+    incoming = [send(outgoing[m - 1], lambda z, y: (z ^ (2 * m), y)) for m in order]
     profile = shape(cells, *plane)
     base, unit, goal = pl.pallas_call(
         inner_kernel,
@@ -494,16 +490,21 @@
         name="inner",
     )(near_velocity, left, right, left_h, right_h, ends, volume, bulk_target.reshape(1, 1),
       outgoing[0])
-    own_in, other_out = pl.pallas_call(
+    own_in, other_out, *tile = pl.pallas_call(
         functools.partial(spread_kernel, order, components),
-        out_shape=[shape(half * 2 * components, *sheet)] * 2,
+        out_shape=[shape(half * 2 * components, *sheet)] * 2
+        + [shape(columns - shift, SUB, LANES) for shift in range(1, columns)],
         in_specs=[vmem] * 3 + [anywhere] + [vmem] * (chips - 1),
-        out_specs=[vmem] * 2,
+        out_specs=[vmem] * (1 + columns),
         compiler_params=options(16),
         cost_estimate=cost(500_000, 1_600_000),
         name="spread",
     )(near, pair, chip_coefs, base, *incoming)
     other_in = to_mate(other_out)
+    tiles = [tile[0]] + [
+        send(tile[shift - 1], lambda z, y: (z, (y + shift) % columns))
+        for shift in range(1, columns)
+    ]
     partial, plain = pl.pallas_call(
         finish_kernel,
         out_shape=[shape(*velocity.shape), profile],
@@ -511,26 +512,26 @@
         out_specs=[anywhere, vmem],
         scratch_shapes=[
             pltpu.VMEM((components - 1, cells) + plane, f32),
-            pltpu.SemaphoreType.DMA(((components - 1) * row_tiles,)),
+            pltpu.SemaphoreType.DMA((row_tiles, components - 1)),
         ],
         compiler_params=options(16),
         cost_estimate=cost(3_000_000, 6_000_000),
         name="finish",
     )(own_in, other_in, base, left, right)
     return pl.pallas_call(
-        correct_kernel,
+        functools.partial(correct_kernel, columns),
         out_shape=shape(*velocity.shape),
-        in_specs=[vmem] * 4 + [anywhere],
+        in_specs=[vmem] * (3 + columns) + [anywhere],
         out_specs=anywhere,
         scratch_shapes=[
             pltpu.VMEM((cells,) + plane, f32),
             pltpu.SemaphoreType.DMA((row_tiles,)),
         ],
-        input_output_aliases={4: 0},
+        input_output_aliases={3 + columns: 0},
         compiler_params=options(16),
         cost_estimate=cost(500_000, 1_600_000),
         name="correct",
-    )(goal, unit, whole_tile, plain, partial)
+    )(goal, unit, *tiles, plain, partial)
 
 
 def solution(mesh):

time: 26.4 us -> 24.3 us (0.920)
  starting transfers between devices: 14.3 us -> 10.7 us
  waiting for transfers between devices: 3.45 us -> 5.25 us
    ppermute x13 -> x8, starting transfers between devices: 14.3 us -> 10.7 us  [send(): return lax.ppermute(array, ('gz', 'gy'), route)]
    ppermute x13 -> x8, waiting for transfers between devices: 3.45 us -> 5.25 us  [send(): return lax.ppermute(array, ('gz', 'gy'), route)]
    pallas_call x4 -> x1, Pallas kernels: 1.22 us -> 1.18 us  [shards(): pl.pallas_call(functools.partial(correct_kernel, columns), out_shape=shap...]
  transfers between devices with their start and end apart: 13 -> 8, of which waited for: 3 -> 4; matrix products, arithmetic and copies ran while one was open for 0% -> 0% of each run, Pallas kernels for 10% -> 10%
where the time goes in v12:
time: 24.3 us; the launch traced here: 24.2 us
  starting transfers between devices  10.7 us (44%)
  Pallas kernels  7.52 us (31%)
  waiting for transfers between devices  5.25 us (22%)
  between operations  0.69 us (3%)
    ppermute x8, starting transfers between devices, send(): return lax.ppermute(array, ('gz', 'gy'), route)  10.7 us
    ppermute x8, waiting for transfers between devices, send(): return lax.ppermute(array, ('gz', 'gy'), route)  5.25 us
    pallas_call x1, Pallas kernels, shards(): pl.pallas_call(functools.partial(ladder_kernel, cells, blocks, chips, lin...  3.67 us
    pallas_call x1, Pallas kernels, shards(): pl.pallas_call(finish_kernel, out_shape=[shape(*velocity.shape), profile]...  1.45 us
    pallas_call x1, Pallas kernels, shards(): pl.pallas_call(functools.partial(correct_kernel, columns), out_shape=shap...  1.18 us
    pallas_call x1, Pallas kernels, shards(): pl.pallas_call(inner_kernel, out_shape=[shape(*velocity.shape), profile,...  1.06 us
  transfers between devices with their start and end apart: 8, of which 4 were waited for; matrix products, arithmetic and copies ran while one was open for 0% of the time, Pallas kernels for 10%

profile of v12, /device:TPU:0, one launch (start us, length us, event | category | flops | bytes accessed | tf_op | source)
XLA Modules:
  0.0 24.2 jit_solution(10354284883580156903)
XLA Ops:
  0.0 3.7 %ladder.1 = (f32[48,8,128]{2,1,0:T(8,128)S(1)}, f32[57,8,128]{2,1,0:T(8,128)S(1)}, f32[3,32,512]{2,1,0:T(8,128)S(1)}, f32[3,32,512]{2,1,0:T(8,128)S(1)}, f32[16,...) custom-call(s32[128]{0:T(128)} %index_hbm.1, ...), custom_call_target="tpu_custom_call" | custom-call | flops 40000000 | bytes 6000000 | tf_op jit(solution)/shard_map/ladder/pallas_call | solution.py:437
  3.7 0.5 %collective-permute-start = (f32[57,8,128]{2,1,0:T(8,128)S(1)}, f32[57,8,128]{2,1,0:T(8,128)S(1)}, u32[]{:S(2)}, u32[]{:S(2)}) collective-permute-start(f32[57,8,128]{2,1,0:T(8,128)S(1)} %get-tuple-element.38.away_ref), channel_id=1, source_target_pairs={{0,4},{1,5},{2,6},{3,7},{4,0},{5,1},{6,2},{7,3},{8,12},{9,13},{10,... | collective-permute-start | bytes 700424 | tf_op jit(solution)/shard_map/ppermute | solution.py:429
  4.2 1.1 %collective-permute-done.mate_ref = f32[57,8,128]{2,1,0:T(8,128)S(1)} collective-permute-done((f32[57,8,128]{2,1,0:T(8,128)S(1)}, f32[57,8,128]{2,1,0:T(8,128)S(1)}, u32[]{:S(2)}, u32[]{:S(2)}) %collective-permute-start) | collective-permute-done | bytes 233504 | tf_op jit(solution)/shard_map/ppermute | solution.py:429
  5.3 0.1 merge.1
  5.4 3.9 %collective-permute-start.1 = (f32[26,8,128]{2,1,0:T(8,128)S(1)}, f32[26,8,128]{2,1,0:T(8,128)S(1)}, u32[]{:S(2)}, u32[]{:S(2)}) collective-permute-start(f32[26,8,128]{2,1,0:T(8,128)S(1)} %get-tuple-element.46), channel_id=1, source_target_pairs={{0,24},{1,25},{2,26},{3,27},{4,28},{5,29},{6,30},{7,31},{8,16},{9,... | collective-permute-start | bytes 319496 | tf_op jit(solution)/shard_map/ppermute | solution.py:429
  9.3 0.5 %collective-permute-start.3 = (f32[25,8,128]{2,1,0:T(8,128)S(1)}, f32[25,8,128]{2,1,0:T(8,128)S(1)}, u32[]{:S(2)}, u32[]{:S(2)}) collective-permute-start(f32[25,8,128]{2,1,0:T(8,128)S(1)} %get-tuple-element.47), channel_id=1, source_target_pairs={{0,16},{1,17},{2,18},{3,19},{4,20},{5,21},{6,22},{7,23},{8,24},{9,... | collective-permute-start | bytes 307208 | tf_op jit(solution)/shard_map/ppermute | solution.py:429
  9.7 0.2 collective-permute-start.2
  10.6 1.1 %inner.1 = (f32[3,16,32,512]{3,2,1,0:T(8,128)S(1)}, f32[16,32,512]{2,1,0:T(8,128)S(1)}, f32[8,128]{1,0:T(8,128)S(1)}) custom-call(f32[3,16,32,512]{3,2,1,0:T(8,128)S(1)} %get-tuple-element.30.velocity_ref, f32[16,32,512]{2,1,0:T(8,128)S(1)} %get-tuple-element.31.left_ref, f32[16,32,512]{2,1,0:T(8,128)S(1)} %get-tuple-element.32.right_ref, ...), custom_call_target="tpu_custom_call" | custom-call | flops 8000000 | bytes 8000000 | tf_op jit(solution)/shard_map/inner/pallas_call | solution.py:483
  11.6 3.1 %collective-permute-done.3.rest_3_ = f32[25,8,128]{2,1,0:T(8,128)S(1)} collective-permute-done((f32[25,8,128]{2,1,0:T(8,128)S(1)}, f32[25,8,128]{2,1,0:T(8,128)S(1)}, u32[]{:S(2)}, u32[]{:S(2)}) %collective-permute-start.3) | collective-permute-done | bytes 102432 | tf_op jit(solution)/shard_map/ppermute | solution.py:429
  14.7 0.2 collective-permute-done.2.rest_2_
  15.0 0.0 collective-permute-done.1.rest_1_
  15.0 0.1 spread.1
  15.1 0.1 collective-permute-start.7
  15.1 1.6 %collective-permute-start.4 = (f32[3,8,128]{2,1,0:T(8,128)S(1)}, f32[3,8,128]{2,1,0:T(8,128)S(1)}, u32[]{:S(2)}, u32[]{:S(2)}) collective-permute-start(f32[3,8,128]{2,1,0:T(8,128)S(1)} %get-tuple-element.48.rest_0_), channel_id=1, source_target_pairs={{0,1},{1,2},{2,3},{3,0},{4,5},{5,6},{6,7},{7,4},{8,9},{9,10},{10,1... | collective-permute-start | bytes 36872 | tf_op jit(solution)/shard_map/ppermute | solution.py:429
  16.8 2.6 %collective-permute-start.5 = (f32[2,8,128]{2,1,0:T(8,128)S(1)}, f32[2,8,128]{2,1,0:T(8,128)S(1)}, u32[]{:S(2)}, u32[]{:S(2)}) collective-permute-start(f32[2,8,128]{2,1,0:T(8,128)S(1)} %get-tuple-element.49), channel_id=1, source_target_pairs={{0,2},{1,3},{2,0},{3,1},{4,6},{5,7},{6,4},{7,5},{8,10},{9,11},{10,... | collective-permute-start | bytes 24584 | tf_op jit(solution)/shard_map/ppermute | solution.py:429
  19.4 1.3 %collective-permute-start.6 = (f32[1,8,128]{2,1,0:T(8,128)S(1)}, f32[1,8,128]{2,1,0:T(8,128)S(1)}, u32[]{:S(2)}, u32[]{:S(2)}) collective-permute-start(f32[1,8,128]{2,1,0:T(8,128)S(1)} %get-tuple-element.50), channel_id=1, source_target_pairs={{0,3},{1,0},{2,1},{3,2},{4,7},{5,4},{6,5},{7,6},{8,11},{9,8},{10,9... | collective-permute-start | bytes 12296 | tf_op jit(solution)/shard_map/ppermute | solution.py:429
  20.7 0.0 collective-permute-done.7.other_ref
  20.7 1.5 %finish.1 = (f32[3,16,32,512]{3,2,1,0:T(8,128)}, f32[16,32,512]{2,1,0:T(8,128)S(1)}) custom-call(f32[12,8,512]{2,1,0:T(8,128)S(1)} %get-tuple-element.51.own_ref, f32[12,8,512]{2,1,0:T(8,128)S(1)} %collective-permute-done.7.other_ref, f32[3,16,32,512]{3,2,1,0:T(8,128)S(1)} %get-tuple-element.45.rest_0_.base_ref, ...), custom_call_target="tpu_custom_call" | custom-call | flops 3000000 | bytes 6000000 | tf_op jit(solution)/shard_map/finish/pallas_call | solution.py:508
  22.2 0.8 %collective-permute-done.6.rest_3_ = f32[1,8,128]{2,1,0:T(8,128)S(1)} collective-permute-done((f32[1,8,128]{2,1,0:T(8,128)S(1)}, f32[1,8,128]{2,1,0:T(8,128)S(1)}, u32[]{:S(2)}, u32[]{:S(2)}) %collective-permute-start.6) | collective-permute-done | bytes 4128 | tf_op jit(solution)/shard_map/ppermute | solution.py:429
  23.0 0.0 collective-permute-done.5.rest_2_
  23.0 0.0 collective-permute-done.4.rest_1_
  23.0 1.2 %correct.1 = f32[3,16,32,512]{3,2,1,0:T(8,128)} custom-call(f32[8,128]{1,0:T(8,128)S(1)} %get-tuple-element.41.goal_ref, f32[16,32,512]{2,1,0:T(8,128)S(1)} %get-tuple-element.42.unit_ref, f32[3,8,128]{2,1,0:T(8,128)S(1)} %get-tuple-element.48.rest_0_, f32[3,8,128]{2,1,0:T(8,128)S(1)} %collective-permute-done.4.rest_1_, ...), custom_call_target="tpu_custom_call", output_to_operand_aliasing={{}: (7, {})} | custom-call | flops 500000 | bytes 1600000 | tf_op jit(solution)/shard_map/correct/pallas_call | solution.py:521
Async XLA Ops:
  3.7 1.6 %collective-permute-start = (f32[57,8,128]{2,1,0:T(8,128)S(1)}, f32[57,8,128]{2,1,0:T(8,128)S(1)}, u32[]{:S(2)}, u32[]{:S(2)}) collective-permute-start(f32[57,8,128]{2,1,0:T(8,128)S(1)} %get-tuple-element.38.away_ref), channel_id=1, source_target_pairs={{0,4},{1,5},{2,6},{3,7},{4,0},{5,1},{6,2},{7,3},{8,12},{9,13},{10,... | collective-permute-start | bytes 700424 | tf_op jit(solution)/shard_map/ppermute | solution.py:429
  5.4 9.6 %collective-permute-start.1 = (f32[26,8,128]{2,1,0:T(8,128)S(1)}, f32[26,8,128]{2,1,0:T(8,128)S(1)}, u32[]{:S(2)}, u32[]{:S(2)}) collective-permute-start(f32[26,8,128]{2,1,0:T(8,128)S(1)} %get-tuple-element.46), channel_id=1, source_target_pairs={{0,24},{1,25},{2,26},{3,27},{4,28},{5,29},{6,30},{7,31},{8,16},{9,... | collective-permute-start | bytes 319496 | tf_op jit(solution)/shard_map/ppermute | solution.py:429
  9.3 5.5 %collective-permute-start.3 = (f32[25,8,128]{2,1,0:T(8,128)S(1)}, f32[25,8,128]{2,1,0:T(8,128)S(1)}, u32[]{:S(2)}, u32[]{:S(2)}) collective-permute-start(f32[25,8,128]{2,1,0:T(8,128)S(1)} %get-tuple-element.47), channel_id=1, source_target_pairs={{0,16},{1,17},{2,18},{3,19},{4,20},{5,21},{6,22},{7,23},{8,24},{9,... | collective-permute-start | bytes 307208 | tf_op jit(solution)/shard_map/ppermute | solution.py:429
  9.7 5.2 %collective-permute-start.2 = (f32[25,8,128]{2,1,0:T(8,128)S(1)}, f32[25,8,128]{2,1,0:T(8,128)S(1)}, u32[]{:S(2)}, u32[]{:S(2)}) collective-permute-start(f32[25,8,128]{2,1,0:T(8,128)S(1)} %get-tuple-element.40._), channel_id=1, source_target_pairs={{0,8},{1,9},{2,10},{3,11},{4,12},{5,13},{6,14},{7,15},{8,0},{9,1},... | collective-permute-start | bytes 307208 | tf_op jit(solution)/shard_map/ppermute | solution.py:429
  15.1 5.6 %collective-permute-start.7 = (f32[12,8,512]{2,1,0:T(8,128)S(1)}, f32[12,8,512]{2,1,0:T(8,128)S(1)}, u32[]{:S(2)}, u32[]{:S(2)}) collective-permute-start(f32[12,8,512]{2,1,0:T(8,128)S(1)} %get-tuple-element.52), channel_id=1, source_target_pairs={{0,4},{1,5},{2,6},{3,7},{4,0},{5,1},{6,2},{7,3},{8,12},{9,13},{10,... | collective-permute-start | bytes 589832 | tf_op jit(solution)/shard_map/ppermute | solution.py:429
  15.1 7.8 %collective-permute-start.4 = (f32[3,8,128]{2,1,0:T(8,128)S(1)}, f32[3,8,128]{2,1,0:T(8,128)S(1)}, u32[]{:S(2)}, u32[]{:S(2)}) collective-permute-start(f32[3,8,128]{2,1,0:T(8,128)S(1)} %get-tuple-element.48.rest_0_), channel_id=1, source_target_pairs={{0,1},{1,2},{2,3},{3,0},{4,5},{5,6},{6,7},{7,4},{8,9},{9,10},{10,1... | collective-permute-start | bytes 36872 | tf_op jit(solution)/shard_map/ppermute | solution.py:429
  16.8 6.2 %collective-permute-start.5 = (f32[2,8,128]{2,1,0:T(8,128)S(1)}, f32[2,8,128]{2,1,0:T(8,128)S(1)}, u32[]{:S(2)}, u32[]{:S(2)}) collective-permute-start(f32[2,8,128]{2,1,0:T(8,128)S(1)} %get-tuple-element.49), channel_id=1, source_target_pairs={{0,2},{1,3},{2,0},{3,1},{4,6},{5,7},{6,4},{7,5},{8,10},{9,11},{10,... | collective-permute-start | bytes 24584 | tf_op jit(solution)/shard_map/ppermute | solution.py:429
  19.4 3.6 %collective-permute-start.6 = (f32[1,8,128]{2,1,0:T(8,128)S(1)}, f32[1,8,128]{2,1,0:T(8,128)S(1)}, u32[]{:S(2)}, u32[]{:S(2)}) collective-permute-start(f32[1,8,128]{2,1,0:T(8,128)S(1)} %get-tuple-element.50), channel_id=1, source_target_pairs={{0,3},{1,0},{2,1},{3,2},{4,7},{5,4},{6,5},{7,6},{8,11},{9,8},{10,9... | collective-permute-start | bytes 12296 | tf_op jit(solution)/shard_map/ppermute | solution.py:429

commit v13 on v12

--- a/solution.py
+++ b/solution.py
@@ -11,6 +11,13 @@
 STRETCHES = 7
 LANES = 128
 MIB = 1024 * 1024
+
+
+def plane_rounds(columns):
+    shifts = [[(y, (y + shift) % columns) for y in range(columns)] for shift in range(1, columns)]
+    if columns != 4:
+        return shifts
+    return [shifts[0], [(2, 0)], shifts[2], [(0, 2), (1, 3), (3, 1)]]
 
 
 def row_tile(t):
@@ -373,9 +380,9 @@
             copy.wait()
 
 
-def correct_kernel(columns, goal_ref, unit_ref, *rest):
-    tile_refs = rest[:columns]
-    plain_ref, _, out_hbm, result_ref, sems = rest[columns:]
+def correct_kernel(count, goal_ref, unit_ref, *rest):
+    tile_refs = rest[:count]
+    plain_ref, _, out_hbm, result_ref, sems = rest[count:]
     totals = functools.reduce(jnp.add, [ref[0] for ref in tile_refs])
     flow = jnp.sum(totals[0:SUB // 2], keepdims=True)
     weight = jnp.sum(totals[SUB // 2:], keepdims=True)
@@ -423,13 +430,17 @@
     def cost(flops, transferred):
         return pl.CostEstimate(flops=flops, bytes_accessed=transferred, transcendentals=0)
 
-    def send(array, partner):
-        pairs = [((z, y), partner(z, y)) for z in range(blocks) for y in range(columns)]
-        route = [(a * columns + b, c * columns + d) for (a, b), (c, d) in pairs]
-        return lax.ppermute(array, ("gz", "gy"), route)
+    def send(array, route):
+        flat = [(a * columns + b, c * columns + d) for (a, b), (c, d) in route]
+        return lax.ppermute(array, ("gz", "gy"), flat)
+
+    def to_block(array, other):
+        return send(array, [
+            ((z, y), (z ^ other, y)) for z in range(blocks) for y in range(columns)
+        ])
 
     def to_mate(array):
-        return send(array, lambda z, y: (z ^ 1, y))
+        return to_block(array, 1)
 
     count = lines_x // LANES
     lines = float(lines_y * columns * lines_x)
@@ -478,7 +489,7 @@
         name="merge",
     )(mine, away, mate, pair)
     order = sorted(range(1, chips), key=lambda m: -m.bit_count())
-    incoming = [send(outgoing[m - 1], lambda z, y: (z ^ (2 * m), y)) for m in order]
+    incoming = [to_block(outgoing[m - 1], 2 * m) for m in order]
     profile = shape(cells, *plane)
     base, unit, goal = pl.pallas_call(
         inner_kernel,
@@ -490,20 +501,21 @@
         name="inner",
     )(near_velocity, left, right, left_h, right_h, ends, volume, bulk_target.reshape(1, 1),
       outgoing[0])
+    rounds = plane_rounds(columns)
     own_in, other_out, *tile = pl.pallas_call(
         functools.partial(spread_kernel, order, components),
         out_shape=[shape(half * 2 * components, *sheet)] * 2
-        + [shape(columns - shift, SUB, LANES) for shift in range(1, columns)],
+        + [shape(len(rounds) - i, SUB, LANES) for i in range(len(rounds))],
         in_specs=[vmem] * 3 + [anywhere] + [vmem] * (chips - 1),
-        out_specs=[vmem] * (1 + columns),
+        out_specs=[vmem] * (2 + len(rounds)),
         compiler_params=options(16),
         cost_estimate=cost(500_000, 1_600_000),
         name="spread",
     )(near, pair, chip_coefs, base, *incoming)
     other_in = to_mate(other_out)
     tiles = [tile[0]] + [
-        send(tile[shift - 1], lambda z, y: (z, (y + shift) % columns))
-        for shift in range(1, columns)
+        send(array, [((z, a), (z, b)) for z in range(blocks) for a, b in route])
+        for array, route in zip(tile, rounds)
     ]
     partial, plain = pl.pallas_call(
         finish_kernel,
@@ -519,15 +531,15 @@
         name="finish",
     )(own_in, other_in, base, left, right)
     return pl.pallas_call(
-        functools.partial(correct_kernel, columns),
+        functools.partial(correct_kernel, len(tiles)),
         out_shape=shape(*velocity.shape),
-        in_specs=[vmem] * (3 + columns) + [anywhere],
+        in_specs=[vmem] * (3 + len(tiles)) + [anywhere],
         out_specs=anywhere,
         scratch_shapes=[
             pltpu.VMEM((cells,) + plane, f32),
             pltpu.SemaphoreType.DMA((row_tiles,)),
         ],
-        input_output_aliases={3 + columns: 0},
+        input_output_aliases={3 + len(tiles): 0},
         compiler_params=options(16),
         cost_estimate=cost(500_000, 1_600_000),
         name="correct",

time: 24.3 us -> 26.5 us (1.091)
  starting transfers between devices: 10.7 us -> 13.5 us
  waiting for transfers between devices: 5.25 us -> 4.46 us
    ppermute x8 -> x9, starting transfers between devices: 10.7 us -> 13.5 us  [send(): return lax.ppermute(array, ('gz', 'gy'), flat)]
    ppermute x8 -> x9, waiting for transfers between devices: 5.25 us -> 4.46 us  [send(): return lax.ppermute(array, ('gz', 'gy'), flat)]
  transfers between devices with their start and end apart: 8 -> 9, of which waited for: 4 -> 3; matrix products, arithmetic and copies ran while one was open for 0% -> 0% of each run, Pallas kernels for 10% -> 10%
where the time goes in v13:
time: 26.5 us; the launch traced here: 26.3 us
  starting transfers between devices  13.5 us (51%)
  Pallas kernels  7.54 us (28%)
  waiting for transfers between devices  4.46 us (17%)
  between operations  0.75 us (3%)
    ppermute x9, starting transfers between devices, send(): return lax.ppermute(array, ('gz', 'gy'), flat)  13.5 us
    ppermute x9, waiting for transfers between devices, send(): return lax.ppermute(array, ('gz', 'gy'), flat)  4.46 us
    pallas_call x1, Pallas kernels, shards(): pl.pallas_call(functools.partial(ladder_kernel, cells, blocks, chips, lin...  3.67 us
    pallas_call x1, Pallas kernels, shards(): pl.pallas_call(finish_kernel, out_shape=[shape(*velocity.shape), profile]...  1.47 us
    pallas_call x1, Pallas kernels, shards(): pl.pallas_call(functools.partial(correct_kernel, len(tiles)), out_shape=s...  1.19 us
    pallas_call x1, Pallas kernels, shards(): pl.pallas_call(inner_kernel, out_shape=[shape(*velocity.shape), profile,...  1.06 us
  transfers between devices with their start and end apart: 9, of which 3 were waited for; matrix products, arithmetic and copies ran while one was open for 0% of the time, Pallas kernels for 10%

profile of v13, /device:TPU:0, one launch (start us, length us, event | category | flops | bytes accessed | tf_op | source)
XLA Modules:
  0.0 26.3 jit_solution(5088884927838553737)
XLA Ops:
  0.0 3.7 %ladder.1 = (f32[48,8,128]{2,1,0:T(8,128)S(1)}, f32[57,8,128]{2,1,0:T(8,128)S(1)}, f32[3,32,512]{2,1,0:T(8,128)S(1)}, f32[3,32,512]{2,1,0:T(8,128)S(1)}, f32[16,...) custom-call(s32[128]{0:T(128)} %index_hbm.1, ...), custom_call_target="tpu_custom_call" | custom-call | flops 40000000 | bytes 6000000 | tf_op jit(solution)/shard_map/ladder/pallas_call | solution.py:448
  3.7 0.5 %collective-permute-start = (f32[57,8,128]{2,1,0:T(8,128)S(1)}, f32[57,8,128]{2,1,0:T(8,128)S(1)}, u32[]{:S(2)}, u32[]{:S(2)}) collective-permute-start(f32[57,8,128]{2,1,0:T(8,128)S(1)} %get-tuple-element.39.away_ref), channel_id=1, source_target_pairs={{0,4},{1,5},{2,6},{3,7},{4,0},{5,1},{6,2},{7,3},{8,12},{9,13},{10,... | collective-permute-start | bytes 700424 | tf_op jit(solution)/shard_map/ppermute | solution.py:435
  4.2 1.1 %collective-permute-done.mate_ref = f32[57,8,128]{2,1,0:T(8,128)S(1)} collective-permute-done((f32[57,8,128]{2,1,0:T(8,128)S(1)}, f32[57,8,128]{2,1,0:T(8,128)S(1)}, u32[]{:S(2)}, u32[]{:S(2)}) %collective-permute-start) | collective-permute-done | bytes 233504 | tf_op jit(solution)/shard_map/ppermute | solution.py:435
  5.3 0.1 merge.1
  5.4 3.9 %collective-permute-start.1 = (f32[26,8,128]{2,1,0:T(8,128)S(1)}, f32[26,8,128]{2,1,0:T(8,128)S(1)}, u32[]{:S(2)}, u32[]{:S(2)}) collective-permute-start(f32[26,8,128]{2,1,0:T(8,128)S(1)} %get-tuple-element.47), channel_id=1, source_target_pairs={{0,24},{1,25},{2,26},{3,27},{4,28},{5,29},{6,30},{7,31},{8,16},{9,... | collective-permute-start | bytes 319496 | tf_op jit(solution)/shard_map/ppermute | solution.py:435
  9.3 0.5 %collective-permute-start.3 = (f32[25,8,128]{2,1,0:T(8,128)S(1)}, f32[25,8,128]{2,1,0:T(8,128)S(1)}, u32[]{:S(2)}, u32[]{:S(2)}) collective-permute-start(f32[25,8,128]{2,1,0:T(8,128)S(1)} %get-tuple-element.48), channel_id=1, source_target_pairs={{0,16},{1,17},{2,18},{3,19},{4,20},{5,21},{6,22},{7,23},{8,24},{9,... | collective-permute-start | bytes 307208 | tf_op jit(solution)/shard_map/ppermute | solution.py:435
  9.7 0.2 collective-permute-start.2
  10.6 1.1 %inner.1 = (f32[3,16,32,512]{3,2,1,0:T(8,128)S(1)}, f32[16,32,512]{2,1,0:T(8,128)S(1)}, f32[8,128]{1,0:T(8,128)S(1)}) custom-call(f32[3,16,32,512]{3,2,1,0:T(8,128)S(1)} %get-tuple-element.31.velocity_ref, f32[16,32,512]{2,1,0:T(8,128)S(1)} %get-tuple-element.32.left_ref, f32[16,32,512]{2,1,0:T(8,128)S(1)} %get-tuple-element.33.right_ref, ...), custom_call_target="tpu_custom_call" | custom-call | flops 8000000 | bytes 8000000 | tf_op jit(solution)/shard_map/inner/pallas_call | solution.py:494
  11.6 3.1 %collective-permute-done.3.rest_3_ = f32[25,8,128]{2,1,0:T(8,128)S(1)} collective-permute-done((f32[25,8,128]{2,1,0:T(8,128)S(1)}, f32[25,8,128]{2,1,0:T(8,128)S(1)}, u32[]{:S(2)}, u32[]{:S(2)}) %collective-permute-start.3) | collective-permute-done | bytes 102432 | tf_op jit(solution)/shard_map/ppermute | solution.py:435
  14.7 0.2 collective-permute-done.2.rest_2_
  15.0 0.0 collective-permute-done.1.rest_1_
  15.0 0.1 spread.1
  15.1 0.1 collective-permute-start.8
  15.1 1.6 %collective-permute-start.4 = (f32[4,8,128]{2,1,0:T(8,128)S(1)}, f32[4,8,128]{2,1,0:T(8,128)S(1)}, u32[]{:S(2)}, u32[]{:S(2)}) collective-permute-start(f32[4,8,128]{2,1,0:T(8,128)S(1)} %get-tuple-element.49.rest_0_), channel_id=1, source_target_pairs={{0,1},{1,2},{2,3},{3,0},{4,5},{5,6},{6,7},{7,4},{8,9},{9,10},{10,1... | collective-permute-start | bytes 49160 | tf_op jit(solution)/shard_map/ppermute | solution.py:435
  16.8 1.3 %collective-permute-start.5 = (f32[3,8,128]{2,1,0:T(8,128)S(1)}, f32[3,8,128]{2,1,0:T(8,128)S(1)}, u32[]{:S(2)}, u32[]{:S(2)}) collective-permute-start(f32[3,8,128]{2,1,0:T(8,128)S(1)} %get-tuple-element.50), channel_id=1, source_target_pairs={{2,0},{6,4},{10,8},{14,12},{18,16},{22,20},{26,24},{30,28}} | collective-permute-start | bytes 36872 | tf_op jit(solution)/shard_map/ppermute | solution.py:435
  18.1 1.7 %collective-permute-start.6 = (f32[2,8,128]{2,1,0:T(8,128)S(1)}, f32[2,8,128]{2,1,0:T(8,128)S(1)}, u32[]{:S(2)}, u32[]{:S(2)}) collective-permute-start(f32[2,8,128]{2,1,0:T(8,128)S(1)} %get-tuple-element.51), channel_id=1, source_target_pairs={{0,3},{1,0},{2,1},{3,2},{4,7},{5,4},{6,5},{7,6},{8,11},{9,8},{10,9... | collective-permute-start | bytes 24584 | tf_op jit(solution)/shard_map/ppermute | solution.py:435
  19.7 3.8 %collective-permute-start.7 = (f32[1,8,128]{2,1,0:T(8,128)S(1)}, f32[1,8,128]{2,1,0:T(8,128)S(1)}, u32[]{:S(2)}, u32[]{:S(2)}) collective-permute-start(f32[1,8,128]{2,1,0:T(8,128)S(1)} %get-tuple-element.52), channel_id=1, source_target_pairs={{0,2},{1,3},{3,1},{4,6},{5,7},{7,5},{8,10},{9,11},{11,9},{12,14},{... | collective-permute-start | bytes 12296 | tf_op jit(solution)/shard_map/ppermute | solution.py:435
  23.6 0.0 collective-permute-done.8.other_ref
  23.6 1.5 %finish.1 = (f32[3,16,32,512]{3,2,1,0:T(8,128)}, f32[16,32,512]{2,1,0:T(8,128)S(1)}) custom-call(f32[12,8,512]{2,1,0:T(8,128)S(1)} %get-tuple-element.53.own_ref, f32[12,8,512]{2,1,0:T(8,128)S(1)} %collective-permute-done.8.other_ref, f32[3,16,32,512]{3,2,1,0:T(8,128)S(1)} %get-tuple-element.46.rest_0_.base_ref, ...), custom_call_target="tpu_custom_call" | custom-call | flops 3000000 | bytes 6000000 | tf_op jit(solution)/shard_map/finish/pallas_call | solution.py:520
  25.1 0.0 collective-permute-done.7.rest_4_
  25.1 0.0 collective-permute-done.6.rest_3_
  25.1 0.0 collective-permute-done.5.rest_2_
  25.1 0.0 collective-permute-done.4.rest_1_
  25.1 1.2 %correct.1 = f32[3,16,32,512]{3,2,1,0:T(8,128)} custom-call(f32[8,128]{1,0:T(8,128)S(1)} %get-tuple-element.42.goal_ref, f32[16,32,512]{2,1,0:T(8,128)S(1)} %get-tuple-element.43.unit_ref, f32[4,8,128]{2,1,0:T(8,128)S(1)} %get-tuple-element.49.rest_0_, f32[4,8,128]{2,1,0:T(8,128)S(1)} %collective-permute-done.4.rest_1_, ...), custom_call_target="tpu_custom_call", output_to_operand_aliasing={{}: (8, {})} | custom-call | flops 500000 | bytes 1600000 | tf_op jit(solution)/shard_map/correct/pallas_call | solution.py:533
Async XLA Ops:
  3.7 1.6 %collective-permute-start = (f32[57,8,128]{2,1,0:T(8,128)S(1)}, f32[57,8,128]{2,1,0:T(8,128)S(1)}, u32[]{:S(2)}, u32[]{:S(2)}) collective-permute-start(f32[57,8,128]{2,1,0:T(8,128)S(1)} %get-tuple-element.39.away_ref), channel_id=1, source_target_pairs={{0,4},{1,5},{2,6},{3,7},{4,0},{5,1},{6,2},{7,3},{8,12},{9,13},{10,... | collective-permute-start | bytes 700424 | tf_op jit(solution)/shard_map/ppermute | solution.py:435
  5.4 9.6 %collective-permute-start.1 = (f32[26,8,128]{2,1,0:T(8,128)S(1)}, f32[26,8,128]{2,1,0:T(8,128)S(1)}, u32[]{:S(2)}, u32[]{:S(2)}) collective-permute-start(f32[26,8,128]{2,1,0:T(8,128)S(1)} %get-tuple-element.47), channel_id=1, source_target_pairs={{0,24},{1,25},{2,26},{3,27},{4,28},{5,29},{6,30},{7,31},{8,16},{9,... | collective-permute-start | bytes 319496 | tf_op jit(solution)/shard_map/ppermute | solution.py:435
  9.3 5.5 %collective-permute-start.3 = (f32[25,8,128]{2,1,0:T(8,128)S(1)}, f32[25,8,128]{2,1,0:T(8,128)S(1)}, u32[]{:S(2)}, u32[]{:S(2)}) collective-permute-start(f32[25,8,128]{2,1,0:T(8,128)S(1)} %get-tuple-element.48), channel_id=1, source_target_pairs={{0,16},{1,17},{2,18},{3,19},{4,20},{5,21},{6,22},{7,23},{8,24},{9,... | collective-permute-start | bytes 307208 | tf_op jit(solution)/shard_map/ppermute | solution.py:435
  9.7 5.2 %collective-permute-start.2 = (f32[25,8,128]{2,1,0:T(8,128)S(1)}, f32[25,8,128]{2,1,0:T(8,128)S(1)}, u32[]{:S(2)}, u32[]{:S(2)}) collective-permute-start(f32[25,8,128]{2,1,0:T(8,128)S(1)} %get-tuple-element.41._), channel_id=1, source_target_pairs={{0,8},{1,9},{2,10},{3,11},{4,12},{5,13},{6,14},{7,15},{8,0},{9,1},... | collective-permute-start | bytes 307208 | tf_op jit(solution)/shard_map/ppermute | solution.py:435
  15.1 8.5 %collective-permute-start.8 = (f32[12,8,512]{2,1,0:T(8,128)S(1)}, f32[12,8,512]{2,1,0:T(8,128)S(1)}, u32[]{:S(2)}, u32[]{:S(2)}) collective-permute-start(f32[12,8,512]{2,1,0:T(8,128)S(1)} %get-tuple-element.54), channel_id=1, source_target_pairs={{0,4},{1,5},{2,6},{3,7},{4,0},{5,1},{6,2},{7,3},{8,12},{9,13},{10,... | collective-permute-start | bytes 589832 | tf_op jit(solution)/shard_map/ppermute | solution.py:435
  15.1 10.0 %collective-permute-start.4 = (f32[4,8,128]{2,1,0:T(8,128)S(1)}, f32[4,8,128]{2,1,0:T(8,128)S(1)}, u32[]{:S(2)}, u32[]{:S(2)}) collective-permute-start(f32[4,8,128]{2,1,0:T(8,128)S(1)} %get-tuple-element.49.rest_0_), channel_id=1, source_target_pairs={{0,1},{1,2},{2,3},{3,0},{4,5},{5,6},{6,7},{7,4},{8,9},{9,10},{10,1... | collective-permute-start | bytes 49160 | tf_op jit(solution)/shard_map/ppermute | solution.py:435
  16.8 8.3 %collective-permute-start.5 = (f32[3,8,128]{2,1,0:T(8,128)S(1)}, f32[3,8,128]{2,1,0:T(8,128)S(1)}, u32[]{:S(2)}, u32[]{:S(2)}) collective-permute-start(f32[3,8,128]{2,1,0:T(8,128)S(1)} %get-tuple-element.50), channel_id=1, source_target_pairs={{2,0},{6,4},{10,8},{14,12},{18,16},{22,20},{26,24},{30,28}} | collective-permute-start | bytes 36872 | tf_op jit(solution)/shard_map/ppermute | solution.py:435
  18.1 7.0 %collective-permute-start.6 = (f32[2,8,128]{2,1,0:T(8,128)S(1)}, f32[2,8,128]{2,1,0:T(8,128)S(1)}, u32[]{:S(2)}, u32[]{:S(2)}) collective-permute-start(f32[2,8,128]{2,1,0:T(8,128)S(1)} %get-tuple-element.51), channel_id=1, source_target_pairs={{0,3},{1,0},{2,1},{3,2},{4,7},{5,4},{6,5},{7,6},{8,11},{9,8},{10,9... | collective-permute-start | bytes 24584 | tf_op jit(solution)/shard_map/ppermute | solution.py:435
  19.7 5.3 %collective-permute-start.7 = (f32[1,8,128]{2,1,0:T(8,128)S(1)}, f32[1,8,128]{2,1,0:T(8,128)S(1)}, u32[]{:S(2)}, u32[]{:S(2)}) collective-permute-start(f32[1,8,128]{2,1,0:T(8,128)S(1)} %get-tuple-element.52), channel_id=1, source_target_pairs={{0,2},{1,3},{3,1},{4,6},{5,7},{7,5},{8,10},{9,11},{11,9},{12,14},{... | collective-permute-start | bytes 12296 | tf_op jit(solution)/shard_map/ppermute | solution.py:435

commit v14 on v12

--- a/solution.py
+++ b/solution.py
@@ -17,6 +17,11 @@
     return pl.ds(pl.multiple_of(t * SUB, SUB), SUB)
 
 
+def inverted(array):
+    guess = pl.reciprocal(array, approx=True)
+    return guess * (2.0 - array * guess)
+
+
 def put(ref, at, sheet):
     count = sheet.shape[1] // LANES
     for i in range(count):
@@ -38,9 +43,9 @@
 def ladder_kernel(
     cells, blocks, chips, lines,
     index_hbm, diffusion_hbm, walls_hbm, velocity_hbm,
-    mine_ref, away_ref, pair_ref, chip_ref, left_ref, right_ref, left_h_ref, right_h_ref,
+    mine_ref, away_ref, pair_ref, through_ref, held_ref, left_ref, right_ref, left_h_ref, right_h_ref,
     ends_ref, volume_ref, velocity_ref,
-    index_ref, diffusion_ref, walls_ref, through_ref, table_ref, held_ref, sems,
+    index_ref, diffusion_ref, walls_ref, table_ref, sems,
 ):
     total = cells * blocks
     components = velocity_ref.shape[0]
@@ -62,7 +67,7 @@
     for copy in small:
         copy.wait()
     diffusion = diffusion_ref[...]
-    inverse = 1.0 / diffusion
+    inverse = inverted(diffusion)
     for i in range(STRETCHES):
         table_ref[i] = (0.5 + 0.25 * i) * inverse
     walls = walls_ref[...]
@@ -86,7 +91,7 @@
                 value = value + half_sum(index_ref, k) * flux
                 flux = flux + table_ref[index_ref[k + 1]] * value
         k = jnp.minimum(start + cells - 1, total - 2)
-        after = 1.0 / (value + half_sum(index_ref, k) * flux)
+        after = inverted(value + half_sum(index_ref, k) * flux)
         return flux * after, after
 
     def backward(block, kappa, scale=None, keep=None):
@@ -103,7 +108,7 @@
                 value = value + half_sum(index_ref, k - 1) * flux
                 flux = flux + table_ref[index_ref[k - 1]] * value
         k = jnp.maximum(start - 1, 0)
-        after = 1.0 / (value + half_sum(index_ref, k) * flux)
+        after = inverted(value + half_sum(index_ref, k) * flux)
         return flux * after, after
 
     def thickness(block):
@@ -145,7 +150,7 @@
         0, blocks - 1 - me, sweep_backward, (upper, ones, extent)
     )
     ends_ref[1] = diffusion_ref[...] * upper * product
-    scale = 1.0 / (diffusion_ref[...] * (held_ref[3] + kappa_right * held_ref[4]))
+    scale = inverted(diffusion_ref[...] * (held_ref[3] + kappa_right * held_ref[4]))
     held_ref[0] = scale
 
     def keep_right(j, flux, value):
@@ -162,6 +167,67 @@
     pair_ref[0] = jnp.where(is_first, back, forth)
     pair_ref[1] = jnp.where(is_first, forth, through_ref[first])
     pair_ref[2] = jnp.where(is_first, through_ref[first + 1], back)
+
+    def fold(array):
+        parts = [array[:, i * LANES:(i + 1) * LANES] for i in range(array.shape[1] // LANES)]
+        return functools.reduce(jnp.add, parts)
+
+    for copy in large:
+        copy.wait()
+    volume_ref[...] = jnp.full(volume_ref.shape, extent * lines)
+    half = row_tiles // 2
+    own_extent = thickness(me)
+    heights = [height(index_ref, me * cells + j) for j in range(cells)]
+
+    def sums(ref, whose, parts):
+        def of_tile(i, state):
+            flow, weight = state
+            rows = row_tile(whose * half + i)
+            from_left = [0.0] * parts
+            from_right = [0.0] * parts
+            plain = 0.0
+            for j in range(cells):
+                left = left_h_ref[j, rows]
+                right = right_h_ref[j, rows]
+                for c in range(parts):
+                    v = velocity_ref[c, j, rows]
+                    from_left[c] = from_left[c] + left * v
+                    from_right[c] = from_right[c] + right * v
+                    if c == 0:
+                        plain = plain + heights[j] * v
+            for c in range(parts):
+                at = i * 2 * parts + c
+                put(ref, at, from_left[c] * held_ref[1, rows])
+                put(ref, at + parts, from_right[c] * held_ref[2, rows])
+            low_part = ends_ref[0, rows]
+            high_part = ends_ref[1, rows] * held_ref[0, rows]
+            totals = low_part * held_ref[6, rows] + high_part * held_ref[5, rows]
+            return (
+                flow + fold(plain - low_part * from_right[0] - high_part * from_left[0]),
+                weight + fold(own_extent - diffusion_ref[rows] * totals),
+            )
+
+        return of_tile
+
+    state = (jnp.zeros((SUB, LANES), jnp.float32),) * 2
+    mates = 1 - (me - first)
+    state = lax.fori_loop(0, half, sums(away_ref, mates, components), state)
+    flow, weight = lax.fori_loop(0, half, sums(mine_ref, me - first, 1), state)
+    for i in range(half):
+        put(away_ref, half * 2 * components + i, pair_ref[0, row_tile(mates * half + i)])
+    slot, middle = away_ref.shape[0] - 1, SUB // 2
+    away_ref[slot, 0:middle] = flow[0:middle] + flow[middle:]
+    away_ref[slot, middle:] = weight[0:middle] + weight[middle:]
+
+
+def rest_kernel(
+    chips, velocity_ref, left_h_ref, right_h_ref, held_ref, through_ref, sums_ref, chip_ref
+):
+    components, cells, _, lines_x = velocity_ref.shape
+    me = lax.axis_index("gz")
+    chip = me // 2
+    half = sums_ref.shape[0] // (2 * (components - 1) * (lines_x // LANES))
+    ones = jnp.ones(chip_ref.shape[1:], jnp.float32)
     for m in range(1, chips):
         other = chip ^ m
         low = jnp.minimum(chip, other)
@@ -173,65 +239,33 @@
             ones,
         )
 
-    def fold(array):
-        parts = [array[:, i * LANES:(i + 1) * LANES] for i in range(array.shape[1] // LANES)]
-        return functools.reduce(jnp.add, parts)
-
-    for copy in large:
-        copy.wait()
-    volume_ref[...] = jnp.full(volume_ref.shape, extent * lines)
-    half = row_tiles // 2
-    own_extent = thickness(me)
-    heights = [height(index_ref, me * cells + j) for j in range(cells)]
-
-    def sums(ref, whose):
-        def of_tile(i, state):
-            flow, weight = state
-            rows = row_tile(whose * half + i)
-            from_left = [0.0] * components
-            from_right = [0.0] * components
-            plain = 0.0
-            for j in range(cells):
-                left = left_h_ref[j, rows]
-                right = right_h_ref[j, rows]
-                for c in range(components):
-                    v = velocity_ref[c, j, rows]
-                    from_left[c] = from_left[c] + left * v
-                    from_right[c] = from_right[c] + right * v
-                    if c == 0:
-                        plain = plain + heights[j] * v
-            for c in range(components):
-                at = i * 2 * components + c
-                put(ref, at, from_left[c] * held_ref[1, rows])
-                put(ref, at + components, from_right[c] * held_ref[2, rows])
-            low_part = ends_ref[0, rows]
-            high_part = ends_ref[1, rows] * held_ref[0, rows]
-            totals = low_part * held_ref[6, rows] + high_part * held_ref[5, rows]
-            return (
-                flow + fold(plain - low_part * from_right[0] - high_part * from_left[0]),
-                weight + fold(own_extent - diffusion_ref[rows] * totals),
-            )
-
-        return of_tile
-
-    state = (jnp.zeros((SUB, LANES), jnp.float32),) * 2
-    mates = 1 - (me - first)
-    state = lax.fori_loop(0, half, sums(away_ref, mates), state)
-    flow, weight = lax.fori_loop(0, half, sums(mine_ref, me - first), state)
-    for i in range(half):
-        put(away_ref, half * 2 * components + i, pair_ref[0, row_tile(mates * half + i)])
-    slot, middle = away_ref.shape[0] - 1, SUB // 2
-    away_ref[slot, 0:middle] = flow[0:middle] + flow[middle:]
-    away_ref[slot, middle:] = weight[0:middle] + weight[middle:]
-
-
-def merge_kernel(chips, components, mine_ref, away_ref, mate_ref, pair_ref, *rest):
+    def of_tile(i, _):
+        rows = row_tile((me - chip * 2) * half + i)
+        from_left = [0.0] * (components - 1)
+        from_right = [0.0] * (components - 1)
+        for j in range(cells):
+            left = left_h_ref[j, rows]
+            right = right_h_ref[j, rows]
+            for c in range(components - 1):
+                v = velocity_ref[c + 1, j, rows]
+                from_left[c] = from_left[c] + left * v
+                from_right[c] = from_right[c] + right * v
+        for c in range(components - 1):
+            at = i * 2 * (components - 1) + c
+            put(sums_ref, at, from_left[c] * held_ref[1, rows])
+            put(sums_ref, at + components - 1, from_right[c] * held_ref[2, rows])
+        return 0
+
+    lax.fori_loop(0, half, of_tile, 0)
+
+
+def merge_kernel(chips, components, mine_ref, sums_ref, away_ref, mate_ref, pair_ref, *rest):
     send_refs, near_ref = rest[:-1], rest[-1]
     me = lax.axis_index("gz")
     chip = me // 2
     is_first = me == chip * 2
     count = pair_ref.shape[2] // LANES
-    half = mine_ref.shape[0] // (2 * components * count)
+    half = mine_ref.shape[0] // (2 * count)
     slot = away_ref.shape[0] - 1
     tile = away_ref[slot] + mate_ref[slot]
     near_ref[near_ref.shape[0] - 1] = tile
@@ -245,13 +279,20 @@
         back = jnp.where(is_first, mine, mate)
         for c in range(components):
             at = i * 2 * components + c
-            mine, mate = get(mine_ref, at, count), get(mate_ref, at, count)
+            if c == 0:
+                own = [get(mine_ref, i * 2 + k, count) for k in range(2)]
+            else:
+                others = components - 1
+                own = [
+                    get(sums_ref, i * 2 * others + k * others + c - 1, count) for k in range(2)
+                ]
+            mine, mate = own[0], get(mate_ref, at, count)
             first = jnp.where(is_first, mine, mate)
             second = jnp.where(is_first, mate, mine)
             put(near_ref, at, first)
             to_right = second + forth * first
             at = at + components
-            mine, mate = get(mine_ref, at, count), get(mate_ref, at, count)
+            mine, mate = own[1], get(mate_ref, at, count)
             first = jnp.where(is_first, mine, mate)
             second = jnp.where(is_first, mate, mine)
             put(near_ref, at, second)
@@ -380,22 +421,24 @@
     flow = jnp.sum(totals[0:SUB // 2], keepdims=True)
     weight = jnp.sum(totals[SUB // 2:], keepdims=True)
     alpha = (goal_ref[0:1, 0:1] - flow) / weight
-    cells, lines_y, _ = plain_ref.shape
-
-    def copy(t):
-        rows = row_tile(t)
-        return pltpu.make_async_copy(result_ref.at[:, rows], out_hbm.at[0, :, rows], sems.at[t])
-
-    def of_tile(t, _):
-        rows = row_tile(t)
-        for j in range(cells):
-            result_ref[j, rows] = plain_ref[j, rows] + alpha * unit_ref[j, rows]
-        copy(t).start()
+    cells = plain_ref.shape[0]
+    pieces = sems.shape[0]
+    step = cells // pieces
+
+    def copy(i):
+        part = pl.ds(i * step, step)
+        return pltpu.make_async_copy(result_ref.at[part], out_hbm.at[0, part], sems.at[i])
+
+    def of_piece(i, _):
+        for j in range(step):
+            at = i * step + j
+            result_ref[at] = plain_ref[at] + alpha * unit_ref[at]
+        copy(i).start()
         return 0
 
-    lax.fori_loop(0, lines_y // SUB, of_tile, 0)
-    for t in range(lines_y // SUB):
-        copy(t).wait()
+    lax.fori_loop(0, pieces, of_piece, 0)
+    for i in range(pieces):
+        copy(i).wait()
 
 
 def shards(velocity, diffusion, wall_types, stretch_index, bulk_target):
@@ -433,14 +476,15 @@
 
     count = lines_x // LANES
     lines = float(lines_y * columns * lines_x)
-    (mine, away, pair, chip_coefs, left, right, left_h, right_h, ends, volume,
+    (mine, away, pair, through, held, left, right, left_h, right_h, ends, volume,
      near_velocity) = pl.pallas_call(
         functools.partial(ladder_kernel, cells, blocks, chips, lines),
         out_shape=[
-            shape(half * 2 * components * count, SUB, LANES),
+            shape(half * 2 * count, SUB, LANES),
             shape(half * (2 * components + 1) * count + 1, SUB, LANES),
             shape(3, *plane),
-            shape(chips - 1, *plane),
+            shape(blocks, *plane),
+            shape(7, *plane),
             shape(cells, *plane),
             shape(cells, *plane),
             shape(cells, *plane),
@@ -450,14 +494,12 @@
             shape(*velocity.shape),
         ],
         in_specs=[anywhere] * 4,
-        out_specs=[vmem] * 11,
+        out_specs=[vmem] * 12,
         scratch_shapes=[
             pltpu.SMEM(stretch_index.shape, jnp.int32),
             pltpu.VMEM(plane, f32),
             pltpu.VMEM(plane, jnp.int32),
-            pltpu.VMEM((blocks,) + plane, f32),
             pltpu.VMEM((STRETCHES,) + plane, f32),
-            pltpu.VMEM((7,) + plane, f32),
             pltpu.SemaphoreType.DMA((3 + components,)),
         ],
         compiler_params=options(24),
@@ -466,17 +508,29 @@
     )(in_hbm(stretch_index), in_hbm(diffusion), in_hbm(wall_types), in_hbm(velocity))
 
     mate = to_mate(away)
+    sums, chip_coefs = pl.pallas_call(
+        functools.partial(rest_kernel, chips),
+        out_shape=[
+            shape(half * 2 * (components - 1) * count, SUB, LANES),
+            shape(chips - 1, *plane),
+        ],
+        in_specs=[vmem] * 5,
+        out_specs=[vmem] * 2,
+        compiler_params=options(16),
+        cost_estimate=cost(2_000_000, 2_000_000),
+        name="rest",
+    )(near_velocity, left_h, right_h, held, through)
     *outgoing, near = pl.pallas_call(
         functools.partial(merge_kernel, chips, components),
         out_shape=[
             shape(half * components * count + m.bit_count(), SUB, LANES) for m in range(1, chips)
         ] + [shape(half * 2 * components * count + 1, SUB, LANES)],
-        in_specs=[vmem] * 4,
+        in_specs=[vmem] * 5,
         out_specs=[vmem] * chips,
         compiler_params=options(16),
         cost_estimate=cost(500_000, 1_600_000),
         name="merge",
-    )(mine, away, mate, pair)
+    )(mine, sums, away, mate, pair)
     order = sorted(range(1, chips), key=lambda m: -m.bit_count())
     incoming = [send(outgoing[m - 1], lambda z, y: (z ^ (2 * m), y)) for m in order]
     profile = shape(cells, *plane)
@@ -525,7 +579,7 @@
         out_specs=anywhere,
         scratch_shapes=[
             pltpu.VMEM((cells,) + plane, f32),
-            pltpu.SemaphoreType.DMA((row_tiles,)),
+            pltpu.SemaphoreType.DMA((cells // 2,)),
         ],
         input_output_aliases={3 + columns: 0},
         compiler_params=options(16),

time: 24.3 us -> 24.2 us (level)
  waiting for transfers between devices: 5.25 us -> 4.92 us
    ppermute x8, waiting for transfers between devices: 5.25 us -> 4.92 us  [send(): return lax.ppermute(array, ('gz', 'gy'), route)]
    pallas_call x0 -> x1, Pallas kernels: none -> 0.31 us  [shards(): pl.pallas_call(functools.partial(rest_kernel, chips), out_shape=[shape(ha...]
  transfers between devices with their start and end apart: 8 -> 8, of which waited for: 4 -> 4; matrix products, arithmetic and copies ran while one was open for 0% -> 0% of each run, Pallas kernels for 10% -> 12%
where the time goes in v14:
time: 24.2 us; the launch traced here: 24 us
  starting transfers between devices  10.7 us (44%)
  Pallas kernels  7.73 us (32%)
  waiting for transfers between devices  4.92 us (20%)
  between operations  0.7 us (3%)
    ppermute x8, starting transfers between devices, send(): return lax.ppermute(array, ('gz', 'gy'), route)  10.7 us
    ppermute x8, waiting for transfers between devices, send(): return lax.ppermute(array, ('gz', 'gy'), route)  4.92 us
    pallas_call x1, Pallas kernels, shards(): pl.pallas_call(functools.partial(ladder_kernel, cells, blocks, chips, lin...  3.48 us
    pallas_call x1, Pallas kernels, shards(): pl.pallas_call(finish_kernel, out_shape=[shape(*velocity.shape), profile]...  1.45 us
    pallas_call x1, Pallas kernels, shards(): pl.pallas_call(functools.partial(correct_kernel, columns), out_shape=shap...  1.23 us
    pallas_call x1, Pallas kernels, shards(): pl.pallas_call(inner_kernel, out_shape=[shape(*velocity.shape), profile,...  1.11 us
  transfers between devices with their start and end apart: 8, of which 4 were waited for; matrix products, arithmetic and copies ran while one was open for 0% of the time, Pallas kernels for 12%

profile of v14, /device:TPU:0, one launch (start us, length us, event | category | flops | bytes accessed | tf_op | source)
XLA Modules:
  0.0 24.0 jit_solution(17071687921982286438)
XLA Ops:
  0.0 3.5 %ladder.1 = (f32[16,8,128]{2,1,0:T(8,128)S(1)}, f32[57,8,128]{2,1,0:T(8,128)S(1)}, f32[3,32,512]{2,1,0:T(8,128)S(1)}, f32[8,32,512]{2,1,0:T(8,128)S(1)}, f32[7,3...) custom-call(s32[128]{0:T(128)} %index_hbm.1, ...), custom_call_target="tpu_custom_call" | custom-call | flops 40000000 | bytes 6000000 | tf_op jit(solution)/shard_map/ladder/pallas_call | solution.py:480
  3.5 0.5 %collective-permute-start = (f32[57,8,128]{2,1,0:T(8,128)S(1)}, f32[57,8,128]{2,1,0:T(8,128)S(1)}, u32[]{:S(2)}, u32[]{:S(2)}) collective-permute-start(f32[57,8,128]{2,1,0:T(8,128)S(1)} %get-tuple-element.44.away_ref), channel_id=1, source_target_pairs={{0,4},{1,5},{2,6},{3,7},{4,0},{5,1},{6,2},{7,3},{8,12},{9,13},{10,... | collective-permute-start | bytes 700424 | tf_op jit(solution)/shard_map/ppermute | solution.py:472
  4.0 0.3 %rest.1 = (f32[32,8,128]{2,1,0:T(8,128)S(1)}, f32[3,32,512]{2,1,0:T(8,128)S(1)}) custom-call(f32[3,16,32,512]{3,2,1,0:T(8,128)S(1)} %get-tuple-element.33.velocity_ref, f32[16,32,512]{2,1,0:T(8,128)S(1)} %get-tuple-element.36.left_h_ref, f32[16,32,512]{2,1,0:T(8,128)S(1)} %get-tuple-element.37.right_h_ref, f32[7,32,512]{2,1,0:T(8,128)S(1)} %get-tuple-element.41.held_ref, ...), custom_call_target="tpu_custom_call" | custom-call | flops 2000000 | bytes 2000000 | tf_op jit(solution)/shard_map/rest/pallas_call | solution.py:511
  4.3 0.8 %collective-permute-done.mate_ref = f32[57,8,128]{2,1,0:T(8,128)S(1)} collective-permute-done((f32[57,8,128]{2,1,0:T(8,128)S(1)}, f32[57,8,128]{2,1,0:T(8,128)S(1)}, u32[]{:S(2)}, u32[]{:S(2)}) %collective-permute-start) | collective-permute-done | bytes 233504 | tf_op jit(solution)/shard_map/ppermute | solution.py:472
  5.1 0.1 merge.1
  5.2 3.9 %collective-permute-start.1 = (f32[26,8,128]{2,1,0:T(8,128)S(1)}, f32[26,8,128]{2,1,0:T(8,128)S(1)}, u32[]{:S(2)}, u32[]{:S(2)}) collective-permute-start(f32[26,8,128]{2,1,0:T(8,128)S(1)} %get-tuple-element.52), channel_id=1, source_target_pairs={{0,24},{1,25},{2,26},{3,27},{4,28},{5,29},{6,30},{7,31},{8,16},{9,... | collective-permute-start | bytes 319496 | tf_op jit(solution)/shard_map/ppermute | solution.py:472
  9.1 0.5 %collective-permute-start.3 = (f32[25,8,128]{2,1,0:T(8,128)S(1)}, f32[25,8,128]{2,1,0:T(8,128)S(1)}, u32[]{:S(2)}, u32[]{:S(2)}) collective-permute-start(f32[25,8,128]{2,1,0:T(8,128)S(1)} %get-tuple-element.53), channel_id=1, source_target_pairs={{0,16},{1,17},{2,18},{3,19},{4,20},{5,21},{6,22},{7,23},{8,24},{9,... | collective-permute-start | bytes 307208 | tf_op jit(solution)/shard_map/ppermute | solution.py:472
  9.6 0.1 collective-permute-start.2
  10.4 1.1 %inner.1 = (f32[3,16,32,512]{3,2,1,0:T(8,128)S(1)}, f32[16,32,512]{2,1,0:T(8,128)S(1)}, f32[8,128]{1,0:T(8,128)S(1)}) custom-call(f32[3,16,32,512]{3,2,1,0:T(8,128)S(1)} %get-tuple-element.33.velocity_ref, f32[16,32,512]{2,1,0:T(8,128)S(1)} %get-tuple-element.34.left_ref, f32[16,32,512]{2,1,0:T(8,128)S(1)} %get-tuple-element.35.right_ref, ...), custom_call_target="tpu_custom_call" | custom-call | flops 8000000 | bytes 8000000 | tf_op jit(solution)/shard_map/inner/pallas_call | solution.py:537
  11.5 3.1 %collective-permute-done.3.rest_3_ = f32[25,8,128]{2,1,0:T(8,128)S(1)} collective-permute-done((f32[25,8,128]{2,1,0:T(8,128)S(1)}, f32[25,8,128]{2,1,0:T(8,128)S(1)}, u32[]{:S(2)}, u32[]{:S(2)}) %collective-permute-start.3) | collective-permute-done | bytes 102432 | tf_op jit(solution)/shard_map/ppermute | solution.py:472
  14.5 0.2 %collective-permute-done.2.rest_2_ = f32[25,8,128]{2,1,0:T(8,128)S(1)} collective-permute-done((f32[25,8,128]{2,1,0:T(8,128)S(1)}, f32[25,8,128]{2,1,0:T(8,128)S(1)}, u32[]{:S(2)}, u32[]{:S(2)}) %collective-permute-start.2) | collective-permute-done | bytes 102432 | tf_op jit(solution)/shard_map/ppermute | solution.py:472
  14.8 0.0 collective-permute-done.1.rest_1_
  14.8 0.1 spread.1
  14.9 0.1 collective-permute-start.7
  15.0 1.6 %collective-permute-start.4 = (f32[3,8,128]{2,1,0:T(8,128)S(1)}, f32[3,8,128]{2,1,0:T(8,128)S(1)}, u32[]{:S(2)}, u32[]{:S(2)}) collective-permute-start(f32[3,8,128]{2,1,0:T(8,128)S(1)} %get-tuple-element.54.rest_0_), channel_id=1, source_target_pairs={{0,1},{1,2},{2,3},{3,0},{4,5},{5,6},{6,7},{7,4},{8,9},{9,10},{10,1... | collective-permute-start | bytes 36872 | tf_op jit(solution)/shard_map/ppermute | solution.py:472
  16.6 2.6 %collective-permute-start.5 = (f32[2,8,128]{2,1,0:T(8,128)S(1)}, f32[2,8,128]{2,1,0:T(8,128)S(1)}, u32[]{:S(2)}, u32[]{:S(2)}) collective-permute-start(f32[2,8,128]{2,1,0:T(8,128)S(1)} %get-tuple-element.55), channel_id=1, source_target_pairs={{0,2},{1,3},{2,0},{3,1},{4,6},{5,7},{6,4},{7,5},{8,10},{9,11},{10,... | collective-permute-start | bytes 24584 | tf_op jit(solution)/shard_map/ppermute | solution.py:472
  19.2 1.3 %collective-permute-start.6 = (f32[1,8,128]{2,1,0:T(8,128)S(1)}, f32[1,8,128]{2,1,0:T(8,128)S(1)}, u32[]{:S(2)}, u32[]{:S(2)}) collective-permute-start(f32[1,8,128]{2,1,0:T(8,128)S(1)} %get-tuple-element.56), channel_id=1, source_target_pairs={{0,3},{1,0},{2,1},{3,2},{4,7},{5,4},{6,5},{7,6},{8,11},{9,8},{10,9... | collective-permute-start | bytes 12296 | tf_op jit(solution)/shard_map/ppermute | solution.py:472
  20.5 0.0 collective-permute-done.7.other_ref
  20.5 1.5 %finish.1 = (f32[3,16,32,512]{3,2,1,0:T(8,128)}, f32[16,32,512]{2,1,0:T(8,128)S(1)}) custom-call(f32[12,8,512]{2,1,0:T(8,128)S(1)} %get-tuple-element.57.own_ref, f32[12,8,512]{2,1,0:T(8,128)S(1)} %collective-permute-done.7.other_ref, f32[3,16,32,512]{3,2,1,0:T(8,128)S(1)} %get-tuple-element.51.rest_0_.base_ref, ...), custom_call_target="tpu_custom_call" | custom-call | flops 3000000 | bytes 6000000 | tf_op jit(solution)/shard_map/finish/pallas_call | solution.py:562
  22.0 0.8 %collective-permute-done.6.rest_3_ = f32[1,8,128]{2,1,0:T(8,128)S(1)} collective-permute-done((f32[1,8,128]{2,1,0:T(8,128)S(1)}, f32[1,8,128]{2,1,0:T(8,128)S(1)}, u32[]{:S(2)}, u32[]{:S(2)}) %collective-permute-start.6) | collective-permute-done | bytes 4128 | tf_op jit(solution)/shard_map/ppermute | solution.py:472
  22.8 0.0 collective-permute-done.5.rest_2_
  22.8 0.0 collective-permute-done.4.rest_1_
  22.8 1.2 %correct.1 = f32[3,16,32,512]{3,2,1,0:T(8,128)} custom-call(f32[8,128]{1,0:T(8,128)S(1)} %get-tuple-element.47.goal_ref, f32[16,32,512]{2,1,0:T(8,128)S(1)} %get-tuple-element.48.unit_ref, f32[3,8,128]{2,1,0:T(8,128)S(1)} %get-tuple-element.54.rest_0_, f32[3,8,128]{2,1,0:T(8,128)S(1)} %collective-permute-done.4.rest_1_, ...), custom_call_target="tpu_custom_call", output_to_operand_aliasing={{}: (7, {})} | custom-call | flops 500000 | bytes 1600000 | tf_op jit(solution)/shard_map/correct/pallas_call | solution.py:575
Async XLA Ops:
  3.5 1.6 %collective-permute-start = (f32[57,8,128]{2,1,0:T(8,128)S(1)}, f32[57,8,128]{2,1,0:T(8,128)S(1)}, u32[]{:S(2)}, u32[]{:S(2)}) collective-permute-start(f32[57,8,128]{2,1,0:T(8,128)S(1)} %get-tuple-element.44.away_ref), channel_id=1, source_target_pairs={{0,4},{1,5},{2,6},{3,7},{4,0},{5,1},{6,2},{7,3},{8,12},{9,13},{10,... | collective-permute-start | bytes 700424 | tf_op jit(solution)/shard_map/ppermute | solution.py:472
  5.2 9.6 %collective-permute-start.1 = (f32[26,8,128]{2,1,0:T(8,128)S(1)}, f32[26,8,128]{2,1,0:T(8,128)S(1)}, u32[]{:S(2)}, u32[]{:S(2)}) collective-permute-start(f32[26,8,128]{2,1,0:T(8,128)S(1)} %get-tuple-element.52), channel_id=1, source_target_pairs={{0,24},{1,25},{2,26},{3,27},{4,28},{5,29},{6,30},{7,31},{8,16},{9,... | collective-permute-start | bytes 319496 | tf_op jit(solution)/shard_map/ppermute | solution.py:472
  9.1 5.5 %collective-permute-start.3 = (f32[25,8,128]{2,1,0:T(8,128)S(1)}, f32[25,8,128]{2,1,0:T(8,128)S(1)}, u32[]{:S(2)}, u32[]{:S(2)}) collective-permute-start(f32[25,8,128]{2,1,0:T(8,128)S(1)} %get-tuple-element.53), channel_id=1, source_target_pairs={{0,16},{1,17},{2,18},{3,19},{4,20},{5,21},{6,22},{7,23},{8,24},{9,... | collective-permute-start | bytes 307208 | tf_op jit(solution)/shard_map/ppermute | solution.py:472
  9.6 5.2 %collective-permute-start.2 = (f32[25,8,128]{2,1,0:T(8,128)S(1)}, f32[25,8,128]{2,1,0:T(8,128)S(1)}, u32[]{:S(2)}, u32[]{:S(2)}) collective-permute-start(f32[25,8,128]{2,1,0:T(8,128)S(1)} %get-tuple-element.46._), channel_id=1, source_target_pairs={{0,8},{1,9},{2,10},{3,11},{4,12},{5,13},{6,14},{7,15},{8,0},{9,1},... | collective-permute-start | bytes 307208 | tf_op jit(solution)/shard_map/ppermute | solution.py:472
  14.9 5.6 %collective-permute-start.7 = (f32[12,8,512]{2,1,0:T(8,128)S(1)}, f32[12,8,512]{2,1,0:T(8,128)S(1)}, u32[]{:S(2)}, u32[]{:S(2)}) collective-permute-start(f32[12,8,512]{2,1,0:T(8,128)S(1)} %get-tuple-element.58), channel_id=1, source_target_pairs={{0,4},{1,5},{2,6},{3,7},{4,0},{5,1},{6,2},{7,3},{8,12},{9,13},{10,... | collective-permute-start | bytes 589832 | tf_op jit(solution)/shard_map/ppermute | solution.py:472
  15.0 7.8 %collective-permute-start.4 = (f32[3,8,128]{2,1,0:T(8,128)S(1)}, f32[3,8,128]{2,1,0:T(8,128)S(1)}, u32[]{:S(2)}, u32[]{:S(2)}) collective-permute-start(f32[3,8,128]{2,1,0:T(8,128)S(1)} %get-tuple-element.54.rest_0_), channel_id=1, source_target_pairs={{0,1},{1,2},{2,3},{3,0},{4,5},{5,6},{6,7},{7,4},{8,9},{9,10},{10,1... | collective-permute-start | bytes 36872 | tf_op jit(solution)/shard_map/ppermute | solution.py:472
  16.6 6.2 %collective-permute-start.5 = (f32[2,8,128]{2,1,0:T(8,128)S(1)}, f32[2,8,128]{2,1,0:T(8,128)S(1)}, u32[]{:S(2)}, u32[]{:S(2)}) collective-permute-start(f32[2,8,128]{2,1,0:T(8,128)S(1)} %get-tuple-element.55), channel_id=1, source_target_pairs={{0,2},{1,3},{2,0},{3,1},{4,6},{5,7},{6,4},{7,5},{8,10},{9,11},{10,... | collective-permute-start | bytes 24584 | tf_op jit(solution)/shard_map/ppermute | solution.py:472
  19.2 3.6 %collective-permute-start.6 = (f32[1,8,128]{2,1,0:T(8,128)S(1)}, f32[1,8,128]{2,1,0:T(8,128)S(1)}, u32[]{:S(2)}, u32[]{:S(2)}) collective-permute-start(f32[1,8,128]{2,1,0:T(8,128)S(1)} %get-tuple-element.56), channel_id=1, source_target_pairs={{0,3},{1,0},{2,1},{3,2},{4,7},{5,4},{6,5},{7,6},{8,11},{9,8},{10,9... | collective-permute-start | bytes 12296 | tf_op jit(solution)/shard_map/ppermute | solution.py:472

commit v15 on v14

--- a/solution.py
+++ b/solution.py
@@ -11,6 +11,12 @@
 STRETCHES = 7
 LANES = 128
 MIB = 1024 * 1024
+
+
+def plane_rounds(columns):
+    if columns == 4:
+        return [(1, 3, 2, 0), (2, 1, 0, 3), (3, 0, 1, 2), (0, 2, 3, 1)]
+    return [[(y + shift) % columns for y in range(columns)] for shift in range(1, columns + 1)]
 
 
 def row_tile(t):
@@ -414,31 +420,29 @@
             copy.wait()
 
 
-def correct_kernel(columns, goal_ref, unit_ref, *rest):
-    tile_refs = rest[:columns]
-    plain_ref, _, out_hbm, result_ref, sems = rest[columns:]
+def correct_kernel(count, goal_ref, unit_ref, *rest):
+    tile_refs = rest[:count]
+    plain_ref, _, out_hbm, result_ref, sems = rest[count:]
     totals = functools.reduce(jnp.add, [ref[0] for ref in tile_refs])
     flow = jnp.sum(totals[0:SUB // 2], keepdims=True)
     weight = jnp.sum(totals[SUB // 2:], keepdims=True)
     alpha = (goal_ref[0:1, 0:1] - flow) / weight
-    cells = plain_ref.shape[0]
-    pieces = sems.shape[0]
-    step = cells // pieces
-
-    def copy(i):
-        part = pl.ds(i * step, step)
-        return pltpu.make_async_copy(result_ref.at[part], out_hbm.at[0, part], sems.at[i])
-
-    def of_piece(i, _):
-        for j in range(step):
-            at = i * step + j
-            result_ref[at] = plain_ref[at] + alpha * unit_ref[at]
-        copy(i).start()
+    cells, lines_y, _ = plain_ref.shape
+
+    def copy(t):
+        rows = row_tile(t)
+        return pltpu.make_async_copy(result_ref.at[:, rows], out_hbm.at[0, :, rows], sems.at[t])
+
+    def of_tile(t, _):
+        rows = row_tile(t)
+        for j in range(cells):
+            result_ref[j, rows] = plain_ref[j, rows] + alpha * unit_ref[j, rows]
+        copy(t).start()
         return 0
 
-    lax.fori_loop(0, pieces, of_piece, 0)
-    for i in range(pieces):
-        copy(i).wait()
+    lax.fori_loop(0, lines_y // SUB, of_tile, 0)
+    for t in range(lines_y // SUB):
+        copy(t).wait()
 
 
 def shards(velocity, diffusion, wall_types, stretch_index, bulk_target):
@@ -544,20 +548,20 @@
         name="inner",
     )(near_velocity, left, right, left_h, right_h, ends, volume, bulk_target.reshape(1, 1),
       outgoing[0])
+    rounds = plane_rounds(columns)
     own_in, other_out, *tile = pl.pallas_call(
         functools.partial(spread_kernel, order, components),
         out_shape=[shape(half * 2 * components, *sheet)] * 2
-        + [shape(columns - shift, SUB, LANES) for shift in range(1, columns)],
+        + [shape(len(rounds) - i, SUB, LANES) for i in range(len(rounds))],
         in_specs=[vmem] * 3 + [anywhere] + [vmem] * (chips - 1),
-        out_specs=[vmem] * (1 + columns),
+        out_specs=[vmem] * (2 + len(rounds)),
         compiler_params=options(16),
         cost_estimate=cost(500_000, 1_600_000),
         name="spread",
     )(near, pair, chip_coefs, base, *incoming)
     other_in = to_mate(other_out)
-    tiles = [tile[0]] + [
-        send(tile[shift - 1], lambda z, y: (z, (y + shift) % columns))
-        for shift in range(1, columns)
+    tiles = [
+        send(array, lambda z, y: (z, targets[y])) for array, targets in zip(tile, rounds)
     ]
     partial, plain = pl.pallas_call(
         finish_kernel,
@@ -573,15 +577,15 @@
         name="finish",
     )(own_in, other_in, base, left, right)
     return pl.pallas_call(
-        functools.partial(correct_kernel, columns),
+        functools.partial(correct_kernel, len(tiles)),
         out_shape=shape(*velocity.shape),
-        in_specs=[vmem] * (3 + columns) + [anywhere],
+        in_specs=[vmem] * (3 + len(tiles)) + [anywhere],
         out_specs=anywhere,
         scratch_shapes=[
             pltpu.VMEM((cells,) + plane, f32),
-            pltpu.SemaphoreType.DMA((cells // 2,)),
+            pltpu.SemaphoreType.DMA((row_tiles,)),
         ],
-        input_output_aliases={3 + columns: 0},
+        input_output_aliases={3 + len(tiles): 0},
         compiler_params=options(16),
         cost_estimate=cost(500_000, 1_600_000),
         name="correct",

time: 24.2 us -> 27.3 us (1.13)
  the two profiles are of different devices: /device:TPU:0 before, /device:TPU:10 now
where the time goes in v15:
time: 27.3 us; the launch traced here: 27.1 us
  starting transfers between devices  13 us (48%)
  Pallas kernels  7.71 us (28%)
  waiting for transfers between devices  5.65 us (21%)
  between operations  0.74 us (3%)
    ppermute x9, starting transfers between devices, send(): return lax.ppermute(array, ('gz', 'gy'), route)  13 us
    ppermute x9, waiting for transfers between devices, send(): return lax.ppermute(array, ('gz', 'gy'), route)  5.65 us
    pallas_call x1, Pallas kernels, shards(): pl.pallas_call(functools.partial(ladder_kernel, cells, blocks, chips, lin...  3.48 us
    pallas_call x1, Pallas kernels, shards(): pl.pallas_call(finish_kernel, out_shape=[shape(*velocity.shape), profile]...  1.47 us
    pallas_call x1, Pallas kernels, shards(): pl.pallas_call(functools.partial(correct_kernel, len(tiles)), out_shape=s...  1.19 us
    pallas_call x1, Pallas kernels, shards(): pl.pallas_call(inner_kernel, out_shape=[shape(*velocity.shape), profile,...  1.11 us
  transfers between devices with their start and end apart: 9, of which 4 were waited for; matrix products, arithmetic and copies ran while one was open for 0% of the time, Pallas kernels for 11%

profile of v15, /device:TPU:10, one launch (start us, length us, event | category | flops | bytes accessed | tf_op | source)
XLA Modules:
  0.0 27.1 jit_solution(15165663410181265230)
XLA Ops:
  0.0 3.5 %ladder.1 = (f32[16,8,128]{2,1,0:T(8,128)S(1)}, f32[57,8,128]{2,1,0:T(8,128)S(1)}, f32[3,32,512]{2,1,0:T(8,128)S(1)}, f32[8,32,512]{2,1,0:T(8,128)S(1)}, f32[7,3...) custom-call(s32[128]{0:T(128)} %index_hbm.1, ...), custom_call_target="tpu_custom_call" | custom-call | flops 40000000 | bytes 6000000 | tf_op jit(solution)/shard_map/ladder/pallas_call | solution.py:484
  3.5 0.1 collective-permute-start
  3.6 0.3 %rest.1 = (f32[32,8,128]{2,1,0:T(8,128)S(1)}, f32[3,32,512]{2,1,0:T(8,128)S(1)}) custom-call(f32[3,16,32,512]{3,2,1,0:T(8,128)S(1)} %get-tuple-element.34.velocity_ref, f32[16,32,512]{2,1,0:T(8,128)S(1)} %get-tuple-element.37.left_h_ref, f32[16,32,512]{2,1,0:T(8,128)S(1)} %get-tuple-element.38.right_h_ref, f32[7,32,512]{2,1,0:T(8,128)S(1)} %get-tuple-element.42.held_ref, ...), custom_call_target="tpu_custom_call" | custom-call | flops 2000000 | bytes 2000000 | tf_op jit(solution)/shard_map/rest/pallas_call | solution.py:515
  3.9 1.2 %collective-permute-done.mate_ref = f32[57,8,128]{2,1,0:T(8,128)S(1)} collective-permute-done((f32[57,8,128]{2,1,0:T(8,128)S(1)}, f32[57,8,128]{2,1,0:T(8,128)S(1)}, u32[]{:S(2)}, u32[]{:S(2)}) %collective-permute-start) | collective-permute-done | bytes 233504 | tf_op jit(solution)/shard_map/ppermute | solution.py:476
  5.0 0.1 merge.1
  5.1 1.6 %collective-permute-start.1 = (f32[26,8,128]{2,1,0:T(8,128)S(1)}, f32[26,8,128]{2,1,0:T(8,128)S(1)}, u32[]{:S(2)}, u32[]{:S(2)}) collective-permute-start(f32[26,8,128]{2,1,0:T(8,128)S(1)} %get-tuple-element.53), channel_id=1, source_target_pairs={{0,24},{1,25},{2,26},{3,27},{4,28},{5,29},{6,30},{7,31},{8,16},{9,... | collective-permute-start | bytes 319496 | tf_op jit(solution)/shard_map/ppermute | solution.py:476
  6.7 0.5 %collective-permute-start.3 = (f32[25,8,128]{2,1,0:T(8,128)S(1)}, f32[25,8,128]{2,1,0:T(8,128)S(1)}, u32[]{:S(2)}, u32[]{:S(2)}) collective-permute-start(f32[25,8,128]{2,1,0:T(8,128)S(1)} %get-tuple-element.54), channel_id=1, source_target_pairs={{0,16},{1,17},{2,18},{3,19},{4,20},{5,21},{6,22},{7,23},{8,24},{9,... | collective-permute-start | bytes 307208 | tf_op jit(solution)/shard_map/ppermute | solution.py:476
  7.2 1.5 %collective-permute-start.2 = (f32[25,8,128]{2,1,0:T(8,128)S(1)}, f32[25,8,128]{2,1,0:T(8,128)S(1)}, u32[]{:S(2)}, u32[]{:S(2)}) collective-permute-start(f32[25,8,128]{2,1,0:T(8,128)S(1)} %get-tuple-element.47._), channel_id=1, source_target_pairs={{0,8},{1,9},{2,10},{3,11},{4,12},{5,13},{6,14},{7,15},{8,0},{9,1},... | collective-permute-start | bytes 307208 | tf_op jit(solution)/shard_map/ppermute | solution.py:476
  9.3 1.1 %inner.1 = (f32[3,16,32,512]{3,2,1,0:T(8,128)S(1)}, f32[16,32,512]{2,1,0:T(8,128)S(1)}, f32[8,128]{1,0:T(8,128)S(1)}) custom-call(f32[3,16,32,512]{3,2,1,0:T(8,128)S(1)} %get-tuple-element.34.velocity_ref, f32[16,32,512]{2,1,0:T(8,128)S(1)} %get-tuple-element.35.left_ref, f32[16,32,512]{2,1,0:T(8,128)S(1)} %get-tuple-element.36.right_ref, ...), custom_call_target="tpu_custom_call" | custom-call | flops 8000000 | bytes 8000000 | tf_op jit(solution)/shard_map/inner/pallas_call | solution.py:541
  10.4 2.8 %collective-permute-done.3.rest_3_ = f32[25,8,128]{2,1,0:T(8,128)S(1)} collective-permute-done((f32[25,8,128]{2,1,0:T(8,128)S(1)}, f32[25,8,128]{2,1,0:T(8,128)S(1)}, u32[]{:S(2)}, u32[]{:S(2)}) %collective-permute-start.3) | collective-permute-done | bytes 102432 | tf_op jit(solution)/shard_map/ppermute | solution.py:476
  13.3 0.1 collective-permute-done.2.rest_2_
  13.4 0.0 collective-permute-done.1.rest_1_
  13.4 0.1 spread.1
  13.5 0.1 collective-permute-start.8
  13.6 4.5 %collective-permute-start.4 = (f32[4,8,128]{2,1,0:T(8,128)S(1)}, f32[4,8,128]{2,1,0:T(8,128)S(1)}, u32[]{:S(2)}, u32[]{:S(2)}) collective-permute-start(f32[4,8,128]{2,1,0:T(8,128)S(1)} %get-tuple-element.55), channel_id=1, source_target_pairs={{0,1},{1,3},{2,2},{3,0},{4,5},{5,7},{6,6},{7,4},{8,9},{9,11},{10,1... | collective-permute-start | bytes 49160 | tf_op jit(solution)/shard_map/ppermute | solution.py:476
  18.1 0.7 %collective-permute-start.5 = (f32[3,8,128]{2,1,0:T(8,128)S(1)}, f32[3,8,128]{2,1,0:T(8,128)S(1)}, u32[]{:S(2)}, u32[]{:S(2)}) collective-permute-start(f32[3,8,128]{2,1,0:T(8,128)S(1)} %get-tuple-element.56), channel_id=1, source_target_pairs={{0,2},{1,1},{2,0},{3,3},{4,6},{5,5},{6,4},{7,7},{8,10},{9,9},{10,8... | collective-permute-start | bytes 36872 | tf_op jit(solution)/shard_map/ppermute | solution.py:476
  18.7 0.7 %collective-permute-start.6 = (f32[2,8,128]{2,1,0:T(8,128)S(1)}, f32[2,8,128]{2,1,0:T(8,128)S(1)}, u32[]{:S(2)}, u32[]{:S(2)}) collective-permute-start(f32[2,8,128]{2,1,0:T(8,128)S(1)} %get-tuple-element.57), channel_id=1, source_target_pairs={{0,3},{1,0},{2,1},{3,2},{4,7},{5,4},{6,5},{7,6},{8,11},{9,8},{10,9... | collective-permute-start | bytes 24584 | tf_op jit(solution)/shard_map/ppermute | solution.py:476
  19.5 3.4 %collective-permute-start.7 = (f32[1,8,128]{2,1,0:T(8,128)S(1)}, f32[1,8,128]{2,1,0:T(8,128)S(1)}, u32[]{:S(2)}, u32[]{:S(2)}) collective-permute-start(f32[1,8,128]{2,1,0:T(8,128)S(1)} %get-tuple-element.58), channel_id=1, source_target_pairs={{0,0},{1,2},{2,3},{3,1},{4,4},{5,6},{6,7},{7,5},{8,8},{9,10},{10,1... | collective-permute-start | bytes 12296 | tf_op jit(solution)/shard_map/ppermute | solution.py:476
  22.9 0.0 collective-permute-done.8.other_ref
  22.9 1.5 %finish.1 = (f32[3,16,32,512]{3,2,1,0:T(8,128)}, f32[16,32,512]{2,1,0:T(8,128)S(1)}) custom-call(f32[12,8,512]{2,1,0:T(8,128)S(1)} %get-tuple-element.59.own_ref, f32[12,8,512]{2,1,0:T(8,128)S(1)} %collective-permute-done.8.other_ref, f32[3,16,32,512]{3,2,1,0:T(8,128)S(1)} %get-tuple-element.52.rest_0_.base_ref, ...), custom_call_target="tpu_custom_call" | custom-call | flops 3000000 | bytes 6000000 | tf_op jit(solution)/shard_map/finish/pallas_call | solution.py:566
  24.4 1.5 %collective-permute-done.7.rest_3_ = f32[1,8,128]{2,1,0:T(8,128)S(1)} collective-permute-done((f32[1,8,128]{2,1,0:T(8,128)S(1)}, f32[1,8,128]{2,1,0:T(8,128)S(1)}, u32[]{:S(2)}, u32[]{:S(2)}) %collective-permute-start.7) | collective-permute-done | bytes 4128 | tf_op jit(solution)/shard_map/ppermute | solution.py:476
  25.9 0.0 collective-permute-done.6.rest_2_
  25.9 0.0 collective-permute-done.5.rest_1_
  25.9 0.0 collective-permute-done.4.rest_0_
  25.9 1.2 %correct.1 = f32[3,16,32,512]{3,2,1,0:T(8,128)} custom-call(f32[8,128]{1,0:T(8,128)S(1)} %get-tuple-element.48.goal_ref, f32[16,32,512]{2,1,0:T(8,128)S(1)} %get-tuple-element.49.unit_ref, f32[4,8,128]{2,1,0:T(8,128)S(1)} %collective-permute-done.4.rest_0_, f32[3,8,128]{2,1,0:T(8,128)S(1)} %collective-permute-done.5.rest_1_, ...), custom_call_target="tpu_custom_call", output_to_operand_aliasing={{}: (7, {})} | custom-call | flops 500000 | bytes 1600000 | tf_op jit(solution)/shard_map/correct/pallas_call | solution.py:579
Async XLA Ops:
  3.5 1.6 %collective-permute-start = (f32[57,8,128]{2,1,0:T(8,128)S(1)}, f32[57,8,128]{2,1,0:T(8,128)S(1)}, u32[]{:S(2)}, u32[]{:S(2)}) collective-permute-start(f32[57,8,128]{2,1,0:T(8,128)S(1)} %get-tuple-element.45.away_ref), channel_id=1, source_target_pairs={{0,4},{1,5},{2,6},{3,7},{4,0},{5,1},{6,2},{7,3},{8,12},{9,13},{10,... | collective-permute-start | bytes 700424 | tf_op jit(solution)/shard_map/ppermute | solution.py:476
  5.1 8.3 %collective-permute-start.1 = (f32[26,8,128]{2,1,0:T(8,128)S(1)}, f32[26,8,128]{2,1,0:T(8,128)S(1)}, u32[]{:S(2)}, u32[]{:S(2)}) collective-permute-start(f32[26,8,128]{2,1,0:T(8,128)S(1)} %get-tuple-element.53), channel_id=1, source_target_pairs={{0,24},{1,25},{2,26},{3,27},{4,28},{5,29},{6,30},{7,31},{8,16},{9,... | collective-permute-start | bytes 319496 | tf_op jit(solution)/shard_map/ppermute | solution.py:476
  6.7 6.6 %collective-permute-start.3 = (f32[25,8,128]{2,1,0:T(8,128)S(1)}, f32[25,8,128]{2,1,0:T(8,128)S(1)}, u32[]{:S(2)}, u32[]{:S(2)}) collective-permute-start(f32[25,8,128]{2,1,0:T(8,128)S(1)} %get-tuple-element.54), channel_id=1, source_target_pairs={{0,16},{1,17},{2,18},{3,19},{4,20},{5,21},{6,22},{7,23},{8,24},{9,... | collective-permute-start | bytes 307208 | tf_op jit(solution)/shard_map/ppermute | solution.py:476
  7.2 6.2 %collective-permute-start.2 = (f32[25,8,128]{2,1,0:T(8,128)S(1)}, f32[25,8,128]{2,1,0:T(8,128)S(1)}, u32[]{:S(2)}, u32[]{:S(2)}) collective-permute-start(f32[25,8,128]{2,1,0:T(8,128)S(1)} %get-tuple-element.47._), channel_id=1, source_target_pairs={{0,8},{1,9},{2,10},{3,11},{4,12},{5,13},{6,14},{7,15},{8,0},{9,1},... | collective-permute-start | bytes 307208 | tf_op jit(solution)/shard_map/ppermute | solution.py:476
  13.5 9.4 %collective-permute-start.8 = (f32[12,8,512]{2,1,0:T(8,128)S(1)}, f32[12,8,512]{2,1,0:T(8,128)S(1)}, u32[]{:S(2)}, u32[]{:S(2)}) collective-permute-start(f32[12,8,512]{2,1,0:T(8,128)S(1)} %get-tuple-element.60), channel_id=1, source_target_pairs={{0,4},{1,5},{2,6},{3,7},{4,0},{5,1},{6,2},{7,3},{8,12},{9,13},{10,... | collective-permute-start | bytes 589832 | tf_op jit(solution)/shard_map/ppermute | solution.py:476
  13.6 12.3 %collective-permute-start.4 = (f32[4,8,128]{2,1,0:T(8,128)S(1)}, f32[4,8,128]{2,1,0:T(8,128)S(1)}, u32[]{:S(2)}, u32[]{:S(2)}) collective-permute-start(f32[4,8,128]{2,1,0:T(8,128)S(1)} %get-tuple-element.55), channel_id=1, source_target_pairs={{0,1},{1,3},{2,2},{3,0},{4,5},{5,7},{6,6},{7,4},{8,9},{9,11},{10,1... | collective-permute-start | bytes 49160 | tf_op jit(solution)/shard_map/ppermute | solution.py:476
  18.1 7.8 %collective-permute-start.5 = (f32[3,8,128]{2,1,0:T(8,128)S(1)}, f32[3,8,128]{2,1,0:T(8,128)S(1)}, u32[]{:S(2)}, u32[]{:S(2)}) collective-permute-start(f32[3,8,128]{2,1,0:T(8,128)S(1)} %get-tuple-element.56), channel_id=1, source_target_pairs={{0,2},{1,1},{2,0},{3,3},{4,6},{5,5},{6,4},{7,7},{8,10},{9,9},{10,8... | collective-permute-start | bytes 36872 | tf_op jit(solution)/shard_map/ppermute | solution.py:476
  18.7 7.1 %collective-permute-start.6 = (f32[2,8,128]{2,1,0:T(8,128)S(1)}, f32[2,8,128]{2,1,0:T(8,128)S(1)}, u32[]{:S(2)}, u32[]{:S(2)}) collective-permute-start(f32[2,8,128]{2,1,0:T(8,128)S(1)} %get-tuple-element.57), channel_id=1, source_target_pairs={{0,3},{1,0},{2,1},{3,2},{4,7},{5,4},{6,5},{7,6},{8,11},{9,8},{10,9... | collective-permute-start | bytes 24584 | tf_op jit(solution)/shard_map/ppermute | solution.py:476
  19.5 6.4 %collective-permute-start.7 = (f32[1,8,128]{2,1,0:T(8,128)S(1)}, f32[1,8,128]{2,1,0:T(8,128)S(1)}, u32[]{:S(2)}, u32[]{:S(2)}) collective-permute-start(f32[1,8,128]{2,1,0:T(8,128)S(1)} %get-tuple-element.58), channel_id=1, source_target_pairs={{0,0},{1,2},{2,3},{3,1},{4,4},{5,6},{6,7},{7,5},{8,8},{9,10},{10,1... | collective-permute-start | bytes 12296 | tf_op jit(solution)/shard_map/ppermute | solution.py:476

commit v16 on v15

--- a/solution.py
+++ b/solution.py
@@ -15,8 +15,17 @@
 
 def plane_rounds(columns):
     if columns == 4:
-        return [(1, 3, 2, 0), (2, 1, 0, 3), (3, 0, 1, 2), (0, 2, 3, 1)]
-    return [[(y + shift) % columns for y in range(columns)] for shift in range(1, columns + 1)]
+        return [(1, 0, 3, 2), (1, 2, 3, 0), (3, 2, 0, 1), (2, 3, 1, 0)]
+    return [[(y + shift) % columns for y in range(columns)] for shift in range(1, columns)]
+
+
+def repeated(rounds):
+    seen, again = set(), []
+    for targets in rounds:
+        pairs = list(enumerate(targets))
+        again.append([b for a, b in pairs if (a, b) in seen])
+        seen.update(pairs)
+    return again
 
 
 def row_tile(t):
@@ -420,10 +429,16 @@
             copy.wait()
 
 
-def correct_kernel(count, goal_ref, unit_ref, *rest):
-    tile_refs = rest[:count]
-    plain_ref, _, out_hbm, result_ref, sems = rest[count:]
-    totals = functools.reduce(jnp.add, [ref[0] for ref in tile_refs])
+def correct_kernel(again, goal_ref, unit_ref, *rest):
+    tile_refs = rest[:len(again) + 1]
+    plain_ref, _, out_hbm, result_ref, sems = rest[len(again) + 1:]
+    me = lax.axis_index("gy")
+    totals = tile_refs[0][0]
+    for planes, ref in zip(again, tile_refs[1:]):
+        term = ref[0]
+        for y in planes:
+            term = jnp.where(me == y, 0.0, term)
+        totals = totals + term
     flow = jnp.sum(totals[0:SUB // 2], keepdims=True)
     weight = jnp.sum(totals[SUB // 2:], keepdims=True)
     alpha = (goal_ref[0:1, 0:1] - flow) / weight
@@ -560,7 +575,7 @@
         name="spread",
     )(near, pair, chip_coefs, base, *incoming)
     other_in = to_mate(other_out)
-    tiles = [
+    tiles = [tile[0]] + [
         send(array, lambda z, y: (z, targets[y])) for array, targets in zip(tile, rounds)
     ]
     partial, plain = pl.pallas_call(
@@ -577,7 +592,7 @@
         name="finish",
     )(own_in, other_in, base, left, right)
     return pl.pallas_call(
-        functools.partial(correct_kernel, len(tiles)),
+        functools.partial(correct_kernel, repeated(rounds)),
         out_shape=shape(*velocity.shape),
         in_specs=[vmem] * (3 + len(tiles)) + [anywhere],
         out_specs=anywhere,

time: 27.3 us -> 27.2 us (level)
  the two profiles are of different devices: /device:TPU:10 before, /device:TPU:0 now
where the time goes in v16:
time: 27.2 us; the launch traced here: 27 us
  starting transfers between devices  10.6 us (39%)
  waiting for transfers between devices  8.06 us (30%)
  Pallas kernels  7.7 us (28%)
  between operations  0.7 us (3%)
    ppermute x9, starting transfers between devices, send(): return lax.ppermute(array, ('gz', 'gy'), route)  10.6 us
    ppermute x9, waiting for transfers between devices, send(): return lax.ppermute(array, ('gz', 'gy'), route)  8.06 us
    pallas_call x1, Pallas kernels, shards(): pl.pallas_call(functools.partial(ladder_kernel, cells, blocks, chips, lin...  3.48 us
    pallas_call x1, Pallas kernels, shards(): pl.pallas_call(finish_kernel, out_shape=[shape(*velocity.shape), profile]...  1.45 us
    pallas_call x1, Pallas kernels, shards(): pl.pallas_call(functools.partial(correct_kernel, repeated(rounds)), out_s...  1.2 us
    pallas_call x1, Pallas kernels, shards(): pl.pallas_call(inner_kernel, out_shape=[shape(*velocity.shape), profile,...  1.11 us
  transfers between devices with their start and end apart: 9, of which 4 were waited for; matrix products, arithmetic and copies ran while one was open for 0% of the time, Pallas kernels for 11%

profile of v16, /device:TPU:0, one launch (start us, length us, event | category | flops | bytes accessed | tf_op | source)
XLA Modules:
  0.0 27.0 jit_solution(8942310599756362587)
XLA Ops:
  0.0 3.5 %ladder.1 = (f32[16,8,128]{2,1,0:T(8,128)S(1)}, f32[57,8,128]{2,1,0:T(8,128)S(1)}, f32[3,32,512]{2,1,0:T(8,128)S(1)}, f32[8,32,512]{2,1,0:T(8,128)S(1)}, f32[7,3...) custom-call(s32[128]{0:T(128)} %index_hbm.1, ...), custom_call_target="tpu_custom_call" | custom-call | flops 40000000 | bytes 6000000 | tf_op jit(solution)/shard_map/ladder/pallas_call | solution.py:499
  3.5 0.5 %collective-permute-start = (f32[57,8,128]{2,1,0:T(8,128)S(1)}, f32[57,8,128]{2,1,0:T(8,128)S(1)}, u32[]{:S(2)}, u32[]{:S(2)}) collective-permute-start(f32[57,8,128]{2,1,0:T(8,128)S(1)} %get-tuple-element.45.away_ref), channel_id=1, source_target_pairs={{0,4},{1,5},{2,6},{3,7},{4,0},{5,1},{6,2},{7,3},{8,12},{9,13},{10,... | collective-permute-start | bytes 700424 | tf_op jit(solution)/shard_map/ppermute | solution.py:491
  4.0 0.3 %rest.1 = (f32[32,8,128]{2,1,0:T(8,128)S(1)}, f32[3,32,512]{2,1,0:T(8,128)S(1)}) custom-call(f32[3,16,32,512]{3,2,1,0:T(8,128)S(1)} %get-tuple-element.34.velocity_ref, f32[16,32,512]{2,1,0:T(8,128)S(1)} %get-tuple-element.37.left_h_ref, f32[16,32,512]{2,1,0:T(8,128)S(1)} %get-tuple-element.38.right_h_ref, f32[7,32,512]{2,1,0:T(8,128)S(1)} %get-tuple-element.42.held_ref, ...), custom_call_target="tpu_custom_call" | custom-call | flops 2000000 | bytes 2000000 | tf_op jit(solution)/shard_map/rest/pallas_call | solution.py:530
  4.3 0.8 %collective-permute-done.mate_ref = f32[57,8,128]{2,1,0:T(8,128)S(1)} collective-permute-done((f32[57,8,128]{2,1,0:T(8,128)S(1)}, f32[57,8,128]{2,1,0:T(8,128)S(1)}, u32[]{:S(2)}, u32[]{:S(2)}) %collective-permute-start) | collective-permute-done | bytes 233504 | tf_op jit(solution)/shard_map/ppermute | solution.py:491
  5.1 0.1 merge.1
  5.2 3.9 %collective-permute-start.1 = (f32[26,8,128]{2,1,0:T(8,128)S(1)}, f32[26,8,128]{2,1,0:T(8,128)S(1)}, u32[]{:S(2)}, u32[]{:S(2)}) collective-permute-start(f32[26,8,128]{2,1,0:T(8,128)S(1)} %get-tuple-element.53), channel_id=1, source_target_pairs={{0,24},{1,25},{2,26},{3,27},{4,28},{5,29},{6,30},{7,31},{8,16},{9,... | collective-permute-start | bytes 319496 | tf_op jit(solution)/shard_map/ppermute | solution.py:491
  9.1 0.5 %collective-permute-start.3 = (f32[25,8,128]{2,1,0:T(8,128)S(1)}, f32[25,8,128]{2,1,0:T(8,128)S(1)}, u32[]{:S(2)}, u32[]{:S(2)}) collective-permute-start(f32[25,8,128]{2,1,0:T(8,128)S(1)} %get-tuple-element.54), channel_id=1, source_target_pairs={{0,16},{1,17},{2,18},{3,19},{4,20},{5,21},{6,22},{7,23},{8,24},{9,... | collective-permute-start | bytes 307208 | tf_op jit(solution)/shard_map/ppermute | solution.py:491
  9.6 0.1 collective-permute-start.2
  10.4 1.1 %inner.1 = (f32[3,16,32,512]{3,2,1,0:T(8,128)S(1)}, f32[16,32,512]{2,1,0:T(8,128)S(1)}, f32[8,128]{1,0:T(8,128)S(1)}) custom-call(f32[3,16,32,512]{3,2,1,0:T(8,128)S(1)} %get-tuple-element.34.velocity_ref, f32[16,32,512]{2,1,0:T(8,128)S(1)} %get-tuple-element.35.left_ref, f32[16,32,512]{2,1,0:T(8,128)S(1)} %get-tuple-element.36.right_ref, ...), custom_call_target="tpu_custom_call" | custom-call | flops 8000000 | bytes 8000000 | tf_op jit(solution)/shard_map/inner/pallas_call | solution.py:556
  11.5 3.1 %collective-permute-done.3.rest_3_ = f32[25,8,128]{2,1,0:T(8,128)S(1)} collective-permute-done((f32[25,8,128]{2,1,0:T(8,128)S(1)}, f32[25,8,128]{2,1,0:T(8,128)S(1)}, u32[]{:S(2)}, u32[]{:S(2)}) %collective-permute-start.3) | collective-permute-done | bytes 102432 | tf_op jit(solution)/shard_map/ppermute | solution.py:491
  14.5 0.2 collective-permute-done.2.rest_2_
  14.8 0.0 collective-permute-done.1.rest_1_
  14.8 0.1 spread.1
  14.9 0.1 collective-permute-start.8
  15.0 1.6 %collective-permute-start.4 = (f32[4,8,128]{2,1,0:T(8,128)S(1)}, f32[4,8,128]{2,1,0:T(8,128)S(1)}, u32[]{:S(2)}, u32[]{:S(2)}) collective-permute-start(f32[4,8,128]{2,1,0:T(8,128)S(1)} %get-tuple-element.55.rest_0_), channel_id=1, source_target_pairs={{0,1},{1,0},{2,3},{3,2},{4,5},{5,4},{6,7},{7,6},{8,9},{9,8},{10,11... | collective-permute-start | bytes 49160 | tf_op jit(solution)/shard_map/ppermute | solution.py:491
  16.6 0.4 %collective-permute-start.5 = (f32[3,8,128]{2,1,0:T(8,128)S(1)}, f32[3,8,128]{2,1,0:T(8,128)S(1)}, u32[]{:S(2)}, u32[]{:S(2)}) collective-permute-start(f32[3,8,128]{2,1,0:T(8,128)S(1)} %get-tuple-element.56), channel_id=1, source_target_pairs={{0,1},{1,2},{2,3},{3,0},{4,5},{5,6},{6,7},{7,4},{8,9},{9,10},{10,1... | collective-permute-start | bytes 36872 | tf_op jit(solution)/shard_map/ppermute | solution.py:491
  17.1 3.4 %collective-permute-start.6 = (f32[2,8,128]{2,1,0:T(8,128)S(1)}, f32[2,8,128]{2,1,0:T(8,128)S(1)}, u32[]{:S(2)}, u32[]{:S(2)}) collective-permute-start(f32[2,8,128]{2,1,0:T(8,128)S(1)} %get-tuple-element.57), channel_id=1, source_target_pairs={{0,3},{1,2},{2,0},{3,1},{4,7},{5,6},{6,4},{7,5},{8,11},{9,10},{10,... | collective-permute-start | bytes 24584 | tf_op jit(solution)/shard_map/ppermute | solution.py:491
  20.4 0.0 collective-permute-start.7
  20.4 0.0 collective-permute-done.8.other_ref
  20.4 1.5 %finish.1 = (f32[3,16,32,512]{3,2,1,0:T(8,128)}, f32[16,32,512]{2,1,0:T(8,128)S(1)}) custom-call(f32[12,8,512]{2,1,0:T(8,128)S(1)} %get-tuple-element.59.own_ref, f32[12,8,512]{2,1,0:T(8,128)S(1)} %collective-permute-done.8.other_ref, f32[3,16,32,512]{3,2,1,0:T(8,128)S(1)} %get-tuple-element.52.rest_0_.base_ref, ...), custom_call_target="tpu_custom_call" | custom-call | flops 3000000 | bytes 6000000 | tf_op jit(solution)/shard_map/finish/pallas_call | solution.py:581
  21.9 3.9 %collective-permute-done.7.rest_4_ = f32[1,8,128]{2,1,0:T(8,128)S(1)} collective-permute-done((f32[1,8,128]{2,1,0:T(8,128)S(1)}, f32[1,8,128]{2,1,0:T(8,128)S(1)}, u32[]{:S(2)}, u32[]{:S(2)}) %collective-permute-start.7) | collective-permute-done | bytes 4128 | tf_op jit(solution)/shard_map/ppermute | solution.py:491
  25.8 0.0 collective-permute-done.6.rest_3_
  25.8 0.0 collective-permute-done.5.rest_2_
  25.8 0.0 collective-permute-done.4.rest_1_
  25.8 1.2 %correct.1 = f32[3,16,32,512]{3,2,1,0:T(8,128)} custom-call(f32[8,128]{1,0:T(8,128)S(1)} %get-tuple-element.48.goal_ref, f32[16,32,512]{2,1,0:T(8,128)S(1)} %get-tuple-element.49.unit_ref, f32[4,8,128]{2,1,0:T(8,128)S(1)} %get-tuple-element.55.rest_0_, f32[4,8,128]{2,1,0:T(8,128)S(1)} %collective-permute-done.4.rest_1_, ...), custom_call_target="tpu_custom_call", output_to_operand_aliasing={{}: (8, {})} | custom-call | flops 500000 | bytes 1600000 | tf_op jit(solution)/shard_map/correct/pallas_call | solution.py:594
Async XLA Ops:
  3.5 1.6 %collective-permute-start = (f32[57,8,128]{2,1,0:T(8,128)S(1)}, f32[57,8,128]{2,1,0:T(8,128)S(1)}, u32[]{:S(2)}, u32[]{:S(2)}) collective-permute-start(f32[57,8,128]{2,1,0:T(8,128)S(1)} %get-tuple-element.45.away_ref), channel_id=1, source_target_pairs={{0,4},{1,5},{2,6},{3,7},{4,0},{5,1},{6,2},{7,3},{8,12},{9,13},{10,... | collective-permute-start | bytes 700424 | tf_op jit(solution)/shard_map/ppermute | solution.py:491
  5.2 9.6 %collective-permute-start.1 = (f32[26,8,128]{2,1,0:T(8,128)S(1)}, f32[26,8,128]{2,1,0:T(8,128)S(1)}, u32[]{:S(2)}, u32[]{:S(2)}) collective-permute-start(f32[26,8,128]{2,1,0:T(8,128)S(1)} %get-tuple-element.53), channel_id=1, source_target_pairs={{0,24},{1,25},{2,26},{3,27},{4,28},{5,29},{6,30},{7,31},{8,16},{9,... | collective-permute-start | bytes 319496 | tf_op jit(solution)/shard_map/ppermute | solution.py:491
  9.1 5.5 %collective-permute-start.3 = (f32[25,8,128]{2,1,0:T(8,128)S(1)}, f32[25,8,128]{2,1,0:T(8,128)S(1)}, u32[]{:S(2)}, u32[]{:S(2)}) collective-permute-start(f32[25,8,128]{2,1,0:T(8,128)S(1)} %get-tuple-element.54), channel_id=1, source_target_pairs={{0,16},{1,17},{2,18},{3,19},{4,20},{5,21},{6,22},{7,23},{8,24},{9,... | collective-permute-start | bytes 307208 | tf_op jit(solution)/shard_map/ppermute | solution.py:491
  9.6 5.2 %collective-permute-start.2 = (f32[25,8,128]{2,1,0:T(8,128)S(1)}, f32[25,8,128]{2,1,0:T(8,128)S(1)}, u32[]{:S(2)}, u32[]{:S(2)}) collective-permute-start(f32[25,8,128]{2,1,0:T(8,128)S(1)} %get-tuple-element.47._), channel_id=1, source_target_pairs={{0,8},{1,9},{2,10},{3,11},{4,12},{5,13},{6,14},{7,15},{8,0},{9,1},... | collective-permute-start | bytes 307208 | tf_op jit(solution)/shard_map/ppermute | solution.py:491
  14.9 5.6 %collective-permute-start.8 = (f32[12,8,512]{2,1,0:T(8,128)S(1)}, f32[12,8,512]{2,1,0:T(8,128)S(1)}, u32[]{:S(2)}, u32[]{:S(2)}) collective-permute-start(f32[12,8,512]{2,1,0:T(8,128)S(1)} %get-tuple-element.60), channel_id=1, source_target_pairs={{0,4},{1,5},{2,6},{3,7},{4,0},{5,1},{6,2},{7,3},{8,12},{9,13},{10,... | collective-permute-start | bytes 589832 | tf_op jit(solution)/shard_map/ppermute | solution.py:491
  15.0 10.9 %collective-permute-start.4 = (f32[4,8,128]{2,1,0:T(8,128)S(1)}, f32[4,8,128]{2,1,0:T(8,128)S(1)}, u32[]{:S(2)}, u32[]{:S(2)}) collective-permute-start(f32[4,8,128]{2,1,0:T(8,128)S(1)} %get-tuple-element.55.rest_0_), channel_id=1, source_target_pairs={{0,1},{1,0},{2,3},{3,2},{4,5},{5,4},{6,7},{7,6},{8,9},{9,8},{10,11... | collective-permute-start | bytes 49160 | tf_op jit(solution)/shard_map/ppermute | solution.py:491
  16.6 9.2 %collective-permute-start.5 = (f32[3,8,128]{2,1,0:T(8,128)S(1)}, f32[3,8,128]{2,1,0:T(8,128)S(1)}, u32[]{:S(2)}, u32[]{:S(2)}) collective-permute-start(f32[3,8,128]{2,1,0:T(8,128)S(1)} %get-tuple-element.56), channel_id=1, source_target_pairs={{0,1},{1,2},{2,3},{3,0},{4,5},{5,6},{6,7},{7,4},{8,9},{9,10},{10,1... | collective-permute-start | bytes 36872 | tf_op jit(solution)/shard_map/ppermute | solution.py:491
  17.1 8.8 %collective-permute-start.6 = (f32[2,8,128]{2,1,0:T(8,128)S(1)}, f32[2,8,128]{2,1,0:T(8,128)S(1)}, u32[]{:S(2)}, u32[]{:S(2)}) collective-permute-start(f32[2,8,128]{2,1,0:T(8,128)S(1)} %get-tuple-element.57), channel_id=1, source_target_pairs={{0,3},{1,2},{2,0},{3,1},{4,7},{5,6},{6,4},{7,5},{8,11},{9,10},{10,... | collective-permute-start | bytes 24584 | tf_op jit(solution)/shard_map/ppermute | solution.py:491
  20.4 5.4 %collective-permute-start.7 = (f32[1,8,128]{2,1,0:T(8,128)S(1)}, f32[1,8,128]{2,1,0:T(8,128)S(1)}, u32[]{:S(2)}, u32[]{:S(2)}) collective-permute-start(f32[1,8,128]{2,1,0:T(8,128)S(1)} %get-tuple-element.58), channel_id=1, source_target_pairs={{0,2},{1,3},{2,1},{3,0},{4,6},{5,7},{6,5},{7,4},{8,10},{9,11},{10,... | collective-permute-start | bytes 12296 | tf_op jit(solution)/shard_map/ppermute | solution.py:491

commit v17 on v15

--- a/solution.py
+++ b/solution.py
@@ -15,8 +15,8 @@
 
 def plane_rounds(columns):
     if columns == 4:
-        return [(1, 3, 2, 0), (2, 1, 0, 3), (3, 0, 1, 2), (0, 2, 3, 1)]
-    return [[(y + shift) % columns for y in range(columns)] for shift in range(1, columns + 1)]
+        return [(2, 3, 1, 0), (3, 2, 0, 1), (1, 0, 3, 2)]
+    return [[(y + shift) % columns for y in range(columns)] for shift in range(1, columns)]
 
 
 def row_tile(t):
@@ -560,7 +560,7 @@
         name="spread",
     )(near, pair, chip_coefs, base, *incoming)
     other_in = to_mate(other_out)
-    tiles = [
+    tiles = [tile[0]] + [
         send(array, lambda z, y: (z, targets[y])) for array, targets in zip(tile, rounds)
     ]
     partial, plain = pl.pallas_call(

time: 27.3 us -> 23.8 us (0.87)
  the two profiles are of different devices: /device:TPU:10 before, /device:TPU:0 now
where the time goes in v17:
time: 23.8 us; the launch traced here: 23.6 us
  starting transfers between devices  9.34 us (39%)
  Pallas kernels  7.68 us (32%)
  waiting for transfers between devices  5.92 us (25%)
  between operations  0.7 us (3%)
    ppermute x8, starting transfers between devices, send(): return lax.ppermute(array, ('gz', 'gy'), route)  9.34 us
    ppermute x8, waiting for transfers between devices, send(): return lax.ppermute(array, ('gz', 'gy'), route)  5.92 us
    pallas_call x1, Pallas kernels, shards(): pl.pallas_call(functools.partial(ladder_kernel, cells, blocks, chips, lin...  3.48 us
    pallas_call x1, Pallas kernels, shards(): pl.pallas_call(finish_kernel, out_shape=[shape(*velocity.shape), profile]...  1.45 us
    pallas_call x1, Pallas kernels, shards(): pl.pallas_call(functools.partial(correct_kernel, len(tiles)), out_shape=s...  1.18 us
    pallas_call x1, Pallas kernels, shards(): pl.pallas_call(inner_kernel, out_shape=[shape(*velocity.shape), profile,...  1.11 us
  transfers between devices with their start and end apart: 8, of which 4 were waited for; matrix products, arithmetic and copies ran while one was open for 0% of the time, Pallas kernels for 12%

profile of v17, /device:TPU:0, one launch (start us, length us, event | category | flops | bytes accessed | tf_op | source)
XLA Modules:
  0.0 23.6 jit_solution(10014586282049954787)
XLA Ops:
  0.0 3.5 %ladder.1 = (f32[16,8,128]{2,1,0:T(8,128)S(1)}, f32[57,8,128]{2,1,0:T(8,128)S(1)}, f32[3,32,512]{2,1,0:T(8,128)S(1)}, f32[8,32,512]{2,1,0:T(8,128)S(1)}, f32[7,3...) custom-call(s32[128]{0:T(128)} %index_hbm.1, ...), custom_call_target="tpu_custom_call" | custom-call | flops 40000000 | bytes 6000000 | tf_op jit(solution)/shard_map/ladder/pallas_call | solution.py:484
  3.5 0.5 %collective-permute-start = (f32[57,8,128]{2,1,0:T(8,128)S(1)}, f32[57,8,128]{2,1,0:T(8,128)S(1)}, u32[]{:S(2)}, u32[]{:S(2)}) collective-permute-start(f32[57,8,128]{2,1,0:T(8,128)S(1)} %get-tuple-element.44.away_ref), channel_id=1, source_target_pairs={{0,4},{1,5},{2,6},{3,7},{4,0},{5,1},{6,2},{7,3},{8,12},{9,13},{10,... | collective-permute-start | bytes 700424 | tf_op jit(solution)/shard_map/ppermute | solution.py:476
  4.0 0.3 %rest.1 = (f32[32,8,128]{2,1,0:T(8,128)S(1)}, f32[3,32,512]{2,1,0:T(8,128)S(1)}) custom-call(f32[3,16,32,512]{3,2,1,0:T(8,128)S(1)} %get-tuple-element.33.velocity_ref, f32[16,32,512]{2,1,0:T(8,128)S(1)} %get-tuple-element.36.left_h_ref, f32[16,32,512]{2,1,0:T(8,128)S(1)} %get-tuple-element.37.right_h_ref, f32[7,32,512]{2,1,0:T(8,128)S(1)} %get-tuple-element.41.held_ref, ...), custom_call_target="tpu_custom_call" | custom-call | flops 2000000 | bytes 2000000 | tf_op jit(solution)/shard_map/rest/pallas_call | solution.py:515
  4.3 0.8 %collective-permute-done.mate_ref = f32[57,8,128]{2,1,0:T(8,128)S(1)} collective-permute-done((f32[57,8,128]{2,1,0:T(8,128)S(1)}, f32[57,8,128]{2,1,0:T(8,128)S(1)}, u32[]{:S(2)}, u32[]{:S(2)}) %collective-permute-start) | collective-permute-done | bytes 233504 | tf_op jit(solution)/shard_map/ppermute | solution.py:476
  5.1 0.1 merge.1
  5.2 3.9 %collective-permute-start.1 = (f32[26,8,128]{2,1,0:T(8,128)S(1)}, f32[26,8,128]{2,1,0:T(8,128)S(1)}, u32[]{:S(2)}, u32[]{:S(2)}) collective-permute-start(f32[26,8,128]{2,1,0:T(8,128)S(1)} %get-tuple-element.52), channel_id=1, source_target_pairs={{0,24},{1,25},{2,26},{3,27},{4,28},{5,29},{6,30},{7,31},{8,16},{9,... | collective-permute-start | bytes 319496 | tf_op jit(solution)/shard_map/ppermute | solution.py:476
  9.1 0.5 %collective-permute-start.3 = (f32[25,8,128]{2,1,0:T(8,128)S(1)}, f32[25,8,128]{2,1,0:T(8,128)S(1)}, u32[]{:S(2)}, u32[]{:S(2)}) collective-permute-start(f32[25,8,128]{2,1,0:T(8,128)S(1)} %get-tuple-element.53), channel_id=1, source_target_pairs={{0,16},{1,17},{2,18},{3,19},{4,20},{5,21},{6,22},{7,23},{8,24},{9,... | collective-permute-start | bytes 307208 | tf_op jit(solution)/shard_map/ppermute | solution.py:476
  9.6 0.1 collective-permute-start.2
  10.4 1.1 %inner.1 = (f32[3,16,32,512]{3,2,1,0:T(8,128)S(1)}, f32[16,32,512]{2,1,0:T(8,128)S(1)}, f32[8,128]{1,0:T(8,128)S(1)}) custom-call(f32[3,16,32,512]{3,2,1,0:T(8,128)S(1)} %get-tuple-element.33.velocity_ref, f32[16,32,512]{2,1,0:T(8,128)S(1)} %get-tuple-element.34.left_ref, f32[16,32,512]{2,1,0:T(8,128)S(1)} %get-tuple-element.35.right_ref, ...), custom_call_target="tpu_custom_call" | custom-call | flops 8000000 | bytes 8000000 | tf_op jit(solution)/shard_map/inner/pallas_call | solution.py:541
  11.5 3.1 %collective-permute-done.3.rest_3_ = f32[25,8,128]{2,1,0:T(8,128)S(1)} collective-permute-done((f32[25,8,128]{2,1,0:T(8,128)S(1)}, f32[25,8,128]{2,1,0:T(8,128)S(1)}, u32[]{:S(2)}, u32[]{:S(2)}) %collective-permute-start.3) | collective-permute-done | bytes 102432 | tf_op jit(solution)/shard_map/ppermute | solution.py:476
  14.5 0.2 %collective-permute-done.2.rest_2_ = f32[25,8,128]{2,1,0:T(8,128)S(1)} collective-permute-done((f32[25,8,128]{2,1,0:T(8,128)S(1)}, f32[25,8,128]{2,1,0:T(8,128)S(1)}, u32[]{:S(2)}, u32[]{:S(2)}) %collective-permute-start.2) | collective-permute-done | bytes 102432 | tf_op jit(solution)/shard_map/ppermute | solution.py:476
  14.8 0.0 collective-permute-done.1.rest_1_
  14.8 0.1 spread.1
  14.9 0.1 collective-permute-start.7
  15.0 2.6 %collective-permute-start.4 = (f32[3,8,128]{2,1,0:T(8,128)S(1)}, f32[3,8,128]{2,1,0:T(8,128)S(1)}, u32[]{:S(2)}, u32[]{:S(2)}) collective-permute-start(f32[3,8,128]{2,1,0:T(8,128)S(1)} %get-tuple-element.54.rest_0_), channel_id=1, source_target_pairs={{0,2},{1,3},{2,1},{3,0},{4,6},{5,7},{6,5},{7,4},{8,10},{9,11},{10,... | collective-permute-start | bytes 36872 | tf_op jit(solution)/shard_map/ppermute | solution.py:476
  17.6 1.2 %collective-permute-start.5 = (f32[2,8,128]{2,1,0:T(8,128)S(1)}, f32[2,8,128]{2,1,0:T(8,128)S(1)}, u32[]{:S(2)}, u32[]{:S(2)}) collective-permute-start(f32[2,8,128]{2,1,0:T(8,128)S(1)} %get-tuple-element.55), channel_id=1, source_target_pairs={{0,3},{1,2},{2,0},{3,1},{4,7},{5,6},{6,4},{7,5},{8,11},{9,10},{10,... | collective-permute-start | bytes 24584 | tf_op jit(solution)/shard_map/ppermute | solution.py:476
  18.8 0.3 %collective-permute-start.6 = (f32[1,8,128]{2,1,0:T(8,128)S(1)}, f32[1,8,128]{2,1,0:T(8,128)S(1)}, u32[]{:S(2)}, u32[]{:S(2)}) collective-permute-start(f32[1,8,128]{2,1,0:T(8,128)S(1)} %get-tuple-element.56), channel_id=1, source_target_pairs={{0,1},{1,0},{2,3},{3,2},{4,5},{5,4},{6,7},{7,6},{8,9},{9,8},{10,11... | collective-permute-start | bytes 12296 | tf_op jit(solution)/shard_map/ppermute | solution.py:476
  19.2 0.0 collective-permute-done.7.other_ref
  19.2 1.5 %finish.1 = (f32[3,16,32,512]{3,2,1,0:T(8,128)}, f32[16,32,512]{2,1,0:T(8,128)S(1)}) custom-call(f32[12,8,512]{2,1,0:T(8,128)S(1)} %get-tuple-element.57.own_ref, f32[12,8,512]{2,1,0:T(8,128)S(1)} %collective-permute-done.7.other_ref, f32[3,16,32,512]{3,2,1,0:T(8,128)S(1)} %get-tuple-element.51.rest_0_.base_ref, ...), custom_call_target="tpu_custom_call" | custom-call | flops 3000000 | bytes 6000000 | tf_op jit(solution)/shard_map/finish/pallas_call | solution.py:566
  20.6 1.8 %collective-permute-done.6.rest_3_ = f32[1,8,128]{2,1,0:T(8,128)S(1)} collective-permute-done((f32[1,8,128]{2,1,0:T(8,128)S(1)}, f32[1,8,128]{2,1,0:T(8,128)S(1)}, u32[]{:S(2)}, u32[]{:S(2)}) %collective-permute-start.6) | collective-permute-done | bytes 4128 | tf_op jit(solution)/shard_map/ppermute | solution.py:476
  22.4 0.0 collective-permute-done.5.rest_2_
  22.5 0.0 collective-permute-done.4.rest_1_
  22.5 1.2 %correct.1 = f32[3,16,32,512]{3,2,1,0:T(8,128)} custom-call(f32[8,128]{1,0:T(8,128)S(1)} %get-tuple-element.47.goal_ref, f32[16,32,512]{2,1,0:T(8,128)S(1)} %get-tuple-element.48.unit_ref, f32[3,8,128]{2,1,0:T(8,128)S(1)} %get-tuple-element.54.rest_0_, f32[3,8,128]{2,1,0:T(8,128)S(1)} %collective-permute-done.4.rest_1_, ...), custom_call_target="tpu_custom_call", output_to_operand_aliasing={{}: (7, {})} | custom-call | flops 500000 | bytes 1600000 | tf_op jit(solution)/shard_map/correct/pallas_call | solution.py:579
Async XLA Ops:
  3.5 1.6 %collective-permute-start = (f32[57,8,128]{2,1,0:T(8,128)S(1)}, f32[57,8,128]{2,1,0:T(8,128)S(1)}, u32[]{:S(2)}, u32[]{:S(2)}) collective-permute-start(f32[57,8,128]{2,1,0:T(8,128)S(1)} %get-tuple-element.44.away_ref), channel_id=1, source_target_pairs={{0,4},{1,5},{2,6},{3,7},{4,0},{5,1},{6,2},{7,3},{8,12},{9,13},{10,... | collective-permute-start | bytes 700424 | tf_op jit(solution)/shard_map/ppermute | solution.py:476
  5.2 9.6 %collective-permute-start.1 = (f32[26,8,128]{2,1,0:T(8,128)S(1)}, f32[26,8,128]{2,1,0:T(8,128)S(1)}, u32[]{:S(2)}, u32[]{:S(2)}) collective-permute-start(f32[26,8,128]{2,1,0:T(8,128)S(1)} %get-tuple-element.52), channel_id=1, source_target_pairs={{0,24},{1,25},{2,26},{3,27},{4,28},{5,29},{6,30},{7,31},{8,16},{9,... | collective-permute-start | bytes 319496 | tf_op jit(solution)/shard_map/ppermute | solution.py:476
  9.1 5.5 %collective-permute-start.3 = (f32[25,8,128]{2,1,0:T(8,128)S(1)}, f32[25,8,128]{2,1,0:T(8,128)S(1)}, u32[]{:S(2)}, u32[]{:S(2)}) collective-permute-start(f32[25,8,128]{2,1,0:T(8,128)S(1)} %get-tuple-element.53), channel_id=1, source_target_pairs={{0,16},{1,17},{2,18},{3,19},{4,20},{5,21},{6,22},{7,23},{8,24},{9,... | collective-permute-start | bytes 307208 | tf_op jit(solution)/shard_map/ppermute | solution.py:476
  9.6 5.2 %collective-permute-start.2 = (f32[25,8,128]{2,1,0:T(8,128)S(1)}, f32[25,8,128]{2,1,0:T(8,128)S(1)}, u32[]{:S(2)}, u32[]{:S(2)}) collective-permute-start(f32[25,8,128]{2,1,0:T(8,128)S(1)} %get-tuple-element.46._), channel_id=1, source_target_pairs={{0,8},{1,9},{2,10},{3,11},{4,12},{5,13},{6,14},{7,15},{8,0},{9,1},... | collective-permute-start | bytes 307208 | tf_op jit(solution)/shard_map/ppermute | solution.py:476
  14.9 4.3 %collective-permute-start.7 = (f32[12,8,512]{2,1,0:T(8,128)S(1)}, f32[12,8,512]{2,1,0:T(8,128)S(1)}, u32[]{:S(2)}, u32[]{:S(2)}) collective-permute-start(f32[12,8,512]{2,1,0:T(8,128)S(1)} %get-tuple-element.58), channel_id=1, source_target_pairs={{0,4},{1,5},{2,6},{3,7},{4,0},{5,1},{6,2},{7,3},{8,12},{9,13},{10,... | collective-permute-start | bytes 589832 | tf_op jit(solution)/shard_map/ppermute | solution.py:476
  15.0 7.5 %collective-permute-start.4 = (f32[3,8,128]{2,1,0:T(8,128)S(1)}, f32[3,8,128]{2,1,0:T(8,128)S(1)}, u32[]{:S(2)}, u32[]{:S(2)}) collective-permute-start(f32[3,8,128]{2,1,0:T(8,128)S(1)} %get-tuple-element.54.rest_0_), channel_id=1, source_target_pairs={{0,2},{1,3},{2,1},{3,0},{4,6},{5,7},{6,5},{7,4},{8,10},{9,11},{10,... | collective-permute-start | bytes 36872 | tf_op jit(solution)/shard_map/ppermute | solution.py:476
  17.6 4.8 %collective-permute-start.5 = (f32[2,8,128]{2,1,0:T(8,128)S(1)}, f32[2,8,128]{2,1,0:T(8,128)S(1)}, u32[]{:S(2)}, u32[]{:S(2)}) collective-permute-start(f32[2,8,128]{2,1,0:T(8,128)S(1)} %get-tuple-element.55), channel_id=1, source_target_pairs={{0,3},{1,2},{2,0},{3,1},{4,7},{5,6},{6,4},{7,5},{8,11},{9,10},{10,... | collective-permute-start | bytes 24584 | tf_op jit(solution)/shard_map/ppermute | solution.py:476
  18.8 3.6 %collective-permute-start.6 = (f32[1,8,128]{2,1,0:T(8,128)S(1)}, f32[1,8,128]{2,1,0:T(8,128)S(1)}, u32[]{:S(2)}, u32[]{:S(2)}) collective-permute-start(f32[1,8,128]{2,1,0:T(8,128)S(1)} %get-tuple-element.56), channel_id=1, source_target_pairs={{0,1},{1,0},{2,3},{3,2},{4,5},{5,4},{6,7},{7,6},{8,9},{9,8},{10,11... | collective-permute-start | bytes 12296 | tf_op jit(solution)/shard_map/ppermute | solution.py:476

commit v18 on v17

--- a/solution.py
+++ b/solution.py
@@ -11,6 +11,10 @@
 STRETCHES = 7
 LANES = 128
 MIB = 1024 * 1024
+
+
+def extra(m):
+    return 2 if m % 2 == 0 else int(m > 1)
 
 
 def plane_rounds(columns):
@@ -527,7 +531,7 @@
     *outgoing, near = pl.pallas_call(
         functools.partial(merge_kernel, chips, components),
         out_shape=[
-            shape(half * components * count + m.bit_count(), SUB, LANES) for m in range(1, chips)
+            shape(half * components * count + 1 + extra(m), SUB, LANES) for m in range(1, chips)
         ] + [shape(half * 2 * components * count + 1, SUB, LANES)],
         in_specs=[vmem] * 5,
         out_specs=[vmem] * chips,
@@ -535,7 +539,7 @@
         cost_estimate=cost(500_000, 1_600_000),
         name="merge",
     )(mine, sums, away, mate, pair)
-    order = sorted(range(1, chips), key=lambda m: -m.bit_count())
+    order = sorted(range(1, chips), key=extra, reverse=True)
     incoming = [send(outgoing[m - 1], lambda z, y: (z ^ (2 * m), y)) for m in order]
     profile = shape(cells, *plane)
     base, unit, goal = pl.pallas_call(

time: 23.8 us -> 23.9 us (level)
  transfers between devices with their start and end apart: 8 -> 8, of which waited for: 4 -> 3; matrix products, arithmetic and copies ran while one was open for 0% -> 0% of each run, Pallas kernels for 12% -> 12%
where the time goes in v18:
time: 23.9 us; the launch traced here: 23.8 us
  starting transfers between devices  9.45 us (40%)
  Pallas kernels  7.69 us (32%)
  waiting for transfers between devices  5.95 us (25%)
  between operations  0.7 us (3%)
    ppermute x8, starting transfers between devices, send(): return lax.ppermute(array, ('gz', 'gy'), route)  9.45 us
    ppermute x8, waiting for transfers between devices, send(): return lax.ppermute(array, ('gz', 'gy'), route)  5.95 us
    pallas_call x1, Pallas kernels, shards(): pl.pallas_call(functools.partial(ladder_kernel, cells, blocks, chips, lin...  3.48 us
    pallas_call x1, Pallas kernels, shards(): pl.pallas_call(finish_kernel, out_shape=[shape(*velocity.shape), profile]...  1.45 us
    pallas_call x1, Pallas kernels, shards(): pl.pallas_call(functools.partial(correct_kernel, len(tiles)), out_shape=s...  1.18 us
    pallas_call x1, Pallas kernels, shards(): pl.pallas_call(inner_kernel, out_shape=[shape(*velocity.shape), profile,...  1.11 us
  transfers between devices with their start and end apart: 8, of which 3 were waited for; matrix products, arithmetic and copies ran while one was open for 0% of the time, Pallas kernels for 12%

profile of v18, /device:TPU:0, one launch (start us, length us, event | category | flops | bytes accessed | tf_op | source)
XLA Modules:
  0.0 23.8 jit_solution(18135843879398354970)
XLA Ops:
  0.0 3.5 %ladder.1 = (f32[16,8,128]{2,1,0:T(8,128)S(1)}, f32[57,8,128]{2,1,0:T(8,128)S(1)}, f32[3,32,512]{2,1,0:T(8,128)S(1)}, f32[8,32,512]{2,1,0:T(8,128)S(1)}, f32[7,3...) custom-call(s32[128]{0:T(128)} %index_hbm.1, ...), custom_call_target="tpu_custom_call" | custom-call | flops 40000000 | bytes 6000000 | tf_op jit(solution)/shard_map/ladder/pallas_call | solution.py:488
  3.5 0.5 %collective-permute-start = (f32[57,8,128]{2,1,0:T(8,128)S(1)}, f32[57,8,128]{2,1,0:T(8,128)S(1)}, u32[]{:S(2)}, u32[]{:S(2)}) collective-permute-start(f32[57,8,128]{2,1,0:T(8,128)S(1)} %get-tuple-element.44.away_ref), channel_id=1, source_target_pairs={{0,4},{1,5},{2,6},{3,7},{4,0},{5,1},{6,2},{7,3},{8,12},{9,13},{10,... | collective-permute-start | bytes 700424 | tf_op jit(solution)/shard_map/ppermute | solution.py:480
  4.0 0.3 %rest.1 = (f32[32,8,128]{2,1,0:T(8,128)S(1)}, f32[3,32,512]{2,1,0:T(8,128)S(1)}) custom-call(f32[3,16,32,512]{3,2,1,0:T(8,128)S(1)} %get-tuple-element.33.velocity_ref, f32[16,32,512]{2,1,0:T(8,128)S(1)} %get-tuple-element.36.left_h_ref, f32[16,32,512]{2,1,0:T(8,128)S(1)} %get-tuple-element.37.right_h_ref, f32[7,32,512]{2,1,0:T(8,128)S(1)} %get-tuple-element.41.held_ref, ...), custom_call_target="tpu_custom_call" | custom-call | flops 2000000 | bytes 2000000 | tf_op jit(solution)/shard_map/rest/pallas_call | solution.py:519
  4.3 0.8 %collective-permute-done.mate_ref = f32[57,8,128]{2,1,0:T(8,128)S(1)} collective-permute-done((f32[57,8,128]{2,1,0:T(8,128)S(1)}, f32[57,8,128]{2,1,0:T(8,128)S(1)}, u32[]{:S(2)}, u32[]{:S(2)}) %collective-permute-start) | collective-permute-done | bytes 233504 | tf_op jit(solution)/shard_map/ppermute | solution.py:480
  5.1 0.1 merge.1
  5.2 3.0 %collective-permute-start.1 = (f32[27,8,128]{2,1,0:T(8,128)S(1)}, f32[27,8,128]{2,1,0:T(8,128)S(1)}, u32[]{:S(2)}, u32[]{:S(2)}) collective-permute-start(f32[27,8,128]{2,1,0:T(8,128)S(1)} %get-tuple-element.52), channel_id=1, source_target_pairs={{0,16},{1,17},{2,18},{3,19},{4,20},{5,21},{6,22},{7,23},{8,24},{9,... | collective-permute-start | bytes 331784 | tf_op jit(solution)/shard_map/ppermute | solution.py:480
  8.1 1.4 %collective-permute-start.2 = (f32[26,8,128]{2,1,0:T(8,128)S(1)}, f32[26,8,128]{2,1,0:T(8,128)S(1)}, u32[]{:S(2)}, u32[]{:S(2)}) collective-permute-start(f32[26,8,128]{2,1,0:T(8,128)S(1)} %get-tuple-element.53), channel_id=1, source_target_pairs={{0,24},{1,25},{2,26},{3,27},{4,28},{5,29},{6,30},{7,31},{8,16},{9,... | collective-permute-start | bytes 319496 | tf_op jit(solution)/shard_map/ppermute | solution.py:480
  9.6 0.1 collective-permute-start.3
  10.3 1.1 %inner.1 = (f32[3,16,32,512]{3,2,1,0:T(8,128)S(1)}, f32[16,32,512]{2,1,0:T(8,128)S(1)}, f32[8,128]{1,0:T(8,128)S(1)}) custom-call(f32[3,16,32,512]{3,2,1,0:T(8,128)S(1)} %get-tuple-element.33.velocity_ref, f32[16,32,512]{2,1,0:T(8,128)S(1)} %get-tuple-element.34.left_ref, f32[16,32,512]{2,1,0:T(8,128)S(1)} %get-tuple-element.35.right_ref, ...), custom_call_target="tpu_custom_call" | custom-call | flops 8000000 | bytes 8000000 | tf_op jit(solution)/shard_map/inner/pallas_call | solution.py:545
  11.5 3.5 %collective-permute-done.3.rest_3_ = f32[25,8,128]{2,1,0:T(8,128)S(1)} collective-permute-done((f32[25,8,128]{2,1,0:T(8,128)S(1)}, f32[25,8,128]{2,1,0:T(8,128)S(1)}, u32[]{:S(2)}, u32[]{:S(2)}) %collective-permute-start.3) | collective-permute-done | bytes 102432 | tf_op jit(solution)/shard_map/ppermute | solution.py:480
  14.9 0.0 collective-permute-done.2.rest_2_
  14.9 0.0 collective-permute-done.1.rest_1_
  14.9 0.1 spread.1
  15.0 0.1 collective-permute-start.7
  15.1 2.8 %collective-permute-start.4 = (f32[3,8,128]{2,1,0:T(8,128)S(1)}, f32[3,8,128]{2,1,0:T(8,128)S(1)}, u32[]{:S(2)}, u32[]{:S(2)}) collective-permute-start(f32[3,8,128]{2,1,0:T(8,128)S(1)} %get-tuple-element.54.rest_0_), channel_id=1, source_target_pairs={{0,2},{1,3},{2,1},{3,0},{4,6},{5,7},{6,5},{7,4},{8,10},{9,11},{10,... | collective-permute-start | bytes 36872 | tf_op jit(solution)/shard_map/ppermute | solution.py:480
  17.9 1.1 %collective-permute-start.5 = (f32[2,8,128]{2,1,0:T(8,128)S(1)}, f32[2,8,128]{2,1,0:T(8,128)S(1)}, u32[]{:S(2)}, u32[]{:S(2)}) collective-permute-start(f32[2,8,128]{2,1,0:T(8,128)S(1)} %get-tuple-element.55), channel_id=1, source_target_pairs={{0,3},{1,2},{2,0},{3,1},{4,7},{5,6},{6,4},{7,5},{8,11},{9,10},{10,... | collective-permute-start | bytes 24584 | tf_op jit(solution)/shard_map/ppermute | solution.py:480
  19.0 0.5 %collective-permute-start.6 = (f32[1,8,128]{2,1,0:T(8,128)S(1)}, f32[1,8,128]{2,1,0:T(8,128)S(1)}, u32[]{:S(2)}, u32[]{:S(2)}) collective-permute-start(f32[1,8,128]{2,1,0:T(8,128)S(1)} %get-tuple-element.56), channel_id=1, source_target_pairs={{0,1},{1,0},{2,3},{3,2},{4,5},{5,4},{6,7},{7,6},{8,9},{9,8},{10,11... | collective-permute-start | bytes 12296 | tf_op jit(solution)/shard_map/ppermute | solution.py:480
  19.5 0.0 collective-permute-done.7.other_ref
  19.5 1.5 %finish.1 = (f32[3,16,32,512]{3,2,1,0:T(8,128)}, f32[16,32,512]{2,1,0:T(8,128)S(1)}) custom-call(f32[12,8,512]{2,1,0:T(8,128)S(1)} %get-tuple-element.57.own_ref, f32[12,8,512]{2,1,0:T(8,128)S(1)} %collective-permute-done.7.other_ref, f32[3,16,32,512]{3,2,1,0:T(8,128)S(1)} %get-tuple-element.51.rest_0_.base_ref, ...), custom_call_target="tpu_custom_call" | custom-call | flops 3000000 | bytes 6000000 | tf_op jit(solution)/shard_map/finish/pallas_call | solution.py:570
  20.9 1.7 %collective-permute-done.6.rest_3_ = f32[1,8,128]{2,1,0:T(8,128)S(1)} collective-permute-done((f32[1,8,128]{2,1,0:T(8,128)S(1)}, f32[1,8,128]{2,1,0:T(8,128)S(1)}, u32[]{:S(2)}, u32[]{:S(2)}) %collective-permute-start.6) | collective-permute-done | bytes 4128 | tf_op jit(solution)/shard_map/ppermute | solution.py:480
  22.6 0.0 collective-permute-done.5.rest_2_
  22.6 0.0 collective-permute-done.4.rest_1_
  22.6 1.2 %correct.1 = f32[3,16,32,512]{3,2,1,0:T(8,128)} custom-call(f32[8,128]{1,0:T(8,128)S(1)} %get-tuple-element.47.goal_ref, f32[16,32,512]{2,1,0:T(8,128)S(1)} %get-tuple-element.48.unit_ref, f32[3,8,128]{2,1,0:T(8,128)S(1)} %get-tuple-element.54.rest_0_, f32[3,8,128]{2,1,0:T(8,128)S(1)} %collective-permute-done.4.rest_1_, ...), custom_call_target="tpu_custom_call", output_to_operand_aliasing={{}: (7, {})} | custom-call | flops 500000 | bytes 1600000 | tf_op jit(solution)/shard_map/correct/pallas_call | solution.py:583
Async XLA Ops:
  3.5 1.6 %collective-permute-start = (f32[57,8,128]{2,1,0:T(8,128)S(1)}, f32[57,8,128]{2,1,0:T(8,128)S(1)}, u32[]{:S(2)}, u32[]{:S(2)}) collective-permute-start(f32[57,8,128]{2,1,0:T(8,128)S(1)} %get-tuple-element.44.away_ref), channel_id=1, source_target_pairs={{0,4},{1,5},{2,6},{3,7},{4,0},{5,1},{6,2},{7,3},{8,12},{9,13},{10,... | collective-permute-start | bytes 700424 | tf_op jit(solution)/shard_map/ppermute | solution.py:480
  5.2 9.7 %collective-permute-start.1 = (f32[27,8,128]{2,1,0:T(8,128)S(1)}, f32[27,8,128]{2,1,0:T(8,128)S(1)}, u32[]{:S(2)}, u32[]{:S(2)}) collective-permute-start(f32[27,8,128]{2,1,0:T(8,128)S(1)} %get-tuple-element.52), channel_id=1, source_target_pairs={{0,16},{1,17},{2,18},{3,19},{4,20},{5,21},{6,22},{7,23},{8,24},{9,... | collective-permute-start | bytes 331784 | tf_op jit(solution)/shard_map/ppermute | solution.py:480
  8.1 6.8 %collective-permute-start.2 = (f32[26,8,128]{2,1,0:T(8,128)S(1)}, f32[26,8,128]{2,1,0:T(8,128)S(1)}, u32[]{:S(2)}, u32[]{:S(2)}) collective-permute-start(f32[26,8,128]{2,1,0:T(8,128)S(1)} %get-tuple-element.53), channel_id=1, source_target_pairs={{0,24},{1,25},{2,26},{3,27},{4,28},{5,29},{6,30},{7,31},{8,16},{9,... | collective-permute-start | bytes 319496 | tf_op jit(solution)/shard_map/ppermute | solution.py:480
  9.6 5.3 %collective-permute-start.3 = (f32[25,8,128]{2,1,0:T(8,128)S(1)}, f32[25,8,128]{2,1,0:T(8,128)S(1)}, u32[]{:S(2)}, u32[]{:S(2)}) collective-permute-start(f32[25,8,128]{2,1,0:T(8,128)S(1)} %get-tuple-element.46._), channel_id=1, source_target_pairs={{0,8},{1,9},{2,10},{3,11},{4,12},{5,13},{6,14},{7,15},{8,0},{9,1},... | collective-permute-start | bytes 307208 | tf_op jit(solution)/shard_map/ppermute | solution.py:480
  15.0 4.4 %collective-permute-start.7 = (f32[12,8,512]{2,1,0:T(8,128)S(1)}, f32[12,8,512]{2,1,0:T(8,128)S(1)}, u32[]{:S(2)}, u32[]{:S(2)}) collective-permute-start(f32[12,8,512]{2,1,0:T(8,128)S(1)} %get-tuple-element.58), channel_id=1, source_target_pairs={{0,4},{1,5},{2,6},{3,7},{4,0},{5,1},{6,2},{7,3},{8,12},{9,13},{10,... | collective-permute-start | bytes 589832 | tf_op jit(solution)/shard_map/ppermute | solution.py:480
  15.1 7.5 %collective-permute-start.4 = (f32[3,8,128]{2,1,0:T(8,128)S(1)}, f32[3,8,128]{2,1,0:T(8,128)S(1)}, u32[]{:S(2)}, u32[]{:S(2)}) collective-permute-start(f32[3,8,128]{2,1,0:T(8,128)S(1)} %get-tuple-element.54.rest_0_), channel_id=1, source_target_pairs={{0,2},{1,3},{2,1},{3,0},{4,6},{5,7},{6,5},{7,4},{8,10},{9,11},{10,... | collective-permute-start | bytes 36872 | tf_op jit(solution)/shard_map/ppermute | solution.py:480
  17.9 4.7 %collective-permute-start.5 = (f32[2,8,128]{2,1,0:T(8,128)S(1)}, f32[2,8,128]{2,1,0:T(8,128)S(1)}, u32[]{:S(2)}, u32[]{:S(2)}) collective-permute-start(f32[2,8,128]{2,1,0:T(8,128)S(1)} %get-tuple-element.55), channel_id=1, source_target_pairs={{0,3},{1,2},{2,0},{3,1},{4,7},{5,6},{6,4},{7,5},{8,11},{9,10},{10,... | collective-permute-start | bytes 24584 | tf_op jit(solution)/shard_map/ppermute | solution.py:480
  19.0 3.6 %collective-permute-start.6 = (f32[1,8,128]{2,1,0:T(8,128)S(1)}, f32[1,8,128]{2,1,0:T(8,128)S(1)}, u32[]{:S(2)}, u32[]{:S(2)}) collective-permute-start(f32[1,8,128]{2,1,0:T(8,128)S(1)} %get-tuple-element.56), channel_id=1, source_target_pairs={{0,1},{1,0},{2,3},{3,2},{4,5},{5,4},{6,7},{7,6},{8,9},{9,8},{10,11... | collective-permute-start | bytes 12296 | tf_op jit(solution)/shard_map/ppermute | solution.py:480

commit v19 on v17

--- a/solution.py
+++ b/solution.py
@@ -265,11 +265,12 @@
     lax.fori_loop(0, half, of_tile, 0)
 
 
-def merge_kernel(chips, components, mine_ref, sums_ref, away_ref, mate_ref, pair_ref, *rest):
+def merge_kernel(orders, components, mine_ref, sums_ref, away_ref, mate_ref, pair_ref, *rest):
     send_refs, near_ref = rest[:-1], rest[-1]
     me = lax.axis_index("gz")
     chip = me // 2
     is_first = me == chip * 2
+    steps = [jnp.where(is_first, a, b) for a, b in zip(*orders)]
     count = pair_ref.shape[2] // LANES
     half = mine_ref.shape[0] // (2 * count)
     slot = away_ref.shape[0] - 1
@@ -303,18 +304,19 @@
             second = jnp.where(is_first, mate, mine)
             put(near_ref, at, second)
             to_left = first + back * second
-            for m in range(1, chips):
+            for m, ref in zip(steps, send_refs):
                 goes_right = (chip ^ m) > chip
-                sheet = jnp.where(goes_right, to_right, to_left)
-                put(send_refs[m - 1], i * components + c, sheet)
-
-
-def spread_kernel(order, components, near_ref, pair_ref, chip_ref, *rest):
-    recv_refs = rest[1:len(order) + 1]
-    own_ref, other_ref, *tile_refs = rest[len(order) + 1:]
+                put(ref, i * components + c, jnp.where(goes_right, to_right, to_left))
+
+
+def spread_kernel(orders, components, near_ref, pair_ref, chip_ref, *rest):
+    count = len(orders[0])
+    recv_refs = rest[1:count + 1]
+    own_ref, other_ref, *tile_refs = rest[count + 1:]
     me = lax.axis_index("gz")
     chip = me // 2
     is_first = me == chip * 2
+    steps = [jnp.where(is_first, a, b) for a, b in zip(*orders)]
     count = pair_ref.shape[2] // LANES
     half = near_ref.shape[0] // (2 * components * count)
     tiles = [ref[ref.shape[0] - 1] for ref in (near_ref, *recv_refs)]
@@ -324,11 +326,11 @@
             ref[i] = tile
     for i in range(half):
         rows = row_tile((me - chip * 2) * half + i)
-        coefs = [chip_ref[m - 1, rows] for m in order]
+        coefs = [chip_ref[m - 1, rows] for m in steps]
         for c in range(components):
             left_in = jnp.zeros(own_ref.shape[1:], jnp.float32)
             right_in = jnp.zeros(own_ref.shape[1:], jnp.float32)
-            for m, coef, ref in zip(order, coefs, recv_refs):
+            for m, coef, ref in zip(steps, coefs, recv_refs):
                 term = coef * get(ref, i * components + c, count)
                 from_left = (chip ^ m) < chip
                 left_in = left_in + jnp.where(from_left, term, 0.0)
@@ -524,10 +526,14 @@
         cost_estimate=cost(2_000_000, 2_000_000),
         name="rest",
     )(near_velocity, left_h, right_h, held, through)
+    even = sorted(range(1, chips), key=lambda m: (m.bit_count(), m), reverse=True)
+    odd = even[-1:] + even[:-1]
+    orders = (even, odd)
     *outgoing, near = pl.pallas_call(
-        functools.partial(merge_kernel, chips, components),
+        functools.partial(merge_kernel, orders, components),
         out_shape=[
-            shape(half * components * count + m.bit_count(), SUB, LANES) for m in range(1, chips)
+            shape(half * components * count + 1 + max(0, 2 - k), SUB, LANES)
+            for k in range(chips - 1)
         ] + [shape(half * 2 * components * count + 1, SUB, LANES)],
         in_specs=[vmem] * 5,
         out_specs=[vmem] * chips,
@@ -535,8 +541,10 @@
         cost_estimate=cost(500_000, 1_600_000),
         name="merge",
     )(mine, sums, away, mate, pair)
-    order = sorted(range(1, chips), key=lambda m: -m.bit_count())
-    incoming = [send(outgoing[m - 1], lambda z, y: (z ^ (2 * m), y)) for m in order]
+    incoming = [
+        send(array, lambda z, y: (z ^ (2 * orders[z % 2][k]), y))
+        for k, array in enumerate(outgoing)
+    ]
     profile = shape(cells, *plane)
     base, unit, goal = pl.pallas_call(
         inner_kernel,
@@ -550,7 +558,7 @@
       outgoing[0])
     rounds = plane_rounds(columns)
     own_in, other_out, *tile = pl.pallas_call(
-        functools.partial(spread_kernel, order, components),
+        functools.partial(spread_kernel, orders, components),
         out_shape=[shape(half * 2 * components, *sheet)] * 2
         + [shape(len(rounds) - i, SUB, LANES) for i in range(len(rounds))],
         in_specs=[vmem] * 3 + [anywhere] + [vmem] * (chips - 1),

time: 23.8 us -> 24.9 us (1.046)
  waiting for transfers between devices: 5.92 us -> 6.7 us
    ppermute x8, waiting for transfers between devices: 5.92 us -> 6.7 us  [send(): return lax.ppermute(array, ('gz', 'gy'), route)]
where the time goes in v19:
time: 24.9 us; the launch traced here: 24.7 us
  starting transfers between devices  9.55 us (38%)
  Pallas kernels  7.75 us (31%)
  waiting for transfers between devices  6.7 us (27%)
  between operations  0.7 us (3%)
    ppermute x8, starting transfers between devices, send(): return lax.ppermute(array, ('gz', 'gy'), route)  9.55 us
    ppermute x8, waiting for transfers between devices, send(): return lax.ppermute(array, ('gz', 'gy'), route)  6.7 us
    pallas_call x1, Pallas kernels, shards(): pl.pallas_call(functools.partial(ladder_kernel, cells, blocks, chips, lin...  3.49 us
    pallas_call x1, Pallas kernels, shards(): pl.pallas_call(finish_kernel, out_shape=[shape(*velocity.shape), profile]...  1.47 us
    pallas_call x1, Pallas kernels, shards(): pl.pallas_call(functools.partial(correct_kernel, len(tiles)), out_shape=s...  1.18 us
    pallas_call x1, Pallas kernels, shards(): pl.pallas_call(inner_kernel, out_shape=[shape(*velocity.shape), profile,...  1.15 us
  transfers between devices with their start and end apart: 8, of which 4 were waited for; matrix products, arithmetic and copies ran while one was open for 0% of the time, Pallas kernels for 12%

profile of v19, /device:TPU:0, one launch (start us, length us, event | category | flops | bytes accessed | tf_op | source)
XLA Modules:
  0.0 24.7 jit_solution(17491557001802424885)
XLA Ops:
  0.0 3.5 %ladder.1 = (f32[16,8,128]{2,1,0:T(8,128)S(1)}, f32[57,8,128]{2,1,0:T(8,128)S(1)}, f32[3,32,512]{2,1,0:T(8,128)S(1)}, f32[8,32,512]{2,1,0:T(8,128)S(1)}, f32[7,3...) custom-call(s32[128]{0:T(128)} %index_hbm.1, ...), custom_call_target="tpu_custom_call" | custom-call | flops 40000000 | bytes 6000000 | tf_op jit(solution)/shard_map/ladder/pallas_call | solution.py:486
  3.5 0.5 %collective-permute-start = (f32[57,8,128]{2,1,0:T(8,128)S(1)}, f32[57,8,128]{2,1,0:T(8,128)S(1)}, u32[]{:S(2)}, u32[]{:S(2)}) collective-permute-start(f32[57,8,128]{2,1,0:T(8,128)S(1)} %get-tuple-element.44.away_ref), channel_id=1, source_target_pairs={{0,4},{1,5},{2,6},{3,7},{4,0},{5,1},{6,2},{7,3},{8,12},{9,13},{10,... | collective-permute-start | bytes 700424 | tf_op jit(solution)/shard_map/ppermute | solution.py:478
  4.0 0.3 %rest.1 = (f32[32,8,128]{2,1,0:T(8,128)S(1)}, f32[3,32,512]{2,1,0:T(8,128)S(1)}) custom-call(f32[3,16,32,512]{3,2,1,0:T(8,128)S(1)} %get-tuple-element.33.velocity_ref, f32[16,32,512]{2,1,0:T(8,128)S(1)} %get-tuple-element.36.left_h_ref, f32[16,32,512]{2,1,0:T(8,128)S(1)} %get-tuple-element.37.right_h_ref, f32[7,32,512]{2,1,0:T(8,128)S(1)} %get-tuple-element.41.held_ref, ...), custom_call_target="tpu_custom_call" | custom-call | flops 2000000 | bytes 2000000 | tf_op jit(solution)/shard_map/rest/pallas_call | solution.py:517
  4.3 0.8 %collective-permute-done.mate_ref = f32[57,8,128]{2,1,0:T(8,128)S(1)} collective-permute-done((f32[57,8,128]{2,1,0:T(8,128)S(1)}, f32[57,8,128]{2,1,0:T(8,128)S(1)}, u32[]{:S(2)}, u32[]{:S(2)}) %collective-permute-start) | collective-permute-done | bytes 233504 | tf_op jit(solution)/shard_map/ppermute | solution.py:478
  5.1 0.1 merge.1
  5.2 3.9 %collective-permute-start.1 = (f32[27,8,128]{2,1,0:T(8,128)S(1)}, f32[27,8,128]{2,1,0:T(8,128)S(1)}, u32[]{:S(2)}, u32[]{:S(2)}) collective-permute-start(f32[27,8,128]{2,1,0:T(8,128)S(1)} %get-tuple-element.46._), channel_id=1, source_target_pairs={{0,24},{1,25},{2,26},{3,27},{4,12},{5,13},{6,14},{7,15},{8,16},{9,... | collective-permute-start | bytes 331784 | tf_op jit(solution)/shard_map/ppermute | solution.py:478
  9.1 0.5 %collective-permute-start.2 = (f32[26,8,128]{2,1,0:T(8,128)S(1)}, f32[26,8,128]{2,1,0:T(8,128)S(1)}, u32[]{:S(2)}, u32[]{:S(2)}) collective-permute-start(f32[26,8,128]{2,1,0:T(8,128)S(1)} %get-tuple-element.52), channel_id=1, source_target_pairs={{0,16},{1,17},{2,18},{3,19},{4,28},{5,29},{6,30},{7,31},{8,24},{9,... | collective-permute-start | bytes 319496 | tf_op jit(solution)/shard_map/ppermute | solution.py:478
  9.6 0.1 collective-permute-start.3
  10.4 1.1 %inner.1 = (f32[3,16,32,512]{3,2,1,0:T(8,128)S(1)}, f32[16,32,512]{2,1,0:T(8,128)S(1)}, f32[8,128]{1,0:T(8,128)S(1)}) custom-call(f32[3,16,32,512]{3,2,1,0:T(8,128)S(1)} %get-tuple-element.33.velocity_ref, f32[16,32,512]{2,1,0:T(8,128)S(1)} %get-tuple-element.34.left_ref, f32[16,32,512]{2,1,0:T(8,128)S(1)} %get-tuple-element.35.right_ref, ...), custom_call_target="tpu_custom_call" | custom-call | flops 8000000 | bytes 8000000 | tf_op jit(solution)/shard_map/inner/pallas_call | solution.py:549
  11.5 3.1 %collective-permute-done.3.rest_3_ = f32[25,8,128]{2,1,0:T(8,128)S(1)} collective-permute-done((f32[25,8,128]{2,1,0:T(8,128)S(1)}, f32[25,8,128]{2,1,0:T(8,128)S(1)}, u32[]{:S(2)}, u32[]{:S(2)}) %collective-permute-start.3) | collective-permute-done | bytes 102432 | tf_op jit(solution)/shard_map/ppermute | solution.py:478
  14.6 1.1 %collective-permute-done.2.rest_2_ = f32[26,8,128]{2,1,0:T(8,128)S(1)} collective-permute-done((f32[26,8,128]{2,1,0:T(8,128)S(1)}, f32[26,8,128]{2,1,0:T(8,128)S(1)}, u32[]{:S(2)}, u32[]{:S(2)}) %collective-permute-start.2) | collective-permute-done | bytes 106528 | tf_op jit(solution)/shard_map/ppermute | solution.py:478
  15.8 0.0 collective-permute-done.1.rest_1_
  15.8 0.1 spread.1
  15.9 0.1 collective-permute-start.7
  16.0 2.9 %collective-permute-start.4 = (f32[3,8,128]{2,1,0:T(8,128)S(1)}, f32[3,8,128]{2,1,0:T(8,128)S(1)}, u32[]{:S(2)}, u32[]{:S(2)}) collective-permute-start(f32[3,8,128]{2,1,0:T(8,128)S(1)} %get-tuple-element.54.rest_0_), channel_id=1, source_target_pairs={{0,2},{1,3},{2,1},{3,0},{4,6},{5,7},{6,5},{7,4},{8,10},{9,11},{10,... | collective-permute-start | bytes 36872 | tf_op jit(solution)/shard_map/ppermute | solution.py:478
  18.8 1.1 %collective-permute-start.5 = (f32[2,8,128]{2,1,0:T(8,128)S(1)}, f32[2,8,128]{2,1,0:T(8,128)S(1)}, u32[]{:S(2)}, u32[]{:S(2)}) collective-permute-start(f32[2,8,128]{2,1,0:T(8,128)S(1)} %get-tuple-element.55), channel_id=1, source_target_pairs={{0,3},{1,2},{2,0},{3,1},{4,7},{5,6},{6,4},{7,5},{8,11},{9,10},{10,... | collective-permute-start | bytes 24584 | tf_op jit(solution)/shard_map/ppermute | solution.py:478
  19.9 0.5 %collective-permute-start.6 = (f32[1,8,128]{2,1,0:T(8,128)S(1)}, f32[1,8,128]{2,1,0:T(8,128)S(1)}, u32[]{:S(2)}, u32[]{:S(2)}) collective-permute-start(f32[1,8,128]{2,1,0:T(8,128)S(1)} %get-tuple-element.56), channel_id=1, source_target_pairs={{0,1},{1,0},{2,3},{3,2},{4,5},{5,4},{6,7},{7,6},{8,9},{9,8},{10,11... | collective-permute-start | bytes 12296 | tf_op jit(solution)/shard_map/ppermute | solution.py:478
  20.4 0.0 collective-permute-done.7.other_ref
  20.4 1.5 %finish.1 = (f32[3,16,32,512]{3,2,1,0:T(8,128)}, f32[16,32,512]{2,1,0:T(8,128)S(1)}) custom-call(f32[12,8,512]{2,1,0:T(8,128)S(1)} %get-tuple-element.57.own_ref, f32[12,8,512]{2,1,0:T(8,128)S(1)} %collective-permute-done.7.other_ref, f32[3,16,32,512]{3,2,1,0:T(8,128)S(1)} %get-tuple-element.51.rest_0_.base_ref, ...), custom_call_target="tpu_custom_call" | custom-call | flops 3000000 | bytes 6000000 | tf_op jit(solution)/shard_map/finish/pallas_call | solution.py:574
  21.9 1.6 %collective-permute-done.6.rest_3_ = f32[1,8,128]{2,1,0:T(8,128)S(1)} collective-permute-done((f32[1,8,128]{2,1,0:T(8,128)S(1)}, f32[1,8,128]{2,1,0:T(8,128)S(1)}, u32[]{:S(2)}, u32[]{:S(2)}) %collective-permute-start.6) | collective-permute-done | bytes 4128 | tf_op jit(solution)/shard_map/ppermute | solution.py:478
  23.5 0.0 collective-permute-done.5.rest_2_
  23.5 0.0 collective-permute-done.4.rest_1_
  23.5 1.2 %correct.1 = f32[3,16,32,512]{3,2,1,0:T(8,128)} custom-call(f32[8,128]{1,0:T(8,128)S(1)} %get-tuple-element.47.goal_ref, f32[16,32,512]{2,1,0:T(8,128)S(1)} %get-tuple-element.48.unit_ref, f32[3,8,128]{2,1,0:T(8,128)S(1)} %get-tuple-element.54.rest_0_, f32[3,8,128]{2,1,0:T(8,128)S(1)} %collective-permute-done.4.rest_1_, ...), custom_call_target="tpu_custom_call", output_to_operand_aliasing={{}: (7, {})} | custom-call | flops 500000 | bytes 1600000 | tf_op jit(solution)/shard_map/correct/pallas_call | solution.py:587
Async XLA Ops:
  3.5 1.6 %collective-permute-start = (f32[57,8,128]{2,1,0:T(8,128)S(1)}, f32[57,8,128]{2,1,0:T(8,128)S(1)}, u32[]{:S(2)}, u32[]{:S(2)}) collective-permute-start(f32[57,8,128]{2,1,0:T(8,128)S(1)} %get-tuple-element.44.away_ref), channel_id=1, source_target_pairs={{0,4},{1,5},{2,6},{3,7},{4,0},{5,1},{6,2},{7,3},{8,12},{9,13},{10,... | collective-permute-start | bytes 700424 | tf_op jit(solution)/shard_map/ppermute | solution.py:478
  5.2 10.6 %collective-permute-start.1 = (f32[27,8,128]{2,1,0:T(8,128)S(1)}, f32[27,8,128]{2,1,0:T(8,128)S(1)}, u32[]{:S(2)}, u32[]{:S(2)}) collective-permute-start(f32[27,8,128]{2,1,0:T(8,128)S(1)} %get-tuple-element.46._), channel_id=1, source_target_pairs={{0,24},{1,25},{2,26},{3,27},{4,12},{5,13},{6,14},{7,15},{8,16},{9,... | collective-permute-start | bytes 331784 | tf_op jit(solution)/shard_map/ppermute | solution.py:478
  9.1 6.7 %collective-permute-start.2 = (f32[26,8,128]{2,1,0:T(8,128)S(1)}, f32[26,8,128]{2,1,0:T(8,128)S(1)}, u32[]{:S(2)}, u32[]{:S(2)}) collective-permute-start(f32[26,8,128]{2,1,0:T(8,128)S(1)} %get-tuple-element.52), channel_id=1, source_target_pairs={{0,16},{1,17},{2,18},{3,19},{4,28},{5,29},{6,30},{7,31},{8,24},{9,... | collective-permute-start | bytes 319496 | tf_op jit(solution)/shard_map/ppermute | solution.py:478
  9.6 5.0 %collective-permute-start.3 = (f32[25,8,128]{2,1,0:T(8,128)S(1)}, f32[25,8,128]{2,1,0:T(8,128)S(1)}, u32[]{:S(2)}, u32[]{:S(2)}) collective-permute-start(f32[25,8,128]{2,1,0:T(8,128)S(1)} %get-tuple-element.53), channel_id=1, source_target_pairs={{0,8},{1,9},{2,10},{3,11},{4,20},{5,21},{6,22},{7,23},{8,0},{9,1},... | collective-permute-start | bytes 307208 | tf_op jit(solution)/shard_map/ppermute | solution.py:478
  15.9 4.5 %collective-permute-start.7 = (f32[12,8,512]{2,1,0:T(8,128)S(1)}, f32[12,8,512]{2,1,0:T(8,128)S(1)}, u32[]{:S(2)}, u32[]{:S(2)}) collective-permute-start(f32[12,8,512]{2,1,0:T(8,128)S(1)} %get-tuple-element.58), channel_id=1, source_target_pairs={{0,4},{1,5},{2,6},{3,7},{4,0},{5,1},{6,2},{7,3},{8,12},{9,13},{10,... | collective-permute-start | bytes 589832 | tf_op jit(solution)/shard_map/ppermute | solution.py:478
  16.0 7.6 %collective-permute-start.4 = (f32[3,8,128]{2,1,0:T(8,128)S(1)}, f32[3,8,128]{2,1,0:T(8,128)S(1)}, u32[]{:S(2)}, u32[]{:S(2)}) collective-permute-start(f32[3,8,128]{2,1,0:T(8,128)S(1)} %get-tuple-element.54.rest_0_), channel_id=1, source_target_pairs={{0,2},{1,3},{2,1},{3,0},{4,6},{5,7},{6,5},{7,4},{8,10},{9,11},{10,... | collective-permute-start | bytes 36872 | tf_op jit(solution)/shard_map/ppermute | solution.py:478
  18.8 4.7 %collective-permute-start.5 = (f32[2,8,128]{2,1,0:T(8,128)S(1)}, f32[2,8,128]{2,1,0:T(8,128)S(1)}, u32[]{:S(2)}, u32[]{:S(2)}) collective-permute-start(f32[2,8,128]{2,1,0:T(8,128)S(1)} %get-tuple-element.55), channel_id=1, source_target_pairs={{0,3},{1,2},{2,0},{3,1},{4,7},{5,6},{6,4},{7,5},{8,11},{9,10},{10,... | collective-permute-start | bytes 24584 | tf_op jit(solution)/shard_map/ppermute | solution.py:478
  19.9 3.6 %collective-permute-start.6 = (f32[1,8,128]{2,1,0:T(8,128)S(1)}, f32[1,8,128]{2,1,0:T(8,128)S(1)}, u32[]{:S(2)}, u32[]{:S(2)}) collective-permute-start(f32[1,8,128]{2,1,0:T(8,128)S(1)} %get-tuple-element.56), channel_id=1, source_target_pairs={{0,1},{1,0},{2,3},{3,2},{4,5},{5,4},{6,7},{7,6},{8,9},{9,8},{10,11... | collective-permute-start | bytes 12296 | tf_op jit(solution)/shard_map/ppermute | solution.py:478

commit v20 on v17

--- a/solution.py
+++ b/solution.py
@@ -85,9 +85,9 @@
     lower = wall(walls & 1, 0)
     upper = wall(walls >> 1, total - 1)
 
-    def forward(block, kappa, keep=None):
+    def forward(block, kappa, part=slice(None), keep=None):
         start = block * cells
-        flux = table_ref[index_ref[start]] + kappa
+        flux = table_ref[index_ref[start], part] + kappa
         value = jnp.ones_like(flux)
         for j in range(cells):
             if keep is not None:
@@ -95,14 +95,14 @@
             k = start + j
             if j < cells - 1:
                 value = value + half_sum(index_ref, k) * flux
-                flux = flux + table_ref[index_ref[k + 1]] * value
+                flux = flux + table_ref[index_ref[k + 1], part] * value
         k = jnp.minimum(start + cells - 1, total - 2)
         after = inverted(value + half_sum(index_ref, k) * flux)
         return flux * after, after
 
-    def backward(block, kappa, scale=None, keep=None):
+    def backward(block, kappa, part=slice(None), scale=None, keep=None):
         start = block * cells
-        flux = table_ref[index_ref[start + cells - 1]] + kappa
+        flux = table_ref[index_ref[start + cells - 1], part] + kappa
         value = jnp.ones_like(flux)
         if scale is not None:
             flux, value = flux * scale, scale
@@ -112,7 +112,7 @@
             k = start + j
             if j > 0:
                 value = value + half_sum(index_ref, k - 1) * flux
-                flux = flux + table_ref[index_ref[k - 1]] * value
+                flux = flux + table_ref[index_ref[k - 1], part] * value
         k = jnp.maximum(start - 1, 0)
         after = inverted(value + half_sum(index_ref, k) * flux)
         return flux * after, after
@@ -121,23 +121,32 @@
         parts = [height(index_ref, block * cells + j) for j in range(cells)]
         return functools.reduce(jnp.add, parts)
 
-    def sweep_forward(block, state):
-        kappa, product, extent = state
-        kappa, after = forward(block, kappa)
-        through_ref[block] = after
-        return kappa, product * after, extent + thickness(block)
-
-    def sweep_backward(step, state):
-        block = blocks - 1 - step
-        kappa, product, extent = state
-        kappa, after = backward(block, kappa)
-        through_ref[block] = after
-        return kappa, product * after, extent + thickness(block)
-
-    ones = jnp.ones_like(diffusion)
-    kappa_left, product, extent = lax.fori_loop(
-        0, me, sweep_forward, (lower, ones, thickness(me))
-    )
+    def sweeps(count, step, ends, extent):
+        size = diffusion.shape[0] // 2
+        parts = []
+        for start in (0, size):
+            part = slice(start, start + size)
+
+            def sweep(i, state, part=part):
+                kappa, product, extent = state
+                block, (kappa, after) = step(i, kappa, part)
+                through_ref[block, part] = after
+                if part.start == 0:
+                    extent = extent + thickness(block)
+                return kappa, product * after, extent
+
+            state = (ends[part], jnp.ones_like(ends[part]), extent)
+            *arrays, extent = lax.fori_loop(0, count, sweep, state)
+            parts.append(arrays)
+        return [jnp.concatenate(pair, axis=0) for pair in zip(*parts)] + [extent]
+
+    def step_forward(block, kappa, part):
+        return block, forward(block, kappa, part)
+
+    def step_backward(i, kappa, part):
+        return blocks - 1 - i, backward(blocks - 1 - i, kappa, part)
+
+    kappa_left, product, extent = sweeps(me, step_forward, lower, thickness(me))
     ends_ref[0] = diffusion * lower * product
     state = {}
 
@@ -146,15 +155,13 @@
         left_h_ref[j] = height(index_ref, me * cells + j) * value
         state["flux"], state["value"] = flux, value
 
-    _, own_forward = forward(me, kappa_left, keep_left)
+    _, own_forward = forward(me, kappa_left, keep=keep_left)
     held_ref[1] = own_forward
     held_ref[3] = state["flux"]
     held_ref[4] = state["value"]
     held_ref[5] = state["flux"] - kappa_left
 
-    kappa_right, product, extent = lax.fori_loop(
-        0, blocks - 1 - me, sweep_backward, (upper, ones, extent)
-    )
+    kappa_right, product, extent = sweeps(blocks - 1 - me, step_backward, upper, extent)
     ends_ref[1] = diffusion_ref[...] * upper * product
     scale = inverted(diffusion_ref[...] * (held_ref[3] + kappa_right * held_ref[4]))
     held_ref[0] = scale
@@ -164,7 +171,7 @@
         right_h_ref[j] = height(index_ref, me * cells + j) * value
         state["flux"] = flux
 
-    _, own_backward = backward(me, kappa_right, scale, keep_right)
+    _, own_backward = backward(me, kappa_right, scale=scale, keep=keep_right)
     held_ref[2] = own_backward
     held_ref[6] = state["flux"] - kappa_right * scale
 

time: 23.8 us -> 24 us (level)
  no operation moved by 1% of the time
where the time goes in v20:
time: 24 us; the launch traced here: 23.8 us
  starting transfers between devices  9.33 us (39%)
  Pallas kernels  7.85 us (33%)
  waiting for transfers between devices  5.92 us (25%)
  between operations  0.7 us (3%)
    ppermute x8, starting transfers between devices, send(): return lax.ppermute(array, ('gz', 'gy'), route)  9.33 us
    ppermute x8, waiting for transfers between devices, send(): return lax.ppermute(array, ('gz', 'gy'), route)  5.92 us
    pallas_call x1, Pallas kernels, shards(): pl.pallas_call(functools.partial(ladder_kernel, cells, blocks, chips, lin...  3.65 us
    pallas_call x1, Pallas kernels, shards(): pl.pallas_call(finish_kernel, out_shape=[shape(*velocity.shape), profile]...  1.45 us
    pallas_call x1, Pallas kernels, shards(): pl.pallas_call(functools.partial(correct_kernel, len(tiles)), out_shape=s...  1.18 us
    pallas_call x1, Pallas kernels, shards(): pl.pallas_call(inner_kernel, out_shape=[shape(*velocity.shape), profile,...  1.11 us
  transfers between devices with their start and end apart: 8, of which 4 were waited for; matrix products, arithmetic and copies ran while one was open for 0% of the time, Pallas kernels for 12%

profile of v20, /device:TPU:0, one launch (start us, length us, event | category | flops | bytes accessed | tf_op | source)
XLA Modules:
  0.0 23.8 jit_solution(6789706754711102366)
XLA Ops:
  0.0 3.6 %ladder.1 = (f32[16,8,128]{2,1,0:T(8,128)S(1)}, f32[57,8,128]{2,1,0:T(8,128)S(1)}, f32[3,32,512]{2,1,0:T(8,128)S(1)}, f32[8,32,512]{2,1,0:T(8,128)S(1)}, f32[7,3...) custom-call(s32[128]{0:T(128)} %index_hbm.1, ...), custom_call_target="tpu_custom_call" | custom-call | flops 40000000 | bytes 6000000 | tf_op jit(solution)/shard_map/ladder/pallas_call | solution.py:491
  3.7 0.5 %collective-permute-start = (f32[57,8,128]{2,1,0:T(8,128)S(1)}, f32[57,8,128]{2,1,0:T(8,128)S(1)}, u32[]{:S(2)}, u32[]{:S(2)}) collective-permute-start(f32[57,8,128]{2,1,0:T(8,128)S(1)} %get-tuple-element.44.away_ref), channel_id=1, source_target_pairs={{0,4},{1,5},{2,6},{3,7},{4,0},{5,1},{6,2},{7,3},{8,12},{9,13},{10,... | collective-permute-start | bytes 700424 | tf_op jit(solution)/shard_map/ppermute | solution.py:483
  4.2 0.3 %rest.1 = (f32[32,8,128]{2,1,0:T(8,128)S(1)}, f32[3,32,512]{2,1,0:T(8,128)S(1)}) custom-call(f32[3,16,32,512]{3,2,1,0:T(8,128)S(1)} %get-tuple-element.33.velocity_ref, f32[16,32,512]{2,1,0:T(8,128)S(1)} %get-tuple-element.36.left_h_ref, f32[16,32,512]{2,1,0:T(8,128)S(1)} %get-tuple-element.37.right_h_ref, f32[7,32,512]{2,1,0:T(8,128)S(1)} %get-tuple-element.41.held_ref, ...), custom_call_target="tpu_custom_call" | custom-call | flops 2000000 | bytes 2000000 | tf_op jit(solution)/shard_map/rest/pallas_call | solution.py:522
  4.5 0.8 %collective-permute-done.mate_ref = f32[57,8,128]{2,1,0:T(8,128)S(1)} collective-permute-done((f32[57,8,128]{2,1,0:T(8,128)S(1)}, f32[57,8,128]{2,1,0:T(8,128)S(1)}, u32[]{:S(2)}, u32[]{:S(2)}) %collective-permute-start) | collective-permute-done | bytes 233504 | tf_op jit(solution)/shard_map/ppermute | solution.py:483
  5.3 0.1 merge.1
  5.4 3.9 %collective-permute-start.1 = (f32[26,8,128]{2,1,0:T(8,128)S(1)}, f32[26,8,128]{2,1,0:T(8,128)S(1)}, u32[]{:S(2)}, u32[]{:S(2)}) collective-permute-start(f32[26,8,128]{2,1,0:T(8,128)S(1)} %get-tuple-element.52), channel_id=1, source_target_pairs={{0,24},{1,25},{2,26},{3,27},{4,28},{5,29},{6,30},{7,31},{8,16},{9,... | collective-permute-start | bytes 319496 | tf_op jit(solution)/shard_map/ppermute | solution.py:483
  9.2 0.5 %collective-permute-start.3 = (f32[25,8,128]{2,1,0:T(8,128)S(1)}, f32[25,8,128]{2,1,0:T(8,128)S(1)}, u32[]{:S(2)}, u32[]{:S(2)}) collective-permute-start(f32[25,8,128]{2,1,0:T(8,128)S(1)} %get-tuple-element.53), channel_id=1, source_target_pairs={{0,16},{1,17},{2,18},{3,19},{4,20},{5,21},{6,22},{7,23},{8,24},{9,... | collective-permute-start | bytes 307208 | tf_op jit(solution)/shard_map/ppermute | solution.py:483
  9.7 0.1 collective-permute-start.2
  10.5 1.1 %inner.1 = (f32[3,16,32,512]{3,2,1,0:T(8,128)S(1)}, f32[16,32,512]{2,1,0:T(8,128)S(1)}, f32[8,128]{1,0:T(8,128)S(1)}) custom-call(f32[3,16,32,512]{3,2,1,0:T(8,128)S(1)} %get-tuple-element.33.velocity_ref, f32[16,32,512]{2,1,0:T(8,128)S(1)} %get-tuple-element.34.left_ref, f32[16,32,512]{2,1,0:T(8,128)S(1)} %get-tuple-element.35.right_ref, ...), custom_call_target="tpu_custom_call" | custom-call | flops 8000000 | bytes 8000000 | tf_op jit(solution)/shard_map/inner/pallas_call | solution.py:548
  11.6 3.1 %collective-permute-done.3.rest_3_ = f32[25,8,128]{2,1,0:T(8,128)S(1)} collective-permute-done((f32[25,8,128]{2,1,0:T(8,128)S(1)}, f32[25,8,128]{2,1,0:T(8,128)S(1)}, u32[]{:S(2)}, u32[]{:S(2)}) %collective-permute-start.3) | collective-permute-done | bytes 102432 | tf_op jit(solution)/shard_map/ppermute | solution.py:483
  14.7 0.2 %collective-permute-done.2.rest_2_ = f32[25,8,128]{2,1,0:T(8,128)S(1)} collective-permute-done((f32[25,8,128]{2,1,0:T(8,128)S(1)}, f32[25,8,128]{2,1,0:T(8,128)S(1)}, u32[]{:S(2)}, u32[]{:S(2)}) %collective-permute-start.2) | collective-permute-done | bytes 102432 | tf_op jit(solution)/shard_map/ppermute | solution.py:483
  15.0 0.0 collective-permute-done.1.rest_1_
  15.0 0.1 spread.1
  15.1 0.1 collective-permute-start.7
  15.1 2.6 %collective-permute-start.4 = (f32[3,8,128]{2,1,0:T(8,128)S(1)}, f32[3,8,128]{2,1,0:T(8,128)S(1)}, u32[]{:S(2)}, u32[]{:S(2)}) collective-permute-start(f32[3,8,128]{2,1,0:T(8,128)S(1)} %get-tuple-element.54.rest_0_), channel_id=1, source_target_pairs={{0,2},{1,3},{2,1},{3,0},{4,6},{5,7},{6,5},{7,4},{8,10},{9,11},{10,... | collective-permute-start | bytes 36872 | tf_op jit(solution)/shard_map/ppermute | solution.py:483
  17.8 1.2 %collective-permute-start.5 = (f32[2,8,128]{2,1,0:T(8,128)S(1)}, f32[2,8,128]{2,1,0:T(8,128)S(1)}, u32[]{:S(2)}, u32[]{:S(2)}) collective-permute-start(f32[2,8,128]{2,1,0:T(8,128)S(1)} %get-tuple-element.55), channel_id=1, source_target_pairs={{0,3},{1,2},{2,0},{3,1},{4,7},{5,6},{6,4},{7,5},{8,11},{9,10},{10,... | collective-permute-start | bytes 24584 | tf_op jit(solution)/shard_map/ppermute | solution.py:483
  19.0 0.3 %collective-permute-start.6 = (f32[1,8,128]{2,1,0:T(8,128)S(1)}, f32[1,8,128]{2,1,0:T(8,128)S(1)}, u32[]{:S(2)}, u32[]{:S(2)}) collective-permute-start(f32[1,8,128]{2,1,0:T(8,128)S(1)} %get-tuple-element.56), channel_id=1, source_target_pairs={{0,1},{1,0},{2,3},{3,2},{4,5},{5,4},{6,7},{7,6},{8,9},{9,8},{10,11... | collective-permute-start | bytes 12296 | tf_op jit(solution)/shard_map/ppermute | solution.py:483
  19.4 0.0 collective-permute-done.7.other_ref
  19.4 1.5 %finish.1 = (f32[3,16,32,512]{3,2,1,0:T(8,128)}, f32[16,32,512]{2,1,0:T(8,128)S(1)}) custom-call(f32[12,8,512]{2,1,0:T(8,128)S(1)} %get-tuple-element.57.own_ref, f32[12,8,512]{2,1,0:T(8,128)S(1)} %collective-permute-done.7.other_ref, f32[3,16,32,512]{3,2,1,0:T(8,128)S(1)} %get-tuple-element.51.rest_0_.base_ref, ...), custom_call_target="tpu_custom_call" | custom-call | flops 3000000 | bytes 6000000 | tf_op jit(solution)/shard_map/finish/pallas_call | solution.py:573
  20.8 1.8 %collective-permute-done.6.rest_3_ = f32[1,8,128]{2,1,0:T(8,128)S(1)} collective-permute-done((f32[1,8,128]{2,1,0:T(8,128)S(1)}, f32[1,8,128]{2,1,0:T(8,128)S(1)}, u32[]{:S(2)}, u32[]{:S(2)}) %collective-permute-start.6) | collective-permute-done | bytes 4128 | tf_op jit(solution)/shard_map/ppermute | solution.py:483
  22.6 0.0 collective-permute-done.5.rest_2_
  22.6 0.0 collective-permute-done.4.rest_1_
  22.6 1.2 %correct.1 = f32[3,16,32,512]{3,2,1,0:T(8,128)} custom-call(f32[8,128]{1,0:T(8,128)S(1)} %get-tuple-element.47.goal_ref, f32[16,32,512]{2,1,0:T(8,128)S(1)} %get-tuple-element.48.unit_ref, f32[3,8,128]{2,1,0:T(8,128)S(1)} %get-tuple-element.54.rest_0_, f32[3,8,128]{2,1,0:T(8,128)S(1)} %collective-permute-done.4.rest_1_, ...), custom_call_target="tpu_custom_call", output_to_operand_aliasing={{}: (7, {})} | custom-call | flops 500000 | bytes 1600000 | tf_op jit(solution)/shard_map/correct/pallas_call | solution.py:586
Async XLA Ops:
  3.7 1.6 %collective-permute-start = (f32[57,8,128]{2,1,0:T(8,128)S(1)}, f32[57,8,128]{2,1,0:T(8,128)S(1)}, u32[]{:S(2)}, u32[]{:S(2)}) collective-permute-start(f32[57,8,128]{2,1,0:T(8,128)S(1)} %get-tuple-element.44.away_ref), channel_id=1, source_target_pairs={{0,4},{1,5},{2,6},{3,7},{4,0},{5,1},{6,2},{7,3},{8,12},{9,13},{10,... | collective-permute-start | bytes 700424 | tf_op jit(solution)/shard_map/ppermute | solution.py:483
  5.4 9.6 %collective-permute-start.1 = (f32[26,8,128]{2,1,0:T(8,128)S(1)}, f32[26,8,128]{2,1,0:T(8,128)S(1)}, u32[]{:S(2)}, u32[]{:S(2)}) collective-permute-start(f32[26,8,128]{2,1,0:T(8,128)S(1)} %get-tuple-element.52), channel_id=1, source_target_pairs={{0,24},{1,25},{2,26},{3,27},{4,28},{5,29},{6,30},{7,31},{8,16},{9,... | collective-permute-start | bytes 319496 | tf_op jit(solution)/shard_map/ppermute | solution.py:483
  9.2 5.5 %collective-permute-start.3 = (f32[25,8,128]{2,1,0:T(8,128)S(1)}, f32[25,8,128]{2,1,0:T(8,128)S(1)}, u32[]{:S(2)}, u32[]{:S(2)}) collective-permute-start(f32[25,8,128]{2,1,0:T(8,128)S(1)} %get-tuple-element.53), channel_id=1, source_target_pairs={{0,16},{1,17},{2,18},{3,19},{4,20},{5,21},{6,22},{7,23},{8,24},{9,... | collective-permute-start | bytes 307208 | tf_op jit(solution)/shard_map/ppermute | solution.py:483
  9.7 5.2 %collective-permute-start.2 = (f32[25,8,128]{2,1,0:T(8,128)S(1)}, f32[25,8,128]{2,1,0:T(8,128)S(1)}, u32[]{:S(2)}, u32[]{:S(2)}) collective-permute-start(f32[25,8,128]{2,1,0:T(8,128)S(1)} %get-tuple-element.46._), channel_id=1, source_target_pairs={{0,8},{1,9},{2,10},{3,11},{4,12},{5,13},{6,14},{7,15},{8,0},{9,1},... | collective-permute-start | bytes 307208 | tf_op jit(solution)/shard_map/ppermute | solution.py:483
  15.1 4.3 %collective-permute-start.7 = (f32[12,8,512]{2,1,0:T(8,128)S(1)}, f32[12,8,512]{2,1,0:T(8,128)S(1)}, u32[]{:S(2)}, u32[]{:S(2)}) collective-permute-start(f32[12,8,512]{2,1,0:T(8,128)S(1)} %get-tuple-element.58), channel_id=1, source_target_pairs={{0,4},{1,5},{2,6},{3,7},{4,0},{5,1},{6,2},{7,3},{8,12},{9,13},{10,... | collective-permute-start | bytes 589832 | tf_op jit(solution)/shard_map/ppermute | solution.py:483
  15.1 7.5 %collective-permute-start.4 = (f32[3,8,128]{2,1,0:T(8,128)S(1)}, f32[3,8,128]{2,1,0:T(8,128)S(1)}, u32[]{:S(2)}, u32[]{:S(2)}) collective-permute-start(f32[3,8,128]{2,1,0:T(8,128)S(1)} %get-tuple-element.54.rest_0_), channel_id=1, source_target_pairs={{0,2},{1,3},{2,1},{3,0},{4,6},{5,7},{6,5},{7,4},{8,10},{9,11},{10,... | collective-permute-start | bytes 36872 | tf_op jit(solution)/shard_map/ppermute | solution.py:483
  17.8 4.8 %collective-permute-start.5 = (f32[2,8,128]{2,1,0:T(8,128)S(1)}, f32[2,8,128]{2,1,0:T(8,128)S(1)}, u32[]{:S(2)}, u32[]{:S(2)}) collective-permute-start(f32[2,8,128]{2,1,0:T(8,128)S(1)} %get-tuple-element.55), channel_id=1, source_target_pairs={{0,3},{1,2},{2,0},{3,1},{4,7},{5,6},{6,4},{7,5},{8,11},{9,10},{10,... | collective-permute-start | bytes 24584 | tf_op jit(solution)/shard_map/ppermute | solution.py:483
  19.0 3.6 %collective-permute-start.6 = (f32[1,8,128]{2,1,0:T(8,128)S(1)}, f32[1,8,128]{2,1,0:T(8,128)S(1)}, u32[]{:S(2)}, u32[]{:S(2)}) collective-permute-start(f32[1,8,128]{2,1,0:T(8,128)S(1)} %get-tuple-element.56), channel_id=1, source_target_pairs={{0,1},{1,0},{2,3},{3,2},{4,5},{5,4},{6,7},{7,6},{8,9},{9,8},{10,11... | collective-permute-start | bytes 12296 | tf_op jit(solution)/shard_map/ppermute | solution.py:483

commit v21 on v17

--- a/solution.py
+++ b/solution.py
@@ -424,8 +424,9 @@
     tile_refs = rest[:count]
     plain_ref, _, out_hbm, result_ref, sems = rest[count:]
     totals = functools.reduce(jnp.add, [ref[0] for ref in tile_refs])
-    flow = jnp.sum(totals[0:SUB // 2], keepdims=True)
-    weight = jnp.sum(totals[SUB // 2:], keepdims=True)
+    lanes = jnp.sum(totals, axis=1, keepdims=True)
+    flow = jnp.sum(lanes[0:SUB // 2], axis=0, keepdims=True)
+    weight = jnp.sum(lanes[SUB // 2:], axis=0, keepdims=True)
     alpha = (goal_ref[0:1, 0:1] - flow) / weight
     cells, lines_y, _ = plain_ref.shape
 
@@ -433,14 +434,11 @@
         rows = row_tile(t)
         return pltpu.make_async_copy(result_ref.at[:, rows], out_hbm.at[0, :, rows], sems.at[t])
 
-    def of_tile(t, _):
+    for t in range(lines_y // SUB):
         rows = row_tile(t)
         for j in range(cells):
             result_ref[j, rows] = plain_ref[j, rows] + alpha * unit_ref[j, rows]
         copy(t).start()
-        return 0
-
-    lax.fori_loop(0, lines_y // SUB, of_tile, 0)
     for t in range(lines_y // SUB):
         copy(t).wait()
 

time: 23.8 us -> 23.8 us (level)
  no operation moved by 1% of the time
where the time goes in v21:
time: 23.8 us; the launch traced here: 23.6 us
  starting transfers between devices  9.34 us (39%)
  Pallas kernels  7.66 us (32%)
  waiting for transfers between devices  5.92 us (25%)
  between operations  0.7 us (3%)
    ppermute x8, starting transfers between devices, send(): return lax.ppermute(array, ('gz', 'gy'), route)  9.34 us
    ppermute x8, waiting for transfers between devices, send(): return lax.ppermute(array, ('gz', 'gy'), route)  5.92 us
    pallas_call x1, Pallas kernels, shards(): pl.pallas_call(functools.partial(ladder_kernel, cells, blocks, chips, lin...  3.48 us
    pallas_call x1, Pallas kernels, shards(): pl.pallas_call(finish_kernel, out_shape=[shape(*velocity.shape), profile]...  1.45 us
    pallas_call x1, Pallas kernels, shards(): pl.pallas_call(functools.partial(correct_kernel, len(tiles)), out_shape=s...  1.16 us
    pallas_call x1, Pallas kernels, shards(): pl.pallas_call(inner_kernel, out_shape=[shape(*velocity.shape), profile,...  1.11 us
  transfers between devices with their start and end apart: 8, of which 4 were waited for; matrix products, arithmetic and copies ran while one was open for 0% of the time, Pallas kernels for 12%

profile of v21, /device:TPU:0, one launch (start us, length us, event | category | flops | bytes accessed | tf_op | source)
XLA Modules:
  0.0 23.6 jit_solution(8060719102002769984)
XLA Ops:
  0.0 3.5 %ladder.1 = (f32[16,8,128]{2,1,0:T(8,128)S(1)}, f32[57,8,128]{2,1,0:T(8,128)S(1)}, f32[3,32,512]{2,1,0:T(8,128)S(1)}, f32[8,32,512]{2,1,0:T(8,128)S(1)}, f32[7,3...) custom-call(s32[128]{0:T(128)} %index_hbm.1, ...), custom_call_target="tpu_custom_call" | custom-call | flops 40000000 | bytes 6000000 | tf_op jit(solution)/shard_map/ladder/pallas_call | solution.py:482
  3.5 0.5 %collective-permute-start = (f32[57,8,128]{2,1,0:T(8,128)S(1)}, f32[57,8,128]{2,1,0:T(8,128)S(1)}, u32[]{:S(2)}, u32[]{:S(2)}) collective-permute-start(f32[57,8,128]{2,1,0:T(8,128)S(1)} %get-tuple-element.44.away_ref), channel_id=1, source_target_pairs={{0,4},{1,5},{2,6},{3,7},{4,0},{5,1},{6,2},{7,3},{8,12},{9,13},{10,... | collective-permute-start | bytes 700424 | tf_op jit(solution)/shard_map/ppermute | solution.py:474
  4.0 0.3 %rest.1 = (f32[32,8,128]{2,1,0:T(8,128)S(1)}, f32[3,32,512]{2,1,0:T(8,128)S(1)}) custom-call(f32[3,16,32,512]{3,2,1,0:T(8,128)S(1)} %get-tuple-element.33.velocity_ref, f32[16,32,512]{2,1,0:T(8,128)S(1)} %get-tuple-element.36.left_h_ref, f32[16,32,512]{2,1,0:T(8,128)S(1)} %get-tuple-element.37.right_h_ref, f32[7,32,512]{2,1,0:T(8,128)S(1)} %get-tuple-element.41.held_ref, ...), custom_call_target="tpu_custom_call" | custom-call | flops 2000000 | bytes 2000000 | tf_op jit(solution)/shard_map/rest/pallas_call | solution.py:513
  4.3 0.8 %collective-permute-done.mate_ref = f32[57,8,128]{2,1,0:T(8,128)S(1)} collective-permute-done((f32[57,8,128]{2,1,0:T(8,128)S(1)}, f32[57,8,128]{2,1,0:T(8,128)S(1)}, u32[]{:S(2)}, u32[]{:S(2)}) %collective-permute-start) | collective-permute-done | bytes 233504 | tf_op jit(solution)/shard_map/ppermute | solution.py:474
  5.1 0.1 merge.1
  5.2 3.9 %collective-permute-start.1 = (f32[26,8,128]{2,1,0:T(8,128)S(1)}, f32[26,8,128]{2,1,0:T(8,128)S(1)}, u32[]{:S(2)}, u32[]{:S(2)}) collective-permute-start(f32[26,8,128]{2,1,0:T(8,128)S(1)} %get-tuple-element.52), channel_id=1, source_target_pairs={{0,24},{1,25},{2,26},{3,27},{4,28},{5,29},{6,30},{7,31},{8,16},{9,... | collective-permute-start | bytes 319496 | tf_op jit(solution)/shard_map/ppermute | solution.py:474
  9.1 0.5 %collective-permute-start.3 = (f32[25,8,128]{2,1,0:T(8,128)S(1)}, f32[25,8,128]{2,1,0:T(8,128)S(1)}, u32[]{:S(2)}, u32[]{:S(2)}) collective-permute-start(f32[25,8,128]{2,1,0:T(8,128)S(1)} %get-tuple-element.53), channel_id=1, source_target_pairs={{0,16},{1,17},{2,18},{3,19},{4,20},{5,21},{6,22},{7,23},{8,24},{9,... | collective-permute-start | bytes 307208 | tf_op jit(solution)/shard_map/ppermute | solution.py:474
  9.6 0.1 collective-permute-start.2
  10.4 1.1 %inner.1 = (f32[3,16,32,512]{3,2,1,0:T(8,128)S(1)}, f32[16,32,512]{2,1,0:T(8,128)S(1)}, f32[8,128]{1,0:T(8,128)S(1)}) custom-call(f32[3,16,32,512]{3,2,1,0:T(8,128)S(1)} %get-tuple-element.33.velocity_ref, f32[16,32,512]{2,1,0:T(8,128)S(1)} %get-tuple-element.34.left_ref, f32[16,32,512]{2,1,0:T(8,128)S(1)} %get-tuple-element.35.right_ref, ...), custom_call_target="tpu_custom_call" | custom-call | flops 8000000 | bytes 8000000 | tf_op jit(solution)/shard_map/inner/pallas_call | solution.py:539
  11.5 3.1 %collective-permute-done.3.rest_3_ = f32[25,8,128]{2,1,0:T(8,128)S(1)} collective-permute-done((f32[25,8,128]{2,1,0:T(8,128)S(1)}, f32[25,8,128]{2,1,0:T(8,128)S(1)}, u32[]{:S(2)}, u32[]{:S(2)}) %collective-permute-start.3) | collective-permute-done | bytes 102432 | tf_op jit(solution)/shard_map/ppermute | solution.py:474
  14.5 0.2 %collective-permute-done.2.rest_2_ = f32[25,8,128]{2,1,0:T(8,128)S(1)} collective-permute-done((f32[25,8,128]{2,1,0:T(8,128)S(1)}, f32[25,8,128]{2,1,0:T(8,128)S(1)}, u32[]{:S(2)}, u32[]{:S(2)}) %collective-permute-start.2) | collective-permute-done | bytes 102432 | tf_op jit(solution)/shard_map/ppermute | solution.py:474
  14.8 0.0 collective-permute-done.1.rest_1_
  14.8 0.1 spread.1
  14.9 0.1 collective-permute-start.7
  15.0 2.6 %collective-permute-start.4 = (f32[3,8,128]{2,1,0:T(8,128)S(1)}, f32[3,8,128]{2,1,0:T(8,128)S(1)}, u32[]{:S(2)}, u32[]{:S(2)}) collective-permute-start(f32[3,8,128]{2,1,0:T(8,128)S(1)} %get-tuple-element.54.rest_0_), channel_id=1, source_target_pairs={{0,2},{1,3},{2,1},{3,0},{4,6},{5,7},{6,5},{7,4},{8,10},{9,11},{10,... | collective-permute-start | bytes 36872 | tf_op jit(solution)/shard_map/ppermute | solution.py:474
  17.6 1.2 %collective-permute-start.5 = (f32[2,8,128]{2,1,0:T(8,128)S(1)}, f32[2,8,128]{2,1,0:T(8,128)S(1)}, u32[]{:S(2)}, u32[]{:S(2)}) collective-permute-start(f32[2,8,128]{2,1,0:T(8,128)S(1)} %get-tuple-element.55), channel_id=1, source_target_pairs={{0,3},{1,2},{2,0},{3,1},{4,7},{5,6},{6,4},{7,5},{8,11},{9,10},{10,... | collective-permute-start | bytes 24584 | tf_op jit(solution)/shard_map/ppermute | solution.py:474
  18.8 0.3 %collective-permute-start.6 = (f32[1,8,128]{2,1,0:T(8,128)S(1)}, f32[1,8,128]{2,1,0:T(8,128)S(1)}, u32[]{:S(2)}, u32[]{:S(2)}) collective-permute-start(f32[1,8,128]{2,1,0:T(8,128)S(1)} %get-tuple-element.56), channel_id=1, source_target_pairs={{0,1},{1,0},{2,3},{3,2},{4,5},{5,4},{6,7},{7,6},{8,9},{9,8},{10,11... | collective-permute-start | bytes 12296 | tf_op jit(solution)/shard_map/ppermute | solution.py:474
  19.2 0.0 collective-permute-done.7.other_ref
  19.2 1.5 %finish.1 = (f32[3,16,32,512]{3,2,1,0:T(8,128)}, f32[16,32,512]{2,1,0:T(8,128)S(1)}) custom-call(f32[12,8,512]{2,1,0:T(8,128)S(1)} %get-tuple-element.57.own_ref, f32[12,8,512]{2,1,0:T(8,128)S(1)} %collective-permute-done.7.other_ref, f32[3,16,32,512]{3,2,1,0:T(8,128)S(1)} %get-tuple-element.51.rest_0_.base_ref, ...), custom_call_target="tpu_custom_call" | custom-call | flops 3000000 | bytes 6000000 | tf_op jit(solution)/shard_map/finish/pallas_call | solution.py:564
  20.6 1.8 %collective-permute-done.6.rest_3_ = f32[1,8,128]{2,1,0:T(8,128)S(1)} collective-permute-done((f32[1,8,128]{2,1,0:T(8,128)S(1)}, f32[1,8,128]{2,1,0:T(8,128)S(1)}, u32[]{:S(2)}, u32[]{:S(2)}) %collective-permute-start.6) | collective-permute-done | bytes 4128 | tf_op jit(solution)/shard_map/ppermute | solution.py:474
  22.4 0.0 collective-permute-done.5.rest_2_
  22.5 0.0 collective-permute-done.4.rest_1_
  22.5 1.2 %correct.1 = f32[3,16,32,512]{3,2,1,0:T(8,128)} custom-call(f32[8,128]{1,0:T(8,128)S(1)} %get-tuple-element.47.goal_ref, f32[16,32,512]{2,1,0:T(8,128)S(1)} %get-tuple-element.48.unit_ref, f32[3,8,128]{2,1,0:T(8,128)S(1)} %get-tuple-element.54.rest_0_, f32[3,8,128]{2,1,0:T(8,128)S(1)} %collective-permute-done.4.rest_1_, ...), custom_call_target="tpu_custom_call", output_to_operand_aliasing={{}: (7, {})} | custom-call | flops 500000 | bytes 1600000 | tf_op jit(solution)/shard_map/correct/pallas_call | solution.py:577
Async XLA Ops:
  3.5 1.6 %collective-permute-start = (f32[57,8,128]{2,1,0:T(8,128)S(1)}, f32[57,8,128]{2,1,0:T(8,128)S(1)}, u32[]{:S(2)}, u32[]{:S(2)}) collective-permute-start(f32[57,8,128]{2,1,0:T(8,128)S(1)} %get-tuple-element.44.away_ref), channel_id=1, source_target_pairs={{0,4},{1,5},{2,6},{3,7},{4,0},{5,1},{6,2},{7,3},{8,12},{9,13},{10,... | collective-permute-start | bytes 700424 | tf_op jit(solution)/shard_map/ppermute | solution.py:474
  5.2 9.6 %collective-permute-start.1 = (f32[26,8,128]{2,1,0:T(8,128)S(1)}, f32[26,8,128]{2,1,0:T(8,128)S(1)}, u32[]{:S(2)}, u32[]{:S(2)}) collective-permute-start(f32[26,8,128]{2,1,0:T(8,128)S(1)} %get-tuple-element.52), channel_id=1, source_target_pairs={{0,24},{1,25},{2,26},{3,27},{4,28},{5,29},{6,30},{7,31},{8,16},{9,... | collective-permute-start | bytes 319496 | tf_op jit(solution)/shard_map/ppermute | solution.py:474
  9.1 5.5 %collective-permute-start.3 = (f32[25,8,128]{2,1,0:T(8,128)S(1)}, f32[25,8,128]{2,1,0:T(8,128)S(1)}, u32[]{:S(2)}, u32[]{:S(2)}) collective-permute-start(f32[25,8,128]{2,1,0:T(8,128)S(1)} %get-tuple-element.53), channel_id=1, source_target_pairs={{0,16},{1,17},{2,18},{3,19},{4,20},{5,21},{6,22},{7,23},{8,24},{9,... | collective-permute-start | bytes 307208 | tf_op jit(solution)/shard_map/ppermute | solution.py:474
  9.6 5.2 %collective-permute-start.2 = (f32[25,8,128]{2,1,0:T(8,128)S(1)}, f32[25,8,128]{2,1,0:T(8,128)S(1)}, u32[]{:S(2)}, u32[]{:S(2)}) collective-permute-start(f32[25,8,128]{2,1,0:T(8,128)S(1)} %get-tuple-element.46._), channel_id=1, source_target_pairs={{0,8},{1,9},{2,10},{3,11},{4,12},{5,13},{6,14},{7,15},{8,0},{9,1},... | collective-permute-start | bytes 307208 | tf_op jit(solution)/shard_map/ppermute | solution.py:474
  14.9 4.3 %collective-permute-start.7 = (f32[12,8,512]{2,1,0:T(8,128)S(1)}, f32[12,8,512]{2,1,0:T(8,128)S(1)}, u32[]{:S(2)}, u32[]{:S(2)}) collective-permute-start(f32[12,8,512]{2,1,0:T(8,128)S(1)} %get-tuple-element.58), channel_id=1, source_target_pairs={{0,4},{1,5},{2,6},{3,7},{4,0},{5,1},{6,2},{7,3},{8,12},{9,13},{10,... | collective-permute-start | bytes 589832 | tf_op jit(solution)/shard_map/ppermute | solution.py:474
  15.0 7.5 %collective-permute-start.4 = (f32[3,8,128]{2,1,0:T(8,128)S(1)}, f32[3,8,128]{2,1,0:T(8,128)S(1)}, u32[]{:S(2)}, u32[]{:S(2)}) collective-permute-start(f32[3,8,128]{2,1,0:T(8,128)S(1)} %get-tuple-element.54.rest_0_), channel_id=1, source_target_pairs={{0,2},{1,3},{2,1},{3,0},{4,6},{5,7},{6,5},{7,4},{8,10},{9,11},{10,... | collective-permute-start | bytes 36872 | tf_op jit(solution)/shard_map/ppermute | solution.py:474
  17.6 4.8 %collective-permute-start.5 = (f32[2,8,128]{2,1,0:T(8,128)S(1)}, f32[2,8,128]{2,1,0:T(8,128)S(1)}, u32[]{:S(2)}, u32[]{:S(2)}) collective-permute-start(f32[2,8,128]{2,1,0:T(8,128)S(1)} %get-tuple-element.55), channel_id=1, source_target_pairs={{0,3},{1,2},{2,0},{3,1},{4,7},{5,6},{6,4},{7,5},{8,11},{9,10},{10,... | collective-permute-start | bytes 24584 | tf_op jit(solution)/shard_map/ppermute | solution.py:474
  18.8 3.6 %collective-permute-start.6 = (f32[1,8,128]{2,1,0:T(8,128)S(1)}, f32[1,8,128]{2,1,0:T(8,128)S(1)}, u32[]{:S(2)}, u32[]{:S(2)}) collective-permute-start(f32[1,8,128]{2,1,0:T(8,128)S(1)} %get-tuple-element.56), channel_id=1, source_target_pairs={{0,1},{1,0},{2,3},{3,2},{4,5},{5,4},{6,7},{7,6},{8,9},{9,8},{10,11... | collective-permute-start | bytes 12296 | tf_op jit(solution)/shard_map/ppermute | solution.py:474

commit v22 on v21

--- a/solution.py
+++ b/solution.py
@@ -217,8 +217,10 @@
 
     state = (jnp.zeros((SUB, LANES), jnp.float32),) * 2
     mates = 1 - (me - first)
-    state = lax.fori_loop(0, half, sums(away_ref, mates, components), state)
-    flow, weight = lax.fori_loop(0, half, sums(mine_ref, me - first, 1), state)
+    for of_tile in (sums(away_ref, mates, components), sums(mine_ref, me - first, 1)):
+        for i in range(half):
+            state = of_tile(i, state)
+    flow, weight = state
     for i in range(half):
         put(away_ref, half * 2 * components + i, pair_ref[0, row_tile(mates * half + i)])
     slot, middle = away_ref.shape[0] - 1, SUB // 2

time: 23.8 us -> 23.8 us (level)
  no operation moved by 1% of the time
where the time goes in v22:
time: 23.8 us; the launch traced here: 23.6 us
  starting transfers between devices  9.34 us (39%)
  Pallas kernels  7.68 us (32%)
  waiting for transfers between devices  5.92 us (25%)
  between operations  0.7 us (3%)
    ppermute x8, starting transfers between devices, send(): return lax.ppermute(array, ('gz', 'gy'), route)  9.34 us
    ppermute x8, waiting for transfers between devices, send(): return lax.ppermute(array, ('gz', 'gy'), route)  5.92 us
    pallas_call x1, Pallas kernels, shards(): pl.pallas_call(functools.partial(ladder_kernel, cells, blocks, chips, lin...  3.5 us
    pallas_call x1, Pallas kernels, shards(): pl.pallas_call(finish_kernel, out_shape=[shape(*velocity.shape), profile]...  1.45 us
    pallas_call x1, Pallas kernels, shards(): pl.pallas_call(functools.partial(correct_kernel, len(tiles)), out_shape=s...  1.16 us
    pallas_call x1, Pallas kernels, shards(): pl.pallas_call(inner_kernel, out_shape=[shape(*velocity.shape), profile,...  1.11 us
  transfers between devices with their start and end apart: 8, of which 4 were waited for; matrix products, arithmetic and copies ran while one was open for 0% of the time, Pallas kernels for 12%

profile of v22, /device:TPU:0, one launch (start us, length us, event | category | flops | bytes accessed | tf_op | source)
XLA Modules:
  0.0 23.6 jit_solution(2041786766415457057)
XLA Ops:
  0.0 3.5 %ladder.1 = (f32[16,8,128]{2,1,0:T(8,128)S(1)}, f32[57,8,128]{2,1,0:T(8,128)S(1)}, f32[3,32,512]{2,1,0:T(8,128)S(1)}, f32[8,32,512]{2,1,0:T(8,128)S(1)}, f32[7,3...) custom-call(s32[128]{0:T(128)} %index_hbm.1, ...), custom_call_target="tpu_custom_call" | custom-call | flops 40000000 | bytes 6000000 | tf_op jit(solution)/shard_map/ladder/pallas_call | solution.py:484
  3.5 0.5 %collective-permute-start = (f32[57,8,128]{2,1,0:T(8,128)S(1)}, f32[57,8,128]{2,1,0:T(8,128)S(1)}, u32[]{:S(2)}, u32[]{:S(2)}) collective-permute-start(f32[57,8,128]{2,1,0:T(8,128)S(1)} %get-tuple-element.44.away_ref), channel_id=1, source_target_pairs={{0,4},{1,5},{2,6},{3,7},{4,0},{5,1},{6,2},{7,3},{8,12},{9,13},{10,... | collective-permute-start | bytes 700424 | tf_op jit(solution)/shard_map/ppermute | solution.py:476
  4.0 0.3 %rest.1 = (f32[32,8,128]{2,1,0:T(8,128)S(1)}, f32[3,32,512]{2,1,0:T(8,128)S(1)}) custom-call(f32[3,16,32,512]{3,2,1,0:T(8,128)S(1)} %get-tuple-element.33.velocity_ref, f32[16,32,512]{2,1,0:T(8,128)S(1)} %get-tuple-element.36.left_h_ref, f32[16,32,512]{2,1,0:T(8,128)S(1)} %get-tuple-element.37.right_h_ref, f32[7,32,512]{2,1,0:T(8,128)S(1)} %get-tuple-element.41.held_ref, ...), custom_call_target="tpu_custom_call" | custom-call | flops 2000000 | bytes 2000000 | tf_op jit(solution)/shard_map/rest/pallas_call | solution.py:515
  4.3 0.8 %collective-permute-done.mate_ref = f32[57,8,128]{2,1,0:T(8,128)S(1)} collective-permute-done((f32[57,8,128]{2,1,0:T(8,128)S(1)}, f32[57,8,128]{2,1,0:T(8,128)S(1)}, u32[]{:S(2)}, u32[]{:S(2)}) %collective-permute-start) | collective-permute-done | bytes 233504 | tf_op jit(solution)/shard_map/ppermute | solution.py:476
  5.1 0.1 merge.1
  5.2 3.9 %collective-permute-start.1 = (f32[26,8,128]{2,1,0:T(8,128)S(1)}, f32[26,8,128]{2,1,0:T(8,128)S(1)}, u32[]{:S(2)}, u32[]{:S(2)}) collective-permute-start(f32[26,8,128]{2,1,0:T(8,128)S(1)} %get-tuple-element.52), channel_id=1, source_target_pairs={{0,24},{1,25},{2,26},{3,27},{4,28},{5,29},{6,30},{7,31},{8,16},{9,... | collective-permute-start | bytes 319496 | tf_op jit(solution)/shard_map/ppermute | solution.py:476
  9.1 0.5 %collective-permute-start.3 = (f32[25,8,128]{2,1,0:T(8,128)S(1)}, f32[25,8,128]{2,1,0:T(8,128)S(1)}, u32[]{:S(2)}, u32[]{:S(2)}) collective-permute-start(f32[25,8,128]{2,1,0:T(8,128)S(1)} %get-tuple-element.53), channel_id=1, source_target_pairs={{0,16},{1,17},{2,18},{3,19},{4,20},{5,21},{6,22},{7,23},{8,24},{9,... | collective-permute-start | bytes 307208 | tf_op jit(solution)/shard_map/ppermute | solution.py:476
  9.6 0.1 collective-permute-start.2
  10.4 1.1 %inner.1 = (f32[3,16,32,512]{3,2,1,0:T(8,128)S(1)}, f32[16,32,512]{2,1,0:T(8,128)S(1)}, f32[8,128]{1,0:T(8,128)S(1)}) custom-call(f32[3,16,32,512]{3,2,1,0:T(8,128)S(1)} %get-tuple-element.33.velocity_ref, f32[16,32,512]{2,1,0:T(8,128)S(1)} %get-tuple-element.34.left_ref, f32[16,32,512]{2,1,0:T(8,128)S(1)} %get-tuple-element.35.right_ref, ...), custom_call_target="tpu_custom_call" | custom-call | flops 8000000 | bytes 8000000 | tf_op jit(solution)/shard_map/inner/pallas_call | solution.py:541
  11.5 3.1 %collective-permute-done.3.rest_3_ = f32[25,8,128]{2,1,0:T(8,128)S(1)} collective-permute-done((f32[25,8,128]{2,1,0:T(8,128)S(1)}, f32[25,8,128]{2,1,0:T(8,128)S(1)}, u32[]{:S(2)}, u32[]{:S(2)}) %collective-permute-start.3) | collective-permute-done | bytes 102432 | tf_op jit(solution)/shard_map/ppermute | solution.py:476
  14.6 0.2 %collective-permute-done.2.rest_2_ = f32[25,8,128]{2,1,0:T(8,128)S(1)} collective-permute-done((f32[25,8,128]{2,1,0:T(8,128)S(1)}, f32[25,8,128]{2,1,0:T(8,128)S(1)}, u32[]{:S(2)}, u32[]{:S(2)}) %collective-permute-start.2) | collective-permute-done | bytes 102432 | tf_op jit(solution)/shard_map/ppermute | solution.py:476
  14.8 0.0 collective-permute-done.1.rest_1_
  14.8 0.1 spread.1
  14.9 0.1 collective-permute-start.7
  15.0 2.6 %collective-permute-start.4 = (f32[3,8,128]{2,1,0:T(8,128)S(1)}, f32[3,8,128]{2,1,0:T(8,128)S(1)}, u32[]{:S(2)}, u32[]{:S(2)}) collective-permute-start(f32[3,8,128]{2,1,0:T(8,128)S(1)} %get-tuple-element.54.rest_0_), channel_id=1, source_target_pairs={{0,2},{1,3},{2,1},{3,0},{4,6},{5,7},{6,5},{7,4},{8,10},{9,11},{10,... | collective-permute-start | bytes 36872 | tf_op jit(solution)/shard_map/ppermute | solution.py:476
  17.6 1.2 %collective-permute-start.5 = (f32[2,8,128]{2,1,0:T(8,128)S(1)}, f32[2,8,128]{2,1,0:T(8,128)S(1)}, u32[]{:S(2)}, u32[]{:S(2)}) collective-permute-start(f32[2,8,128]{2,1,0:T(8,128)S(1)} %get-tuple-element.55), channel_id=1, source_target_pairs={{0,3},{1,2},{2,0},{3,1},{4,7},{5,6},{6,4},{7,5},{8,11},{9,10},{10,... | collective-permute-start | bytes 24584 | tf_op jit(solution)/shard_map/ppermute | solution.py:476
  18.9 0.3 %collective-permute-start.6 = (f32[1,8,128]{2,1,0:T(8,128)S(1)}, f32[1,8,128]{2,1,0:T(8,128)S(1)}, u32[]{:S(2)}, u32[]{:S(2)}) collective-permute-start(f32[1,8,128]{2,1,0:T(8,128)S(1)} %get-tuple-element.56), channel_id=1, source_target_pairs={{0,1},{1,0},{2,3},{3,2},{4,5},{5,4},{6,7},{7,6},{8,9},{9,8},{10,11... | collective-permute-start | bytes 12296 | tf_op jit(solution)/shard_map/ppermute | solution.py:476
  19.2 0.0 collective-permute-done.7.other_ref
  19.2 1.5 %finish.1 = (f32[3,16,32,512]{3,2,1,0:T(8,128)}, f32[16,32,512]{2,1,0:T(8,128)S(1)}) custom-call(f32[12,8,512]{2,1,0:T(8,128)S(1)} %get-tuple-element.57.own_ref, f32[12,8,512]{2,1,0:T(8,128)S(1)} %collective-permute-done.7.other_ref, f32[3,16,32,512]{3,2,1,0:T(8,128)S(1)} %get-tuple-element.51.rest_0_.base_ref, ...), custom_call_target="tpu_custom_call" | custom-call | flops 3000000 | bytes 6000000 | tf_op jit(solution)/shard_map/finish/pallas_call | solution.py:566
  20.7 1.8 %collective-permute-done.6.rest_3_ = f32[1,8,128]{2,1,0:T(8,128)S(1)} collective-permute-done((f32[1,8,128]{2,1,0:T(8,128)S(1)}, f32[1,8,128]{2,1,0:T(8,128)S(1)}, u32[]{:S(2)}, u32[]{:S(2)}) %collective-permute-start.6) | collective-permute-done | bytes 4128 | tf_op jit(solution)/shard_map/ppermute | solution.py:476
  22.5 0.0 collective-permute-done.5.rest_2_
  22.5 0.0 collective-permute-done.4.rest_1_
  22.5 1.2 %correct.1 = f32[3,16,32,512]{3,2,1,0:T(8,128)} custom-call(f32[8,128]{1,0:T(8,128)S(1)} %get-tuple-element.47.goal_ref, f32[16,32,512]{2,1,0:T(8,128)S(1)} %get-tuple-element.48.unit_ref, f32[3,8,128]{2,1,0:T(8,128)S(1)} %get-tuple-element.54.rest_0_, f32[3,8,128]{2,1,0:T(8,128)S(1)} %collective-permute-done.4.rest_1_, ...), custom_call_target="tpu_custom_call", output_to_operand_aliasing={{}: (7, {})} | custom-call | flops 500000 | bytes 1600000 | tf_op jit(solution)/shard_map/correct/pallas_call | solution.py:579
Async XLA Ops:
  3.5 1.6 %collective-permute-start = (f32[57,8,128]{2,1,0:T(8,128)S(1)}, f32[57,8,128]{2,1,0:T(8,128)S(1)}, u32[]{:S(2)}, u32[]{:S(2)}) collective-permute-start(f32[57,8,128]{2,1,0:T(8,128)S(1)} %get-tuple-element.44.away_ref), channel_id=1, source_target_pairs={{0,4},{1,5},{2,6},{3,7},{4,0},{5,1},{6,2},{7,3},{8,12},{9,13},{10,... | collective-permute-start | bytes 700424 | tf_op jit(solution)/shard_map/ppermute | solution.py:476
  5.2 9.6 %collective-permute-start.1 = (f32[26,8,128]{2,1,0:T(8,128)S(1)}, f32[26,8,128]{2,1,0:T(8,128)S(1)}, u32[]{:S(2)}, u32[]{:S(2)}) collective-permute-start(f32[26,8,128]{2,1,0:T(8,128)S(1)} %get-tuple-element.52), channel_id=1, source_target_pairs={{0,24},{1,25},{2,26},{3,27},{4,28},{5,29},{6,30},{7,31},{8,16},{9,... | collective-permute-start | bytes 319496 | tf_op jit(solution)/shard_map/ppermute | solution.py:476
  9.1 5.5 %collective-permute-start.3 = (f32[25,8,128]{2,1,0:T(8,128)S(1)}, f32[25,8,128]{2,1,0:T(8,128)S(1)}, u32[]{:S(2)}, u32[]{:S(2)}) collective-permute-start(f32[25,8,128]{2,1,0:T(8,128)S(1)} %get-tuple-element.53), channel_id=1, source_target_pairs={{0,16},{1,17},{2,18},{3,19},{4,20},{5,21},{6,22},{7,23},{8,24},{9,... | collective-permute-start | bytes 307208 | tf_op jit(solution)/shard_map/ppermute | solution.py:476
  9.6 5.2 %collective-permute-start.2 = (f32[25,8,128]{2,1,0:T(8,128)S(1)}, f32[25,8,128]{2,1,0:T(8,128)S(1)}, u32[]{:S(2)}, u32[]{:S(2)}) collective-permute-start(f32[25,8,128]{2,1,0:T(8,128)S(1)} %get-tuple-element.46._), channel_id=1, source_target_pairs={{0,8},{1,9},{2,10},{3,11},{4,12},{5,13},{6,14},{7,15},{8,0},{9,1},... | collective-permute-start | bytes 307208 | tf_op jit(solution)/shard_map/ppermute | solution.py:476
  14.9 4.3 %collective-permute-start.7 = (f32[12,8,512]{2,1,0:T(8,128)S(1)}, f32[12,8,512]{2,1,0:T(8,128)S(1)}, u32[]{:S(2)}, u32[]{:S(2)}) collective-permute-start(f32[12,8,512]{2,1,0:T(8,128)S(1)} %get-tuple-element.58), channel_id=1, source_target_pairs={{0,4},{1,5},{2,6},{3,7},{4,0},{5,1},{6,2},{7,3},{8,12},{9,13},{10,... | collective-permute-start | bytes 589832 | tf_op jit(solution)/shard_map/ppermute | solution.py:476
  15.0 7.5 %collective-permute-start.4 = (f32[3,8,128]{2,1,0:T(8,128)S(1)}, f32[3,8,128]{2,1,0:T(8,128)S(1)}, u32[]{:S(2)}, u32[]{:S(2)}) collective-permute-start(f32[3,8,128]{2,1,0:T(8,128)S(1)} %get-tuple-element.54.rest_0_), channel_id=1, source_target_pairs={{0,2},{1,3},{2,1},{3,0},{4,6},{5,7},{6,5},{7,4},{8,10},{9,11},{10,... | collective-permute-start | bytes 36872 | tf_op jit(solution)/shard_map/ppermute | solution.py:476
  17.6 4.8 %collective-permute-start.5 = (f32[2,8,128]{2,1,0:T(8,128)S(1)}, f32[2,8,128]{2,1,0:T(8,128)S(1)}, u32[]{:S(2)}, u32[]{:S(2)}) collective-permute-start(f32[2,8,128]{2,1,0:T(8,128)S(1)} %get-tuple-element.55), channel_id=1, source_target_pairs={{0,3},{1,2},{2,0},{3,1},{4,7},{5,6},{6,4},{7,5},{8,11},{9,10},{10,... | collective-permute-start | bytes 24584 | tf_op jit(solution)/shard_map/ppermute | solution.py:476
  18.9 3.6 %collective-permute-start.6 = (f32[1,8,128]{2,1,0:T(8,128)S(1)}, f32[1,8,128]{2,1,0:T(8,128)S(1)}, u32[]{:S(2)}, u32[]{:S(2)}) collective-permute-start(f32[1,8,128]{2,1,0:T(8,128)S(1)} %get-tuple-element.56), channel_id=1, source_target_pairs={{0,1},{1,0},{2,3},{3,2},{4,5},{5,4},{6,7},{7,6},{8,9},{9,8},{10,11... | collective-permute-start | bytes 12296 | tf_op jit(solution)/shard_map/ppermute | solution.py:476
